TPU v7x, 512 devices: a whole 4x8x8 slice. The times are simulated.
512 devices in a mesh: node: 64 (over z_hi, x, y), local: 8 (over z_lo, core).
Axes of the slice: x: 4, y: 8, z: 8 (z_hi: 2, z_lo: 4; z = z_hi * 4 + z_lo), core: 2. Of those that a mesh axis runs over, the one named last changes fastest.
Arguments:
- tokens: bfloat16 [2048, 8192], P('node', 'local'), may hold values from -6 to 6
- cotangent: bfloat16 [2048, 8192], P('node', 'local'), may hold values from -6 to 6
- gate_weight: bfloat16 [3584, 8192], P('node', 'local'), may hold values from -0.0625 to 0.0625
- up_weight: bfloat16 [3584, 8192], P('node', 'local'), may hold values from -0.0625 to 0.0625
- down_weight: bfloat16 [3584, 8192], P('node', 'local'), may hold values from -0.09375 to 0.09375
- gate_probe: bfloat16 [3584, 8192], P('node', 'local'), may hold values from -6 to 6
- up_probe: bfloat16 [3584, 8192], P('node', 'local'), may hold values from -6 to 6
Outputs:
- gate_diag: float32 [3584, 8192], P('node', 'local')
- up_diag: float32 [3584, 8192], P('node', 'local')
All inputs are finite; a program needn't handle non-finite values.
Results may differ from a plain program's by a relative error of at most 0.0029.
Values may be sent and summed in bfloat16 or wider, within the bound.
No kernel may reach another device: no remote copies, remote signals or barrier semaphores. Data moves between devices by JAX's collectives and lax.ppermute only.
A program may use at most 64 MiB of HBM per device.

v0:
```python
import jax
import jax.numpy as jnp
from jax import lax
from jax.sharding import PartitionSpec as P


def project(weight, rows):
    return lax.dot_general(
        weight, rows, (((1,), (1,)), ((), ())), preferred_element_type=jnp.float32
    )


def factors(pre_gate, pre_up, tan_gate, tan_up, back):
    sig = jax.nn.sigmoid(pre_gate)
    slope = sig * (1.0 + pre_gate * (1.0 - sig))
    bend = sig * (1.0 - sig) * (2.0 + pre_gate * (1.0 - 2.0 * sig))
    fac_gate = (back * (tan_up * slope + pre_up * bend * tan_gate)).astype(jnp.bfloat16)
    fac_up = (back * slope * tan_gate).astype(jnp.bfloat16)
    return (fac_gate, fac_up)


def on_device(tokens, cotangent, gate_weight, up_weight, down_weight, gate_probe, up_probe):
    total = tokens.shape[0] * lax.axis_size("node")
    rows_x, rows_g = (
        lax.all_to_all(tokens, "local", split_axis=0, concat_axis=1, tiled=True),
        lax.all_to_all(cotangent, "local", split_axis=0, concat_axis=1, tiled=True),
    )
    rows_x, rows_g = (
        lax.all_gather(rows_x, "node", axis=0, tiled=True),
        lax.all_gather(rows_g, "node", axis=0, tiled=True),
    )
    w_gate, w_up, w_down, p_gate, p_up = (
        lax.all_gather(gate_weight, "local", axis=1, tiled=True),
        lax.all_gather(up_weight, "local", axis=1, tiled=True),
        lax.all_gather(down_weight, "local", axis=1, tiled=True),
        lax.all_gather(gate_probe, "local", axis=1, tiled=True),
        lax.all_gather(up_probe, "local", axis=1, tiled=True),
    )
    fac_gate, fac_up = factors(
        project(w_gate, rows_x),
        project(w_up, rows_x),
        project(p_gate, rows_x),
        project(p_up, rows_x),
        project(w_down, rows_g),
    )
    part_gate = jnp.dot(fac_gate, rows_x, preferred_element_type=jnp.float32)
    part_up = jnp.dot(fac_up, rows_x, preferred_element_type=jnp.float32)
    hvp_gate, hvp_up = (
        lax.psum_scatter(part_gate, "local", scatter_dimension=1, tiled=True),
        lax.psum_scatter(part_up, "local", scatter_dimension=1, tiled=True),
    )
    gate_diag = gate_probe.astype(jnp.float32) * (hvp_gate / total)
    up_diag = up_probe.astype(jnp.float32) * (hvp_up / total)
    return (gate_diag, up_diag)


def solution(mesh):
    placed = (
        P("node", "local"),
        P("node", "local"),
        P("node", "local"),
        P("node", "local"),
        P("node", "local"),
        P("node", "local"),
        P("node", "local"),
    )
    return jax.shard_map(
        on_device,
        mesh=mesh,
        in_specs=placed,
        out_specs=(P("node", "local"), P("node", "local")),
        check_vma=False,
    )
```

profile of v0, /device:TPU:1, one launch (start us, length us, event | category | flops | bytes accessed | tf_op | source)
XLA Modules:
  0.0 446.3 jit_solution(8831786649256468629)
XLA Ops:
  7.2 0.0 all-gather.7.cloned.1.call-start
  7.2 0.9 all_to_all.32
  8.1 15.0 %all_to_all.38 = bf16[8,4,1024]{2,1,0:T(4,128)(2,1)} all-to-all(bf16[8,4,1024]{2,1,0:T(4,128)(2,1)S(1)} %all_to_all.32), channel_id=1, replica_groups=mesh['node'=64,'local'=8] {'local'}, dimensions={0} | all-to-all | bytes 131072 | tf_op jit(solution)/shard_map/all_to_all | solution.py:25
  23.1 0.0 all-gather.7.cloned.1.call-update
  23.1 0.0 all-gather.5.cloned.1.call-start
  23.2 0.9 all_to_all.28
  24.0 9.0 %all_to_all.39 = bf16[8,4,1024]{2,1,0:T(4,128)(2,1)} all-to-all(bf16[8,4,1024]{2,1,0:T(4,128)(2,1)S(1)} %all_to_all.28), channel_id=1, replica_groups=mesh['node'=64,'local'=8] {'local'}, dimensions={0} | all-to-all | bytes 131072 | tf_op jit(solution)/shard_map/all_to_all | solution.py:26
  33.0 0.0 all-gather.5.cloned.1.call-update
  33.0 0.0 reduce-scatter.5.cloned.1.call-start
  33.1 17.5 %all_gather.25 = bf16[56,8192]{1,0:T(8,128)(2,1)S(1)} all-gather(bf16[56,1024]{1,0:T(8,128)(2,1)} %param.9), channel_id=1, replica_groups=mesh['node'=64,'local'=8] {'local'}, dimensions={1}, use_global_device_ids=true | all-gather | bytes 1032192 | tf_op jit(solution)/shard_map/all_gather | solution.py:33
  50.6 16.9 %all_gather.21 = bf16[56,8192]{1,0:T(8,128)(2,1)S(1)} all-gather(bf16[56,1024]{1,0:T(8,128)(2,1)} %param.11), channel_id=1, replica_groups=mesh['node'=64,'local'=8] {'local'}, dimensions={1}, use_global_device_ids=true | all-gather | bytes 1032192 | tf_op jit(solution)/shard_map/all_gather | solution.py:35
  67.4 16.9 %all_gather.27 = bf16[56,8192]{1,0:T(8,128)(2,1)S(1)} all-gather(bf16[56,1024]{1,0:T(8,128)(2,1)} %param.12), channel_id=1, replica_groups=mesh['node'=64,'local'=8] {'local'}, dimensions={1}, use_global_device_ids=true | all-gather | bytes 1032192 | tf_op jit(solution)/shard_map/all_gather | solution.py:36
  84.3 95.9 %all-gather.7.cloned.1.call-done = bf16[64,4,8192]{2,1,0:T(4,128)(2,1)} async-done(((bf16[1,4,8192]{2,1,0:T(4,128)(2,1)}), bf16[64,4,8192]{2,1,0:T(4,128)(2,1)}) %all-gather.7.cloned.1.call-update) | async-done | bytes 4194320 | tf_op jit(solution)/shard_map/all_gather | solution.py:29
  180.3 6.9 %reshape.13 = bf16[256,8192]{1,0:T(8,128)(2,1)} reshape(bf16[64,4,8192]{2,1,0:T(4,128)(2,1)} %all-gather.7.cloned.1.call-done) | data formatting | bytes 8388608
  187.2 0.0 copy-start
  187.2 3.7 fusion.12
  190.9 0.0 copy-done
  190.9 1.4 fusion.13
  192.3 144.7 %all-gather.5.cloned.1.call-done = bf16[64,4,8192]{2,1,0:T(4,128)(2,1)} async-done(((bf16[1,4,8192]{2,1,0:T(4,128)(2,1)}), bf16[64,4,8192]{2,1,0:T(4,128)(2,1)}) %all-gather.5.cloned.1.call-update) | async-done | bytes 4194320 | tf_op jit(solution)/shard_map/all_gather | solution.py:30
  337.1 6.9 %reshape.11 = bf16[256,8192]{1,0:T(8,128)(2,1)} reshape(bf16[64,4,8192]{2,1,0:T(4,128)(2,1)} %all-gather.5.cloned.1.call-done) | data formatting | bytes 8388608
  344.0 0.0 copy-start.1
  344.0 3.7 fusion.11
  347.7 0.0 copy-done.1
  347.7 0.0 copy-start.4
  347.7 0.0 copy-start.2
  347.7 2.1 fusion.8
  349.8 0.0 reduce-scatter.5.cloned.1.call-update
  349.8 0.0 reduce-scatter.3.cloned.1.call-start
  349.9 0.0 copy-done.4
  349.9 21.4 %all_gather.26 = bf16[56,8192]{1,0:T(8,128)(2,1)S(1)} all-gather(bf16[56,1024]{1,0:T(8,128)(2,1)S(1)} %copy-done.4), channel_id=1, replica_groups=mesh['node'=64,'local'=8] {'local'}, dimensions={1}, use_global_device_ids=true | all-gather | bytes 1032192 | tf_op jit(solution)/shard_map/all_gather | solution.py:34
  371.3 0.0 copy-done.2
  371.3 20.7 %all_gather.23 = bf16[56,8192]{1,0:T(8,128)(2,1)S(1)} all-gather(bf16[56,1024]{1,0:T(8,128)(2,1)S(1)} %copy-done.2), channel_id=1, replica_groups=mesh['node'=64,'local'=8] {'local'}, dimensions={1}, use_global_device_ids=true | all-gather | bytes 1032192 | tf_op jit(solution)/shard_map/all_gather | solution.py:37
  391.9 3.6 fusion
  395.5 0.0 copy-start.3
  395.6 7.7 %fusion.4 = f32[56,8192]{1,0:T(8,128)} fusion(bf16[256,8192]{1,0:T(8,128)(2,1)} %reshape.13, f32[56,256]{1,0:T(8,128)S(1)} %fusion.11, f32[56,256]{1,0:T(8,128)S(1)} %fusion, bf16[56,8192]{1,0:T(8,128)(2,1)S(1)} %all_gather.23, f32[56,256]{1,0:T(8,128)S(1)} %fusion.12), kind=kOutput, calls=%fused_computation.6 | convolution fusion | flops 469919744 | bytes 7118848 | tf_op jit(solution)/shard_map/dot_general | solution.py:46
  403.3 0.0 reduce-scatter.3.cloned.1.call-update
  403.3 0.0 reduce-scatter.5.cloned.1.call-done
  403.3 1.7 multiply_multiply_fusion
  405.0 33.2 %reduce-scatter.3.cloned.1.call-done = f32[56,1024]{1,0:T(8,128)} async-done(((f32[56,8192]{1,0:T(8,128)}), f32[56,1024]{1,0:T(8,128)}) %reduce-scatter.3.cloned.1.call-update) | async-done | bytes 229392 | tf_op jit(solution)/shard_map/reduce_scatter | solution.py:49
  438.1 0.0 copy-done.3
  438.1 1.7 multiply_multiply_fusion.1
Async XLA Ops:
  7.2 173.1 %all-gather.7.cloned.1.call-start = ((), (), s32[]{:S(2)}) async-start(), calls=%async_computation.7 | async-start | bytes 4259840 | tf_op jit(solution)/shard_map/all_gather | solution.py:29
  23.1 313.9 %all-gather.5.cloned.1.call-start = ((), (), s32[]{:S(2)}) async-start(), calls=%async_computation.6 | async-start | bytes 4259840 | tf_op jit(solution)/shard_map/all_gather | solution.py:30
  33.0 370.3 %reduce-scatter.5.cloned.1.call-start = ((), (), s32[]{:S(2)}) async-start(), calls=%async_computation.5 | async-start | bytes 2064384 | tf_op jit(solution)/shard_map/reduce_scatter | solution.py:50
  187.2 3.7 copy-start
  344.0 3.7 copy-start.1
  347.7 2.2 copy-start.4
  347.7 23.6 %copy-start.2 = (bf16[56,1024]{1,0:T(8,128)(2,1)S(1)}, bf16[56,1024]{1,0:T(8,128)(2,1)}, u32[]{:S(2)}) copy-start(bf16[56,1024]{1,0:T(8,128)(2,1)} %param.13) | copy-start | bytes 344068
  349.8 88.3 %reduce-scatter.3.cloned.1.call-start = ((), (), s32[]{:S(2)}) async-start(), calls=%async_computation.4 | async-start | bytes 2064384 | tf_op jit(solution)/shard_map/reduce_scatter | solution.py:49
  395.5 42.6 %copy-start.3 = (bf16[56,1024]{1,0:T(8,128)(2,1)S(1)}, bf16[56,1024]{1,0:T(8,128)(2,1)}, u32[]{:S(2)}) copy-start(bf16[56,1024]{1,0:T(8,128)(2,1)} %param.12) | copy-start | bytes 344068
Sparse Core Ops, SparseCore 0:
  23.2 156.9 all-gather.6
  184.8 152.2 all-gather.4
  349.9 43.2 reduce-scatter.4
  403.4 34.6 reduce-scatter.2
where the time goes:
time: 449 us; the launch traced here: 446 us
  waiting for transfers between devices  274 us (61%)
  blocking collectives  117 us (26%)
  matrix products  22.3 us (5%)
  local copies, waits for them, and re-layouts  15.6 us (3%)
  between operations  13.8 us (3%)
    all_gather x1, waiting for transfers between devices, on_device(): lax.all_gather(rows_g, 'node', axis=0, tiled=True)  145 us
    all_gather x1, waiting for transfers between devices, on_device(): lax.all_gather(rows_x, 'node', axis=0, tiled=True)  95.9 us
    reduce_scatter x1, waiting for transfers between devices, on_device(): lax.psum_scatter(part_gate, 'local', scatter_dimension=1, tiled=True)  33.2 us
    all_gather x1, blocking collectives, on_device(): lax.all_gather(up_weight, 'local', axis=1, tiled=True)  21.4 us
    all_gather x1, blocking collectives, on_device(): lax.all_gather(up_probe, 'local', axis=1, tiled=True)  20.7 us
    all_gather x1, blocking collectives, on_device(): lax.all_gather(gate_weight, 'local', axis=1, tiled=True)  17.5 us
    all_gather x1, blocking collectives, on_device(): lax.all_gather(gate_probe, 'local', axis=1, tiled=True)  16.9 us
    all_gather x1, blocking collectives, on_device(): lax.all_gather(down_weight, 'local', axis=1, tiled=True)  16.9 us
  transfers between devices with their start and end apart: 4, of which 3 were waited for; matrix products, arithmetic and copies ran while one was open for 6% of the time, Pallas kernels for 0%

commit v1 on v0

v1 whole, which is shorter than its diff:
```python
import jax
import jax.numpy as jnp
from jax import lax
from jax.sharding import Mesh, PartitionSpec as P

NODE = {"zh": 2, "x": 4, "y": 8}
LOCAL = {"zl": 4, "c": 2}

PRE_SCALE = 64.0
TAN_SCALE = 0.5
BACK_SCALE = 32.0


def swap(value, axis):
    return lax.ppermute(value, axis, [(0, 1), (1, 0)])


def shift(value, axis, by):
    size = lax.axis_size(axis)
    return lax.ppermute(value, axis, [(i, (i + by) % size) for i in range(size)])


def ring_blocks(block, axis):
    size = lax.axis_size(axis)
    half = block.shape[0] // 2
    ahead = behind = block
    blocks = [block]
    for _ in range(size // 2 - 1):
        ahead, behind = shift(ahead, axis, 1), shift(behind, axis, -1)
        blocks += [ahead, behind]
    far = (shift(ahead[:half], axis, 1), shift(behind[half:], axis, -1))
    blocks.append(jnp.concatenate(far, axis=0))
    return blocks


def project(rows, weight):
    return lax.dot_general(
        rows, weight, (((1,), (1,)), ((), ())), preferred_element_type=jnp.float32
    )


def factors(pre_gate, pre_up, tan_gate, tan_up, back):
    sig = jax.nn.sigmoid(pre_gate)
    slope = sig * (1.0 + pre_gate * (1.0 - sig))
    bend = sig * (1.0 - sig) * (2.0 + pre_gate * (1.0 - 2.0 * sig))
    fac_gate = (back * (tan_up * slope + pre_up * bend * tan_gate)).astype(jnp.bfloat16)
    fac_up = (back * slope * tan_gate).astype(jnp.bfloat16)
    return (fac_gate, fac_up)


def on_device(tokens, cotangent, gate_weight, up_weight, down_weight, gate_probe, up_probe):
    nx, nzl, nc = lax.axis_size("x"), lax.axis_size("zl"), lax.axis_size("c")
    own, feats = tokens.shape
    hid = gate_weight.shape[0]
    total = own * lax.axis_size(("zh", "x", "y"))
    core = lax.axis_index("c")

    mats = jnp.concatenate([gate_weight, up_weight, gate_probe, up_probe, down_weight], axis=0)
    mats = lax.all_gather(mats, "x", axis=0, tiled=False)
    mats = mats.reshape(nx, 5, hid, feats).transpose(1, 0, 2, 3).reshape(5 * nx * hid, feats)
    w_tok, w_cot = mats[: 4 * nx * hid], mats[4 * nx * hid :]

    rows = jnp.concatenate([tokens, cotangent], axis=0)
    rows = jnp.stack([rows, swap(rows, "zh")], axis=0)
    blocks = ring_blocks(rows, "y")
    x_rows = jnp.concatenate([b[:, :own] for b in blocks], axis=0).reshape(-1, feats)
    g_rows = jnp.concatenate([b[:, own:] for b in blocks], axis=0).reshape(-1, feats)
    x_all = lax.all_gather(x_rows, "x", axis=0, tiled=True)

    count = x_rows.shape[0] // nc
    def term(which):
        x_half = lax.dynamic_slice_in_dim(x_rows, which * count, count, 0)
        g_half = lax.dynamic_slice_in_dim(g_rows, which * count, count, 0)
        return jnp.concatenate([project(x_half, w_tok), project(g_half, w_cot)], axis=1)
    other = swap(term(1 - core), "c")
    terms = term(core) + other

    width = nx * hid
    scale = jnp.repeat(
        jnp.array([PRE_SCALE, PRE_SCALE, TAN_SCALE, TAN_SCALE, BACK_SCALE], jnp.float32), width
    )[None, :]
    sent = (terms * scale).astype(jnp.float16)
    got = lax.all_to_all(sent.reshape(nzl, count // nzl, 5 * width), "zl", 0, 0, tiled=True)
    proj = jnp.sum(got.astype(jnp.float32), axis=0) * (1.0 / scale)
    parts = [proj[:, i * width : (i + 1) * width] for i in range(5)]
    fac_gate, fac_up = factors(*parts)

    share = count // nzl
    fac = jnp.stack([fac_gate, fac_up], axis=1).reshape(share, 2, nx, hid)
    fac = fac.transpose(2, 0, 1, 3).reshape(nx, 1, share, 2 * hid)
    fac = jnp.broadcast_to(fac, (nx, nzl, share, 2 * hid)).reshape(nx * nzl, share, 2 * hid)
    fac = lax.all_to_all(fac, ("x", "zl"), 0, 0, tiled=True)
    fac = fac.reshape(nx, 1, count, 2 * hid)
    fac_other = swap(fac, "c")
    fac = jnp.where(
        core == 0,
        jnp.concatenate([fac, fac_other], axis=1),
        jnp.concatenate([fac_other, fac], axis=1),
    ).reshape(-1, 2 * hid)

    hvp = lax.dot_general(
        fac, x_all, (((0,), (0,)), ((), ())), preferred_element_type=jnp.float32
    ) / total
    gate_diag = gate_probe.astype(jnp.float32) * hvp[:hid]
    up_diag = up_probe.astype(jnp.float32) * hvp[hid:]
    return (gate_diag, up_diag)


def solution(mesh):
    sizes = {**NODE, **LOCAL}
    cut = Mesh(mesh.devices.reshape(tuple(sizes.values())), tuple(sizes))
    placed = P(tuple(NODE), tuple(LOCAL))
    return jax.shard_map(
        on_device,
        mesh=cut,
        in_specs=(placed,) * 7,
        out_specs=(placed, placed),
        check_vma=False,
    )
```

time: 449 us -> 146 us (0.33)
  waiting for transfers between devices: 274 us -> 28.1 us
  blocking collectives: 117 us -> 14.2 us
  starting transfers between devices: 0.16 us -> 59.2 us
  matrix products: 22.3 us -> 7.85 us
    all_gather x2, waiting for transfers between devices: 241 us -> 0.04 us  [the longest x1 0.02 us: on_device(): x_all = lax.all_gather(x_rows, 'x', axis=0, tiled=True)]
    all_gather x5 -> x0, blocking collectives: 93.3 us -> none  [the longest x1 21.4 us: on_device(): lax.all_gather(up_weight, 'local', axis=1, tiled=True)]
    ppermute x0 -> x11, starting transfers between devices: none -> 50.5 us  [the longest x8 26.9 us: shift(): lax.ppermute(value, axis, [(i, (i + by) % size) for i in range(size)])]
    reduce_scatter x2 -> x0, waiting for transfers between devices: 33.2 us -> none  [the longest x1 33.2 us: on_device(): lax.psum_scatter(part_gate, 'local', scatter_dimension=1, tiled=True)]
    all_to_all x0 -> x1, waiting for transfers between devices: none -> 15.8 us  [on_device(): lax.all_to_all(sent.reshape(nzl, count // nzl, 5 * width), 'zl', 0, 0, ti...]
    dot_general x6 -> x5, matrix products: 22.3 us -> 7.85 us  [the longest x4 4.84 us: project(): lax.dot_general(rows, weight, (((1,), (1,)), ((), ())), preferred_element...]
    ppermute x0 -> x11, waiting for transfers between devices: none -> 12.2 us  [the longest x8 7.18 us: shift(): lax.ppermute(value, axis, [(i, (i + by) % size) for i in range(size)])]
    all_to_all x2 -> x1, blocking collectives: 24 us -> 14.2 us  [on_device(): fac = lax.all_to_all(fac, ('x', 'zl'), 0, 0, tiled=True)]
  transfers between devices with their start and end apart: 4 -> 14, of which waited for: 3 -> 8; matrix products, arithmetic and copies ran while one was open for 6% -> 11% of each run, Pallas kernels for 0% -> 0%
where the time goes in v1:
time: 146 us; the launch traced here: 144 us
  starting transfers between devices  59.2 us (41%)
  waiting for transfers between devices  28.1 us (19%)
  local copies, waits for them, and re-layouts  16.5 us (11%)
  between operations  14.5 us (10%)
  blocking collectives  14.2 us (10%)
  matrix products  7.85 us (5%)
  other arithmetic  3.51 us (2%)
    ppermute x8, starting transfers between devices, shift(): lax.ppermute(value, axis, [(i, (i + by) % size) for i in range(size)])  26.9 us
    ppermute x3, starting transfers between devices, swap(): return lax.ppermute(value, axis, [(0, 1), (1, 0)])  23.5 us
    all_to_all x1, waiting for transfers between devices, on_device(): lax.all_to_all(sent.reshape(nzl, count // nzl, 5 * width), 'zl', 0, 0, ti...  15.8 us
    all_to_all x1, blocking collectives, on_device(): fac = lax.all_to_all(fac, ('x', 'zl'), 0, 0, tiled=True)  14.2 us
    all_to_all x1, starting transfers between devices, on_device(): lax.all_to_all(sent.reshape(nzl, count // nzl, 5 * width), 'zl', 0, 0, ti...  8.68 us
    unnamed x36, local copies, waits for them, and re-layouts  7.71 us
    ppermute x8, waiting for transfers between devices, shift(): lax.ppermute(value, axis, [(i, (i + by) % size) for i in range(size)])  7.18 us
    ppermute x3, waiting for transfers between devices, swap(): return lax.ppermute(value, axis, [(0, 1), (1, 0)])  5.03 us
  transfers between devices with their start and end apart: 14, of which 8 were waited for; matrix products, arithmetic and copies ran while one was open for 11% of the time, Pallas kernels for 0%

profile of v1, /device:TPU:1, one launch (start us, length us, event | category | flops | bytes accessed | tf_op | source)
XLA Modules:
  0.0 143.9 jit_solution(9337783405879391127)
XLA Ops:
  7.2 0.0 all-gather.6.cloned.1.call-start
  7.2 0.9 constant_dynamic-update-slice_fusion.8
  8.1 0.9 constant_dynamic-update-slice_fusion.7
  9.0 0.9 constant_dynamic-update-slice_fusion.6
  10.0 0.9 constant_dynamic-update-slice_fusion.5
  10.9 0.9 constant_dynamic-update-slice_fusion.4
  11.8 0.8 copy-done.6
  12.6 0.0 all-gather.6.cloned.1.call-update
  12.6 0.0 all-gather.4.cloned.1.call-start
  12.7 11.5 %collective-permute-start = (bf16[64,1024]{1,0:T(8,128)(2,1)S(1)}, bf16[64,1024]{1,0:T(8,128)(2,1)S(1)}, u32[]{:S(2)}, u32[]{:S(2)}) collective-permute-start(bf16[64,1024]{1,0:T(8,128)(2,1)S(1)} %constant_dynamic-update-slice_fusion), channel_id=1, source_target_pairs={{0,256},{256,0},{1,257},{257,1},{2,258},{258,2},{3,259},{259,3},{4... | collective-permute-start | bytes 393224 | tf_op jit(solution)/shard_map/ppermute | solution.py:15
  24.2 3.9 %collective-permute-done = bf16[64,1024]{1,0:T(8,128)(2,1)S(1)} collective-permute-done((bf16[64,1024]{1,0:T(8,128)(2,1)S(1)}, bf16[64,1024]{1,0:T(8,128)(2,1)S(1)}, u32[]{:S(2)}, u32[]{:S(2)}) %collective-permute-start) | collective-permute-done | bytes 131104 | tf_op jit(solution)/shard_map/ppermute | solution.py:15
  28.1 2.5 %collective-permute-start.1 = (bf16[2,64,1024]{2,1,0:T(8,128)(2,1)S(1)}, bf16[2,64,1024]{2,1,0:T(8,128)(2,1)S(1)}, u32[]{:S(2)}, u32[]{:S(2)}) collective-permute-start(bf16[2,64,1024]{2,1,0:T(8,128)(2,1)S(1)} %pad_maximum_fusion.1), channel_id=1, source_target_pairs={{0,8},{8,16},{16,24},{24,32},{32,40},{40,48},{48,56},{56,0},{1,9},... | collective-permute-start | bytes 786440 | tf_op jit(solution)/shard_map/ppermute | solution.py:20
  30.6 4.0 %collective-permute-start.2 = (bf16[2,64,1024]{2,1,0:T(8,128)(2,1)S(1)}, bf16[2,64,1024]{2,1,0:T(8,128)(2,1)S(1)}, u32[]{:S(2)}, u32[]{:S(2)}) collective-permute-start(bf16[2,64,1024]{2,1,0:T(8,128)(2,1)S(1)} %pad_maximum_fusion.1), channel_id=1, source_target_pairs={{0,56},{8,0},{16,8},{24,16},{32,24},{40,32},{48,40},{56,48},{1,57}... | collective-permute-start | bytes 786440 | tf_op jit(solution)/shard_map/ppermute | solution.py:20
  34.7 1.8 %collective-permute-done.1 = bf16[2,64,1024]{2,1,0:T(8,128)(2,1)S(1)} collective-permute-done((bf16[2,64,1024]{2,1,0:T(8,128)(2,1)S(1)}, bf16[2,64,1024]{2,1,0:T(8,128)(2,1)S(1)}, u32[]{:S(2)}, u32[]{:S(2)}) %collective-permute-start.1) | collective-permute-done | bytes 262176 | tf_op jit(solution)/shard_map/ppermute | solution.py:20
  36.4 2.4 %collective-permute-start.3 = (bf16[2,64,1024]{2,1,0:T(8,128)(2,1)S(1)}, bf16[2,64,1024]{2,1,0:T(8,128)(2,1)S(1)}, u32[]{:S(2)}, u32[]{:S(2)}) collective-permute-start(bf16[2,64,1024]{2,1,0:T(8,128)(2,1)S(1)} %collective-permute-done.1), channel_id=1, source_target_pairs={{0,8},{8,16},{16,24},{24,32},{32,40},{40,48},{48,56},{56,0},{1,9},... | collective-permute-start | bytes 786440 | tf_op jit(solution)/shard_map/ppermute | solution.py:20
  38.8 0.0 collective-permute-done.2
  38.8 4.5 %collective-permute-start.4 = (bf16[2,64,1024]{2,1,0:T(8,128)(2,1)S(1)}, bf16[2,64,1024]{2,1,0:T(8,128)(2,1)S(1)}, u32[]{:S(2)}, u32[]{:S(2)}) collective-permute-start(bf16[2,64,1024]{2,1,0:T(8,128)(2,1)S(1)} %collective-permute-done.2), channel_id=1, source_target_pairs={{0,56},{8,0},{16,8},{24,16},{32,24},{40,32},{48,40},{56,48},{1,57}... | collective-permute-start | bytes 786440 | tf_op jit(solution)/shard_map/ppermute | solution.py:20
  43.4 1.8 %collective-permute-done.3 = bf16[2,64,1024]{2,1,0:T(8,128)(2,1)S(1)} collective-permute-done((bf16[2,64,1024]{2,1,0:T(8,128)(2,1)S(1)}, bf16[2,64,1024]{2,1,0:T(8,128)(2,1)S(1)}, u32[]{:S(2)}, u32[]{:S(2)}) %collective-permute-start.3) | collective-permute-done | bytes 262176 | tf_op jit(solution)/shard_map/ppermute | solution.py:20
  45.2 1.9 %collective-permute-start.5 = (bf16[2,64,1024]{2,1,0:T(8,128)(2,1)S(1)}, bf16[2,64,1024]{2,1,0:T(8,128)(2,1)S(1)}, u32[]{:S(2)}, u32[]{:S(2)}) collective-permute-start(bf16[2,64,1024]{2,1,0:T(8,128)(2,1)S(1)} %collective-permute-done.3), channel_id=1, source_target_pairs={{0,8},{8,16},{16,24},{24,32},{32,40},{40,48},{48,56},{56,0},{1,9},... | collective-permute-start | bytes 786440 | tf_op jit(solution)/shard_map/ppermute | solution.py:20
  47.1 0.0 collective-permute-done.4
  47.1 5.0 %collective-permute-start.6 = (bf16[2,64,1024]{2,1,0:T(8,128)(2,1)S(1)}, bf16[2,64,1024]{2,1,0:T(8,128)(2,1)S(1)}, u32[]{:S(2)}, u32[]{:S(2)}) collective-permute-start(bf16[2,64,1024]{2,1,0:T(8,128)(2,1)S(1)} %collective-permute-done.4), channel_id=1, source_target_pairs={{0,56},{8,0},{16,8},{24,16},{32,24},{40,32},{48,40},{56,48},{1,57}... | collective-permute-start | bytes 786440 | tf_op jit(solution)/shard_map/ppermute | solution.py:20
  52.1 1.8 %collective-permute-done.5 = bf16[2,64,1024]{2,1,0:T(8,128)(2,1)S(1)} collective-permute-done((bf16[2,64,1024]{2,1,0:T(8,128)(2,1)S(1)}, bf16[2,64,1024]{2,1,0:T(8,128)(2,1)S(1)}, u32[]{:S(2)}, u32[]{:S(2)}) %collective-permute-start.5) | collective-permute-done | bytes 262176 | tf_op jit(solution)/shard_map/ppermute | solution.py:20
  53.9 1.9 %collective-permute-start.7 = (bf16[1,64,1024]{2,1,0:T(8,128)(2,1)S(1)}, bf16[1,64,1024]{2,1,0:T(8,128)(2,1)S(1)}, u32[]{:S(2)}, u32[]{:S(2)}) collective-permute-start(bf16[1,64,1024]{2,1,0:T(8,128)(2,1)S(1)} %slice.124), channel_id=1, source_target_pairs={{0,8},{8,16},{16,24},{24,32},{32,40},{40,48},{48,56},{56,0},{1,9},... | collective-permute-start | bytes 393224 | tf_op jit(solution)/shard_map/ppermute | solution.py:20
  55.8 4.8 %collective-permute-start.8 = (bf16[1,64,1024]{2,1,0:T(8,128)(2,1)S(1)}, bf16[1,64,1024]{2,1,0:T(8,128)(2,1)S(1)}, u32[]{:S(2)}, u32[]{:S(2)}) collective-permute-start(bf16[1,64,1024]{2,1,0:T(8,128)(2,1)S(1)} %slice.125), channel_id=1, source_target_pairs={{0,56},{8,0},{16,8},{24,16},{32,24},{40,32},{48,40},{56,48},{1,57}... | collective-permute-start | bytes 393224 | tf_op jit(solution)/shard_map/ppermute | solution.py:20
  60.7 0.1 collective-permute-done.7
  60.8 1.7 %collective-permute-done.8 = bf16[1,64,1024]{2,1,0:T(8,128)(2,1)S(1)} collective-permute-done((bf16[1,64,1024]{2,1,0:T(8,128)(2,1)S(1)}, bf16[1,64,1024]{2,1,0:T(8,128)(2,1)S(1)}, u32[]{:S(2)}, u32[]{:S(2)}) %collective-permute-start.8) | collective-permute-done | bytes 131104 | tf_op jit(solution)/shard_map/ppermute | solution.py:20
  62.6 1.0 copy-done.3
  63.6 1.0 copy-done
  64.6 0.0 all-gather.4.cloned.1.call-update
  64.6 0.0 all-gather.6.cloned.1.call-done
  64.7 1.1 slice.137
  65.7 1.6 %slice.127 = bf16[4,4,56,1024]{3,2,0,1:T(8,128)(2,1)S(1)} slice(bf16[5,4,56,1024]{3,2,0,1:T(8,128)(2,1)} %bitcast.29), slice={[0:4], [0:4], [0:56], [0:1024]} | slice | bytes 3670016 | tf_op jit(solution)/shard_map/slice | solution.py:61
  67.4 0.1 copy.19
  67.5 1.1 copy-done.4
  68.6 0.3 fusion.2
  68.9 0.0 copy-done.1
  69.0 0.7 fusion.4
  69.7 1.2 pad_maximum_fusion
  70.9 2.7 %copy.22 = f32[256,1120]{0,1:T(8,128)} copy(f32[256,1120]{1,0:T(8,128)} %pad_maximum_fusion) | data formatting | bytes 2293760 | tf_op jit(solution)/shard_map/concatenate | solution.py:74
  73.5 7.9 %collective-permute-start.9 = (f32[256,1120]{0,1:T(8,128)}, f32[256,1120]{0,1:T(8,128)}, u32[]{:S(2)}, u32[]{:S(2)}) collective-permute-start(f32[256,1120]{0,1:T(8,128)} %copy.22), channel_id=1, source_target_pairs={{0,1},{1,0},{2,3},{3,2},{4,5},{5,4},{6,7},{7,6},{8,9},{9,8},{10,11... | collective-permute-start | bytes 3440648 | tf_op jit(solution)/shard_map/ppermute | solution.py:15
  81.4 0.1 broadcast_in_dim.10
  81.5 0.1 mul.70
  81.6 2.1 %fusion.6 = f32[256,224]{1,0:T(8,128)} fusion(bf16[224,1024]{1,0:T(8,128)(2,1)S(1)} %bitcast.27, bf16[512,1024]{1,0:T(8,128)(2,1)} %bitcast.31, s32[]{:T(128)S(6)} %select_n.21), kind=kOutput, calls=%fused_computation.11 | convolution fusion | flops 117440512 | bytes 1212420 | tf_op jit(solution)/shard_map/dot_general | solution.py:37
  83.7 1.7 %fusion.8 = f32[256,896]{1,0:T(8,128)} fusion(bf16[896,1024]{1,0:T(8,128)(2,1)S(1)} %bitcast.22, bf16[512,1024]{1,0:T(8,128)(2,1)S(1)} %bitcast.25, s32[]{:T(128)S(6)} %select_n.21), kind=kOutput, calls=%fused_computation.13 | convolution fusion | flops 469762048 | bytes 3276804 | tf_op jit(solution)/shard_map/dot_general | solution.py:37
  85.4 1.7 %copy.23 = f32[256,1120]{1,0:T(8,128)S(1)} copy(f32[256,1120]{0,1:T(8,128)} %collective-permute-done.9) | data formatting | bytes 2293760 | tf_op jit(solution)/shard_map/ppermute | solution.py:15
  87.1 1.0 fusion.1
  88.1 8.7 %all-to-all-start = ((f16[4,64,1120]{2,1,0:T(8,128)(2,1)}), f16[4,64,1120]{2,1,0:T(8,128)(2,1)S(1)}, u32[]{:S(2)}, u32[]{:S(2)}) async-start(f16[4,64,1120]{2,1,0:T(8,128)(2,1)} %bitcast.9), calls=%async_computation | async-start | bytes 1179648 | tf_op jit(solution)/shard_map/all_to_all | solution.py:83
  96.7 15.8 %all-to-all-done = f16[4,64,1120]{2,1,0:T(8,128)(2,1)S(1)} async-done(((f16[4,64,1120]{2,1,0:T(8,128)(2,1)}), f16[4,64,1120]{2,1,0:T(8,128)(2,1)S(1)}, u32[]{:S(2)}, u32[]{:S(2)}) %all-to-all-start) | async-done | bytes 573472 | tf_op jit(solution)/shard_map/all_to_all | solution.py:83
  112.6 0.1 convert_reduce_fusion
  112.7 0.1 fusion.21
  112.8 0.1 stack.22
  112.9 0.1 stack.21
  113.0 0.1 maximum_bitcast_fusion
  113.2 0.1 copy.24
  113.3 0.1 broadcast_in_dim.11
  113.5 14.2 %all_to_all.10 = bf16[16,64,112]{2,1,0:T(8,128)(2,1)S(1)} all-to-all(bf16[16,64,112]{2,1,0:T(8,128)(2,1)S(1)} %bitcast.33), channel_id=1, replica_groups=mesh['zh'=2,'x'=4,'y'=8,'zl'=4,'c'=2] {'x','zl'}, dimensions={0} | all-to-all | bytes 458752 | tf_op jit(solution)/shard_map/all_to_all | solution.py:92
  127.6 4.2 %collective-permute-start.10 = (bf16[4,1,256,112]{3,2,1,0:T(8,128)(2,1)S(1)}, bf16[4,1,256,112]{3,2,1,0:T(8,128)(2,1)S(1)}, u32[]{:S(2)}, u32[]{:S(2)}) collective-permute-start(bf16[4,1,256,112]{3,2,1,0:T(8,128)(2,1)S(1)} %bitcast.34), channel_id=1, source_target_pairs={{0,1},{1,0},{2,3},{3,2},{4,5},{5,4},{6,7},{7,6},{8,9},{9,8},{10,11... | collective-permute-start | bytes 688136 | tf_op jit(solution)/shard_map/ppermute | solution.py:15
  131.9 1.1 collective-permute-done.10
  133.0 0.2 maximum_select_fusion
  133.2 0.0 all-gather.4.cloned.1.call-done
  133.2 0.0 copy-start.7
  133.2 0.0 copy-start.8
  133.2 3.0 %convolution_multiply_fusion = f32[112,1024]{1,0:T(8,128)S(1)} fusion(bf16[2048,112]{1,0:T(8,128)(2,1)S(1)} %bitcast.30, bf16[2048,1024]{1,0:T(8,128)(2,1)} %all-gather.4.cloned.1.call-done), kind=kOutput, calls=%fused_computation | convolution fusion | flops 469876736 | bytes 5111808 | tf_op jit(solution)/shard_map/dot_general | solution.py:101
  136.3 0.8 slice_multiply_fusion
  (37 shorter events, 0.3 us)
Async XLA Ops:
  7.2 5.5 %copy-start.9 = (bf16[32,1024]{1,0:T(8,128)(2,1)S(1)}, bf16[32,1024]{1,0:T(8,128)(2,1)}, u32[]{:S(2)}) copy-start(bf16[32,1024]{1,0:T(8,128)(2,1)} %param.8) | copy-start | bytes 196612
  7.2 5.5 %copy-start.10 = (bf16[32,1024]{1,0:T(8,128)(2,1)S(1)}, bf16[32,1024]{1,0:T(8,128)(2,1)}, u32[]{:S(2)}) copy-start(bf16[32,1024]{1,0:T(8,128)(2,1)} %param.9) | copy-start | bytes 196612
  7.2 57.5 %all-gather.6.cloned.1.call-start = ((), (), s32[]{:S(2)}) async-start(), calls=%async_computation.3 | async-start | bytes 2867200 | tf_op jit(solution)/shard_map/all_gather | solution.py:59
  11.8 0.8 copy-start.6
  12.6 120.6 %all-gather.4.cloned.1.call-start = ((), (), s32[]{:S(2)}) async-start(), calls=%async_computation.2 | async-start | bytes 5242880 | tf_op jit(solution)/shard_map/all_gather | solution.py:68
  12.7 15.4 %collective-permute-start = (bf16[64,1024]{1,0:T(8,128)(2,1)S(1)}, bf16[64,1024]{1,0:T(8,128)(2,1)S(1)}, u32[]{:S(2)}, u32[]{:S(2)}) collective-permute-start(bf16[64,1024]{1,0:T(8,128)(2,1)S(1)} %constant_dynamic-update-slice_fusion), channel_id=1, source_target_pairs={{0,256},{256,0},{1,257},{257,1},{2,258},{258,2},{3,259},{259,3},{4... | collective-permute-start | bytes 393224 | tf_op jit(solution)/shard_map/ppermute | solution.py:15
  28.1 8.3 %collective-permute-start.1 = (bf16[2,64,1024]{2,1,0:T(8,128)(2,1)S(1)}, bf16[2,64,1024]{2,1,0:T(8,128)(2,1)S(1)}, u32[]{:S(2)}, u32[]{:S(2)}) collective-permute-start(bf16[2,64,1024]{2,1,0:T(8,128)(2,1)S(1)} %pad_maximum_fusion.1), channel_id=1, source_target_pairs={{0,8},{8,16},{16,24},{24,32},{32,40},{40,48},{48,56},{56,0},{1,9},... | collective-permute-start | bytes 786440 | tf_op jit(solution)/shard_map/ppermute | solution.py:20
  30.6 8.2 %collective-permute-start.2 = (bf16[2,64,1024]{2,1,0:T(8,128)(2,1)S(1)}, bf16[2,64,1024]{2,1,0:T(8,128)(2,1)S(1)}, u32[]{:S(2)}, u32[]{:S(2)}) collective-permute-start(bf16[2,64,1024]{2,1,0:T(8,128)(2,1)S(1)} %pad_maximum_fusion.1), channel_id=1, source_target_pairs={{0,56},{8,0},{16,8},{24,16},{32,24},{40,32},{48,40},{56,48},{1,57}... | collective-permute-start | bytes 786440 | tf_op jit(solution)/shard_map/ppermute | solution.py:20
  36.4 8.7 %collective-permute-start.3 = (bf16[2,64,1024]{2,1,0:T(8,128)(2,1)S(1)}, bf16[2,64,1024]{2,1,0:T(8,128)(2,1)S(1)}, u32[]{:S(2)}, u32[]{:S(2)}) collective-permute-start(bf16[2,64,1024]{2,1,0:T(8,128)(2,1)S(1)} %collective-permute-done.1), channel_id=1, source_target_pairs={{0,8},{8,16},{16,24},{24,32},{32,40},{40,48},{48,56},{56,0},{1,9},... | collective-permute-start | bytes 786440 | tf_op jit(solution)/shard_map/ppermute | solution.py:20
  38.8 8.2 %collective-permute-start.4 = (bf16[2,64,1024]{2,1,0:T(8,128)(2,1)S(1)}, bf16[2,64,1024]{2,1,0:T(8,128)(2,1)S(1)}, u32[]{:S(2)}, u32[]{:S(2)}) collective-permute-start(bf16[2,64,1024]{2,1,0:T(8,128)(2,1)S(1)} %collective-permute-done.2), channel_id=1, source_target_pairs={{0,56},{8,0},{16,8},{24,16},{32,24},{40,32},{48,40},{56,48},{1,57}... | collective-permute-start | bytes 786440 | tf_op jit(solution)/shard_map/ppermute | solution.py:20
  45.2 8.7 %collective-permute-start.5 = (bf16[2,64,1024]{2,1,0:T(8,128)(2,1)S(1)}, bf16[2,64,1024]{2,1,0:T(8,128)(2,1)S(1)}, u32[]{:S(2)}, u32[]{:S(2)}) collective-permute-start(bf16[2,64,1024]{2,1,0:T(8,128)(2,1)S(1)} %collective-permute-done.3), channel_id=1, source_target_pairs={{0,8},{8,16},{16,24},{24,32},{32,40},{40,48},{48,56},{56,0},{1,9},... | collective-permute-start | bytes 786440 | tf_op jit(solution)/shard_map/ppermute | solution.py:20
  47.1 8.7 %collective-permute-start.6 = (bf16[2,64,1024]{2,1,0:T(8,128)(2,1)S(1)}, bf16[2,64,1024]{2,1,0:T(8,128)(2,1)S(1)}, u32[]{:S(2)}, u32[]{:S(2)}) collective-permute-start(bf16[2,64,1024]{2,1,0:T(8,128)(2,1)S(1)} %collective-permute-done.4), channel_id=1, source_target_pairs={{0,56},{8,0},{16,8},{24,16},{32,24},{40,32},{48,40},{56,48},{1,57}... | collective-permute-start | bytes 786440 | tf_op jit(solution)/shard_map/ppermute | solution.py:20
  53.9 6.9 %collective-permute-start.7 = (bf16[1,64,1024]{2,1,0:T(8,128)(2,1)S(1)}, bf16[1,64,1024]{2,1,0:T(8,128)(2,1)S(1)}, u32[]{:S(2)}, u32[]{:S(2)}) collective-permute-start(bf16[1,64,1024]{2,1,0:T(8,128)(2,1)S(1)} %slice.124), channel_id=1, source_target_pairs={{0,8},{8,16},{16,24},{24,32},{32,40},{40,48},{48,56},{56,0},{1,9},... | collective-permute-start | bytes 393224 | tf_op jit(solution)/shard_map/ppermute | solution.py:20
  55.8 6.7 %collective-permute-start.8 = (bf16[1,64,1024]{2,1,0:T(8,128)(2,1)S(1)}, bf16[1,64,1024]{2,1,0:T(8,128)(2,1)S(1)}, u32[]{:S(2)}, u32[]{:S(2)}) collective-permute-start(bf16[1,64,1024]{2,1,0:T(8,128)(2,1)S(1)} %slice.125), channel_id=1, source_target_pairs={{0,56},{8,0},{16,8},{24,16},{32,24},{40,32},{48,40},{56,48},{1,57}... | collective-permute-start | bytes 393224 | tf_op jit(solution)/shard_map/ppermute | solution.py:20
  62.6 1.0 copy-start.3
  63.6 1.0 copy-start
  67.4 1.2 copy-start.4
  67.5 1.4 copy-start.1
  70.9 10.5 %copy-start.11 = (f32[5]{0:T(128)S(1)}, f32[5]{0:T(128)}, u32[]{:S(2)}) copy-start(f32[5]{0:T(128)} %constant.24.clone) | copy-start | bytes 64
  73.5 11.8 %collective-permute-start.9 = (f32[256,1120]{0,1:T(8,128)}, f32[256,1120]{0,1:T(8,128)}, u32[]{:S(2)}, u32[]{:S(2)}) collective-permute-start(f32[256,1120]{0,1:T(8,128)} %copy.22), channel_id=1, source_target_pairs={{0,1},{1,0},{2,3},{3,2},{4,5},{5,4},{6,7},{7,6},{8,9},{9,8},{10,11... | collective-permute-start | bytes 3440648 | tf_op jit(solution)/shard_map/ppermute | solution.py:15
  85.3 1.7 %copy-start.2 = (f32[256,896]{1,0:T(8,128)S(1)}, f32[256,896]{1,0:T(8,128)}, u32[]{:S(2)}) copy-start(f32[256,896]{1,0:T(8,128)} %fusion.8) | copy-start | bytes 2752516
  85.4 1.7 %copy-start.5 = (f32[256,224]{1,0:T(8,128)S(1)}, f32[256,224]{1,0:T(8,128)}, u32[]{:S(2)}) copy-start(f32[256,224]{1,0:T(8,128)} %fusion.6) | copy-start | bytes 688132
  88.1 24.5 %all-to-all-start = ((f16[4,64,1120]{2,1,0:T(8,128)(2,1)}), f16[4,64,1120]{2,1,0:T(8,128)(2,1)S(1)}, u32[]{:S(2)}, u32[]{:S(2)}) async-start(f16[4,64,1120]{2,1,0:T(8,128)(2,1)} %bitcast.9), calls=%async_computation | async-start | bytes 1179648 | tf_op jit(solution)/shard_map/all_to_all | solution.py:83
  127.6 5.4 %collective-permute-start.10 = (bf16[4,1,256,112]{3,2,1,0:T(8,128)(2,1)S(1)}, bf16[4,1,256,112]{3,2,1,0:T(8,128)(2,1)S(1)}, u32[]{:S(2)}, u32[]{:S(2)}) collective-permute-start(bf16[4,1,256,112]{3,2,1,0:T(8,128)(2,1)S(1)} %bitcast.34), channel_id=1, source_target_pairs={{0,1},{1,0},{2,3},{3,2},{4,5},{5,4},{6,7},{7,6},{8,9},{9,8},{10,11... | collective-permute-start | bytes 688136 | tf_op jit(solution)/shard_map/ppermute | solution.py:15
  133.2 3.0 %copy-start.7 = (bf16[56,1024]{1,0:T(8,128)(2,1)S(1)}, bf16[56,1024]{1,0:T(8,128)(2,1)}, u32[]{:S(2)}) copy-start(bf16[56,1024]{1,0:T(8,128)(2,1)} %param.13) | copy-start | bytes 344068
  133.2 3.0 %copy-start.8 = (bf16[56,1024]{1,0:T(8,128)(2,1)S(1)}, bf16[56,1024]{1,0:T(8,128)(2,1)}, u32[]{:S(2)}) copy-start(bf16[56,1024]{1,0:T(8,128)(2,1)} %param.14) | copy-start | bytes 344068
Sparse Core Ops, SparseCore 0:
  12.7 43.2 all-gather.5
  64.8 67.7 all-gather.3

commit v2 on v1

v2 whole, which is shorter than its diff:
```python
import jax
import jax.numpy as jnp
from jax import lax
from jax.sharding import Mesh, PartitionSpec as P

NODE = {"zh": 2, "x": 4, "y": 8}
LOCAL = {"zl": 4, "c": 2}

PRE_SCALE = 64.0
TAN_SCALE = 0.5
BACK_SCALE = 32.0

SHIFTS = (1, -1, 2)


def swap(value, axis):
    return lax.ppermute(value, axis, [(0, 1), (1, 0)])


def shift(value, axis, by):
    size = lax.axis_size(axis)
    return lax.ppermute(value, axis, [(i, (i + by) % size) for i in range(size)])


def ring_step(value):
    size = lax.axis_size("y")
    pairs = []
    for y in range(size):
        pairs.append((2 * y, 2 * ((y + 1) % size)))
        pairs.append((2 * y + 1, 2 * ((y - 1) % size) + 1))
    return lax.ppermute(value, ("y", "c"), pairs)


def contract(left, right, dims):
    return lax.dot_general(left, right, (dims, ((), ())), preferred_element_type=jnp.float32)


def factors(pre_gate, pre_up, tan_gate, tan_up, back):
    sig = jax.nn.sigmoid(pre_gate)
    slope = sig * (1.0 + pre_gate * (1.0 - sig))
    bend = sig * (1.0 - sig) * (2.0 + pre_gate * (1.0 - 2.0 * sig))
    fac_gate = (back * (tan_up * slope + pre_up * bend * tan_gate)).astype(jnp.bfloat16)
    fac_up = (back * slope * tan_gate).astype(jnp.bfloat16)
    return (fac_gate, fac_up)


def on_device(tokens, cotangent, gate_weight, up_weight, down_weight, gate_probe, up_probe):
    nx, ny, nzl = lax.axis_size("x"), lax.axis_size("y"), lax.axis_size("zl")
    own, feats = tokens.shape
    hid = gate_weight.shape[0]
    total = own * lax.axis_size(("zh", "x", "y"))
    x, core = lax.axis_index("x"), lax.axis_index("c")

    rows = jnp.concatenate([tokens, cotangent], axis=0)
    rows = jnp.stack([rows, swap(rows, "zh")], axis=0)
    others = swap(rows, "c")
    tok = jnp.stack([rows[:, :own], others[:, :own]], axis=0)
    cot = jnp.stack([rows[:, own:], others[:, own:]], axis=0)

    tall = -(-hid // 16) * 16
    fill = jnp.zeros((tall - hid, feats), jnp.bfloat16)
    mats = jnp.concatenate(
        [gate_weight, up_weight, gate_probe, up_probe, down_weight, fill], axis=0
    )
    width = mats.shape[0]
    w_own = jnp.zeros((nx, width, feats), jnp.bfloat16)
    w_own = lax.dynamic_update_index_in_dim(w_own, mats, x, 0)
    for by in SHIFTS:
        w_own = lax.dynamic_update_index_in_dim(
            w_own, shift(mats, "x", by), (x - by) % nx, 0
        )
    w_other = swap(w_own, "c")

    def half(block):
        return lax.dynamic_slice_in_dim(block, core, 1, 1)
    toks, cots = [half(tok)], [half(cot)]
    for _ in range(ny // 2 - 1):
        tok, cot = ring_step(tok), ring_step(cot)
        toks.append(tok)
        cots.append(cot)
    toks.append(ring_step(half(tok)))
    cots.append(ring_step(half(cot)))
    toks = jnp.concatenate(toks, axis=1).reshape(2, -1, feats)
    cots = jnp.concatenate(cots, axis=1).reshape(2, -1, feats)
    count = toks.shape[1]
    toks_x = [toks] + [shift(toks, "x", by) for by in SHIFTS]

    w_own, w_other = w_own.reshape(nx * width, feats), w_other.reshape(nx * width, feats)
    def term(block):
        return contract(block[0], w_own, ((1,), (1,))) + contract(block[1], w_other, ((1,), (1,)))
    column = lax.broadcasted_iota(jnp.int32, (1, nx * width), 1) % width
    terms = jnp.where(column >= 4 * hid, term(cots), term(toks))
    scale = jnp.where(
        column >= 4 * hid, BACK_SCALE, jnp.where(column >= 2 * hid, TAN_SCALE, PRE_SCALE)
    )
    share = count // nzl
    sent = (terms * scale).astype(jnp.float16).reshape(nzl, share, nx * width)
    got = lax.all_to_all(sent, "zl", 0, 0, tiled=True)
    proj = jnp.sum(got.astype(jnp.float32), axis=0) * (1.0 / scale)
    proj = proj.reshape(share, nx, width)
    parts = [proj[:, :, i * hid : (i + 1) * hid] for i in range(5)]
    fac = jnp.concatenate(factors(*parts), axis=2)

    fac = fac.transpose(1, 0, 2).reshape(nx, 1, share, 2 * hid)
    fac = jnp.broadcast_to(fac, (nx, nzl, share, 2 * hid)).reshape(nx * nzl, share, 2 * hid)
    fac = lax.all_to_all(fac, ("x", "zl"), 0, 0, tiled=True)
    fac = fac.reshape(nx, count, 2 * hid)

    facs = [lax.dynamic_index_in_dim(fac, (x - by) % nx, 0, False) for by in (0,) + SHIFTS]
    def hvp(which):
        return sum(contract(f, t[which], ((0,), (0,))) for f, t in zip(facs, toks_x))
    other = swap(hvp(1), "c")
    both = (hvp(0) + other) / total
    gate_diag = gate_probe.astype(jnp.float32) * both[:hid]
    up_diag = up_probe.astype(jnp.float32) * both[hid:]
    return (gate_diag, up_diag)


def solution(mesh):
    sizes = {**NODE, **LOCAL}
    cut = Mesh(mesh.devices.reshape(tuple(sizes.values())), tuple(sizes))
    placed = P(tuple(NODE), tuple(LOCAL))
    return jax.shard_map(
        on_device,
        mesh=cut,
        in_specs=(placed,) * 7,
        out_specs=(placed, placed),
        check_vma=False,
    )
```

time: 146 us -> 162 us (1.11)
  starting transfers between devices: 59.2 us -> 94.8 us
  blocking collectives: 14.2 us -> 0 us
  between operations: 14.5 us -> 1.31 us
  waiting for transfers between devices: 28.1 us -> 35.4 us
  matrix products: 7.85 us -> 14.3 us
  local copies, waits for them, and re-layouts: 16.5 us -> 12.3 us
    ppermute x0 -> x8, starting transfers between devices: none -> 31.5 us  [ring_step(): return lax.ppermute(value, ('y', 'c'), pairs)]
    all_to_all x1 -> x0, blocking collectives: 14.2 us -> none  [on_device(): fac = lax.all_to_all(fac, ('x', 'zl'), 0, 0, tiled=True)]
    all_to_all x1 -> x2, waiting for transfers between devices: 15.8 us -> 28 us  [the longest x1 26.3 us: on_device(): fac = lax.all_to_all(fac, ('x', 'zl'), 0, 0, tiled=True)]
    dot_general x5 -> x12, matrix products: 7.85 us -> 14.3 us  [contract(): lax.dot_general(left, right, (dims, ((), ())), preferred_element_type=jnp...]
    all_to_all x1 -> x2, starting transfers between devices: 8.68 us -> 14.6 us  [the longest x1 7.59 us: on_device(): fac = lax.all_to_all(fac, ('x', 'zl'), 0, 0, tiled=True)]
    ppermute x8 -> x6, starting transfers between devices: 26.9 us -> 21.2 us  [shift(): lax.ppermute(value, axis, [(i, (i + by) % size) for i in range(size)])]
    ppermute x8 -> x6, waiting for transfers between devices: 7.18 us -> 2.97 us  [shift(): lax.ppermute(value, axis, [(i, (i + by) % size) for i in range(size)])]
    ppermute x3 -> x4, starting transfers between devices: 23.5 us -> 27.5 us  [swap(): return lax.ppermute(value, axis, [(0, 1), (1, 0)])]
  transfers between devices with their start and end apart: 14 -> 20, of which waited for: 8 -> 5; matrix products, arithmetic and copies ran while one was open for 11% -> 8% of each run, Pallas kernels for 0% -> 0%
where the time goes in v2:
time: 162 us; the launch traced here: 160 us
  starting transfers between devices  94.8 us (59%)
  waiting for transfers between devices  35.4 us (22%)
  matrix products  14.3 us (9%)
  local copies, waits for them, and re-layouts  12.3 us (8%)
  other arithmetic  2.15 us (1%)
    ppermute x8, starting transfers between devices, ring_step(): return lax.ppermute(value, ('y', 'c'), pairs)  31.5 us
    ppermute x4, starting transfers between devices, swap(): return lax.ppermute(value, axis, [(0, 1), (1, 0)])  27.5 us
    all_to_all x1, waiting for transfers between devices, on_device(): fac = lax.all_to_all(fac, ('x', 'zl'), 0, 0, tiled=True)  26.3 us
    ppermute x6, starting transfers between devices, shift(): lax.ppermute(value, axis, [(i, (i + by) % size) for i in range(size)])  21.2 us
    dot_general x12, matrix products, contract(): lax.dot_general(left, right, (dims, ((), ())), preferred_element_type=jnp...  14.3 us
    all_to_all x1, starting transfers between devices, on_device(): fac = lax.all_to_all(fac, ('x', 'zl'), 0, 0, tiled=True)  7.59 us
    all_to_all x1, starting transfers between devices, on_device(): got = lax.all_to_all(sent, 'zl', 0, 0, tiled=True)  6.98 us
    unnamed x22, local copies, waits for them, and re-layouts  6.47 us
  transfers between devices with their start and end apart: 20, of which 5 were waited for; matrix products, arithmetic and copies ran while one was open for 8% of the time, Pallas kernels for 0%

profile of v2, /device:TPU:1, one launch (start us, length us, event | category | flops | bytes accessed | tf_op | source)
XLA Modules:
  0.0 160.2 jit_solution(11171067357002052035)
XLA Ops:
  0.6 0.9 constant_dynamic-update-slice_fusion.11
  1.5 0.9 constant_dynamic-update-slice_fusion.10
  2.4 0.9 constant_dynamic-update-slice_fusion.9
  3.3 0.9 constant_dynamic-update-slice_fusion.8
  4.3 0.9 constant_dynamic-update-slice_fusion.7
  5.2 4.0 %collective-permute-start.6 = (bf16[288,1024]{1,0:T(8,128)(2,1)S(1)}, bf16[288,1024]{1,0:T(8,128)(2,1)}, u32[]{:S(2)}, u32[]{:S(2)}) collective-permute-start(bf16[288,1024]{1,0:T(8,128)(2,1)S(1)} %constant_dynamic-update-slice_fusion.6), channel_id=1, source_target_pairs={{0,64},{64,128},{128,192},{192,0},{1,65},{65,129},{129,193},{193,1... | collective-permute-start | bytes 1769480 | tf_op jit(solution)/shard_map/ppermute | solution.py:22
  9.1 3.2 %collective-permute-start.7 = (bf16[288,1024]{1,0:T(8,128)(2,1)S(1)}, bf16[288,1024]{1,0:T(8,128)(2,1)}, u32[]{:S(2)}, u32[]{:S(2)}) collective-permute-start(bf16[288,1024]{1,0:T(8,128)(2,1)S(1)} %constant_dynamic-update-slice_fusion.6), channel_id=1, source_target_pairs={{0,192},{64,0},{128,64},{192,128},{1,193},{65,1},{129,65},{193,129... | collective-permute-start | bytes 1769480 | tf_op jit(solution)/shard_map/ppermute | solution.py:22
  12.3 3.6 %collective-permute-start.8 = (bf16[288,1024]{1,0:T(8,128)(2,1)S(1)}, bf16[288,1024]{1,0:T(8,128)(2,1)}, u32[]{:S(2)}, u32[]{:S(2)}) collective-permute-start(bf16[288,1024]{1,0:T(8,128)(2,1)S(1)} %constant_dynamic-update-slice_fusion.6), channel_id=1, source_target_pairs={{0,128},{64,192},{128,0},{192,64},{1,129},{65,193},{129,1},{193,65... | collective-permute-start | bytes 1769480 | tf_op jit(solution)/shard_map/ppermute | solution.py:22
  16.0 0.8 constant_dynamic-update-slice_fusion.1
  16.8 0.8 constant_dynamic-update-slice_fusion
  17.6 10.6 %collective-permute-start = (bf16[64,1024]{1,0:T(8,128)(2,1)S(1)}, bf16[64,1024]{1,0:T(8,128)(2,1)S(1)}, u32[]{:S(2)}, u32[]{:S(2)}) collective-permute-start(bf16[64,1024]{1,0:T(8,128)(2,1)S(1)} %constant_dynamic-update-slice_fusion), channel_id=1, source_target_pairs={{0,256},{256,0},{1,257},{257,1},{2,258},{258,2},{3,259},{259,3},{4... | collective-permute-start | bytes 393224 | tf_op jit(solution)/shard_map/ppermute | solution.py:17
  28.3 0.3 broadcast_in_dim.51
  28.6 0.1 bitcast_dynamic-update-slice_fusion.3
  28.7 2.0 %collective-permute-done = bf16[64,1024]{1,0:T(8,128)(2,1)S(1)} collective-permute-done((bf16[64,1024]{1,0:T(8,128)(2,1)S(1)}, bf16[64,1024]{1,0:T(8,128)(2,1)S(1)}, u32[]{:S(2)}, u32[]{:S(2)}) %collective-permute-start) | collective-permute-done | bytes 131104 | tf_op jit(solution)/shard_map/ppermute | solution.py:17
  30.8 4.8 %collective-permute-start.1 = (bf16[2,64,1024]{2,1,0:T(8,128)(2,1)S(1)}, bf16[2,64,1024]{2,1,0:T(8,128)(2,1)S(1)}, u32[]{:S(2)}, u32[]{:S(2)}) collective-permute-start(bf16[2,64,1024]{2,1,0:T(8,128)(2,1)S(1)} %pad_maximum_fusion), channel_id=1, source_target_pairs={{0,1},{1,0},{2,3},{3,2},{4,5},{5,4},{6,7},{7,6},{8,9},{9,8},{10,11... | collective-permute-start | bytes 786440 | tf_op jit(solution)/shard_map/ppermute | solution.py:17
  35.6 1.1 bitcast_dynamic-update-slice_fusion.2
  36.7 0.0 collective-permute-done.7
  36.7 1.1 bitcast_dynamic-update-slice_fusion.1
  37.8 0.0 collective-permute-done.8
  37.8 1.1 bitcast_dynamic-update-slice_fusion
  39.0 4.4 %collective-permute-start.9 = (bf16[4,288,1024]{2,1,0:T(8,128)(2,1)S(1)}, bf16[4,288,1024]{2,1,0:T(8,128)(2,1)}, u32[]{:S(2)}, u32[]{:S(2)}) collective-permute-start(bf16[4,288,1024]{2,1,0:T(8,128)(2,1)S(1)} %bitcast_dynamic-update-slice_fusion), channel_id=1, source_target_pairs={{0,1},{1,0},{2,3},{3,2},{4,5},{5,4},{6,7},{7,6},{8,9},{9,8},{10,11... | collective-permute-start | bytes 7077896 | tf_op jit(solution)/shard_map/ppermute | solution.py:17
  43.4 4.6 %collective-permute-start.2 = (bf16[2,2,32,1024]{3,2,1,0:T(8,128)(2,1)S(1)}, bf16[2,2,32,1024]{3,2,1,0:T(8,128)(2,1)}, u32[]{:S(2)}, u32[]{:S(2)}) collective-permute-start(bf16[2,2,32,1024]{3,2,1,0:T(8,128)(2,1)S(1)} %pad_maximum_fusion.1), channel_id=1, source_target_pairs={{0,8},{1,57},{8,16},{9,1},{16,24},{17,9},{24,32},{25,17},{32,40},{... | collective-permute-start | bytes 786440 | tf_op jit(solution)/shard_map/ppermute | solution.py:31
  48.0 0.7 pad_maximum_fusion.2
  48.8 3.0 %collective-permute-start.10 = (bf16[2,2,32,1024]{3,2,1,0:T(8,128)(2,1)}, bf16[2,2,32,1024]{3,2,1,0:T(8,128)(2,1)S(1)}, u32[]{:S(2)}, u32[]{:S(2)}) collective-permute-start(bf16[2,2,32,1024]{3,2,1,0:T(8,128)(2,1)} %pad_maximum_fusion.2), channel_id=1, source_target_pairs={{0,8},{1,57},{8,16},{9,1},{16,24},{17,9},{24,32},{25,17},{32,40},{... | collective-permute-start | bytes 786440 | tf_op jit(solution)/shard_map/ppermute | solution.py:31
  51.8 4.7 %collective-permute-start.3 = (bf16[2,2,32,1024]{3,2,1,0:T(8,128)(2,1)}, bf16[2,2,32,1024]{3,2,1,0:T(8,128)(2,1)S(1)}, u32[]{:S(2)}, u32[]{:S(2)}) collective-permute-start(bf16[2,2,32,1024]{3,2,1,0:T(8,128)(2,1)} %collective-permute-done.2), channel_id=1, source_target_pairs={{0,8},{1,57},{8,16},{9,1},{16,24},{17,9},{24,32},{25,17},{32,40},{... | collective-permute-start | bytes 786440 | tf_op jit(solution)/shard_map/ppermute | solution.py:31
  56.5 3.8 %collective-permute-start.11 = (bf16[2,2,32,1024]{3,2,1,0:T(8,128)(2,1)S(1)}, bf16[2,2,32,1024]{3,2,1,0:T(8,128)(2,1)S(1)}, u32[]{:S(2)}, u32[]{:S(2)}) collective-permute-start(bf16[2,2,32,1024]{3,2,1,0:T(8,128)(2,1)S(1)} %collective-permute-done.10), channel_id=1, source_target_pairs={{0,8},{1,57},{8,16},{9,1},{16,24},{17,9},{24,32},{25,17},{32,40},{... | collective-permute-start | bytes 786440 | tf_op jit(solution)/shard_map/ppermute | solution.py:31
  60.3 1.0 constant_dynamic-update-slice_fusion.5
  61.3 3.7 %collective-permute-start.4 = (bf16[2,2,32,1024]{3,2,1,0:T(8,128)(2,1)S(1)}, bf16[2,2,32,1024]{3,2,1,0:T(8,128)(2,1)S(1)}, u32[]{:S(2)}, u32[]{:S(2)}) collective-permute-start(bf16[2,2,32,1024]{3,2,1,0:T(8,128)(2,1)S(1)} %collective-permute-done.3), channel_id=1, source_target_pairs={{0,8},{1,57},{8,16},{9,1},{16,24},{17,9},{24,32},{25,17},{32,40},{... | collective-permute-start | bytes 786440 | tf_op jit(solution)/shard_map/ppermute | solution.py:31
  65.0 3.6 %collective-permute-start.12 = (bf16[2,2,32,1024]{3,2,1,0:T(8,128)(2,1)S(1)}, bf16[2,2,32,1024]{3,2,1,0:T(8,128)(2,1)S(1)}, u32[]{:S(2)}, u32[]{:S(2)}) collective-permute-start(bf16[2,2,32,1024]{3,2,1,0:T(8,128)(2,1)S(1)} %collective-permute-done.11), channel_id=1, source_target_pairs={{0,8},{1,57},{8,16},{9,1},{16,24},{17,9},{24,32},{25,17},{32,40},{... | collective-permute-start | bytes 786440 | tf_op jit(solution)/shard_map/ppermute | solution.py:31
  68.7 4.6 %collective-permute-start.5 = (bf16[2,1,32,1024]{3,2,1,0:T(8,128)(2,1)S(1)}, bf16[2,1,32,1024]{3,2,1,0:T(8,128)(2,1)S(1)}, u32[]{:S(2)}, u32[]{:S(2)}) collective-permute-start(bf16[2,1,32,1024]{3,2,1,0:T(8,128)(2,1)S(1)} %constant_dynamic-slice_fusion.1), channel_id=1, source_target_pairs={{0,8},{1,57},{8,16},{9,1},{16,24},{17,9},{24,32},{25,17},{32,40},{... | collective-permute-start | bytes 393224 | tf_op jit(solution)/shard_map/ppermute | solution.py:31
  73.3 3.6 %collective-permute-start.13 = (bf16[2,1,32,1024]{3,2,1,0:T(8,128)(2,1)S(1)}, bf16[2,1,32,1024]{3,2,1,0:T(8,128)(2,1)S(1)}, u32[]{:S(2)}, u32[]{:S(2)}) collective-permute-start(bf16[2,1,32,1024]{3,2,1,0:T(8,128)(2,1)S(1)} %constant_dynamic-slice_fusion), channel_id=1, source_target_pairs={{0,8},{1,57},{8,16},{9,1},{16,24},{17,9},{24,32},{25,17},{32,40},{... | collective-permute-start | bytes 393224 | tf_op jit(solution)/shard_map/ppermute | solution.py:31
  77.0 2.3 %collective-permute-done.13 = bf16[2,1,32,1024]{3,2,1,0:T(8,128)(2,1)S(1)} collective-permute-done((bf16[2,1,32,1024]{3,2,1,0:T(8,128)(2,1)S(1)}, bf16[2,1,32,1024]{3,2,1,0:T(8,128)(2,1)S(1)}, u32[]{:S(2)}, u32[]{:S(2)}) %collective-permute-start.13) | collective-permute-done | bytes 131104 | tf_op jit(solution)/shard_map/ppermute | solution.py:31
  79.4 0.1 fusion.63
  79.5 0.1 fusion.64
  79.6 2.7 %fusion.65 = f32[256,1152]{1,0:T(8,128)S(1)} fusion(bf16[256,1024]{1,0:T(8,128)(2,1)S(1)} %bitcast.96, bf16[1152,1024]{1,0:T(8,128)(2,1)} %bitcast.11), kind=kOutput, calls=%fused_computation.126 | convolution fusion | flops 603979776 | bytes 4063232 | tf_op jit(solution)/shard_map/dot_general | solution.py:35
  82.3 2.5 %fusion.66 = f32[256,1152]{1,0:T(8,128)S(1)} fusion(bf16[256,1024]{1,0:T(8,128)(2,1)S(1)} %bitcast.83, bf16[1152,1024]{1,0:T(8,128)(2,1)} %bitcast.11), kind=kOutput, calls=%fused_computation.127 | convolution fusion | flops 603979776 | bytes 4063232 | tf_op jit(solution)/shard_map/dot_general | solution.py:35
  84.9 0.9 convolution_add_fusion
  85.8 1.8 %fusion.2 = f16[256,1152]{1,0:T(8,128)(2,1)} fusion(f32[256,1152]{1,0:T(8,128)S(1)} %convolution_add_fusion, f32[256,1152]{1,0:T(8,128)S(1)} %fusion.65, bf16[256,1024]{1,0:T(8,128)(2,1)S(1)} %bitcast.95, bf16[1152,1024]{1,0:T(8,128)(2,1)S(1)} %bitcast.80, f32[1152]{0:T(1024)S(1)} %select_select_fusion, pred[1152]{0:T(1024)(128)(4,1)S(1)} %fusion.50), kind=kOutput, calls=%fused_computation.4 | convolution fusion | flops 605159424 | bytes 5838464 | tf_op jit(solution)/shard_map/dot_general | solution.py:35
  87.6 7.0 %all-to-all-start = ((f16[4,64,1152]{2,1,0:T(8,128)(2,1)}), f16[4,64,1152]{2,1,0:T(8,128)(2,1)S(1)}, u32[]{:S(2)}, u32[]{:S(2)}) async-start(f16[4,64,1152]{2,1,0:T(8,128)(2,1)} %bitcast.86), calls=%async_computation | async-start | bytes 1179648 | tf_op jit(solution)/shard_map/all_to_all | solution.py:98
  94.6 3.4 %collective-permute-start.14 = (bf16[2,256,1024]{2,1,0:T(8,128)(2,1)}, bf16[2,256,1024]{2,1,0:T(8,128)(2,1)S(1)}, u32[]{:S(2)}, u32[]{:S(2)}) collective-permute-start(bf16[2,256,1024]{2,1,0:T(8,128)(2,1)} %bitcast.97), channel_id=1, source_target_pairs={{0,64},{64,128},{128,192},{192,0},{1,65},{65,129},{129,193},{193,1... | collective-permute-start | bytes 3145736 | tf_op jit(solution)/shard_map/ppermute | solution.py:22
  98.0 3.9 %collective-permute-start.15 = (bf16[2,256,1024]{2,1,0:T(8,128)(2,1)}, bf16[2,256,1024]{2,1,0:T(8,128)(2,1)}, u32[]{:S(2)}, u32[]{:S(2)}) collective-permute-start(bf16[2,256,1024]{2,1,0:T(8,128)(2,1)} %bitcast.98), channel_id=1, source_target_pairs={{0,192},{64,0},{128,64},{192,128},{1,193},{65,1},{129,65},{193,129... | collective-permute-start | bytes 3145736 | tf_op jit(solution)/shard_map/ppermute | solution.py:22
  101.9 3.1 %collective-permute-start.16 = (bf16[2,256,1024]{2,1,0:T(8,128)(2,1)}, bf16[2,256,1024]{2,1,0:T(8,128)(2,1)}, u32[]{:S(2)}, u32[]{:S(2)}) collective-permute-start(bf16[2,256,1024]{2,1,0:T(8,128)(2,1)} %bitcast.99), channel_id=1, source_target_pairs={{0,128},{64,192},{128,0},{192,64},{1,129},{65,193},{129,1},{193,65... | collective-permute-start | bytes 3145736 | tf_op jit(solution)/shard_map/ppermute | solution.py:22
  105.0 1.7 %all-to-all-done = f16[4,64,1152]{2,1,0:T(8,128)(2,1)S(1)} async-done(((f16[4,64,1152]{2,1,0:T(8,128)(2,1)}), f16[4,64,1152]{2,1,0:T(8,128)(2,1)S(1)}, u32[]{:S(2)}, u32[]{:S(2)}) %all-to-all-start) | async-done | bytes 589856 | tf_op jit(solution)/shard_map/all_to_all | solution.py:98
  106.7 0.1 convert_reduce_fusion
  106.8 0.2 copy.11
  107.0 0.2 broadcast_multiply_fusion
  107.3 0.1 fusion.30
  107.4 0.1 copy.12
  107.5 0.8 broadcast_in_dim.63
  108.3 7.6 %all-to-all-start.1 = ((bf16[16,64,112]{2,1,0:T(8,128)(2,1)}), bf16[16,64,112]{2,1,0:T(8,128)(2,1)S(1)}, u32[]{:S(2)}, u32[]{:S(2)}) async-start(bf16[16,64,112]{2,1,0:T(8,128)(2,1)} %bitcast.19), calls=%async_computation.1 | async-start | bytes 524288 | tf_op jit(solution)/shard_map/all_to_all | solution.py:106
  115.9 3.0 %collective-permute-done.14 = bf16[2,256,1024]{2,1,0:T(8,128)(2,1)S(1)} collective-permute-done((bf16[2,256,1024]{2,1,0:T(8,128)(2,1)}, bf16[2,256,1024]{2,1,0:T(8,128)(2,1)S(1)}, u32[]{:S(2)}, u32[]{:S(2)}) %collective-permute-start.14) | collective-permute-done | bytes 1048608 | tf_op jit(solution)/shard_map/ppermute | solution.py:22
  118.8 26.3 %all-to-all-done.1 = bf16[16,64,112]{2,1,0:T(8,128)(2,1)S(1)} async-done(((bf16[16,64,112]{2,1,0:T(8,128)(2,1)}), bf16[16,64,112]{2,1,0:T(8,128)(2,1)S(1)}, u32[]{:S(2)}, u32[]{:S(2)}) %all-to-all-start.1) | async-done | bytes 229408 | tf_op jit(solution)/shard_map/all_to_all | solution.py:106
  145.1 0.2 fusion.11
  145.4 1.3 fusion.10
  146.7 1.4 fusion.9
  148.1 0.3 fusion.4
  148.4 7.8 %collective-permute-start.17 = (f32[112,1024]{1,0:T(8,128)S(1)}, f32[112,1024]{1,0:T(8,128)S(1)}, u32[]{:S(2)}, u32[]{:S(2)}) collective-permute-start(f32[112,1024]{1,0:T(8,128)S(1)} %fusion.4), channel_id=1, source_target_pairs={{0,1},{1,0},{2,3},{3,2},{4,5},{5,4},{6,7},{7,6},{8,9},{9,8},{10,11... | collective-permute-start | bytes 1376264 | tf_op jit(solution)/shard_map/ppermute | solution.py:17
  156.1 0.3 fusion.14
  156.4 0.0 copy-start.3
  156.4 0.0 copy-start.4
  156.4 1.3 fusion.13
  157.8 1.3 fusion.12
  159.1 0.3 fusion.8
  159.4 0.8 slice_multiply_fusion
  (40 shorter events, 0.4 us)
Async XLA Ops:
  5.2 30.4 %collective-permute-start.6 = (bf16[288,1024]{1,0:T(8,128)(2,1)S(1)}, bf16[288,1024]{1,0:T(8,128)(2,1)}, u32[]{:S(2)}, u32[]{:S(2)}) collective-permute-start(bf16[288,1024]{1,0:T(8,128)(2,1)S(1)} %constant_dynamic-update-slice_fusion.6), channel_id=1, source_target_pairs={{0,64},{64,128},{128,192},{192,0},{1,65},{65,129},{129,193},{193,1... | collective-permute-start | bytes 1769480 | tf_op jit(solution)/shard_map/ppermute | solution.py:22
  9.1 27.6 %collective-permute-start.7 = (bf16[288,1024]{1,0:T(8,128)(2,1)S(1)}, bf16[288,1024]{1,0:T(8,128)(2,1)}, u32[]{:S(2)}, u32[]{:S(2)}) collective-permute-start(bf16[288,1024]{1,0:T(8,128)(2,1)S(1)} %constant_dynamic-update-slice_fusion.6), channel_id=1, source_target_pairs={{0,192},{64,0},{128,64},{192,128},{1,193},{65,1},{129,65},{193,129... | collective-permute-start | bytes 1769480 | tf_op jit(solution)/shard_map/ppermute | solution.py:22
  12.3 25.5 %collective-permute-start.8 = (bf16[288,1024]{1,0:T(8,128)(2,1)S(1)}, bf16[288,1024]{1,0:T(8,128)(2,1)}, u32[]{:S(2)}, u32[]{:S(2)}) collective-permute-start(bf16[288,1024]{1,0:T(8,128)(2,1)S(1)} %constant_dynamic-update-slice_fusion.6), channel_id=1, source_target_pairs={{0,128},{64,192},{128,0},{192,64},{1,129},{65,193},{129,1},{193,65... | collective-permute-start | bytes 1769480 | tf_op jit(solution)/shard_map/ppermute | solution.py:22
  17.6 13.1 %collective-permute-start = (bf16[64,1024]{1,0:T(8,128)(2,1)S(1)}, bf16[64,1024]{1,0:T(8,128)(2,1)S(1)}, u32[]{:S(2)}, u32[]{:S(2)}) collective-permute-start(bf16[64,1024]{1,0:T(8,128)(2,1)S(1)} %constant_dynamic-update-slice_fusion), channel_id=1, source_target_pairs={{0,256},{256,0},{1,257},{257,1},{2,258},{258,2},{3,259},{259,3},{4... | collective-permute-start | bytes 393224 | tf_op jit(solution)/shard_map/ppermute | solution.py:17
  30.8 12.6 %collective-permute-start.1 = (bf16[2,64,1024]{2,1,0:T(8,128)(2,1)S(1)}, bf16[2,64,1024]{2,1,0:T(8,128)(2,1)S(1)}, u32[]{:S(2)}, u32[]{:S(2)}) collective-permute-start(bf16[2,64,1024]{2,1,0:T(8,128)(2,1)S(1)} %pad_maximum_fusion), channel_id=1, source_target_pairs={{0,1},{1,0},{2,3},{3,2},{4,5},{5,4},{6,7},{7,6},{8,9},{9,8},{10,11... | collective-permute-start | bytes 786440 | tf_op jit(solution)/shard_map/ppermute | solution.py:17
  39.0 40.6 %collective-permute-start.9 = (bf16[4,288,1024]{2,1,0:T(8,128)(2,1)S(1)}, bf16[4,288,1024]{2,1,0:T(8,128)(2,1)}, u32[]{:S(2)}, u32[]{:S(2)}) collective-permute-start(bf16[4,288,1024]{2,1,0:T(8,128)(2,1)S(1)} %bitcast_dynamic-update-slice_fusion), channel_id=1, source_target_pairs={{0,1},{1,0},{2,3},{3,2},{4,5},{5,4},{6,7},{7,6},{8,9},{9,8},{10,11... | collective-permute-start | bytes 7077896 | tf_op jit(solution)/shard_map/ppermute | solution.py:17
  43.4 8.4 %collective-permute-start.2 = (bf16[2,2,32,1024]{3,2,1,0:T(8,128)(2,1)S(1)}, bf16[2,2,32,1024]{3,2,1,0:T(8,128)(2,1)}, u32[]{:S(2)}, u32[]{:S(2)}) collective-permute-start(bf16[2,2,32,1024]{3,2,1,0:T(8,128)(2,1)S(1)} %pad_maximum_fusion.1), channel_id=1, source_target_pairs={{0,8},{1,57},{8,16},{9,1},{16,24},{17,9},{24,32},{25,17},{32,40},{... | collective-permute-start | bytes 786440 | tf_op jit(solution)/shard_map/ppermute | solution.py:31
  48.8 7.7 %collective-permute-start.10 = (bf16[2,2,32,1024]{3,2,1,0:T(8,128)(2,1)}, bf16[2,2,32,1024]{3,2,1,0:T(8,128)(2,1)S(1)}, u32[]{:S(2)}, u32[]{:S(2)}) collective-permute-start(bf16[2,2,32,1024]{3,2,1,0:T(8,128)(2,1)} %pad_maximum_fusion.2), channel_id=1, source_target_pairs={{0,8},{1,57},{8,16},{9,1},{16,24},{17,9},{24,32},{25,17},{32,40},{... | collective-permute-start | bytes 786440 | tf_op jit(solution)/shard_map/ppermute | solution.py:31
  51.8 9.5 %collective-permute-start.3 = (bf16[2,2,32,1024]{3,2,1,0:T(8,128)(2,1)}, bf16[2,2,32,1024]{3,2,1,0:T(8,128)(2,1)S(1)}, u32[]{:S(2)}, u32[]{:S(2)}) collective-permute-start(bf16[2,2,32,1024]{3,2,1,0:T(8,128)(2,1)} %collective-permute-done.2), channel_id=1, source_target_pairs={{0,8},{1,57},{8,16},{9,1},{16,24},{17,9},{24,32},{25,17},{32,40},{... | collective-permute-start | bytes 786440 | tf_op jit(solution)/shard_map/ppermute | solution.py:31
  56.5 8.5 %collective-permute-start.11 = (bf16[2,2,32,1024]{3,2,1,0:T(8,128)(2,1)S(1)}, bf16[2,2,32,1024]{3,2,1,0:T(8,128)(2,1)S(1)}, u32[]{:S(2)}, u32[]{:S(2)}) collective-permute-start(bf16[2,2,32,1024]{3,2,1,0:T(8,128)(2,1)S(1)} %collective-permute-done.10), channel_id=1, source_target_pairs={{0,8},{1,57},{8,16},{9,1},{16,24},{17,9},{24,32},{25,17},{32,40},{... | collective-permute-start | bytes 786440 | tf_op jit(solution)/shard_map/ppermute | solution.py:31
  61.3 7.4 %collective-permute-start.4 = (bf16[2,2,32,1024]{3,2,1,0:T(8,128)(2,1)S(1)}, bf16[2,2,32,1024]{3,2,1,0:T(8,128)(2,1)S(1)}, u32[]{:S(2)}, u32[]{:S(2)}) collective-permute-start(bf16[2,2,32,1024]{3,2,1,0:T(8,128)(2,1)S(1)} %collective-permute-done.3), channel_id=1, source_target_pairs={{0,8},{1,57},{8,16},{9,1},{16,24},{17,9},{24,32},{25,17},{32,40},{... | collective-permute-start | bytes 786440 | tf_op jit(solution)/shard_map/ppermute | solution.py:31
  65.0 8.3 %collective-permute-start.12 = (bf16[2,2,32,1024]{3,2,1,0:T(8,128)(2,1)S(1)}, bf16[2,2,32,1024]{3,2,1,0:T(8,128)(2,1)S(1)}, u32[]{:S(2)}, u32[]{:S(2)}) collective-permute-start(bf16[2,2,32,1024]{3,2,1,0:T(8,128)(2,1)S(1)} %collective-permute-done.11), channel_id=1, source_target_pairs={{0,8},{1,57},{8,16},{9,1},{16,24},{17,9},{24,32},{25,17},{32,40},{... | collective-permute-start | bytes 786440 | tf_op jit(solution)/shard_map/ppermute | solution.py:31
  68.7 8.3 %collective-permute-start.5 = (bf16[2,1,32,1024]{3,2,1,0:T(8,128)(2,1)S(1)}, bf16[2,1,32,1024]{3,2,1,0:T(8,128)(2,1)S(1)}, u32[]{:S(2)}, u32[]{:S(2)}) collective-permute-start(bf16[2,1,32,1024]{3,2,1,0:T(8,128)(2,1)S(1)} %constant_dynamic-slice_fusion.1), channel_id=1, source_target_pairs={{0,8},{1,57},{8,16},{9,1},{16,24},{17,9},{24,32},{25,17},{32,40},{... | collective-permute-start | bytes 393224 | tf_op jit(solution)/shard_map/ppermute | solution.py:31
  73.3 6.0 %collective-permute-start.13 = (bf16[2,1,32,1024]{3,2,1,0:T(8,128)(2,1)S(1)}, bf16[2,1,32,1024]{3,2,1,0:T(8,128)(2,1)S(1)}, u32[]{:S(2)}, u32[]{:S(2)}) collective-permute-start(bf16[2,1,32,1024]{3,2,1,0:T(8,128)(2,1)S(1)} %constant_dynamic-slice_fusion), channel_id=1, source_target_pairs={{0,8},{1,57},{8,16},{9,1},{16,24},{17,9},{24,32},{25,17},{32,40},{... | collective-permute-start | bytes 393224 | tf_op jit(solution)/shard_map/ppermute | solution.py:31
  79.4 2.9 %copy-start = (bf16[2,8,32,1024]{3,2,1,0:T(8,128)(2,1)}, bf16[2,8,32,1024]{3,2,1,0:T(8,128)(2,1)S(1)}, u32[]{:S(2)}) copy-start(bf16[2,8,32,1024]{3,2,1,0:T(8,128)(2,1)S(1)} %constant_dynamic-update-slice_fusion.12) | copy-start | bytes 3145732
  87.6 19.2 %all-to-all-start = ((f16[4,64,1152]{2,1,0:T(8,128)(2,1)}), f16[4,64,1152]{2,1,0:T(8,128)(2,1)S(1)}, u32[]{:S(2)}, u32[]{:S(2)}) async-start(f16[4,64,1152]{2,1,0:T(8,128)(2,1)} %bitcast.86), calls=%async_computation | async-start | bytes 1179648 | tf_op jit(solution)/shard_map/all_to_all | solution.py:98
  94.6 24.3 %collective-permute-start.14 = (bf16[2,256,1024]{2,1,0:T(8,128)(2,1)}, bf16[2,256,1024]{2,1,0:T(8,128)(2,1)S(1)}, u32[]{:S(2)}, u32[]{:S(2)}) collective-permute-start(bf16[2,256,1024]{2,1,0:T(8,128)(2,1)} %bitcast.97), channel_id=1, source_target_pairs={{0,64},{64,128},{128,192},{192,0},{1,65},{65,129},{129,193},{193,1... | collective-permute-start | bytes 3145736 | tf_op jit(solution)/shard_map/ppermute | solution.py:22
  98.0 47.4 %collective-permute-start.15 = (bf16[2,256,1024]{2,1,0:T(8,128)(2,1)}, bf16[2,256,1024]{2,1,0:T(8,128)(2,1)}, u32[]{:S(2)}, u32[]{:S(2)}) collective-permute-start(bf16[2,256,1024]{2,1,0:T(8,128)(2,1)} %bitcast.98), channel_id=1, source_target_pairs={{0,192},{64,0},{128,64},{192,128},{1,193},{65,1},{129,65},{193,129... | collective-permute-start | bytes 3145736 | tf_op jit(solution)/shard_map/ppermute | solution.py:22
  101.9 44.8 %collective-permute-start.16 = (bf16[2,256,1024]{2,1,0:T(8,128)(2,1)}, bf16[2,256,1024]{2,1,0:T(8,128)(2,1)}, u32[]{:S(2)}, u32[]{:S(2)}) collective-permute-start(bf16[2,256,1024]{2,1,0:T(8,128)(2,1)} %bitcast.99), channel_id=1, source_target_pairs={{0,128},{64,192},{128,0},{192,64},{1,129},{65,193},{129,1},{193,65... | collective-permute-start | bytes 3145736 | tf_op jit(solution)/shard_map/ppermute | solution.py:22
  108.3 36.8 %all-to-all-start.1 = ((bf16[16,64,112]{2,1,0:T(8,128)(2,1)}), bf16[16,64,112]{2,1,0:T(8,128)(2,1)S(1)}, u32[]{:S(2)}, u32[]{:S(2)}) async-start(bf16[16,64,112]{2,1,0:T(8,128)(2,1)} %bitcast.19), calls=%async_computation.1 | async-start | bytes 524288 | tf_op jit(solution)/shard_map/all_to_all | solution.py:106
  118.8 27.8 %copy-start.1 = (bf16[2,256,1024]{2,1,0:T(8,128)(2,1)}, bf16[2,256,1024]{2,1,0:T(8,128)(2,1)S(1)}, u32[]{:S(2)}) copy-start(bf16[2,256,1024]{2,1,0:T(8,128)(2,1)S(1)} %collective-permute-done.14) | copy-start | bytes 3145732
  146.7 9.4 %copy-start.2 = (bf16[2,256,1024]{2,1,0:T(8,128)(2,1)S(1)}, bf16[2,256,1024]{2,1,0:T(8,128)(2,1)}, u32[]{:S(2)}) copy-start(bf16[2,256,1024]{2,1,0:T(8,128)(2,1)} %copy-done.1) | copy-start | bytes 3145732
  148.4 10.7 %collective-permute-start.17 = (f32[112,1024]{1,0:T(8,128)S(1)}, f32[112,1024]{1,0:T(8,128)S(1)}, u32[]{:S(2)}, u32[]{:S(2)}) collective-permute-start(f32[112,1024]{1,0:T(8,128)S(1)} %fusion.4), channel_id=1, source_target_pairs={{0,1},{1,0},{2,3},{3,2},{4,5},{5,4},{6,7},{7,6},{8,9},{9,8},{10,11... | collective-permute-start | bytes 1376264 | tf_op jit(solution)/shard_map/ppermute | solution.py:17
  156.4 3.0 %copy-start.3 = (bf16[56,1024]{1,0:T(8,128)(2,1)S(1)}, bf16[56,1024]{1,0:T(8,128)(2,1)}, u32[]{:S(2)}) copy-start(bf16[56,1024]{1,0:T(8,128)(2,1)} %param.12) | copy-start | bytes 344068
  156.4 3.0 %copy-start.4 = (bf16[56,1024]{1,0:T(8,128)(2,1)S(1)}, bf16[56,1024]{1,0:T(8,128)(2,1)}, u32[]{:S(2)}) copy-start(bf16[56,1024]{1,0:T(8,128)(2,1)} %param.13) | copy-start | bytes 344068

commit v3 on v2

v3 whole, which is shorter than its diff:
```python
import functools

import jax
import jax.numpy as jnp
from jax import lax
from jax.experimental import pallas as pl
from jax.experimental.pallas import tpu as pltpu
from jax.sharding import Mesh, PartitionSpec as P

NODE = {"zh": 2, "x": 4, "y": 8}
LOCAL = {"zl": 4, "c": 2}

PRE_SCALE = 64.0
TAN_SCALE = 0.5
BACK_SCALE = 32.0

VMEM = pl.BlockSpec(memory_space=pltpu.VMEM)
SMEM = pl.BlockSpec(memory_space=pltpu.SMEM)


def swap(value, axis):
    return lax.ppermute(value, axis, [(0, 1), (1, 0)])


def shift(value, axis, by):
    size = lax.axis_size(axis)
    return lax.ppermute(value, axis, [(i, (i + by) % size) for i in range(size)])


def local_call(body, out_shape, scratch, flops, moved, interpret, *args):
    return pl.pallas_call(
        body,
        out_shape=out_shape,
        in_specs=[SMEM] + [VMEM] * (len(args) - 1),
        out_specs=jax.tree.map(lambda _: VMEM, out_shape),
        scratch_shapes=scratch,
        cost_estimate=pl.CostEstimate(flops=flops, bytes_accessed=moved, transcendentals=0),
        compiler_params=pltpu.CompilerParams(vmem_limit_bytes=24 * 1024 * 1024),
        interpret=interpret,
    )(*args)


def terms_kernel(own, place, *refs):
    *refs, out, x_half, g_half, w_all = refs
    blocks, weights = refs[:-4], refs[-4:]
    middle = len(blocks) // 2
    tall = weights[0].shape[0]
    tok_rows = tall * 7 // 9
    cot_rows = tall - tok_rows
    for i, weight in enumerate(weights):
        w_all[i * tok_rows : (i + 1) * tok_rows] = weight[:tok_rows]
        start = 4 * tok_rows + i * cot_rows
        w_all[start : start + cot_rows] = weight[tok_rows:]

    def take(chosen):
        row = 0
        for block in chosen:
            for z in range(block.shape[0]):
                x_half[row : row + own] = block[z, :own]
                g_half[row : row + own] = block[z, own:]
                row += own

    @pl.when(place[0] == 0)
    def _():
        take(blocks[:middle])

    @pl.when(place[0] != 0)
    def _():
        take(blocks[middle:])

    across = (((1,), (1,)), ((), ()))
    cut = 4 * tok_rows
    out[:, :cut] = lax.dot_general(
        x_half[...], w_all[:cut], across, preferred_element_type=jnp.float32
    )
    out[:, cut:] = lax.dot_general(
        g_half[...], w_all[cut:], across, preferred_element_type=jnp.float32
    )


def hvp_kernel(total, place, mine, other, *refs):
    *tokens, gate_probe, up_probe, gate_diag, up_diag = refs
    x, core = place[0], place[1]
    sizes = len(tokens) // 4
    acc = None
    for by in range(4):
        source = lax.rem(x - by + 4, 4)
        first, second = mine[source], other[source]
        fac = jnp.concatenate(
            [jnp.where(core == 0, first, second), jnp.where(core == 0, second, first)], axis=0
        )
        row = 0
        for part in tokens[by * sizes : (by + 1) * sizes]:
            rows = part.shape[0]
            term = lax.dot_general(
                fac[row : row + rows], part[...], (((0,), (0,)), ((), ())),
                preferred_element_type=jnp.float32,
            )
            acc = term if acc is None else acc + term
            row += rows
    acc = acc / total
    hid = gate_diag.shape[0]
    gate_diag[...] = gate_probe[...].astype(jnp.float32) * acc[:hid]
    up_diag[...] = up_probe[...].astype(jnp.float32) * acc[hid:]


def factors(pre_gate, pre_up, tan_gate, tan_up, back):
    sig = jax.nn.sigmoid(pre_gate)
    slope = sig * (1.0 + pre_gate * (1.0 - sig))
    bend = sig * (1.0 - sig) * (2.0 + pre_gate * (1.0 - 2.0 * sig))
    fac_gate = (back * (tan_up * slope + pre_up * bend * tan_gate)).astype(jnp.bfloat16)
    fac_up = (back * slope * tan_gate).astype(jnp.bfloat16)
    return (fac_gate, fac_up)


def stacked(parts, rows):
    row, out = 0, None
    for part in parts:
        padded = lax.pad(
            part, jnp.zeros((), part.dtype),
            ((row, rows - row - part.shape[0], 0), (0, 0, 0)),
        )
        out = padded if out is None else out + padded
        row += part.shape[0]
    return out


def on_device(
    tokens, cotangent, gate_weight, up_weight, down_weight, gate_probe, up_probe, interpret
):
    nx, ny, nzl = lax.axis_size("x"), lax.axis_size("y"), lax.axis_size("zl")
    own, feats = tokens.shape
    hid = gate_weight.shape[0]
    total = own * lax.axis_size(("zh", "x", "y"))
    x, core = lax.axis_index("x"), lax.axis_index("c")

    rows = stacked([tokens, cotangent], 2 * own)
    block = jnp.stack([rows, swap(rows, "zh")], axis=0)

    tok_rows, cot_rows = 4 * hid, hid * 8 // 7
    mats = stacked(
        [gate_weight, up_weight, gate_probe, up_probe, down_weight], tok_rows + cot_rows
    )
    weights = [mats] + [shift(mats, "x", by) for by in (1, 2, -1)]

    ahead = behind = block
    blocks = [block]
    for _ in range(ny // 2 - 1):
        ahead, behind = shift(ahead, "y", 1), shift(behind, "y", -1)
        blocks += [ahead, behind]
    far = (shift(ahead[:1], "y", 1), shift(behind[1:], "y", -1))
    blocks.append(jnp.concatenate(far, axis=0))

    near = len(blocks) - 3
    chunks = []
    for part in (blocks[:near], blocks[near:]):
        part = jnp.concatenate([b[:, :own] for b in part], axis=0).reshape(-1, feats)
        chunks.append([part] + [shift(part, "x", by) for by in (1, 2, -1)])

    count = len(blocks) * own
    columns = nx * (tok_rows + cot_rows)
    term = functools.partial(
        local_call,
        functools.partial(terms_kernel, own),
        jax.ShapeDtypeStruct((count, columns), jnp.float32),
        [
            pltpu.VMEM((count, feats), jnp.bfloat16),
            pltpu.VMEM((count, feats), jnp.bfloat16),
            pltpu.VMEM((columns, feats), jnp.bfloat16),
        ],
        2 * count * columns * feats,
        2 * columns * feats,
        interpret,
    )
    other = swap(term((1 - core).reshape(1), *blocks, *weights), "c")
    terms = term(core.reshape(1), *blocks, *weights) + other

    column = lax.broadcasted_iota(jnp.int32, (1, columns), 1)
    scale = jnp.where(
        column >= nx * tok_rows,
        BACK_SCALE,
        jnp.where(column % tok_rows >= 2 * hid, TAN_SCALE, PRE_SCALE),
    )
    share = count // nzl
    sent = (terms * scale).astype(jnp.float16).reshape(nzl, share, columns)
    got = lax.all_to_all(sent, "zl", 0, 0, tiled=True)
    proj = jnp.sum(got.astype(jnp.float32), axis=0) * (1.0 / scale)
    tok_part = proj[:, : nx * tok_rows].reshape(share, nx, 4, hid)
    back = proj[:, nx * tok_rows :].reshape(share, nx, cot_rows)[:, :, :hid]
    fac = jnp.concatenate(factors(*[tok_part[:, :, i] for i in range(4)], back), axis=2)

    fac = fac.transpose(1, 0, 2)
    fac = jnp.stack(
        [lax.dynamic_index_in_dim(fac, (x - i) % nx, 0, False) for i in range(nx)], axis=0
    ).reshape(nx, 1, share, 2 * hid)
    fac = jnp.broadcast_to(fac, (nx, nzl, share, 2 * hid)).reshape(nx * nzl, share, 2 * hid)
    fac = lax.all_to_all(fac, ("x", "zl"), 0, 0, tiled=True).reshape(nx, count, 2 * hid)
    fac_other = swap(fac, "c")

    diag = jax.ShapeDtypeStruct((hid, feats), jnp.float32)
    return local_call(
        functools.partial(hvp_kernel, total),
        (diag, diag),
        [],
        4 * hid * total * feats,
        2 * total * feats,
        interpret,
        jnp.stack([x, core]),
        fac,
        fac_other,
        *[chunk[by] for by in range(nx) for chunk in chunks],
        gate_probe,
        up_probe,
    )


def solution(mesh, interpret=False):
    sizes = {**NODE, **LOCAL}
    cut = Mesh(mesh.devices.reshape(tuple(sizes.values())), tuple(sizes))
    placed = P(tuple(NODE), tuple(LOCAL))
    return jax.shard_map(
        functools.partial(on_device, interpret=interpret),
        mesh=cut,
        in_specs=(placed,) * 7,
        out_specs=(placed, placed),
        check_vma=False,
    )
```

time: 162 us -> 165 us (1.019); the launches traced: 160 us -> 161 us
  matrix products: 14.3 us -> 0 us
  Pallas kernels: 0 us -> 6.24 us
  other arithmetic: 2.15 us -> 7.96 us
  waiting for transfers between devices: 35.4 us -> 40.6 us
  starting transfers between devices: 94.8 us -> 91 us
  local copies, waits for them, and re-layouts: 12.3 us -> 14.4 us
    ppermute x6 -> x17, starting transfers between devices: 21.2 us -> 58.8 us  [shift(): lax.ppermute(value, axis, [(i, (i + by) % size) for i in range(size)])]
    ppermute x8 -> x0, starting transfers between devices: 31.5 us -> none  [ring_step(): return lax.ppermute(value, ('y', 'c'), pairs)]
    all_to_all x1, waiting for transfers between devices: 26.3 us -> 0.01 us  [on_device(): lax.all_to_all(fac, ('x', 'zl'), 0, 0, tiled=True)]
    ppermute x6 -> x17, waiting for transfers between devices: 2.97 us -> 27.4 us  [shift(): lax.ppermute(value, axis, [(i, (i + by) % size) for i in range(size)])]
    dot_general x12 -> x0, matrix products: 14.3 us -> none  [contract(): lax.dot_general(left, right, (dims, ((), ())), preferred_element_type=jnp...]
    all_to_all x1, waiting for transfers between devices: 1.73 us -> 9.35 us  [on_device(): got = lax.all_to_all(sent, 'zl', 0, 0, tiled=True)]
    ppermute x4 -> x3, starting transfers between devices: 27.5 us -> 20.4 us  [swap(): return lax.ppermute(value, axis, [(0, 1), (1, 0)])]
    pallas_call x0 -> x3, Pallas kernels: none -> 6.24 us  [local_call(): pl.pallas_call(body, out_shape=out_shape, in_specs=[SMEM] + [VMEM] * (len...]
  transfers between devices with their start and end apart: 20 -> 22, of which waited for: 5 -> 11; matrix products, arithmetic and copies ran while one was open for 8% -> 6% of each run, Pallas kernels for 0% -> 1%
where the time goes in v3:
time: 165 us; the launch traced here: 161 us
  starting transfers between devices  91 us (55%)
  waiting for transfers between devices  40.6 us (25%)
  local copies, waits for them, and re-layouts  14.4 us (9%)
  other arithmetic  7.96 us (5%)
  Pallas kernels  6.24 us (4%)
    ppermute x17, starting transfers between devices, shift(): lax.ppermute(value, axis, [(i, (i + by) % size) for i in range(size)])  58.8 us
    ppermute x17, waiting for transfers between devices, shift(): lax.ppermute(value, axis, [(i, (i + by) % size) for i in range(size)])  27.4 us
    ppermute x3, starting transfers between devices, swap(): return lax.ppermute(value, axis, [(0, 1), (1, 0)])  20.4 us
    unnamed x46, local copies, waits for them, and re-layouts  9.94 us
    all_to_all x1, waiting for transfers between devices, on_device(): got = lax.all_to_all(sent, 'zl', 0, 0, tiled=True)  9.35 us
    all_to_all x1, starting transfers between devices, on_device(): got = lax.all_to_all(sent, 'zl', 0, 0, tiled=True)  7.94 us
    pallas_call x3, Pallas kernels, local_call(): pl.pallas_call(body, out_shape=out_shape, in_specs=[SMEM] + [VMEM] * (len...  6.24 us
    all_to_all x1, starting transfers between devices, on_device(): lax.all_to_all(fac, ('x', 'zl'), 0, 0, tiled=True)  3.93 us
  transfers between devices with their start and end apart: 22, of which 11 were waited for; matrix products, arithmetic and copies ran while one was open for 6% of the time, Pallas kernels for 1%

profile of v3, /device:TPU:1, one launch (start us, length us, event | category | flops | bytes accessed | tf_op | source)
XLA Modules:
  0.0 161.5 jit_solution(14601459052283382913)
XLA Ops:
  0.6 0.9 fusion.14
  1.5 11.5 %collective-permute-start = (bf16[64,1024]{1,0:T(8,128)(2,1)S(1)}, bf16[64,1024]{1,0:T(8,128)(2,1)S(1)}, u32[]{:S(2)}, u32[]{:S(2)}) collective-permute-start(bf16[64,1024]{1,0:T(8,128)(2,1)S(1)} %get-tuple-element.13), channel_id=1, source_target_pairs={{0,256},{256,0},{1,257},{257,1},{2,258},{258,2},{3,259},{259,3},{4... | collective-permute-start | bytes 393224 | tf_op jit(solution)/shard_map/ppermute | solution.py:22
  13.0 3.9 %collective-permute-done = bf16[64,1024]{1,0:T(8,128)(2,1)S(1)} collective-permute-done((bf16[64,1024]{1,0:T(8,128)(2,1)S(1)}, bf16[64,1024]{1,0:T(8,128)(2,1)S(1)}, u32[]{:S(2)}, u32[]{:S(2)}) %collective-permute-start) | collective-permute-done | bytes 131104 | tf_op jit(solution)/shard_map/ppermute | solution.py:22
  16.9 0.6 copy-done.19
  17.6 2.5 %collective-permute-start.1 = (bf16[2,64,1024]{2,1,0:T(8,128)(2,1)S(1)}, bf16[2,64,1024]{2,1,0:T(8,128)(2,1)S(1)}, u32[]{:S(2)}, u32[]{:S(2)}) collective-permute-start(bf16[2,64,1024]{2,1,0:T(8,128)(2,1)S(1)} %pad_maximum_fusion.1.refs_0_), channel_id=1, source_target_pairs={{0,8},{8,16},{16,24},{24,32},{32,40},{40,48},{48,56},{56,0},{1,9},... | collective-permute-start | bytes 786440 | tf_op jit(solution)/shard_map/ppermute | solution.py:27
  20.1 4.0 %collective-permute-start.2 = (bf16[2,64,1024]{2,1,0:T(8,128)(2,1)S(1)}, bf16[2,64,1024]{2,1,0:T(8,128)(2,1)S(1)}, u32[]{:S(2)}, u32[]{:S(2)}) collective-permute-start(bf16[2,64,1024]{2,1,0:T(8,128)(2,1)S(1)} %pad_maximum_fusion.1.refs_0_), channel_id=1, source_target_pairs={{0,56},{8,0},{16,8},{24,16},{32,24},{40,32},{48,40},{56,48},{1,57}... | collective-permute-start | bytes 786440 | tf_op jit(solution)/shard_map/ppermute | solution.py:27
  24.1 1.8 %collective-permute-done.1.refs_1_ = bf16[2,64,1024]{2,1,0:T(8,128)(2,1)S(1)} collective-permute-done((bf16[2,64,1024]{2,1,0:T(8,128)(2,1)S(1)}, bf16[2,64,1024]{2,1,0:T(8,128)(2,1)S(1)}, u32[]{:S(2)}, u32[]{:S(2)}) %collective-permute-start.1) | collective-permute-done | bytes 262176 | tf_op jit(solution)/shard_map/ppermute | solution.py:27
  25.9 2.4 %collective-permute-start.3 = (bf16[2,64,1024]{2,1,0:T(8,128)(2,1)S(1)}, bf16[2,64,1024]{2,1,0:T(8,128)(2,1)S(1)}, u32[]{:S(2)}, u32[]{:S(2)}) collective-permute-start(bf16[2,64,1024]{2,1,0:T(8,128)(2,1)S(1)} %collective-permute-done.1.refs_1_), channel_id=1, source_target_pairs={{0,8},{8,16},{16,24},{24,32},{32,40},{40,48},{48,56},{56,0},{1,9},... | collective-permute-start | bytes 786440 | tf_op jit(solution)/shard_map/ppermute | solution.py:27
  28.3 0.7 copy-done
  29.0 4.1 %collective-permute-start.4 = (bf16[2,64,1024]{2,1,0:T(8,128)(2,1)S(1)}, bf16[2,64,1024]{2,1,0:T(8,128)(2,1)S(1)}, u32[]{:S(2)}, u32[]{:S(2)}) collective-permute-start(bf16[2,64,1024]{2,1,0:T(8,128)(2,1)S(1)} %collective-permute-done.2.refs_2_), channel_id=1, source_target_pairs={{0,56},{8,0},{16,8},{24,16},{32,24},{40,32},{48,40},{56,48},{1,57}... | collective-permute-start | bytes 786440 | tf_op jit(solution)/shard_map/ppermute | solution.py:27
  33.1 1.1 collective-permute-done.3.refs_3_
  34.2 1.9 %collective-permute-start.5 = (bf16[2,64,1024]{2,1,0:T(8,128)(2,1)S(1)}, bf16[2,64,1024]{2,1,0:T(8,128)(2,1)S(1)}, u32[]{:S(2)}, u32[]{:S(2)}) collective-permute-start(bf16[2,64,1024]{2,1,0:T(8,128)(2,1)S(1)} %collective-permute-done.3.refs_3_), channel_id=1, source_target_pairs={{0,8},{8,16},{16,24},{24,32},{32,40},{40,48},{48,56},{56,0},{1,9},... | collective-permute-start | bytes 786440 | tf_op jit(solution)/shard_map/ppermute | solution.py:27
  36.1 1.2 pad_add_fusion.refs_8_
  37.3 6.6 %collective-permute-start.10 = (bf16[288,1024]{1,0:T(8,128)(2,1)S(1)}, bf16[288,1024]{1,0:T(8,128)(2,1)S(1)}, u32[]{:S(2)}, u32[]{:S(2)}) collective-permute-start(bf16[288,1024]{1,0:T(8,128)(2,1)S(1)} %pad_add_fusion.refs_8_), channel_id=1, source_target_pairs={{0,128},{64,192},{128,0},{192,64},{1,129},{65,193},{129,1},{193,65... | collective-permute-start | bytes 1769480 | tf_op jit(solution)/shard_map/ppermute | solution.py:27
  43.9 2.8 %collective-permute-start.11 = (bf16[288,1024]{1,0:T(8,128)(2,1)S(1)}, bf16[288,1024]{1,0:T(8,128)(2,1)S(1)}, u32[]{:S(2)}, u32[]{:S(2)}) collective-permute-start(bf16[288,1024]{1,0:T(8,128)(2,1)S(1)} %pad_add_fusion.refs_8_), channel_id=1, source_target_pairs={{0,192},{64,0},{128,64},{192,128},{1,193},{65,1},{129,65},{193,129... | collective-permute-start | bytes 1769480 | tf_op jit(solution)/shard_map/ppermute | solution.py:27
  46.7 2.5 %collective-permute-start.9 = (bf16[288,1024]{1,0:T(8,128)(2,1)S(1)}, bf16[288,1024]{1,0:T(8,128)(2,1)S(1)}, u32[]{:S(2)}, u32[]{:S(2)}) collective-permute-start(bf16[288,1024]{1,0:T(8,128)(2,1)S(1)} %pad_add_fusion.refs_8_), channel_id=1, source_target_pairs={{0,64},{64,128},{128,192},{192,0},{1,65},{65,129},{129,193},{193,1... | collective-permute-start | bytes 1769480 | tf_op jit(solution)/shard_map/ppermute | solution.py:27
  49.3 4.6 %collective-permute-start.6 = (bf16[2,64,1024]{2,1,0:T(8,128)(2,1)S(1)}, bf16[2,64,1024]{2,1,0:T(8,128)(2,1)S(1)}, u32[]{:S(2)}, u32[]{:S(2)}) collective-permute-start(bf16[2,64,1024]{2,1,0:T(8,128)(2,1)S(1)} %collective-permute-done.4.refs_4_), channel_id=1, source_target_pairs={{0,56},{8,0},{16,8},{24,16},{32,24},{40,32},{48,40},{56,48},{1,57}... | collective-permute-start | bytes 786440 | tf_op jit(solution)/shard_map/ppermute | solution.py:27
  53.9 0.7 slice.68
  54.5 1.9 %collective-permute-start.7 = (bf16[1,64,1024]{2,1,0:T(8,128)(2,1)}, bf16[1,64,1024]{2,1,0:T(8,128)(2,1)}, u32[]{:S(2)}, u32[]{:S(2)}) collective-permute-start(bf16[1,64,1024]{2,1,0:T(8,128)(2,1)} %slice.68), channel_id=1, source_target_pairs={{0,8},{8,16},{16,24},{24,32},{32,40},{40,48},{48,56},{56,0},{1,9},... | collective-permute-start | bytes 393224 | tf_op jit(solution)/shard_map/ppermute | solution.py:27
  56.4 0.7 collective-permute-done.6.refs_6_
  57.1 0.7 slice.69
  57.8 5.3 %collective-permute-start.8 = (bf16[1,64,1024]{2,1,0:T(8,128)(2,1)}, bf16[1,64,1024]{2,1,0:T(8,128)(2,1)}, u32[]{:S(2)}, u32[]{:S(2)}) collective-permute-start(bf16[1,64,1024]{2,1,0:T(8,128)(2,1)} %slice.69), channel_id=1, source_target_pairs={{0,56},{8,0},{16,8},{24,16},{32,24},{40,32},{48,40},{56,48},{1,57}... | collective-permute-start | bytes 393224 | tf_op jit(solution)/shard_map/ppermute | solution.py:27
  63.2 0.9 constant_dynamic-update-slice_fusion.1
  64.1 1.3 collective-permute-done.8
  65.4 0.9 constant_dynamic-update-slice_fusion.refs_7_
  66.3 3.3 %collective-permute-done.11.refs_11_ = bf16[288,1024]{1,0:T(8,128)(2,1)S(1)} collective-permute-done((bf16[288,1024]{1,0:T(8,128)(2,1)S(1)}, bf16[288,1024]{1,0:T(8,128)(2,1)S(1)}, u32[]{:S(2)}, u32[]{:S(2)}) %collective-permute-start.11) | collective-permute-done | bytes 589856 | tf_op jit(solution)/shard_map/ppermute | solution.py:27
  69.6 0.9 copy-done.1
  70.6 0.9 copy-done.5
  71.5 0.9 copy-done.9
  72.5 0.9 copy-done.13
  73.4 2.1 %shard_map.87 = f32[256,1152]{1,0:T(8,128)} custom-call(s32[1]{0:T(128)} %bitcast.4.place, bf16[2,64,1024]{2,1,0:T(8,128)(2,1)S(1)} %pad_maximum_fusion.1.refs_0_, bf16[2,64,1024]{2,1,0:T(8,128)(2,1)S(1)} %copy-done.1, bf16[2,64,1024]{2,1,0:T(8,128)(2,1)S(1)} %copy-done.5, bf16[2,64,1024]{2,1,0:T(8,128)(2,1)S(1)} %copy-done.9, ...), custom_call_target="tpu_custom_call" | custom-call | flops 603979776 | bytes 2359296 | tf_op jit(solution)/shard_map/pallas_call | solution.py:31
  75.6 4.3 %collective-permute-start.12 = (f32[256,1152]{1,0:T(8,128)}, f32[256,1152]{1,0:T(8,128)}, u32[]{:S(2)}, u32[]{:S(2)}) collective-permute-start(f32[256,1152]{1,0:T(8,128)} %shard_map.87), channel_id=1, source_target_pairs={{0,1},{1,0},{2,3},{3,2},{4,5},{5,4},{6,7},{7,6},{8,9},{9,8},{10,11... | collective-permute-start | bytes 3538952 | tf_op jit(solution)/shard_map/ppermute | solution.py:22
  80.0 1.5 fusion.8
  81.5 0.9 copy-done.2
  82.4 0.9 copy-done.6
  83.4 0.9 copy-done.10
  84.3 0.9 copy-done.14
  85.3 1.1 shard_map.86
  86.4 2.3 %multiply_convert_fusion = f16[256,1152]{1,0:T(8,128)(2,1)} fusion(f32[256,1152]{1,0:T(8,128)S(1)} %shard_map.86, f32[256,1152]{1,0:T(8,128)} %collective-permute-done.12, f32[1152]{0:T(1024)S(1)} %select_select_fusion), kind=kLoop, calls=%fused_computation.1 | loop fusion | flops 884736 | bytes 2953728 | tf_op jit(solution)/shard_map/convert_element_type | solution.py:185
  88.7 7.9 %all-to-all-start = ((f16[4,64,1152]{2,1,0:T(8,128)(2,1)}), f16[4,64,1152]{2,1,0:T(8,128)(2,1)}, u32[]{:S(2)}, u32[]{:S(2)}) async-start(f16[4,64,1152]{2,1,0:T(8,128)(2,1)} %bitcast.5), calls=%async_computation | async-start | bytes 1179648 | tf_op jit(solution)/shard_map/all_to_all | solution.py:186
  96.8 3.0 %collective-permute-start.14 = (bf16[320,1024]{1,0:T(8,128)(2,1)S(1)}, bf16[320,1024]{1,0:T(8,128)(2,1)S(1)}, u32[]{:S(2)}, u32[]{:S(2)}) collective-permute-start(bf16[320,1024]{1,0:T(8,128)(2,1)S(1)} %bitcast.37), channel_id=1, source_target_pairs={{0,64},{64,128},{128,192},{192,0},{1,65},{65,129},{129,193},{193,1... | collective-permute-start | bytes 1966088 | tf_op jit(solution)/shard_map/ppermute | solution.py:27
  99.8 4.3 %collective-permute-start.16 = (bf16[320,1024]{1,0:T(8,128)(2,1)S(1)}, bf16[320,1024]{1,0:T(8,128)(2,1)}, u32[]{:S(2)}, u32[]{:S(2)}) collective-permute-start(bf16[320,1024]{1,0:T(8,128)(2,1)S(1)} %bitcast.38), channel_id=1, source_target_pairs={{0,128},{64,192},{128,0},{192,64},{1,129},{65,193},{129,1},{193,65... | collective-permute-start | bytes 1966088 | tf_op jit(solution)/shard_map/ppermute | solution.py:27
  104.1 9.4 %all-to-all-done = f16[4,64,1152]{2,1,0:T(8,128)(2,1)} async-done(((f16[4,64,1152]{2,1,0:T(8,128)(2,1)}), f16[4,64,1152]{2,1,0:T(8,128)(2,1)}, u32[]{:S(2)}, u32[]{:S(2)}) %all-to-all-start) | async-done | bytes 589856 | tf_op jit(solution)/shard_map/all_to_all | solution.py:186
  113.5 1.2 convert_reduce_fusion
  114.7 0.9 reshape.66
  115.6 0.4 fusion.15
  116.0 0.1 reshape.65
  116.1 0.2 fusion.9
  116.3 0.5 dynamic-slice_maximum_fusion.3
  116.9 0.0 copy-start.17
  116.9 0.0 copy-start.18
  116.9 0.8 broadcast_in_dim.20
  117.7 3.9 %all-to-all-start.1 = ((bf16[16,64,112]{2,1,0:T(8,128)(2,1)}), bf16[16,64,112]{2,1,0:T(8,128)(2,1)S(1)}, u32[]{:S(2)}, u32[]{:S(2)}) async-start(bf16[16,64,112]{2,1,0:T(8,128)(2,1)} %bitcast.10), calls=%async_computation.1 | async-start | bytes 524288 | tf_op jit(solution)/shard_map/all_to_all | solution.py:197
  121.6 4.5 %collective-permute-start.18 = (bf16[320,1024]{1,0:T(8,128)(2,1)S(1)}, bf16[320,1024]{1,0:T(8,128)(2,1)}, u32[]{:S(2)}, u32[]{:S(2)}) collective-permute-start(bf16[320,1024]{1,0:T(8,128)(2,1)S(1)} %bitcast.39), channel_id=1, source_target_pairs={{0,192},{64,0},{128,64},{192,128},{1,193},{65,1},{129,65},{193,129... | collective-permute-start | bytes 1966088 | tf_op jit(solution)/shard_map/ppermute | solution.py:27
  126.2 1.9 %collective-permute-start.15 = (bf16[192,1024]{1,0:T(8,128)(2,1)S(1)}, bf16[192,1024]{1,0:T(8,128)(2,1)S(1)}, u32[]{:S(2)}, u32[]{:S(2)}) collective-permute-start(bf16[192,1024]{1,0:T(8,128)(2,1)S(1)} %bitcast.31), channel_id=1, source_target_pairs={{0,64},{64,128},{128,192},{192,0},{1,65},{65,129},{129,193},{193,1... | collective-permute-start | bytes 1179656 | tf_op jit(solution)/shard_map/ppermute | solution.py:27
  128.1 3.7 %collective-permute-start.17 = (bf16[192,1024]{1,0:T(8,128)(2,1)S(1)}, bf16[192,1024]{1,0:T(8,128)(2,1)S(1)}, u32[]{:S(2)}, u32[]{:S(2)}) collective-permute-start(bf16[192,1024]{1,0:T(8,128)(2,1)S(1)} %bitcast.32), channel_id=1, source_target_pairs={{0,128},{64,192},{128,0},{192,64},{1,129},{65,193},{129,1},{193,65... | collective-permute-start | bytes 1179656 | tf_op jit(solution)/shard_map/ppermute | solution.py:27
  131.8 2.8 %collective-permute-start.19 = (bf16[192,1024]{1,0:T(8,128)(2,1)S(1)}, bf16[192,1024]{1,0:T(8,128)(2,1)S(1)}, u32[]{:S(2)}, u32[]{:S(2)}) collective-permute-start(bf16[192,1024]{1,0:T(8,128)(2,1)S(1)} %bitcast.33), channel_id=1, source_target_pairs={{0,192},{64,0},{128,64},{192,128},{1,193},{65,1},{129,65},{193,129... | collective-permute-start | bytes 1179656 | tf_op jit(solution)/shard_map/ppermute | solution.py:27
  134.7 4.6 %collective-permute-start.13 = (bf16[4,256,112]{2,1,0:T(8,128)(2,1)S(1)}, bf16[4,256,112]{2,1,0:T(8,128)(2,1)S(1)}, u32[]{:S(2)}, u32[]{:S(2)}) collective-permute-start(bf16[4,256,112]{2,1,0:T(8,128)(2,1)S(1)} %bitcast.35), channel_id=1, source_target_pairs={{0,1},{1,0},{2,3},{3,2},{4,5},{5,4},{6,7},{7,6},{8,9},{9,8},{10,11... | collective-permute-start | bytes 688136 | tf_op jit(solution)/shard_map/ppermute | solution.py:22
  139.3 0.1 pad_add_fusion.2.place
  139.4 2.3 %collective-permute-done.18.refs_6_ = bf16[320,1024]{1,0:T(8,128)(2,1)} collective-permute-done((bf16[320,1024]{1,0:T(8,128)(2,1)S(1)}, bf16[320,1024]{1,0:T(8,128)(2,1)}, u32[]{:S(2)}, u32[]{:S(2)}) %collective-permute-start.18) | collective-permute-done | bytes 655392 | tf_op jit(solution)/shard_map/ppermute | solution.py:27
  141.7 1.1 collective-permute-done.15.refs_3_
  142.7 7.7 %collective-permute-done.17.refs_5_ = bf16[192,1024]{1,0:T(8,128)(2,1)S(1)} collective-permute-done((bf16[192,1024]{1,0:T(8,128)(2,1)S(1)}, bf16[192,1024]{1,0:T(8,128)(2,1)S(1)}, u32[]{:S(2)}, u32[]{:S(2)}) %collective-permute-start.17) | collective-permute-done | bytes 393248 | tf_op jit(solution)/shard_map/ppermute | solution.py:27
  150.5 8.0 %collective-permute-done.19.refs_7_ = bf16[192,1024]{1,0:T(8,128)(2,1)S(1)} collective-permute-done((bf16[192,1024]{1,0:T(8,128)(2,1)S(1)}, bf16[192,1024]{1,0:T(8,128)(2,1)S(1)}, u32[]{:S(2)}, u32[]{:S(2)}) %collective-permute-start.19) | collective-permute-done | bytes 393248 | tf_op jit(solution)/shard_map/ppermute | solution.py:27
  158.5 3.0 %shard_map.88 = (f32[56,1024]{1,0:T(8,128)}, f32[56,1024]{1,0:T(8,128)}) custom-call(s32[2]{0:T(128)S(1)} %pad_add_fusion.2.place, bf16[4,256,112]{2,1,0:T(8,128)(2,1)S(1)} %bitcast.36, bf16[4,256,112]{2,1,0:T(8,128)(2,1)S(1)} %collective-permute-done.13.other, bf16[320,1024]{1,0:T(8,128)(2,1)S(1)} %bitcast.40, bf16[192,1024]{1,0:T(8,128)(2,1)S(1)} %bitcast.34, ...), custom_call_target="tpu_custom_call" | custom-call | flops 469762048 | bytes 4194304 | tf_op jit(solution)/shard_map/pallas_call | solution.py:31
  (56 shorter events, 0.3 us)
Async XLA Ops:
  1.5 15.4 %collective-permute-start = (bf16[64,1024]{1,0:T(8,128)(2,1)S(1)}, bf16[64,1024]{1,0:T(8,128)(2,1)S(1)}, u32[]{:S(2)}, u32[]{:S(2)}) collective-permute-start(bf16[64,1024]{1,0:T(8,128)(2,1)S(1)} %get-tuple-element.13), channel_id=1, source_target_pairs={{0,256},{256,0},{1,257},{257,1},{2,258},{258,2},{3,259},{259,3},{4... | collective-permute-start | bytes 393224 | tf_op jit(solution)/shard_map/ppermute | solution.py:22
  16.9 0.6 copy-start.19
  17.6 8.3 %collective-permute-start.1 = (bf16[2,64,1024]{2,1,0:T(8,128)(2,1)S(1)}, bf16[2,64,1024]{2,1,0:T(8,128)(2,1)S(1)}, u32[]{:S(2)}, u32[]{:S(2)}) collective-permute-start(bf16[2,64,1024]{2,1,0:T(8,128)(2,1)S(1)} %pad_maximum_fusion.1.refs_0_), channel_id=1, source_target_pairs={{0,8},{8,16},{16,24},{24,32},{32,40},{40,48},{48,56},{56,0},{1,9},... | collective-permute-start | bytes 786440 | tf_op jit(solution)/shard_map/ppermute | solution.py:27
  20.1 8.9 %collective-permute-start.2 = (bf16[2,64,1024]{2,1,0:T(8,128)(2,1)S(1)}, bf16[2,64,1024]{2,1,0:T(8,128)(2,1)S(1)}, u32[]{:S(2)}, u32[]{:S(2)}) collective-permute-start(bf16[2,64,1024]{2,1,0:T(8,128)(2,1)S(1)} %pad_maximum_fusion.1.refs_0_), channel_id=1, source_target_pairs={{0,56},{8,0},{16,8},{24,16},{32,24},{40,32},{48,40},{56,48},{1,57}... | collective-permute-start | bytes 786440 | tf_op jit(solution)/shard_map/ppermute | solution.py:27
  25.9 8.3 %collective-permute-start.3 = (bf16[2,64,1024]{2,1,0:T(8,128)(2,1)S(1)}, bf16[2,64,1024]{2,1,0:T(8,128)(2,1)S(1)}, u32[]{:S(2)}, u32[]{:S(2)}) collective-permute-start(bf16[2,64,1024]{2,1,0:T(8,128)(2,1)S(1)} %collective-permute-done.1.refs_1_), channel_id=1, source_target_pairs={{0,8},{8,16},{16,24},{24,32},{32,40},{40,48},{48,56},{56,0},{1,9},... | collective-permute-start | bytes 786440 | tf_op jit(solution)/shard_map/ppermute | solution.py:27
  28.3 0.7 copy-start
  29.0 20.3 %copy-start.4 = (bf16[2,64,1024]{2,1,0:T(8,128)(2,1)}, bf16[2,64,1024]{2,1,0:T(8,128)(2,1)S(1)}, u32[]{:S(2)}) copy-start(bf16[2,64,1024]{2,1,0:T(8,128)(2,1)S(1)} %collective-permute-done.2.refs_2_) | copy-start | bytes 786436
  29.0 20.3 %collective-permute-start.4 = (bf16[2,64,1024]{2,1,0:T(8,128)(2,1)S(1)}, bf16[2,64,1024]{2,1,0:T(8,128)(2,1)S(1)}, u32[]{:S(2)}, u32[]{:S(2)}) collective-permute-start(bf16[2,64,1024]{2,1,0:T(8,128)(2,1)S(1)} %collective-permute-done.2.refs_2_), channel_id=1, source_target_pairs={{0,56},{8,0},{16,8},{24,16},{32,24},{40,32},{48,40},{56,48},{1,57}... | collective-permute-start | bytes 786440 | tf_op jit(solution)/shard_map/ppermute | solution.py:27
  34.2 28.9 %copy-start.8 = (bf16[2,64,1024]{2,1,0:T(8,128)(2,1)}, bf16[2,64,1024]{2,1,0:T(8,128)(2,1)S(1)}, u32[]{:S(2)}) copy-start(bf16[2,64,1024]{2,1,0:T(8,128)(2,1)S(1)} %collective-permute-done.3.refs_3_) | copy-start | bytes 786436
  34.2 19.6 %collective-permute-start.5 = (bf16[2,64,1024]{2,1,0:T(8,128)(2,1)S(1)}, bf16[2,64,1024]{2,1,0:T(8,128)(2,1)S(1)}, u32[]{:S(2)}, u32[]{:S(2)}) collective-permute-start(bf16[2,64,1024]{2,1,0:T(8,128)(2,1)S(1)} %collective-permute-done.3.refs_3_), channel_id=1, source_target_pairs={{0,8},{8,16},{16,24},{24,32},{32,40},{40,48},{48,56},{56,0},{1,9},... | collective-permute-start | bytes 786440 | tf_op jit(solution)/shard_map/ppermute | solution.py:27
  37.3 29.0 %collective-permute-start.10 = (bf16[288,1024]{1,0:T(8,128)(2,1)S(1)}, bf16[288,1024]{1,0:T(8,128)(2,1)S(1)}, u32[]{:S(2)}, u32[]{:S(2)}) collective-permute-start(bf16[288,1024]{1,0:T(8,128)(2,1)S(1)} %pad_add_fusion.refs_8_), channel_id=1, source_target_pairs={{0,128},{64,192},{128,0},{192,64},{1,129},{65,193},{129,1},{193,65... | collective-permute-start | bytes 1769480 | tf_op jit(solution)/shard_map/ppermute | solution.py:27
  43.9 25.7 %collective-permute-start.11 = (bf16[288,1024]{1,0:T(8,128)(2,1)S(1)}, bf16[288,1024]{1,0:T(8,128)(2,1)S(1)}, u32[]{:S(2)}, u32[]{:S(2)}) collective-permute-start(bf16[288,1024]{1,0:T(8,128)(2,1)S(1)} %pad_add_fusion.refs_8_), channel_id=1, source_target_pairs={{0,192},{64,0},{128,64},{192,128},{1,193},{65,1},{129,65},{193,129... | collective-permute-start | bytes 1769480 | tf_op jit(solution)/shard_map/ppermute | solution.py:27
  46.7 22.9 %collective-permute-start.9 = (bf16[288,1024]{1,0:T(8,128)(2,1)S(1)}, bf16[288,1024]{1,0:T(8,128)(2,1)S(1)}, u32[]{:S(2)}, u32[]{:S(2)}) collective-permute-start(bf16[288,1024]{1,0:T(8,128)(2,1)S(1)} %pad_add_fusion.refs_8_), channel_id=1, source_target_pairs={{0,64},{64,128},{128,192},{192,0},{1,65},{65,129},{129,193},{193,1... | collective-permute-start | bytes 1769480 | tf_op jit(solution)/shard_map/ppermute | solution.py:27
  49.3 7.9 %copy-start.12 = (bf16[2,64,1024]{2,1,0:T(8,128)(2,1)}, bf16[2,64,1024]{2,1,0:T(8,128)(2,1)S(1)}, u32[]{:S(2)}) copy-start(bf16[2,64,1024]{2,1,0:T(8,128)(2,1)S(1)} %collective-permute-done.4.refs_4_) | copy-start | bytes 786436
  49.3 7.9 %collective-permute-start.6 = (bf16[2,64,1024]{2,1,0:T(8,128)(2,1)S(1)}, bf16[2,64,1024]{2,1,0:T(8,128)(2,1)S(1)}, u32[]{:S(2)}, u32[]{:S(2)}) collective-permute-start(bf16[2,64,1024]{2,1,0:T(8,128)(2,1)S(1)} %collective-permute-done.4.refs_4_), channel_id=1, source_target_pairs={{0,56},{8,0},{16,8},{24,16},{32,24},{40,32},{48,40},{56,48},{1,57}... | collective-permute-start | bytes 786440 | tf_op jit(solution)/shard_map/ppermute | solution.py:27
  54.5 8.6 %collective-permute-start.7 = (bf16[1,64,1024]{2,1,0:T(8,128)(2,1)}, bf16[1,64,1024]{2,1,0:T(8,128)(2,1)}, u32[]{:S(2)}, u32[]{:S(2)}) collective-permute-start(bf16[1,64,1024]{2,1,0:T(8,128)(2,1)} %slice.68), channel_id=1, source_target_pairs={{0,8},{8,16},{16,24},{24,32},{32,40},{40,48},{48,56},{56,0},{1,9},... | collective-permute-start | bytes 393224 | tf_op jit(solution)/shard_map/ppermute | solution.py:27
  57.8 7.6 %collective-permute-start.8 = (bf16[1,64,1024]{2,1,0:T(8,128)(2,1)}, bf16[1,64,1024]{2,1,0:T(8,128)(2,1)}, u32[]{:S(2)}, u32[]{:S(2)}) collective-permute-start(bf16[1,64,1024]{2,1,0:T(8,128)(2,1)} %slice.69), channel_id=1, source_target_pairs={{0,56},{8,0},{16,8},{24,16},{32,24},{40,32},{48,40},{56,48},{1,57}... | collective-permute-start | bytes 393224 | tf_op jit(solution)/shard_map/ppermute | solution.py:27
  69.6 1.0 copy-start.1
  70.6 0.9 copy-start.5
  71.5 0.9 copy-start.9
  72.5 0.9 copy-start.13
  75.6 10.8 %collective-permute-start.12 = (f32[256,1152]{1,0:T(8,128)}, f32[256,1152]{1,0:T(8,128)}, u32[]{:S(2)}, u32[]{:S(2)}) collective-permute-start(f32[256,1152]{1,0:T(8,128)} %shard_map.87), channel_id=1, source_target_pairs={{0,1},{1,0},{2,3},{3,2},{4,5},{5,4},{6,7},{7,6},{8,9},{9,8},{10,11... | collective-permute-start | bytes 3538952 | tf_op jit(solution)/shard_map/ppermute | solution.py:22
  81.5 0.9 copy-start.2
  82.4 0.9 copy-start.6
  83.4 0.9 copy-start.10
  84.3 0.9 copy-start.14
  86.4 10.3 %copy-start.16 = (bf16[10,32,1024]{2,1,0:T(8,128)(2,1)S(1)}, bf16[10,32,1024]{2,1,0:T(8,128)(2,1)}, u32[]{:S(2)}) copy-start(bf16[10,32,1024]{2,1,0:T(8,128)(2,1)} %fusion.8) | copy-start | bytes 1966084
  88.7 8.0 %copy-start.3 = (bf16[2,64,1024]{2,1,0:T(8,128)(2,1)S(1)}, bf16[2,64,1024]{2,1,0:T(8,128)(2,1)}, u32[]{:S(2)}) copy-start(bf16[2,64,1024]{2,1,0:T(8,128)(2,1)} %copy-done) | copy-start | bytes 786436
  88.7 8.0 %copy-start.7 = (bf16[2,64,1024]{2,1,0:T(8,128)(2,1)S(1)}, bf16[2,64,1024]{2,1,0:T(8,128)(2,1)}, u32[]{:S(2)}) copy-start(bf16[2,64,1024]{2,1,0:T(8,128)(2,1)} %copy-done.4) | copy-start | bytes 786436
  88.7 8.0 %copy-start.11 = (bf16[2,64,1024]{2,1,0:T(8,128)(2,1)S(1)}, bf16[2,64,1024]{2,1,0:T(8,128)(2,1)}, u32[]{:S(2)}) copy-start(bf16[2,64,1024]{2,1,0:T(8,128)(2,1)} %copy-done.8) | copy-start | bytes 786436
  88.7 8.0 %copy-start.15 = (bf16[2,64,1024]{2,1,0:T(8,128)(2,1)S(1)}, bf16[2,64,1024]{2,1,0:T(8,128)(2,1)}, u32[]{:S(2)}) copy-start(bf16[2,64,1024]{2,1,0:T(8,128)(2,1)} %copy-done.12) | copy-start | bytes 786436
  88.7 24.8 %all-to-all-start = ((f16[4,64,1152]{2,1,0:T(8,128)(2,1)}), f16[4,64,1152]{2,1,0:T(8,128)(2,1)}, u32[]{:S(2)}, u32[]{:S(2)}) async-start(f16[4,64,1152]{2,1,0:T(8,128)(2,1)} %bitcast.5), calls=%async_computation | async-start | bytes 1179648 | tf_op jit(solution)/shard_map/all_to_all | solution.py:186
  96.8 35.0 %collective-permute-start.14 = (bf16[320,1024]{1,0:T(8,128)(2,1)S(1)}, bf16[320,1024]{1,0:T(8,128)(2,1)S(1)}, u32[]{:S(2)}, u32[]{:S(2)}) collective-permute-start(bf16[320,1024]{1,0:T(8,128)(2,1)S(1)} %bitcast.37), channel_id=1, source_target_pairs={{0,64},{64,128},{128,192},{192,0},{1,65},{65,129},{129,193},{193,1... | collective-permute-start | bytes 1966088 | tf_op jit(solution)/shard_map/ppermute | solution.py:27
  99.8 34.9 %collective-permute-start.16 = (bf16[320,1024]{1,0:T(8,128)(2,1)S(1)}, bf16[320,1024]{1,0:T(8,128)(2,1)}, u32[]{:S(2)}, u32[]{:S(2)}) collective-permute-start(bf16[320,1024]{1,0:T(8,128)(2,1)S(1)} %bitcast.38), channel_id=1, source_target_pairs={{0,128},{64,192},{128,0},{192,64},{1,129},{65,193},{129,1},{193,65... | collective-permute-start | bytes 1966088 | tf_op jit(solution)/shard_map/ppermute | solution.py:27
  116.9 41.6 %copy-start.17 = (bf16[56,1024]{1,0:T(8,128)(2,1)S(1)}, bf16[56,1024]{1,0:T(8,128)(2,1)}, u32[]{:S(2)}) copy-start(bf16[56,1024]{1,0:T(8,128)(2,1)} %refs_9_.1) | copy-start | bytes 344068
  116.9 41.6 %copy-start.18 = (bf16[56,1024]{1,0:T(8,128)(2,1)S(1)}, bf16[56,1024]{1,0:T(8,128)(2,1)}, u32[]{:S(2)}) copy-start(bf16[56,1024]{1,0:T(8,128)(2,1)} %refs_8_.1) | copy-start | bytes 344068
  117.7 17.0 %all-to-all-start.1 = ((bf16[16,64,112]{2,1,0:T(8,128)(2,1)}), bf16[16,64,112]{2,1,0:T(8,128)(2,1)S(1)}, u32[]{:S(2)}, u32[]{:S(2)}) async-start(bf16[16,64,112]{2,1,0:T(8,128)(2,1)} %bitcast.10), calls=%async_computation.1 | async-start | bytes 524288 | tf_op jit(solution)/shard_map/all_to_all | solution.py:197
  121.6 20.0 %collective-permute-start.18 = (bf16[320,1024]{1,0:T(8,128)(2,1)S(1)}, bf16[320,1024]{1,0:T(8,128)(2,1)}, u32[]{:S(2)}, u32[]{:S(2)}) collective-permute-start(bf16[320,1024]{1,0:T(8,128)(2,1)S(1)} %bitcast.39), channel_id=1, source_target_pairs={{0,192},{64,0},{128,64},{192,128},{1,193},{65,1},{129,65},{193,129... | collective-permute-start | bytes 1966088 | tf_op jit(solution)/shard_map/ppermute | solution.py:27
  126.2 16.5 %collective-permute-start.15 = (bf16[192,1024]{1,0:T(8,128)(2,1)S(1)}, bf16[192,1024]{1,0:T(8,128)(2,1)S(1)}, u32[]{:S(2)}, u32[]{:S(2)}) collective-permute-start(bf16[192,1024]{1,0:T(8,128)(2,1)S(1)} %bitcast.31), channel_id=1, source_target_pairs={{0,64},{64,128},{128,192},{192,0},{1,65},{65,129},{129,193},{193,1... | collective-permute-start | bytes 1179656 | tf_op jit(solution)/shard_map/ppermute | solution.py:27
  128.1 22.3 %collective-permute-start.17 = (bf16[192,1024]{1,0:T(8,128)(2,1)S(1)}, bf16[192,1024]{1,0:T(8,128)(2,1)S(1)}, u32[]{:S(2)}, u32[]{:S(2)}) collective-permute-start(bf16[192,1024]{1,0:T(8,128)(2,1)S(1)} %bitcast.32), channel_id=1, source_target_pairs={{0,128},{64,192},{128,0},{192,64},{1,129},{65,193},{129,1},{193,65... | collective-permute-start | bytes 1179656 | tf_op jit(solution)/shard_map/ppermute | solution.py:27
  131.8 26.6 %collective-permute-start.19 = (bf16[192,1024]{1,0:T(8,128)(2,1)S(1)}, bf16[192,1024]{1,0:T(8,128)(2,1)S(1)}, u32[]{:S(2)}, u32[]{:S(2)}) collective-permute-start(bf16[192,1024]{1,0:T(8,128)(2,1)S(1)} %bitcast.33), channel_id=1, source_target_pairs={{0,192},{64,0},{128,64},{192,128},{1,193},{65,1},{129,65},{193,129... | collective-permute-start | bytes 1179656 | tf_op jit(solution)/shard_map/ppermute | solution.py:27
  134.7 23.8 %collective-permute-start.13 = (bf16[4,256,112]{2,1,0:T(8,128)(2,1)S(1)}, bf16[4,256,112]{2,1,0:T(8,128)(2,1)S(1)}, u32[]{:S(2)}, u32[]{:S(2)}) collective-permute-start(bf16[4,256,112]{2,1,0:T(8,128)(2,1)S(1)} %bitcast.35), channel_id=1, source_target_pairs={{0,1},{1,0},{2,3},{3,2},{4,5},{5,4},{6,7},{7,6},{8,9},{9,8},{10,11... | collective-permute-start | bytes 688136 | tf_op jit(solution)/shard_map/ppermute | solution.py:22

commit v4 on v3

v4 whole, which is shorter than its diff:
```python
import functools

import jax
import jax.numpy as jnp
from jax import lax
from jax.experimental import pallas as pl
from jax.experimental.pallas import tpu as pltpu
from jax.sharding import Mesh, PartitionSpec as P

NODE = {"zh": 2, "x": 4, "y": 8}
LOCAL = {"zl": 4, "c": 2}

PRE_SCALE = 64.0
TAN_SCALE = 0.5
BACK_SCALE = 32.0

VMEM = pl.BlockSpec(memory_space=pltpu.VMEM)
SMEM = pl.BlockSpec(memory_space=pltpu.SMEM)


def swap(value, axis):
    return lax.ppermute(value, axis, [(0, 1), (1, 0)])


def shift(value, axis, by):
    size = lax.axis_size(axis)
    return lax.ppermute(value, axis, [(i, (i + by) % size) for i in range(size)])


def local_call(body, out_shape, flops, moved, interpret, *args, **options):
    return pl.pallas_call(
        body,
        out_shape=out_shape,
        cost_estimate=pl.CostEstimate(flops=flops, bytes_accessed=moved, transcendentals=0),
        compiler_params=pltpu.CompilerParams(vmem_limit_bytes=12 * 1024 * 1024),
        interpret=interpret,
        **options,
    )(*args)


def reorder_kernel(tok_rows, gathered, out):
    nx, rows, _ = gathered.shape
    cot_rows = rows - tok_rows
    for i in range(nx):
        out[i * tok_rows : (i + 1) * tok_rows] = gathered[i, :tok_rows]
        start = nx * tok_rows + i * cot_rows
        out[start : start + cot_rows] = gathered[i, tok_rows:]


def terms_kernel(own, cut, place, *refs):
    *blocks, weights, out, x_half, g_half = refs
    slabs = [(block, z) for block in blocks for z in range(block.shape[0])]
    middle = len(slabs) // 2

    def take(chosen):
        for i, (block, z) in enumerate(chosen):
            x_half[i * own : (i + 1) * own] = block[z, :own]
            g_half[i * own : (i + 1) * own] = block[z, own:]

    @pl.when(place[0] == 0)
    def _():
        take(slabs[:middle])

    @pl.when(place[0] != 0)
    def _():
        take(slabs[middle:])

    across = (((1,), (1,)), ((), ()))
    out[:, :cut] = lax.dot_general(
        x_half[...], weights[:cut], across, preferred_element_type=jnp.float32
    )
    out[:, cut:] = lax.dot_general(
        g_half[...], weights[cut:], across, preferred_element_type=jnp.float32
    )


def hvp_kernel(total, place, mine, other, *refs):
    *tokens, gate_probe, up_probe, gate_diag, up_diag, acc = refs
    first, second = mine[0], other[0]
    fac = jnp.concatenate(
        [jnp.where(place[0] == 0, first, second), jnp.where(place[0] == 0, second, first)],
        axis=0,
    )
    term, row = None, 0
    for part in tokens:
        rows = part.shape[0]
        piece = lax.dot_general(
            fac[row : row + rows], part[...], (((0,), (0,)), ((), ())),
            preferred_element_type=jnp.float32,
        )
        term = piece if term is None else term + piece
        row += rows

    @pl.when(pl.program_id(0) == 0)
    def _():
        acc[...] = term

    @pl.when(pl.program_id(0) != 0)
    def _():
        acc[...] += term

    @pl.when(pl.program_id(0) == pl.num_programs(0) - 1)
    def _():
        hid = gate_diag.shape[0]
        gate_diag[...] = gate_probe[...].astype(jnp.float32) * (acc[:hid] / total)
        up_diag[...] = up_probe[...].astype(jnp.float32) * (acc[hid:] / total)


def factors(pre_gate, pre_up, tan_gate, tan_up, back):
    sig = jax.nn.sigmoid(pre_gate)
    slope = sig * (1.0 + pre_gate * (1.0 - sig))
    bend = sig * (1.0 - sig) * (2.0 + pre_gate * (1.0 - 2.0 * sig))
    fac_gate = (back * (tan_up * slope + pre_up * bend * tan_gate)).astype(jnp.bfloat16)
    fac_up = (back * slope * tan_gate).astype(jnp.bfloat16)
    return (fac_gate, fac_up)


def stacked(parts, rows):
    row, out = 0, None
    for part in parts:
        padded = lax.pad(
            part, jnp.zeros((), part.dtype),
            ((row, rows - row - part.shape[0], 0), (0, 0, 0)),
        )
        out = padded if out is None else out + padded
        row += part.shape[0]
    return out


def on_device(
    tokens, cotangent, gate_weight, up_weight, down_weight, gate_probe, up_probe, interpret
):
    nx, ny, nzl = lax.axis_size("x"), lax.axis_size("y"), lax.axis_size("zl")
    own, feats = tokens.shape
    hid = gate_weight.shape[0]
    total = own * lax.axis_size(("zh", "x", "y"))
    core = lax.axis_index("c")

    rows = stacked([tokens, cotangent], 2 * own)
    block = jnp.stack([rows, swap(rows, "zh")], axis=0)

    tok_rows, cot_rows = 4 * hid, hid * 8 // 7
    mats = stacked(
        [gate_weight, up_weight, gate_probe, up_probe, down_weight], tok_rows + cot_rows
    )
    mats = lax.all_gather(mats, "x", axis=0, tiled=False)
    cut, columns = nx * tok_rows, nx * (tok_rows + cot_rows)
    weights = local_call(
        functools.partial(reorder_kernel, tok_rows),
        jax.ShapeDtypeStruct((columns, feats), jnp.bfloat16),
        0, 4 * columns * feats, interpret, mats, in_specs=[VMEM], out_specs=VMEM,
    )

    ahead = behind = block
    blocks = [block]
    for _ in range(ny // 2 - 1):
        ahead, behind = shift(ahead, "y", 1), shift(behind, "y", -1)
        blocks += [ahead, behind]
    near = len(blocks) - 2
    blocks += [shift(ahead[:1], "y", 1), shift(behind[1:], "y", -1)]

    chunks = []
    for part in (blocks[:near], blocks[near:]):
        part = jnp.concatenate([b[:, :own] for b in part], axis=0).reshape(-1, feats)
        chunks.append(lax.all_gather(part, "x", axis=0, tiled=True))

    count = ny * own
    term = functools.partial(
        local_call,
        functools.partial(terms_kernel, own, cut),
        jax.ShapeDtypeStruct((count, columns), jnp.float32),
        2 * count * columns * feats,
        2 * columns * feats,
        interpret,
        in_specs=[SMEM] + [VMEM] * (len(blocks) + 1),
        out_specs=VMEM,
        scratch_shapes=[pltpu.VMEM((count, feats), jnp.bfloat16)] * 2,
    )
    other = swap(term((1 - core).reshape(1), *blocks, weights), "c")
    terms = term(core.reshape(1), *blocks, weights) + other

    column = lax.broadcasted_iota(jnp.int32, (1, columns), 1)
    scale = jnp.where(
        column >= nx * tok_rows,
        BACK_SCALE,
        jnp.where(column % tok_rows >= 2 * hid, TAN_SCALE, PRE_SCALE),
    )
    share = count // nzl
    sent = (terms * scale).astype(jnp.float16).reshape(nzl, share, columns)
    got = lax.all_to_all(sent, "zl", 0, 0, tiled=True)
    proj = jnp.sum(got.astype(jnp.float32), axis=0) * (1.0 / scale)
    tok_part = proj[:, : nx * tok_rows].reshape(share, nx, 4, hid)
    back = proj[:, nx * tok_rows :].reshape(share, nx, cot_rows)[:, :, :hid]
    fac = jnp.concatenate(factors(*[tok_part[:, :, i] for i in range(4)], back), axis=2)

    fac = fac.transpose(1, 0, 2).reshape(nx, 1, share, 2 * hid)
    fac = jnp.broadcast_to(fac, (nx, nzl, share, 2 * hid)).reshape(nx * nzl, share, 2 * hid)
    fac = lax.all_to_all(fac, ("x", "zl"), 0, 0, tiled=True).reshape(nx, count, 2 * hid)
    fac_other = swap(fac, "c")

    def whole(shape):
        return pl.BlockSpec(shape, lambda i: (0,) * len(shape))
    by_x = pl.BlockSpec((1, count, 2 * hid), lambda i: (i, 0, 0))
    diag = jax.ShapeDtypeStruct((hid, feats), jnp.float32)
    return local_call(
        functools.partial(hvp_kernel, total),
        (diag, diag),
        4 * hid * total * feats,
        2 * total * feats,
        interpret,
        core.reshape(1),
        fac,
        fac_other,
        *chunks,
        gate_probe,
        up_probe,
        grid=(nx,),
        in_specs=[SMEM, by_x, by_x]
        + [pl.BlockSpec((chunk.shape[0] // nx, feats), lambda i: (i, 0)) for chunk in chunks]
        + [whole(gate_probe.shape)] * 2,
        out_specs=(whole(diag.shape),) * 2,
        scratch_shapes=[pltpu.VMEM((2 * hid, feats), jnp.float32)],
    )


def solution(mesh, interpret=False):
    sizes = {**NODE, **LOCAL}
    cut = Mesh(mesh.devices.reshape(tuple(sizes.values())), tuple(sizes))
    placed = P(tuple(NODE), tuple(LOCAL))
    return jax.shard_map(
        functools.partial(on_device, interpret=interpret),
        mesh=cut,
        in_specs=(placed,) * 7,
        out_specs=(placed, placed),
        check_vma=False,
    )
```

time: 165 us -> 160 us (0.970); the launches traced: 161 us -> 159 us
  starting transfers between devices: 91 us -> 59.3 us
  blocking collectives: 0 us -> 14.1 us
  between operations: 1.23 us -> 14.2 us
  waiting for transfers between devices: 40.6 us -> 46.3 us
  other arithmetic: 7.96 us -> 5.64 us
    ppermute x17 -> x8, starting transfers between devices: 58.8 us -> 28.3 us  [shift(): lax.ppermute(value, axis, [(i, (i + by) % size) for i in range(size)])]
    ppermute x17 -> x8, waiting for transfers between devices: 27.4 us -> 9.96 us  [shift(): lax.ppermute(value, axis, [(i, (i + by) % size) for i in range(size)])]
    all_gather x0 -> x3, waiting for transfers between devices: none -> 16.7 us  [the longest x2 16.6 us: on_device(): chunks.append(lax.all_gather(part, 'x', axis=0, tiled=True))]
    all_to_all x0 -> x1, blocking collectives: none -> 14.1 us  [on_device(): lax.all_to_all(fac, ('x', 'zl'), 0, 0, tiled=True)]
    all_to_all x1, waiting for transfers between devices: 9.35 us -> 15.7 us  [on_device(): got = lax.all_to_all(sent, 'zl', 0, 0, tiled=True)]
    all_to_all x1 -> x0, starting transfers between devices: 3.93 us -> none  [on_device(): lax.all_to_all(fac, ('x', 'zl'), 0, 0, tiled=True)]
    ppermute x3, starting transfers between devices: 20.4 us -> 22.9 us  [swap(): return lax.ppermute(value, axis, [(0, 1), (1, 0)])]
    unnamed x46 -> x43, local copies, waits for them, and re-layouts: 9.94 us -> 11.7 us
  transfers between devices with their start and end apart: 22 -> 15, of which waited for: 11 -> 7; matrix products, arithmetic and copies ran while one was open for 6% -> 4% of each run, Pallas kernels for 1% -> 2%
where the time goes in v4:
time: 160 us; the launch traced here: 159 us
  starting transfers between devices  59.3 us (37%)
  waiting for transfers between devices  46.3 us (29%)
  between operations  14.2 us (9%)
  blocking collectives  14.1 us (9%)
  local copies, waits for them, and re-layouts  13.8 us (9%)
  Pallas kernels  5.67 us (4%)
  other arithmetic  5.64 us (4%)
    ppermute x8, starting transfers between devices, shift(): lax.ppermute(value, axis, [(i, (i + by) % size) for i in range(size)])  28.3 us
    ppermute x3, starting transfers between devices, swap(): return lax.ppermute(value, axis, [(0, 1), (1, 0)])  22.9 us
    all_gather x2, waiting for transfers between devices, on_device(): chunks.append(lax.all_gather(part, 'x', axis=0, tiled=True))  16.6 us
    all_to_all x1, waiting for transfers between devices, on_device(): got = lax.all_to_all(sent, 'zl', 0, 0, tiled=True)  15.7 us
    all_to_all x1, blocking collectives, on_device(): lax.all_to_all(fac, ('x', 'zl'), 0, 0, tiled=True)  14.1 us
    unnamed x43, local copies, waits for them, and re-layouts  11.7 us
    ppermute x8, waiting for transfers between devices, shift(): lax.ppermute(value, axis, [(i, (i + by) % size) for i in range(size)])  9.96 us
    all_to_all x1, starting transfers between devices, on_device(): got = lax.all_to_all(sent, 'zl', 0, 0, tiled=True)  8.04 us
  transfers between devices with their start and end apart: 15, of which 7 were waited for; matrix products, arithmetic and copies ran while one was open for 4% of the time, Pallas kernels for 2%

profile of v4, /device:TPU:1, one launch (start us, length us, event | category | flops | bytes accessed | tf_op | source)
XLA Modules:
  0.0 159.0 jit_solution(6523950192586344014)
XLA Ops:
  7.2 0.0 all-gather.9.cloned.1.call-start
  7.2 2.0 %pad_add_fusion = bf16[288,1024]{1,0:T(8,128)(2,1)} fusion(bf16[56,1024]{1,0:T(8,128)(2,1)} %param.11, bf16[56,1024]{1,0:T(8,128)(2,1)} %refs_3_.1, bf16[56,1024]{1,0:T(8,128)(2,1)} %refs_2_.1, bf16[56,1024]{1,0:T(8,128)(2,1)} %param.10, bf16[56,1024]{1,0:T(8,128)(2,1)} %param.9), kind=kLoop, calls=%fused_computation.2 | loop fusion | flops 2949120 | bytes 1163264 | tf_op jit(solution)/shard_map/add | solution.py:125
  9.2 0.0 all-gather.9.cloned.1.call-update
  9.2 0.0 all-gather.7.cloned.1.call-start
  9.3 11.5 %collective-permute-start = (bf16[64,1024]{1,0:T(8,128)(2,1)S(1)}, bf16[64,1024]{1,0:T(8,128)(2,1)S(1)}, u32[]{:S(2)}, u32[]{:S(2)}) collective-permute-start(bf16[64,1024]{1,0:T(8,128)(2,1)S(1)} %get-tuple-element.9), channel_id=1, source_target_pairs={{0,256},{256,0},{1,257},{257,1},{2,258},{258,2},{3,259},{259,3},{4... | collective-permute-start | bytes 393224 | tf_op jit(solution)/shard_map/ppermute | solution.py:22
  20.8 3.9 %collective-permute-done = bf16[64,1024]{1,0:T(8,128)(2,1)S(1)} collective-permute-done((bf16[64,1024]{1,0:T(8,128)(2,1)S(1)}, bf16[64,1024]{1,0:T(8,128)(2,1)S(1)}, u32[]{:S(2)}, u32[]{:S(2)}) %collective-permute-start) | collective-permute-done | bytes 131104 | tf_op jit(solution)/shard_map/ppermute | solution.py:22
  24.7 4.4 %collective-permute-start.2 = (bf16[2,64,1024]{2,1,0:T(8,128)(2,1)S(1)}, bf16[2,64,1024]{2,1,0:T(8,128)(2,1)S(1)}, u32[]{:S(2)}, u32[]{:S(2)}) collective-permute-start(bf16[2,64,1024]{2,1,0:T(8,128)(2,1)S(1)} %pad_maximum_fusion.1.refs_0_), channel_id=1, source_target_pairs={{0,56},{8,0},{16,8},{24,16},{32,24},{40,32},{48,40},{56,48},{1,57}... | collective-permute-start | bytes 786440 | tf_op jit(solution)/shard_map/ppermute | solution.py:27
  29.2 1.9 %collective-permute-start.1 = (bf16[2,64,1024]{2,1,0:T(8,128)(2,1)S(1)}, bf16[2,64,1024]{2,1,0:T(8,128)(2,1)S(1)}, u32[]{:S(2)}, u32[]{:S(2)}) collective-permute-start(bf16[2,64,1024]{2,1,0:T(8,128)(2,1)S(1)} %pad_maximum_fusion.1.refs_0_), channel_id=1, source_target_pairs={{0,8},{8,16},{16,24},{24,32},{32,40},{40,48},{48,56},{56,0},{1,9},... | collective-permute-start | bytes 786440 | tf_op jit(solution)/shard_map/ppermute | solution.py:27
  31.1 2.3 %collective-permute-done.2.refs_2_ = bf16[2,64,1024]{2,1,0:T(8,128)(2,1)S(1)} collective-permute-done((bf16[2,64,1024]{2,1,0:T(8,128)(2,1)S(1)}, bf16[2,64,1024]{2,1,0:T(8,128)(2,1)S(1)}, u32[]{:S(2)}, u32[]{:S(2)}) %collective-permute-start.2) | collective-permute-done | bytes 262176 | tf_op jit(solution)/shard_map/ppermute | solution.py:27
  33.4 5.3 %collective-permute-start.4 = (bf16[2,64,1024]{2,1,0:T(8,128)(2,1)S(1)}, bf16[2,64,1024]{2,1,0:T(8,128)(2,1)S(1)}, u32[]{:S(2)}, u32[]{:S(2)}) collective-permute-start(bf16[2,64,1024]{2,1,0:T(8,128)(2,1)S(1)} %collective-permute-done.2.refs_2_), channel_id=1, source_target_pairs={{0,56},{8,0},{16,8},{24,16},{32,24},{40,32},{48,40},{56,48},{1,57}... | collective-permute-start | bytes 786440 | tf_op jit(solution)/shard_map/ppermute | solution.py:27
  38.7 0.0 collective-permute-done.1.refs_1_
  38.7 1.9 %collective-permute-start.3 = (bf16[2,64,1024]{2,1,0:T(8,128)(2,1)S(1)}, bf16[2,64,1024]{2,1,0:T(8,128)(2,1)S(1)}, u32[]{:S(2)}, u32[]{:S(2)}) collective-permute-start(bf16[2,64,1024]{2,1,0:T(8,128)(2,1)S(1)} %collective-permute-done.1.refs_1_), channel_id=1, source_target_pairs={{0,8},{8,16},{16,24},{24,32},{32,40},{40,48},{48,56},{56,0},{1,9},... | collective-permute-start | bytes 786440 | tf_op jit(solution)/shard_map/ppermute | solution.py:27
  40.7 1.3 collective-permute-done.4.refs_4_
  42.0 5.4 %collective-permute-start.6 = (bf16[2,64,1024]{2,1,0:T(8,128)(2,1)S(1)}, bf16[2,64,1024]{2,1,0:T(8,128)(2,1)S(1)}, u32[]{:S(2)}, u32[]{:S(2)}) collective-permute-start(bf16[2,64,1024]{2,1,0:T(8,128)(2,1)S(1)} %collective-permute-done.4.refs_4_), channel_id=1, source_target_pairs={{0,56},{8,0},{16,8},{24,16},{32,24},{40,32},{48,40},{56,48},{1,57}... | collective-permute-start | bytes 786440 | tf_op jit(solution)/shard_map/ppermute | solution.py:27
  47.5 0.0 collective-permute-done.3.refs_3_
  47.5 1.9 %collective-permute-start.5 = (bf16[2,64,1024]{2,1,0:T(8,128)(2,1)S(1)}, bf16[2,64,1024]{2,1,0:T(8,128)(2,1)S(1)}, u32[]{:S(2)}, u32[]{:S(2)}) collective-permute-start(bf16[2,64,1024]{2,1,0:T(8,128)(2,1)S(1)} %collective-permute-done.3.refs_3_), channel_id=1, source_target_pairs={{0,8},{8,16},{16,24},{24,32},{32,40},{40,48},{48,56},{56,0},{1,9},... | collective-permute-start | bytes 786440 | tf_op jit(solution)/shard_map/ppermute | solution.py:27
  49.4 1.3 collective-permute-done.6.refs_6_
  50.8 5.4 %collective-permute-start.8 = (bf16[1,64,1024]{2,1,0:T(8,128)(2,1)S(1)}, bf16[1,64,1024]{2,1,0:T(8,128)(2,1)S(1)}, u32[]{:S(2)}, u32[]{:S(2)}) collective-permute-start(bf16[1,64,1024]{2,1,0:T(8,128)(2,1)S(1)} %slice.73), channel_id=1, source_target_pairs={{0,56},{8,0},{16,8},{24,16},{32,24},{40,32},{48,40},{56,48},{1,57}... | collective-permute-start | bytes 393224 | tf_op jit(solution)/shard_map/ppermute | solution.py:27
  56.2 0.0 collective-permute-done.5.refs_5_
  56.2 1.9 %collective-permute-start.7 = (bf16[1,64,1024]{2,1,0:T(8,128)(2,1)S(1)}, bf16[1,64,1024]{2,1,0:T(8,128)(2,1)S(1)}, u32[]{:S(2)}, u32[]{:S(2)}) collective-permute-start(bf16[1,64,1024]{2,1,0:T(8,128)(2,1)S(1)} %slice.72), channel_id=1, source_target_pairs={{0,8},{8,16},{16,24},{24,32},{32,40},{40,48},{48,56},{56,0},{1,9},... | collective-permute-start | bytes 393224 | tf_op jit(solution)/shard_map/ppermute | solution.py:27
  58.2 0.0 collective-permute-done.8.refs_8_
  58.2 4.9 %collective-permute-done.7.refs_7_ = bf16[1,64,1024]{2,1,0:T(8,128)(2,1)S(1)} collective-permute-done((bf16[1,64,1024]{2,1,0:T(8,128)(2,1)S(1)}, bf16[1,64,1024]{2,1,0:T(8,128)(2,1)S(1)}, u32[]{:S(2)}, u32[]{:S(2)}) %collective-permute-start.7) | collective-permute-done | bytes 131104 | tf_op jit(solution)/shard_map/ppermute | solution.py:27
  63.2 0.8 pad_maximum_fusion
  64.0 0.0 all-gather.7.cloned.1.call-update
  64.0 0.0 all-gather.5.cloned.1.call-start
  64.1 0.0 all-gather.9.cloned.1.call-done
  64.2 0.8 copy-done.17
  65.0 1.7 %copy-done.1 = bf16[1152,1024]{1,0:T(8,128)(2,1)S(1)} copy-done((bf16[1152,1024]{1,0:T(8,128)(2,1)S(1)}, bf16[1152,1024]{1,0:T(8,128)(2,1)}, u32[]{:S(2)}) %copy-start.1) | copy-done | bytes 2359320
  66.6 0.2 shard_map.86.refs_9_
  66.8 0.8 copy-done.3
  67.6 0.1 copy-done.6
  67.7 0.1 copy-done.9
  67.7 0.0 copy-done.13
  67.8 2.0 %shard_map.88 = f32[256,1152]{1,0:T(8,128)} custom-call(s32[1]{0:T(128)} %bitcast.4.place, bf16[2,64,1024]{2,1,0:T(8,128)(2,1)S(1)} %pad_maximum_fusion.1.refs_0_, bf16[2,64,1024]{2,1,0:T(8,128)(2,1)S(1)} %copy-done.3, bf16[2,64,1024]{2,1,0:T(8,128)(2,1)S(1)} %collective-permute-done.2.refs_2_, bf16[2,64,1024]{2,1,0:T(8,128)(2,1)S(1)} %copy-done.9, ...), custom_call_target="tpu_custom_call" | custom-call | flops 603979776 | bytes 2359296 | tf_op jit(solution)/shard_map/pallas_call | solution.py:31
  69.8 7.1 %collective-permute-start.9 = (f32[256,1152]{1,0:T(8,128)}, f32[256,1152]{1,0:T(8,128)}, u32[]{:S(2)}, u32[]{:S(2)}) collective-permute-start(f32[256,1152]{1,0:T(8,128)} %shard_map.88), channel_id=1, source_target_pairs={{0,1},{1,0},{2,3},{3,2},{4,5},{5,4},{6,7},{7,6},{8,9},{9,8},{10,11... | collective-permute-start | bytes 3538952 | tf_op jit(solution)/shard_map/ppermute | solution.py:22
  76.9 0.7 slice_dynamic-update-slice_fusion.2
  77.6 0.7 slice_dynamic-update-slice_fusion.1
  78.2 0.7 slice_dynamic-update-slice_fusion
  78.9 0.0 all-gather.5.cloned.1.call-update
  78.9 0.9 copy-done.4
  79.9 0.9 copy-done.7
  80.8 0.9 copy-done.10
  81.8 0.9 copy-done.14
  82.7 0.9 shard_map.87
  83.6 0.0 collective-permute-done.9
  83.7 2.3 %multiply_convert_fusion = f16[256,1152]{1,0:T(8,128)(2,1)} fusion(f32[256,1152]{1,0:T(8,128)S(1)} %shard_map.87, f32[256,1152]{1,0:T(8,128)} %collective-permute-done.9, f32[1152]{0:T(1024)S(1)} %select_select_fusion), kind=kLoop, calls=%fused_computation.1 | loop fusion | flops 884736 | bytes 2953728 | tf_op jit(solution)/shard_map/convert_element_type | solution.py:189
  86.0 8.0 %all-to-all-start = ((f16[4,64,1152]{2,1,0:T(8,128)(2,1)}), f16[4,64,1152]{2,1,0:T(8,128)(2,1)S(1)}, u32[]{:S(2)}, u32[]{:S(2)}) async-start(f16[4,64,1152]{2,1,0:T(8,128)(2,1)} %bitcast.5), calls=%async_computation | async-start | bytes 1179648 | tf_op jit(solution)/shard_map/all_to_all | solution.py:190
  94.0 15.7 %all-to-all-done = f16[4,64,1152]{2,1,0:T(8,128)(2,1)S(1)} async-done(((f16[4,64,1152]{2,1,0:T(8,128)(2,1)}), f16[4,64,1152]{2,1,0:T(8,128)(2,1)S(1)}, u32[]{:S(2)}, u32[]{:S(2)}) %all-to-all-start) | async-done | bytes 589856 | tf_op jit(solution)/shard_map/all_to_all | solution.py:190
  109.8 0.1 convert_reduce_fusion
  109.9 0.9 reshape.66
  110.8 0.1 reshape.65
  110.9 0.4 fusion.15
  111.3 0.0 copy-start.15
  111.3 0.0 copy-start.16
  111.3 0.2 fusion.9
  111.5 0.1 maximum_bitcast_fusion
  111.7 14.1 %all_to_all.10 = bf16[16,64,112]{2,1,0:T(8,128)(2,1)S(1)} all-to-all(bf16[16,64,112]{2,1,0:T(8,128)(2,1)S(1)} %bitcast.29), channel_id=1, replica_groups=mesh['zh'=2,'x'=4,'y'=8,'zl'=4,'c'=2] {'x','zl'}, dimensions={0} | all-to-all | bytes 458752 | tf_op jit(solution)/shard_map/all_to_all | solution.py:198
  125.9 4.2 %collective-permute-start.10 = (bf16[4,256,112]{2,1,0:T(8,128)(2,1)S(1)}, bf16[4,256,112]{2,1,0:T(8,128)(2,1)S(1)}, u32[]{:S(2)}, u32[]{:S(2)}) collective-permute-start(bf16[4,256,112]{2,1,0:T(8,128)(2,1)S(1)} %bitcast.26), channel_id=1, source_target_pairs={{0,1},{1,0},{2,3},{3,2},{4,5},{5,4},{6,7},{7,6},{8,9},{9,8},{10,11... | collective-permute-start | bytes 688136 | tf_op jit(solution)/shard_map/ppermute | solution.py:22
  130.1 0.0 all-gather.7.cloned.1.call-done.refs_1_
  130.1 16.6 %all-gather.5.cloned.1.call-done.refs_0_ = bf16[1280,1024]{1,0:T(8,128)(2,1)} async-done(((bf16[320,1024]{1,0:T(8,128)(2,1)}), bf16[1280,1024]{1,0:T(8,128)(2,1)}) %all-gather.5.cloned.1.call-update) | async-done | bytes 2621456 | tf_op jit(solution)/shard_map/all_gather | solution.py:165
  146.8 0.0 collective-permute-done.10.other
  146.8 1.7 %copy-done = bf16[1280,1024]{1,0:T(8,128)(2,1)S(1)} copy-done((bf16[1280,1024]{1,0:T(8,128)(2,1)S(1)}, bf16[1280,1024]{1,0:T(8,128)(2,1)}, u32[]{:S(2)}) %copy-start) | copy-done | bytes 2621464
  148.5 1.4 copy-done.11
  149.9 2.6 %shard_map.89 = (f32[56,1024]{1,0:T(8,128)}, f32[56,1024]{1,0:T(8,128)}) custom-call(s32[1]{0:T(128)} %bitcast.place, bf16[4,256,112]{2,1,0:T(8,128)(2,1)S(1)} %bitcast.27, bf16[4,256,112]{2,1,0:T(8,128)(2,1)S(1)} %collective-permute-done.10.other, bf16[1280,1024]{1,0:T(8,128)(2,1)S(1)} %copy-done, bf16[768,1024]{1,0:T(8,128)(2,1)S(1)} %copy-done.11, ...), custom_call_target="tpu_custom_call" | custom-call | flops 469762048 | bytes 4194304 | tf_op jit(solution)/shard_map/pallas_call | solution.py:31
  (43 shorter events, 0.3 us)
Async XLA Ops:
  7.2 2.1 %copy-start.18 = (bf16[32,1024]{1,0:T(8,128)(2,1)S(1)}, bf16[32,1024]{1,0:T(8,128)(2,1)}, u32[]{:S(2)}) copy-start(bf16[32,1024]{1,0:T(8,128)(2,1)} %param.8) | copy-start | bytes 196612
  7.2 2.1 %copy-start.19 = (bf16[32,1024]{1,0:T(8,128)(2,1)S(1)}, bf16[32,1024]{1,0:T(8,128)(2,1)}, u32[]{:S(2)}) copy-start(bf16[32,1024]{1,0:T(8,128)(2,1)} %param.7) | copy-start | bytes 196612
  7.2 57.0 %all-gather.9.cloned.1.call-start = ((), (), s32[]{:S(2)}) async-start(), calls=%async_computation.4 | async-start | bytes 2949120 | tf_op jit(solution)/shard_map/all_gather | solution.py:146
  9.2 120.9 %all-gather.7.cloned.1.call-start = ((), (), s32[]{:S(2)}) async-start(), calls=%async_computation.3 | async-start | bytes 1966080 | tf_op jit(solution)/shard_map/all_gather | solution.py:165
  9.3 15.4 %collective-permute-start = (bf16[64,1024]{1,0:T(8,128)(2,1)S(1)}, bf16[64,1024]{1,0:T(8,128)(2,1)S(1)}, u32[]{:S(2)}, u32[]{:S(2)}) collective-permute-start(bf16[64,1024]{1,0:T(8,128)(2,1)S(1)} %get-tuple-element.9), channel_id=1, source_target_pairs={{0,256},{256,0},{1,257},{257,1},{2,258},{258,2},{3,259},{259,3},{4... | collective-permute-start | bytes 393224 | tf_op jit(solution)/shard_map/ppermute | solution.py:22
  24.7 8.7 %collective-permute-start.2 = (bf16[2,64,1024]{2,1,0:T(8,128)(2,1)S(1)}, bf16[2,64,1024]{2,1,0:T(8,128)(2,1)S(1)}, u32[]{:S(2)}, u32[]{:S(2)}) collective-permute-start(bf16[2,64,1024]{2,1,0:T(8,128)(2,1)S(1)} %pad_maximum_fusion.1.refs_0_), channel_id=1, source_target_pairs={{0,56},{8,0},{16,8},{24,16},{32,24},{40,32},{48,40},{56,48},{1,57}... | collective-permute-start | bytes 786440 | tf_op jit(solution)/shard_map/ppermute | solution.py:27
  29.2 9.6 %collective-permute-start.1 = (bf16[2,64,1024]{2,1,0:T(8,128)(2,1)S(1)}, bf16[2,64,1024]{2,1,0:T(8,128)(2,1)S(1)}, u32[]{:S(2)}, u32[]{:S(2)}) collective-permute-start(bf16[2,64,1024]{2,1,0:T(8,128)(2,1)S(1)} %pad_maximum_fusion.1.refs_0_), channel_id=1, source_target_pairs={{0,8},{8,16},{16,24},{24,32},{32,40},{40,48},{48,56},{56,0},{1,9},... | collective-permute-start | bytes 786440 | tf_op jit(solution)/shard_map/ppermute | solution.py:27
  33.4 8.6 %collective-permute-start.4 = (bf16[2,64,1024]{2,1,0:T(8,128)(2,1)S(1)}, bf16[2,64,1024]{2,1,0:T(8,128)(2,1)S(1)}, u32[]{:S(2)}, u32[]{:S(2)}) collective-permute-start(bf16[2,64,1024]{2,1,0:T(8,128)(2,1)S(1)} %collective-permute-done.2.refs_2_), channel_id=1, source_target_pairs={{0,56},{8,0},{16,8},{24,16},{32,24},{40,32},{48,40},{56,48},{1,57}... | collective-permute-start | bytes 786440 | tf_op jit(solution)/shard_map/ppermute | solution.py:27
  38.7 25.4 %copy-start.2 = (bf16[2,64,1024]{2,1,0:T(8,128)(2,1)}, bf16[2,64,1024]{2,1,0:T(8,128)(2,1)S(1)}, u32[]{:S(2)}) copy-start(bf16[2,64,1024]{2,1,0:T(8,128)(2,1)S(1)} %collective-permute-done.1.refs_1_) | copy-start | bytes 786436
  38.7 8.7 %collective-permute-start.3 = (bf16[2,64,1024]{2,1,0:T(8,128)(2,1)S(1)}, bf16[2,64,1024]{2,1,0:T(8,128)(2,1)S(1)}, u32[]{:S(2)}, u32[]{:S(2)}) collective-permute-start(bf16[2,64,1024]{2,1,0:T(8,128)(2,1)S(1)} %collective-permute-done.1.refs_1_), channel_id=1, source_target_pairs={{0,8},{8,16},{16,24},{24,32},{32,40},{40,48},{48,56},{56,0},{1,9},... | collective-permute-start | bytes 786440 | tf_op jit(solution)/shard_map/ppermute | solution.py:27
  42.0 22.0 %copy-start.5 = (bf16[2,64,1024]{2,1,0:T(8,128)(2,1)}, bf16[2,64,1024]{2,1,0:T(8,128)(2,1)S(1)}, u32[]{:S(2)}) copy-start(bf16[2,64,1024]{2,1,0:T(8,128)(2,1)S(1)} %collective-permute-done.4.refs_4_) | copy-start | bytes 786436
  42.0 8.7 %collective-permute-start.6 = (bf16[2,64,1024]{2,1,0:T(8,128)(2,1)S(1)}, bf16[2,64,1024]{2,1,0:T(8,128)(2,1)S(1)}, u32[]{:S(2)}, u32[]{:S(2)}) collective-permute-start(bf16[2,64,1024]{2,1,0:T(8,128)(2,1)S(1)} %collective-permute-done.4.refs_4_), channel_id=1, source_target_pairs={{0,56},{8,0},{16,8},{24,16},{32,24},{40,32},{48,40},{56,48},{1,57}... | collective-permute-start | bytes 786440 | tf_op jit(solution)/shard_map/ppermute | solution.py:27
  47.5 16.5 %copy-start.8 = (bf16[2,64,1024]{2,1,0:T(8,128)(2,1)}, bf16[2,64,1024]{2,1,0:T(8,128)(2,1)S(1)}, u32[]{:S(2)}) copy-start(bf16[2,64,1024]{2,1,0:T(8,128)(2,1)S(1)} %collective-permute-done.3.refs_3_) | copy-start | bytes 786436
  47.5 8.7 %collective-permute-start.5 = (bf16[2,64,1024]{2,1,0:T(8,128)(2,1)S(1)}, bf16[2,64,1024]{2,1,0:T(8,128)(2,1)S(1)}, u32[]{:S(2)}, u32[]{:S(2)}) collective-permute-start(bf16[2,64,1024]{2,1,0:T(8,128)(2,1)S(1)} %collective-permute-done.3.refs_3_), channel_id=1, source_target_pairs={{0,8},{8,16},{16,24},{24,32},{32,40},{40,48},{48,56},{56,0},{1,9},... | collective-permute-start | bytes 786440 | tf_op jit(solution)/shard_map/ppermute | solution.py:27
  50.8 7.4 %collective-permute-start.8 = (bf16[1,64,1024]{2,1,0:T(8,128)(2,1)S(1)}, bf16[1,64,1024]{2,1,0:T(8,128)(2,1)S(1)}, u32[]{:S(2)}, u32[]{:S(2)}) collective-permute-start(bf16[1,64,1024]{2,1,0:T(8,128)(2,1)S(1)} %slice.73), channel_id=1, source_target_pairs={{0,56},{8,0},{16,8},{24,16},{32,24},{40,32},{48,40},{56,48},{1,57}... | collective-permute-start | bytes 393224 | tf_op jit(solution)/shard_map/ppermute | solution.py:27
  56.2 6.9 %collective-permute-start.7 = (bf16[1,64,1024]{2,1,0:T(8,128)(2,1)S(1)}, bf16[1,64,1024]{2,1,0:T(8,128)(2,1)S(1)}, u32[]{:S(2)}, u32[]{:S(2)}) collective-permute-start(bf16[1,64,1024]{2,1,0:T(8,128)(2,1)S(1)} %slice.72), channel_id=1, source_target_pairs={{0,8},{8,16},{16,24},{24,32},{32,40},{40,48},{48,56},{56,0},{1,9},... | collective-permute-start | bytes 393224 | tf_op jit(solution)/shard_map/ppermute | solution.py:27
  63.2 1.0 copy-start.12
  64.0 82.7 %all-gather.5.cloned.1.call-start = ((), (), s32[]{:S(2)}) async-start(), calls=%async_computation.2 | async-start | bytes 3276800 | tf_op jit(solution)/shard_map/all_gather | solution.py:165
  64.1 0.8 copy-start.17
  65.0 1.7 %copy-start.1 = (bf16[1152,1024]{1,0:T(8,128)(2,1)S(1)}, bf16[1152,1024]{1,0:T(8,128)(2,1)}, u32[]{:S(2)}) copy-start(bf16[1152,1024]{1,0:T(8,128)(2,1)} %all-gather.9.cloned.1.call-done) | copy-start | bytes 7077892
  66.6 0.9 copy-start.3
  66.6 1.0 copy-start.6
  66.6 1.1 copy-start.9
  66.6 1.1 copy-start.13
  69.8 13.9 %collective-permute-start.9 = (f32[256,1152]{1,0:T(8,128)}, f32[256,1152]{1,0:T(8,128)}, u32[]{:S(2)}, u32[]{:S(2)}) collective-permute-start(f32[256,1152]{1,0:T(8,128)} %shard_map.88), channel_id=1, source_target_pairs={{0,1},{1,0},{2,3},{3,2},{4,5},{5,4},{6,7},{7,6},{8,9},{9,8},{10,11... | collective-permute-start | bytes 3538952 | tf_op jit(solution)/shard_map/ppermute | solution.py:22
  78.9 1.0 copy-start.4
  79.9 0.9 copy-start.7
  80.8 0.9 copy-start.10
  81.8 0.9 copy-start.14
  86.0 23.8 %all-to-all-start = ((f16[4,64,1152]{2,1,0:T(8,128)(2,1)}), f16[4,64,1152]{2,1,0:T(8,128)(2,1)S(1)}, u32[]{:S(2)}, u32[]{:S(2)}) async-start(f16[4,64,1152]{2,1,0:T(8,128)(2,1)} %bitcast.5), calls=%async_computation | async-start | bytes 1179648 | tf_op jit(solution)/shard_map/all_to_all | solution.py:190
  111.3 35.5 %copy-start.15 = (bf16[56,1024]{1,0:T(8,128)(2,1)S(1)}, bf16[56,1024]{1,0:T(8,128)(2,1)}, u32[]{:S(2)}) copy-start(bf16[56,1024]{1,0:T(8,128)(2,1)} %refs_3_.1) | copy-start | bytes 344068
  111.3 35.5 %copy-start.16 = (bf16[56,1024]{1,0:T(8,128)(2,1)S(1)}, bf16[56,1024]{1,0:T(8,128)(2,1)}, u32[]{:S(2)}) copy-start(bf16[56,1024]{1,0:T(8,128)(2,1)} %refs_2_.1) | copy-start | bytes 344068
  125.9 20.9 %collective-permute-start.10 = (bf16[4,256,112]{2,1,0:T(8,128)(2,1)S(1)}, bf16[4,256,112]{2,1,0:T(8,128)(2,1)S(1)}, u32[]{:S(2)}, u32[]{:S(2)}) collective-permute-start(bf16[4,256,112]{2,1,0:T(8,128)(2,1)S(1)} %bitcast.26), channel_id=1, source_target_pairs={{0,1},{1,0},{2,3},{3,2},{4,5},{5,4},{6,7},{7,6},{8,9},{9,8},{10,11... | collective-permute-start | bytes 688136 | tf_op jit(solution)/shard_map/ppermute | solution.py:22
  146.8 1.7 %copy-start = (bf16[1280,1024]{1,0:T(8,128)(2,1)S(1)}, bf16[1280,1024]{1,0:T(8,128)(2,1)}, u32[]{:S(2)}) copy-start(bf16[1280,1024]{1,0:T(8,128)(2,1)} %all-gather.5.cloned.1.call-done.refs_0_) | copy-start | bytes 7864324
  148.5 1.4 copy-start.11
Sparse Core Ops, SparseCore 0:
  10.1 43.8 all-gather.8
  64.1 39.0 all-gather.6
  105.3 41.3 all-gather.4

commit v5 on v4

v5 whole, which is shorter than its diff:
```python
import functools

import jax
import jax.numpy as jnp
import numpy as np
from jax import lax
from jax.experimental import pallas as pl
from jax.experimental.pallas import tpu as pltpu
from jax.sharding import Mesh, PartitionSpec as P

NODE = {"zh": 2, "x": 4, "y": 8}
LOCAL = {"zl": 4, "c": 2}

PRE_SCALE = 64.0
TAN_SCALE = 0.5
BACK_SCALE = 32.0

VMEM = pl.BlockSpec(memory_space=pltpu.VMEM)
ANY = pl.BlockSpec(memory_space=pl.ANY)
SMEM = pl.BlockSpec(memory_space=pltpu.SMEM)


def swap(value, axis):
    return lax.ppermute(value, axis, [(0, 1), (1, 0)])


def shift(value, axis, by):
    size = lax.axis_size(axis)
    return lax.ppermute(value, axis, [(i, (i + by) % size) for i in range(size)])


def mix(value, axis, by):
    return lax.ppermute(value, axis, [(i, i ^ by) for i in range(lax.axis_size(axis))])


def local_call(body, out_shape, flops, moved, interpret, *args, **options):
    return pl.pallas_call(
        body,
        out_shape=out_shape,
        cost_estimate=pl.CostEstimate(flops=flops, bytes_accessed=moved, transcendentals=0),
        compiler_params=pltpu.CompilerParams(vmem_limit_bytes=16 * 1024 * 1024),
        interpret=interpret,
        **options,
    )(*args)


def terms_kernel(own, tok_rows, place, *refs):
    *blocks, out, x_half, g_half, w_all, row_sems, w_sems = refs
    blocks, weights = blocks[:-4], blocks[-4:]
    slabs = [(block, z) for block in blocks for z in range(block.shape[0])]
    middle = len(slabs) // 2
    cut = 4 * tok_rows
    cot_rows = weights[0].shape[0] - tok_rows

    copies = []
    for i, weight in enumerate(weights):
        tops = w_all.at[pl.ds(i * tok_rows, tok_rows)]
        rest = w_all.at[pl.ds(cut + i * cot_rows, cot_rows)]
        copies.append(
            pltpu.make_async_copy(weight.at[pl.ds(0, tok_rows)], tops, w_sems.at[2 * i])
        )
        copies.append(
            pltpu.make_async_copy(
                weight.at[pl.ds(tok_rows, cot_rows)], rest, w_sems.at[2 * i + 1]
            )
        )
    for copy in copies:
        copy.start()

    def take(chosen):
        moves = []
        for i, (block, z) in enumerate(chosen):
            row = pl.multiple_of((((i // 2) ^ place[1]) * 2 + i % 2) * own, own)
            for j, half in enumerate((x_half, g_half)):
                moves.append(
                    pltpu.make_async_copy(
                        block.at[z, pl.ds(j * own, own)],
                        half.at[pl.ds(row, own)],
                        row_sems.at[2 * i + j],
                    )
                )
        for move in moves:
            move.start()
        for move in moves:
            move.wait()

    @pl.when(place[0] == 0)
    def _():
        take(slabs[:middle])

    @pl.when(place[0] != 0)
    def _():
        take(slabs[middle:])

    for copy in copies:
        copy.wait()
    across = (((1,), (1,)), ((), ()))
    out[:, :cut] = lax.dot_general(
        x_half[...], w_all[:cut], across, preferred_element_type=jnp.float32
    )
    out[:, cut:] = lax.dot_general(
        g_half[...], w_all[cut:], across, preferred_element_type=jnp.float32
    )


def hvp_kernel(first, mine, other, kept, given, *outs):
    down = (((0,), (0,)), ((), ()))
    for i, out in enumerate(outs):
        acc = None
        for fac, rows in ((mine, kept), (other, given)):
            lhs = jnp.concatenate([fac[s, first + i] for s in range(fac.shape[0])], axis=0)
            term = lax.dot_general(lhs, rows[...], down, preferred_element_type=jnp.float32)
            acc = term if acc is None else acc + term
        out[...] = acc.astype(out.dtype)


def factors(pre_gate, pre_up, tan_gate, tan_up, back):
    sig = jax.nn.sigmoid(pre_gate)
    slope = sig * (1.0 + pre_gate * (1.0 - sig))
    bend = sig * (1.0 - sig) * (2.0 + pre_gate * (1.0 - 2.0 * sig))
    fac_gate = (back * (tan_up * slope + pre_up * bend * tan_gate)).astype(jnp.bfloat16)
    fac_up = (back * slope * tan_gate).astype(jnp.bfloat16)
    return (fac_gate, fac_up)


def stacked(parts, rows):
    row, out = 0, None
    for part in parts:
        padded = lax.pad(
            part, jnp.zeros((), part.dtype),
            ((row, rows - row - part.shape[0], 0), (0, 0, 0)),
        )
        out = padded if out is None else out + padded
        row += part.shape[0]
    return out


def on_device(
    tokens, cotangent, gate_weight, up_weight, down_weight, gate_probe, up_probe, interpret
):
    nx, ny, nzl = lax.axis_size("x"), lax.axis_size("y"), lax.axis_size("zl")
    own, feats = tokens.shape
    hid = gate_weight.shape[0]
    total = own * lax.axis_size(("zh", "x", "y"))
    zl, core = lax.axis_index("zl"), lax.axis_index("c")

    rows = stacked([tokens, cotangent], 2 * own)
    block = jnp.stack([rows, swap(rows, "zh")], axis=0)

    tok_rows, cot_rows = 4 * hid, hid * 8 // 7
    mats = stacked(
        [gate_weight, up_weight, gate_probe, up_probe, down_weight], tok_rows + cot_rows
    )
    weights = [mats] + [shift(mats, "x", by) for by in range(1, nx)]

    ahead = behind = block
    blocks = [block]
    for _ in range(ny // 2 - 1):
        ahead, behind = shift(ahead, "y", 1), shift(behind, "y", -1)
        blocks += [ahead, behind]
    blocks += [shift(ahead[:1], "y", 1), shift(behind[1:], "y", -1)]

    count = ny * own
    cut, columns = nx * tok_rows, nx * (tok_rows + cot_rows)
    term = functools.partial(
        local_call,
        functools.partial(terms_kernel, own, tok_rows),
        (
            jax.ShapeDtypeStruct((count, columns), jnp.float32),
            jax.ShapeDtypeStruct((count, feats), jnp.bfloat16),
        ),
        2 * count * columns * feats,
        2 * columns * feats,
        interpret,
        in_specs=[SMEM] + [ANY] * (len(blocks) + nx),
        out_specs=(VMEM, VMEM),
        scratch_shapes=[
            pltpu.VMEM((count, feats), jnp.bfloat16),
            pltpu.VMEM((columns, feats), jnp.bfloat16),
            pltpu.SemaphoreType.DMA((4 * ny,)),
            pltpu.SemaphoreType.DMA((2 * nx,)),
        ],
    )
    given, given_rows = term(jnp.stack([1 - core, zl]), *blocks, *weights)
    other = swap(given, "c")
    kept, kept_rows = term(jnp.stack([core, zl]), *blocks, *weights)
    terms = kept + other

    column = np.arange(columns)
    scale = np.where(
        column >= cut,
        BACK_SCALE,
        np.where(column % tok_rows >= 2 * hid, TAN_SCALE, PRE_SCALE),
    ).astype(np.float32)
    share = count // nzl
    sent = (terms[share:] * scale).astype(jnp.float16)
    got = [
        mix(sent[(by - 1) * share : by * share], "zl", by).astype(jnp.float32)
        for by in range(1, nzl)
    ]
    proj = terms[:share] + sum(got) * (1.0 / scale)
    tok_part = proj[:, :cut].reshape(share, nx, 4, hid)
    back = proj[:, cut:].reshape(share, nx, cot_rows)[:, :, :hid]
    fac = jnp.concatenate(factors(*[tok_part[:, :, i] for i in range(4)], back), axis=2)

    fac = fac.transpose(1, 0, 2)
    fac = jnp.stack([fac] + [mix(fac, "zl", by) for by in range(1, nzl)], axis=0)
    fac_other = swap(fac, "c")

    def hvp(first, kinds):
        return local_call(
            functools.partial(hvp_kernel, first),
            tuple(jax.ShapeDtypeStruct((2 * hid, feats), kind) for kind in kinds),
            8 * len(kinds) * hid * count * feats,
            4 * count * feats,
            interpret,
            fac,
            fac_other,
            kept_rows,
            given_rows,
            in_specs=[VMEM] * 4,
            out_specs=(VMEM,) * len(kinds),
        )
    away = hvp(1, [jnp.bfloat16] * (nx - 1))
    away = [shift(part, "x", -by) for by, part in enumerate(away, 1)]
    (both,) = hvp(0, [jnp.float32])
    both = (both + sum(part.astype(jnp.float32) for part in away)) / total
    gate_diag = gate_probe.astype(jnp.float32) * both[:hid]
    up_diag = up_probe.astype(jnp.float32) * both[hid:]
    return (gate_diag, up_diag)


def solution(mesh, interpret=False):
    sizes = {**NODE, **LOCAL}
    cut = Mesh(mesh.devices.reshape(tuple(sizes.values())), tuple(sizes))
    placed = P(tuple(NODE), tuple(LOCAL))
    return jax.shard_map(
        functools.partial(on_device, interpret=interpret),
        mesh=cut,
        in_specs=(placed,) * 7,
        out_specs=(placed, placed),
        check_vma=False,
    )
```

time: 160 us -> 156 us (0.975)
  starting transfers between devices: 59.3 us -> 86.7 us
  blocking collectives: 14.1 us -> 0 us
  between operations: 14.2 us -> 1.16 us
  Pallas kernels: 5.67 us -> 11.4 us
  local copies, waits for them, and re-layouts: 13.8 us -> 8.91 us
  waiting for transfers between devices: 46.3 us -> 42.7 us
  other arithmetic: 5.64 us -> 3.71 us
    ppermute x0 -> x6, starting transfers between devices: none -> 21.8 us  [mix(): lax.ppermute(value, axis, [(i, i ^ by) for i in range(lax.axis_size(axis))])]
    ppermute x8 -> x14, starting transfers between devices: 28.3 us -> 45.7 us  [shift(): lax.ppermute(value, axis, [(i, (i + by) % size) for i in range(size)])]
    all_gather x3 -> x0, waiting for transfers between devices: 16.7 us -> none  [the longest x2 16.6 us: on_device(): chunks.append(lax.all_gather(part, 'x', axis=0, tiled=True))]
    all_to_all x1 -> x0, waiting for transfers between devices: 15.7 us -> none  [on_device(): got = lax.all_to_all(sent, 'zl', 0, 0, tiled=True)]
    ppermute x0 -> x6, waiting for transfers between devices: none -> 14.6 us  [mix(): lax.ppermute(value, axis, [(i, i ^ by) for i in range(lax.axis_size(axis))])]
    all_to_all x1 -> x0, blocking collectives: 14.1 us -> none  [on_device(): lax.all_to_all(fac, ('x', 'zl'), 0, 0, tiled=True)]
    ppermute x8 -> x14, waiting for transfers between devices: 9.96 us -> 23 us  [shift(): lax.ppermute(value, axis, [(i, (i + by) % size) for i in range(size)])]
    all_to_all x1 -> x0, starting transfers between devices: 8.04 us -> none  [on_device(): got = lax.all_to_all(sent, 'zl', 0, 0, tiled=True)]
  transfers between devices with their start and end apart: 15 -> 23, of which waited for: 7 -> 10; matrix products, arithmetic and copies ran while one was open for 4% -> 2% of each run, Pallas kernels for 2% -> 4%
where the time goes in v5:
time: 156 us; the launch traced here: 155 us
  starting transfers between devices  86.7 us (56%)
  waiting for transfers between devices  42.7 us (27%)
  Pallas kernels  11.4 us (7%)
  local copies, waits for them, and re-layouts  8.91 us (6%)
  other arithmetic  3.71 us (2%)
    ppermute x14, starting transfers between devices, shift(): lax.ppermute(value, axis, [(i, (i + by) % size) for i in range(size)])  45.7 us
    ppermute x14, waiting for transfers between devices, shift(): lax.ppermute(value, axis, [(i, (i + by) % size) for i in range(size)])  23 us
    ppermute x6, starting transfers between devices, mix(): lax.ppermute(value, axis, [(i, i ^ by) for i in range(lax.axis_size(axis))])  21.8 us
    ppermute x3, starting transfers between devices, swap(): return lax.ppermute(value, axis, [(0, 1), (1, 0)])  19.2 us
    ppermute x6, waiting for transfers between devices, mix(): lax.ppermute(value, axis, [(i, i ^ by) for i in range(lax.axis_size(axis))])  14.6 us
    pallas_call x4, Pallas kernels, local_call(): pl.pallas_call(body, out_shape=out_shape, cost_estimate=pl.CostEstimate(f...  11.4 us
    unnamed x38, local copies, waits for them, and re-layouts  6.09 us
    ppermute x3, waiting for transfers between devices, swap(): return lax.ppermute(value, axis, [(0, 1), (1, 0)])  5.04 us
  transfers between devices with their start and end apart: 23, of which 10 were waited for; matrix products, arithmetic and copies ran while one was open for 2% of the time, Pallas kernels for 4%

profile of v5, /device:TPU:1, one launch (start us, length us, event | category | flops | bytes accessed | tf_op | source)
XLA Modules:
  0.0 154.6 jit_solution(336632611634176036)
XLA Ops:
  0.6 0.9 fusion.12
  1.5 11.5 %collective-permute-start = (bf16[64,1024]{1,0:T(8,128)(2,1)S(1)}, bf16[64,1024]{1,0:T(8,128)(2,1)S(1)}, u32[]{:S(2)}, u32[]{:S(2)}) collective-permute-start(bf16[64,1024]{1,0:T(8,128)(2,1)S(1)} %get-tuple-element.30), channel_id=1, source_target_pairs={{0,256},{256,0},{1,257},{257,1},{2,258},{258,2},{3,259},{259,3},{4... | collective-permute-start | bytes 393224 | tf_op jit(solution)/shard_map/ppermute | solution.py:24
  13.0 3.9 %collective-permute-done = bf16[64,1024]{1,0:T(8,128)(2,1)S(1)} collective-permute-done((bf16[64,1024]{1,0:T(8,128)(2,1)S(1)}, bf16[64,1024]{1,0:T(8,128)(2,1)S(1)}, u32[]{:S(2)}, u32[]{:S(2)}) %collective-permute-start) | collective-permute-done | bytes 131104 | tf_op jit(solution)/shard_map/ppermute | solution.py:24
  16.9 4.4 %collective-permute-start.2 = (bf16[2,64,1024]{2,1,0:T(8,128)(2,1)S(1)}, bf16[2,64,1024]{2,1,0:T(8,128)(2,1)S(1)}, u32[]{:S(2)}, u32[]{:S(2)}) collective-permute-start(bf16[2,64,1024]{2,1,0:T(8,128)(2,1)S(1)} %pad_maximum_fusion.refs_0_), channel_id=1, source_target_pairs={{0,56},{8,0},{16,8},{24,16},{32,24},{40,32},{48,40},{56,48},{1,57}... | collective-permute-start | bytes 786440 | tf_op jit(solution)/shard_map/ppermute | solution.py:29
  21.3 1.9 %collective-permute-start.1 = (bf16[2,64,1024]{2,1,0:T(8,128)(2,1)S(1)}, bf16[2,64,1024]{2,1,0:T(8,128)(2,1)S(1)}, u32[]{:S(2)}, u32[]{:S(2)}) collective-permute-start(bf16[2,64,1024]{2,1,0:T(8,128)(2,1)S(1)} %pad_maximum_fusion.refs_0_), channel_id=1, source_target_pairs={{0,8},{8,16},{16,24},{24,32},{32,40},{40,48},{48,56},{56,0},{1,9},... | collective-permute-start | bytes 786440 | tf_op jit(solution)/shard_map/ppermute | solution.py:29
  23.3 2.3 %collective-permute-done.2.refs_2_ = bf16[2,64,1024]{2,1,0:T(8,128)(2,1)S(1)} collective-permute-done((bf16[2,64,1024]{2,1,0:T(8,128)(2,1)S(1)}, bf16[2,64,1024]{2,1,0:T(8,128)(2,1)S(1)}, u32[]{:S(2)}, u32[]{:S(2)}) %collective-permute-start.2) | collective-permute-done | bytes 262176 | tf_op jit(solution)/shard_map/ppermute | solution.py:29
  25.6 5.3 %collective-permute-start.4 = (bf16[2,64,1024]{2,1,0:T(8,128)(2,1)S(1)}, bf16[2,64,1024]{2,1,0:T(8,128)(2,1)S(1)}, u32[]{:S(2)}, u32[]{:S(2)}) collective-permute-start(bf16[2,64,1024]{2,1,0:T(8,128)(2,1)S(1)} %collective-permute-done.2.refs_2_), channel_id=1, source_target_pairs={{0,56},{8,0},{16,8},{24,16},{32,24},{40,32},{48,40},{56,48},{1,57}... | collective-permute-start | bytes 786440 | tf_op jit(solution)/shard_map/ppermute | solution.py:29
  30.9 1.9 %collective-permute-start.3 = (bf16[2,64,1024]{2,1,0:T(8,128)(2,1)S(1)}, bf16[2,64,1024]{2,1,0:T(8,128)(2,1)S(1)}, u32[]{:S(2)}, u32[]{:S(2)}) collective-permute-start(bf16[2,64,1024]{2,1,0:T(8,128)(2,1)S(1)} %collective-permute-done.1.refs_1_), channel_id=1, source_target_pairs={{0,8},{8,16},{16,24},{24,32},{32,40},{40,48},{48,56},{56,0},{1,9},... | collective-permute-start | bytes 786440 | tf_op jit(solution)/shard_map/ppermute | solution.py:29
  32.9 1.2 pad_add_fusion.refs_9_
  34.0 4.4 %collective-permute-start.11 = (bf16[288,1024]{1,0:T(8,128)(2,1)S(1)}, bf16[288,1024]{1,0:T(8,128)(2,1)S(1)}, u32[]{:S(2)}, u32[]{:S(2)}) collective-permute-start(bf16[288,1024]{1,0:T(8,128)(2,1)S(1)} %pad_add_fusion.refs_9_), channel_id=1, source_target_pairs={{0,192},{64,0},{128,64},{192,128},{1,193},{65,1},{129,65},{193,129... | collective-permute-start | bytes 1769480 | tf_op jit(solution)/shard_map/ppermute | solution.py:29
  38.4 2.4 %collective-permute-start.10 = (bf16[288,1024]{1,0:T(8,128)(2,1)S(1)}, bf16[288,1024]{1,0:T(8,128)(2,1)S(1)}, u32[]{:S(2)}, u32[]{:S(2)}) collective-permute-start(bf16[288,1024]{1,0:T(8,128)(2,1)S(1)} %pad_add_fusion.refs_9_), channel_id=1, source_target_pairs={{0,128},{64,192},{128,0},{192,64},{1,129},{65,193},{129,1},{193,65... | collective-permute-start | bytes 1769480 | tf_op jit(solution)/shard_map/ppermute | solution.py:29
  40.9 2.5 %collective-permute-start.9 = (bf16[288,1024]{1,0:T(8,128)(2,1)S(1)}, bf16[288,1024]{1,0:T(8,128)(2,1)S(1)}, u32[]{:S(2)}, u32[]{:S(2)}) collective-permute-start(bf16[288,1024]{1,0:T(8,128)(2,1)S(1)} %pad_add_fusion.refs_9_), channel_id=1, source_target_pairs={{0,64},{64,128},{128,192},{192,0},{1,65},{65,129},{129,193},{193,1... | collective-permute-start | bytes 1769480 | tf_op jit(solution)/shard_map/ppermute | solution.py:29
  43.4 4.6 %collective-permute-start.6 = (bf16[2,64,1024]{2,1,0:T(8,128)(2,1)S(1)}, bf16[2,64,1024]{2,1,0:T(8,128)(2,1)S(1)}, u32[]{:S(2)}, u32[]{:S(2)}) collective-permute-start(bf16[2,64,1024]{2,1,0:T(8,128)(2,1)S(1)} %collective-permute-done.4.refs_4_), channel_id=1, source_target_pairs={{0,56},{8,0},{16,8},{24,16},{32,24},{40,32},{48,40},{56,48},{1,57}... | collective-permute-start | bytes 786440 | tf_op jit(solution)/shard_map/ppermute | solution.py:29
  48.0 1.9 %collective-permute-start.5 = (bf16[2,64,1024]{2,1,0:T(8,128)(2,1)S(1)}, bf16[2,64,1024]{2,1,0:T(8,128)(2,1)S(1)}, u32[]{:S(2)}, u32[]{:S(2)}) collective-permute-start(bf16[2,64,1024]{2,1,0:T(8,128)(2,1)S(1)} %collective-permute-done.3.refs_3_), channel_id=1, source_target_pairs={{0,8},{8,16},{16,24},{24,32},{32,40},{40,48},{48,56},{56,0},{1,9},... | collective-permute-start | bytes 786440 | tf_op jit(solution)/shard_map/ppermute | solution.py:29
  49.9 0.7 copy-done.13
  50.6 0.6 collective-permute-done.6.refs_6_
  51.3 0.7 slice.65
  51.9 5.3 %collective-permute-start.8 = (bf16[1,64,1024]{2,1,0:T(8,128)(2,1)}, bf16[1,64,1024]{2,1,0:T(8,128)(2,1)S(1)}, u32[]{:S(2)}, u32[]{:S(2)}) collective-permute-start(bf16[1,64,1024]{2,1,0:T(8,128)(2,1)} %slice.65), channel_id=1, source_target_pairs={{0,56},{8,0},{16,8},{24,16},{32,24},{40,32},{48,40},{56,48},{1,57}... | collective-permute-start | bytes 393224 | tf_op jit(solution)/shard_map/ppermute | solution.py:29
  57.3 0.7 slice.64
  58.0 1.9 %collective-permute-start.7 = (bf16[1,64,1024]{2,1,0:T(8,128)(2,1)}, bf16[1,64,1024]{2,1,0:T(8,128)(2,1)}, u32[]{:S(2)}, u32[]{:S(2)}) collective-permute-start(bf16[1,64,1024]{2,1,0:T(8,128)(2,1)} %slice.64), channel_id=1, source_target_pairs={{0,8},{8,16},{16,24},{24,32},{32,40},{40,48},{48,56},{56,0},{1,9},... | collective-permute-start | bytes 393224 | tf_op jit(solution)/shard_map/ppermute | solution.py:29
  59.9 0.1 pad_add_fusion.2
  60.0 9.8 %collective-permute-done.9.refs_10_ = bf16[288,1024]{1,0:T(8,128)(2,1)S(1)} collective-permute-done((bf16[288,1024]{1,0:T(8,128)(2,1)S(1)}, bf16[288,1024]{1,0:T(8,128)(2,1)S(1)}, u32[]{:S(2)}, u32[]{:S(2)}) %collective-permute-start.9) | collective-permute-done | bytes 589856 | tf_op jit(solution)/shard_map/ppermute | solution.py:29
  69.8 0.9 copy-done.3
  70.8 0.9 copy-done.6
  71.7 0.9 copy-done.9
  72.7 0.9 copy-done.11
  73.6 0.9 copy-done.14
  74.6 4.9 %shard_map.105 = (f32[256,1152]{1,0:T(8,128)S(1)}, bf16[256,1024]{1,0:T(8,128)(2,1)S(1)}) custom-call(s32[2]{0:T(128)S(1)} %get-tuple-element.32.place, bf16[2,64,1024]{2,1,0:T(8,128)(2,1)S(1)} %pad_maximum_fusion.refs_0_, bf16[2,64,1024]{2,1,0:T(8,128)(2,1)S(1)} %copy-done.9, bf16[2,64,1024]{2,1,0:T(8,128)(2,1)S(1)} %copy-done.6, ...), custom_call_target="tpu_custom_call" | custom-call | flops 603979776 | bytes 2359296 | tf_op jit(solution)/shard_map/pallas_call | solution.py:37
  79.5 3.8 %collective-permute-start.12 = (f32[256,1152]{1,0:T(8,128)S(1)}, f32[256,1152]{1,0:T(8,128)S(1)}, u32[]{:S(2)}, u32[]{:S(2)}) collective-permute-start(f32[256,1152]{1,0:T(8,128)S(1)} %get-tuple-element.10), channel_id=1, source_target_pairs={{0,1},{1,0},{2,3},{3,2},{4,5},{5,4},{6,7},{7,6},{8,9},{9,8},{10,11... | collective-permute-start | bytes 3538952 | tf_op jit(solution)/shard_map/ppermute | solution.py:24
  83.3 5.5 %shard_map.104 = (f32[256,1152]{1,0:T(8,128)S(1)}, bf16[256,1024]{1,0:T(8,128)(2,1)S(1)}) custom-call(s32[2]{0:T(128)S(1)} %get-tuple-element.31.place, bf16[2,64,1024]{2,1,0:T(8,128)(2,1)S(1)} %pad_maximum_fusion.refs_0_, bf16[2,64,1024]{2,1,0:T(8,128)(2,1)S(1)} %copy-done.9, bf16[2,64,1024]{2,1,0:T(8,128)(2,1)S(1)} %copy-done.7, ...), custom_call_target="tpu_custom_call" | custom-call | flops 603979776 | bytes 2359296 | tf_op jit(solution)/shard_map/pallas_call | solution.py:37
  88.8 0.0 copy-start.18
  88.9 0.2 add.67
  89.0 0.6 copy-done
  89.6 0.1 fusion
  89.7 0.1 fusion.14
  89.8 5.9 %collective-permute-start.13 = (f16[64,1152]{1,0:T(8,128)(2,1)S(1)}, f16[64,1152]{1,0:T(8,128)(2,1)S(1)}, u32[]{:S(2)}, u32[]{:S(2)}) collective-permute-start(f16[64,1152]{1,0:T(8,128)(2,1)S(1)} %get-tuple-element.22), channel_id=1, source_target_pairs={{0,2},{2,0},{4,6},{6,4},{1,3},{3,1},{5,7},{7,5},{8,10},{10,8},{12,... | collective-permute-start | bytes 442376 | tf_op jit(solution)/shard_map/ppermute | solution.py:33
  95.7 4.7 %collective-permute-start.15 = (f16[64,1152]{1,0:T(8,128)(2,1)S(1)}, f16[64,1152]{1,0:T(8,128)(2,1)S(1)}, u32[]{:S(2)}, u32[]{:S(2)}) collective-permute-start(f16[64,1152]{1,0:T(8,128)(2,1)S(1)} %get-tuple-element.23), channel_id=1, source_target_pairs={{0,6},{2,4},{4,2},{6,0},{1,7},{3,5},{5,3},{7,1},{8,14},{10,12},{12... | collective-permute-start | bytes 442376 | tf_op jit(solution)/shard_map/ppermute | solution.py:33
  100.4 1.9 %collective-permute-start.14 = (f16[64,1152]{1,0:T(8,128)(2,1)S(1)}, f16[64,1152]{1,0:T(8,128)(2,1)S(1)}, u32[]{:S(2)}, u32[]{:S(2)}) collective-permute-start(f16[64,1152]{1,0:T(8,128)(2,1)S(1)} %get-tuple-element.24), channel_id=1, source_target_pairs={{0,4},{2,6},{4,0},{6,2},{1,5},{3,7},{5,1},{7,3},{8,12},{10,14},{12... | collective-permute-start | bytes 442376 | tf_op jit(solution)/shard_map/ppermute | solution.py:33
  102.4 3.6 %collective-permute-done.15 = f16[64,1152]{1,0:T(8,128)(2,1)S(1)} collective-permute-done((f16[64,1152]{1,0:T(8,128)(2,1)S(1)}, f16[64,1152]{1,0:T(8,128)(2,1)S(1)}, u32[]{:S(2)}, u32[]{:S(2)}) %collective-permute-start.15) | collective-permute-done | bytes 147488 | tf_op jit(solution)/shard_map/ppermute | solution.py:33
  106.0 6.5 %collective-permute-done.14 = f16[64,1152]{1,0:T(8,128)(2,1)S(1)} collective-permute-done((f16[64,1152]{1,0:T(8,128)(2,1)S(1)}, f16[64,1152]{1,0:T(8,128)(2,1)S(1)}, u32[]{:S(2)}, u32[]{:S(2)}) %collective-permute-start.14) | collective-permute-done | bytes 147488 | tf_op jit(solution)/shard_map/ppermute | solution.py:33
  112.5 0.1 slice_add_fusion
  112.7 0.1 reshape.12
  112.8 0.9 reshape.13
  113.6 0.4 fusion.13
  114.0 0.1 fusion.8
  114.2 0.1 fusion.10
  114.3 1.9 %collective-permute-start.17 = (bf16[4,64,112]{2,1,0:T(8,128)(2,1)S(1)}, bf16[4,64,112]{2,1,0:T(8,128)(2,1)S(1)}, u32[]{:S(2)}, u32[]{:S(2)}) collective-permute-start(bf16[4,64,112]{2,1,0:T(8,128)(2,1)S(1)} %get-tuple-element.28), channel_id=1, source_target_pairs={{0,4},{2,6},{4,0},{6,2},{1,5},{3,7},{5,1},{7,3},{8,12},{10,14},{12... | collective-permute-start | bytes 172040 | tf_op jit(solution)/shard_map/ppermute | solution.py:33
  116.2 5.1 %collective-permute-start.16 = (bf16[4,64,112]{2,1,0:T(8,128)(2,1)S(1)}, bf16[4,64,112]{2,1,0:T(8,128)(2,1)S(1)}, u32[]{:S(2)}, u32[]{:S(2)}) collective-permute-start(bf16[4,64,112]{2,1,0:T(8,128)(2,1)S(1)} %get-tuple-element.28), channel_id=1, source_target_pairs={{0,2},{2,0},{4,6},{6,4},{1,3},{3,1},{5,7},{7,5},{8,10},{10,8},{12,... | collective-permute-start | bytes 172040 | tf_op jit(solution)/shard_map/ppermute | solution.py:33
  121.3 2.3 %collective-permute-start.18 = (bf16[4,64,112]{2,1,0:T(8,128)(2,1)S(1)}, bf16[4,64,112]{2,1,0:T(8,128)(2,1)S(1)}, u32[]{:S(2)}, u32[]{:S(2)}) collective-permute-start(bf16[4,64,112]{2,1,0:T(8,128)(2,1)S(1)} %get-tuple-element.28), channel_id=1, source_target_pairs={{0,6},{2,4},{4,2},{6,0},{1,7},{3,5},{5,3},{7,1},{8,14},{10,12},{12... | collective-permute-start | bytes 172040 | tf_op jit(solution)/shard_map/ppermute | solution.py:33
  123.6 4.5 %collective-permute-done.18 = bf16[4,64,112]{2,1,0:T(8,128)(2,1)S(1)} collective-permute-done((bf16[4,64,112]{2,1,0:T(8,128)(2,1)S(1)}, bf16[4,64,112]{2,1,0:T(8,128)(2,1)S(1)}, u32[]{:S(2)}, u32[]{:S(2)}) %collective-permute-start.18) | collective-permute-done | bytes 57376 | tf_op jit(solution)/shard_map/ppermute | solution.py:33
  128.1 0.1 pad_maximum_fusion.1.mine
  128.1 4.0 %collective-permute-start.19 = (bf16[4,4,64,112]{3,2,1,0:T(8,128)(2,1)S(1)}, bf16[4,4,64,112]{3,2,1,0:T(8,128)(2,1)S(1)}, u32[]{:S(2)}, u32[]{:S(2)}) collective-permute-start(bf16[4,4,64,112]{3,2,1,0:T(8,128)(2,1)S(1)} %pad_maximum_fusion.1.mine), channel_id=1, source_target_pairs={{0,1},{1,0},{2,3},{3,2},{4,5},{5,4},{6,7},{7,6},{8,9},{9,8},{10,11... | collective-permute-start | bytes 688136 | tf_op jit(solution)/shard_map/ppermute | solution.py:24
  132.2 1.1 collective-permute-done.19.other
  133.3 0.6 shard_map.107
  133.9 4.0 %collective-permute-start.20 = (bf16[112,1024]{1,0:T(8,128)(2,1)S(1)}, bf16[112,1024]{1,0:T(8,128)(2,1)S(1)}, u32[]{:S(2)}, u32[]{:S(2)}) collective-permute-start(bf16[112,1024]{1,0:T(8,128)(2,1)S(1)} %get-tuple-element.13), channel_id=1, source_target_pairs={{0,192},{64,0},{128,64},{192,128},{1,193},{65,1},{129,65},{193,129... | collective-permute-start | bytes 688136 | tf_op jit(solution)/shard_map/ppermute | solution.py:29
  137.9 3.2 %collective-permute-start.21 = (bf16[112,1024]{1,0:T(8,128)(2,1)S(1)}, bf16[112,1024]{1,0:T(8,128)(2,1)S(1)}, u32[]{:S(2)}, u32[]{:S(2)}) collective-permute-start(bf16[112,1024]{1,0:T(8,128)(2,1)S(1)} %get-tuple-element.14), channel_id=1, source_target_pairs={{0,128},{64,192},{128,0},{192,64},{1,129},{65,193},{129,1},{193,65... | collective-permute-start | bytes 688136 | tf_op jit(solution)/shard_map/ppermute | solution.py:29
  141.1 1.9 %collective-permute-start.22 = (bf16[112,1024]{1,0:T(8,128)(2,1)S(1)}, bf16[112,1024]{1,0:T(8,128)(2,1)S(1)}, u32[]{:S(2)}, u32[]{:S(2)}) collective-permute-start(bf16[112,1024]{1,0:T(8,128)(2,1)S(1)} %get-tuple-element.15), channel_id=1, source_target_pairs={{0,64},{64,128},{128,192},{192,0},{1,65},{65,129},{129,193},{193,1... | collective-permute-start | bytes 688136 | tf_op jit(solution)/shard_map/ppermute | solution.py:29
  143.0 0.3 shard_map.106
  143.3 0.0 copy-start.15
  143.4 0.0 copy-start.16
  143.4 4.4 %collective-permute-done.21 = bf16[112,1024]{1,0:T(8,128)(2,1)S(1)} collective-permute-done((bf16[112,1024]{1,0:T(8,128)(2,1)S(1)}, bf16[112,1024]{1,0:T(8,128)(2,1)S(1)}, u32[]{:S(2)}, u32[]{:S(2)}) %collective-permute-start.21) | collective-permute-done | bytes 229408 | tf_op jit(solution)/shard_map/ppermute | solution.py:29
  147.8 5.8 %collective-permute-done.22 = bf16[112,1024]{1,0:T(8,128)(2,1)S(1)} collective-permute-done((bf16[112,1024]{1,0:T(8,128)(2,1)S(1)}, bf16[112,1024]{1,0:T(8,128)(2,1)S(1)}, u32[]{:S(2)}, u32[]{:S(2)}) %collective-permute-start.22) | collective-permute-done | bytes 229408 | tf_op jit(solution)/shard_map/ppermute | solution.py:29
  153.6 0.1 add_multiply_fusion
  153.7 0.8 slice_multiply_fusion.1
  (44 shorter events, 0.1 us)
Async XLA Ops:
  1.5 15.4 %collective-permute-start = (bf16[64,1024]{1,0:T(8,128)(2,1)S(1)}, bf16[64,1024]{1,0:T(8,128)(2,1)S(1)}, u32[]{:S(2)}, u32[]{:S(2)}) collective-permute-start(bf16[64,1024]{1,0:T(8,128)(2,1)S(1)} %get-tuple-element.30), channel_id=1, source_target_pairs={{0,256},{256,0},{1,257},{257,1},{2,258},{258,2},{3,259},{259,3},{4... | collective-permute-start | bytes 393224 | tf_op jit(solution)/shard_map/ppermute | solution.py:24
  16.9 8.7 %collective-permute-start.2 = (bf16[2,64,1024]{2,1,0:T(8,128)(2,1)S(1)}, bf16[2,64,1024]{2,1,0:T(8,128)(2,1)S(1)}, u32[]{:S(2)}, u32[]{:S(2)}) collective-permute-start(bf16[2,64,1024]{2,1,0:T(8,128)(2,1)S(1)} %pad_maximum_fusion.refs_0_), channel_id=1, source_target_pairs={{0,56},{8,0},{16,8},{24,16},{32,24},{40,32},{48,40},{56,48},{1,57}... | collective-permute-start | bytes 786440 | tf_op jit(solution)/shard_map/ppermute | solution.py:29
  21.3 9.6 %collective-permute-start.1 = (bf16[2,64,1024]{2,1,0:T(8,128)(2,1)S(1)}, bf16[2,64,1024]{2,1,0:T(8,128)(2,1)S(1)}, u32[]{:S(2)}, u32[]{:S(2)}) collective-permute-start(bf16[2,64,1024]{2,1,0:T(8,128)(2,1)S(1)} %pad_maximum_fusion.refs_0_), channel_id=1, source_target_pairs={{0,8},{8,16},{16,24},{24,32},{32,40},{40,48},{48,56},{56,0},{1,9},... | collective-permute-start | bytes 786440 | tf_op jit(solution)/shard_map/ppermute | solution.py:29
  25.6 31.7 %copy-start.5 = (bf16[2,64,1024]{2,1,0:T(8,128)(2,1)}, bf16[2,64,1024]{2,1,0:T(8,128)(2,1)S(1)}, u32[]{:S(2)}) copy-start(bf16[2,64,1024]{2,1,0:T(8,128)(2,1)S(1)} %collective-permute-done.2.refs_2_) | copy-start | bytes 786436
  25.6 17.8 %collective-permute-start.4 = (bf16[2,64,1024]{2,1,0:T(8,128)(2,1)S(1)}, bf16[2,64,1024]{2,1,0:T(8,128)(2,1)S(1)}, u32[]{:S(2)}, u32[]{:S(2)}) collective-permute-start(bf16[2,64,1024]{2,1,0:T(8,128)(2,1)S(1)} %collective-permute-done.2.refs_2_), channel_id=1, source_target_pairs={{0,56},{8,0},{16,8},{24,16},{32,24},{40,32},{48,40},{56,48},{1,57}... | collective-permute-start | bytes 786440 | tf_op jit(solution)/shard_map/ppermute | solution.py:29
  30.9 17.1 %copy-start.8 = (bf16[2,64,1024]{2,1,0:T(8,128)(2,1)}, bf16[2,64,1024]{2,1,0:T(8,128)(2,1)S(1)}, u32[]{:S(2)}) copy-start(bf16[2,64,1024]{2,1,0:T(8,128)(2,1)S(1)} %collective-permute-done.1.refs_1_) | copy-start | bytes 786436
  30.9 17.1 %collective-permute-start.3 = (bf16[2,64,1024]{2,1,0:T(8,128)(2,1)S(1)}, bf16[2,64,1024]{2,1,0:T(8,128)(2,1)S(1)}, u32[]{:S(2)}, u32[]{:S(2)}) collective-permute-start(bf16[2,64,1024]{2,1,0:T(8,128)(2,1)S(1)} %collective-permute-done.1.refs_1_), channel_id=1, source_target_pairs={{0,8},{8,16},{16,24},{24,32},{32,40},{40,48},{48,56},{56,0},{1,9},... | collective-permute-start | bytes 786440 | tf_op jit(solution)/shard_map/ppermute | solution.py:29
  34.0 26.0 %collective-permute-start.11 = (bf16[288,1024]{1,0:T(8,128)(2,1)S(1)}, bf16[288,1024]{1,0:T(8,128)(2,1)S(1)}, u32[]{:S(2)}, u32[]{:S(2)}) collective-permute-start(bf16[288,1024]{1,0:T(8,128)(2,1)S(1)} %pad_add_fusion.refs_9_), channel_id=1, source_target_pairs={{0,192},{64,0},{128,64},{192,128},{1,193},{65,1},{129,65},{193,129... | collective-permute-start | bytes 1769480 | tf_op jit(solution)/shard_map/ppermute | solution.py:29
  38.4 21.6 %collective-permute-start.10 = (bf16[288,1024]{1,0:T(8,128)(2,1)S(1)}, bf16[288,1024]{1,0:T(8,128)(2,1)S(1)}, u32[]{:S(2)}, u32[]{:S(2)}) collective-permute-start(bf16[288,1024]{1,0:T(8,128)(2,1)S(1)} %pad_add_fusion.refs_9_), channel_id=1, source_target_pairs={{0,128},{64,192},{128,0},{192,64},{1,129},{65,193},{129,1},{193,65... | collective-permute-start | bytes 1769480 | tf_op jit(solution)/shard_map/ppermute | solution.py:29
  40.9 29.0 %collective-permute-start.9 = (bf16[288,1024]{1,0:T(8,128)(2,1)S(1)}, bf16[288,1024]{1,0:T(8,128)(2,1)S(1)}, u32[]{:S(2)}, u32[]{:S(2)}) collective-permute-start(bf16[288,1024]{1,0:T(8,128)(2,1)S(1)} %pad_add_fusion.refs_9_), channel_id=1, source_target_pairs={{0,64},{64,128},{128,192},{192,0},{1,65},{65,129},{129,193},{193,1... | collective-permute-start | bytes 1769480 | tf_op jit(solution)/shard_map/ppermute | solution.py:29
  43.4 26.4 %copy-start.10 = (bf16[2,64,1024]{2,1,0:T(8,128)(2,1)}, bf16[2,64,1024]{2,1,0:T(8,128)(2,1)S(1)}, u32[]{:S(2)}) copy-start(bf16[2,64,1024]{2,1,0:T(8,128)(2,1)S(1)} %collective-permute-done.4.refs_4_) | copy-start | bytes 786436
  43.4 7.9 %collective-permute-start.6 = (bf16[2,64,1024]{2,1,0:T(8,128)(2,1)S(1)}, bf16[2,64,1024]{2,1,0:T(8,128)(2,1)S(1)}, u32[]{:S(2)}, u32[]{:S(2)}) collective-permute-start(bf16[2,64,1024]{2,1,0:T(8,128)(2,1)S(1)} %collective-permute-done.4.refs_4_), channel_id=1, source_target_pairs={{0,56},{8,0},{16,8},{24,16},{32,24},{40,32},{48,40},{56,48},{1,57}... | collective-permute-start | bytes 786440 | tf_op jit(solution)/shard_map/ppermute | solution.py:29
  48.0 9.3 %collective-permute-start.5 = (bf16[2,64,1024]{2,1,0:T(8,128)(2,1)S(1)}, bf16[2,64,1024]{2,1,0:T(8,128)(2,1)S(1)}, u32[]{:S(2)}, u32[]{:S(2)}) collective-permute-start(bf16[2,64,1024]{2,1,0:T(8,128)(2,1)S(1)} %collective-permute-done.3.refs_3_), channel_id=1, source_target_pairs={{0,8},{8,16},{16,24},{24,32},{32,40},{40,48},{48,56},{56,0},{1,9},... | collective-permute-start | bytes 786440 | tf_op jit(solution)/shard_map/ppermute | solution.py:29
  49.9 0.7 copy-start.13
  51.9 17.9 %collective-permute-start.8 = (bf16[1,64,1024]{2,1,0:T(8,128)(2,1)}, bf16[1,64,1024]{2,1,0:T(8,128)(2,1)S(1)}, u32[]{:S(2)}, u32[]{:S(2)}) collective-permute-start(bf16[1,64,1024]{2,1,0:T(8,128)(2,1)} %slice.65), channel_id=1, source_target_pairs={{0,56},{8,0},{16,8},{24,16},{32,24},{40,32},{48,40},{56,48},{1,57}... | collective-permute-start | bytes 393224 | tf_op jit(solution)/shard_map/ppermute | solution.py:29
  57.3 12.6 %copy-start.2 = (bf16[2,64,1024]{2,1,0:T(8,128)(2,1)}, bf16[2,64,1024]{2,1,0:T(8,128)(2,1)S(1)}, u32[]{:S(2)}) copy-start(bf16[2,64,1024]{2,1,0:T(8,128)(2,1)S(1)} %collective-permute-done.5.refs_5_) | copy-start | bytes 786436
  58.0 11.8 %collective-permute-start.7 = (bf16[1,64,1024]{2,1,0:T(8,128)(2,1)}, bf16[1,64,1024]{2,1,0:T(8,128)(2,1)}, u32[]{:S(2)}, u32[]{:S(2)}) collective-permute-start(bf16[1,64,1024]{2,1,0:T(8,128)(2,1)} %slice.64), channel_id=1, source_target_pairs={{0,8},{8,16},{16,24},{24,32},{32,40},{40,48},{48,56},{56,0},{1,9},... | collective-permute-start | bytes 393224 | tf_op jit(solution)/shard_map/ppermute | solution.py:29
  69.8 1.0 copy-start.3
  70.8 0.9 copy-start.6
  71.7 0.9 copy-start.9
  72.7 0.9 copy-start.11
  73.6 0.9 copy-start.14
  74.6 8.7 %copy-start.4 = (bf16[2,64,1024]{2,1,0:T(8,128)(2,1)S(1)}, bf16[2,64,1024]{2,1,0:T(8,128)(2,1)}, u32[]{:S(2)}) copy-start(bf16[2,64,1024]{2,1,0:T(8,128)(2,1)} %copy-done.2) | copy-start | bytes 786436
  74.6 8.7 %copy-start.7 = (bf16[2,64,1024]{2,1,0:T(8,128)(2,1)S(1)}, bf16[2,64,1024]{2,1,0:T(8,128)(2,1)}, u32[]{:S(2)}) copy-start(bf16[2,64,1024]{2,1,0:T(8,128)(2,1)} %copy-done.5) | copy-start | bytes 786436
  74.6 8.7 %copy-start.12 = (bf16[2,64,1024]{2,1,0:T(8,128)(2,1)S(1)}, bf16[2,64,1024]{2,1,0:T(8,128)(2,1)}, u32[]{:S(2)}) copy-start(bf16[2,64,1024]{2,1,0:T(8,128)(2,1)} %copy-done.10) | copy-start | bytes 786436
  79.5 9.3 %collective-permute-start.12 = (f32[256,1152]{1,0:T(8,128)S(1)}, f32[256,1152]{1,0:T(8,128)S(1)}, u32[]{:S(2)}, u32[]{:S(2)}) collective-permute-start(f32[256,1152]{1,0:T(8,128)S(1)} %get-tuple-element.10), channel_id=1, source_target_pairs={{0,1},{1,0},{2,3},{3,2},{4,5},{5,4},{6,7},{7,6},{8,9},{9,8},{10,11... | collective-permute-start | bytes 3538952 | tf_op jit(solution)/shard_map/ppermute | solution.py:24
  88.8 0.8 copy-start
  88.8 0.8 copy-start.18
  89.6 22.9 %copy-start.17 = (f32[1152]{0:T(1024)S(1)}, f32[1152]{0:T(1024)}, u32[]{:S(2)}) copy-start(f32[1152]{0:T(1024)} %constant.24.clone) | copy-start | bytes 13828
  89.8 12.6 %collective-permute-start.13 = (f16[64,1152]{1,0:T(8,128)(2,1)S(1)}, f16[64,1152]{1,0:T(8,128)(2,1)S(1)}, u32[]{:S(2)}, u32[]{:S(2)}) collective-permute-start(f16[64,1152]{1,0:T(8,128)(2,1)S(1)} %get-tuple-element.22), channel_id=1, source_target_pairs={{0,2},{2,0},{4,6},{6,4},{1,3},{3,1},{5,7},{7,5},{8,10},{10,8},{12,... | collective-permute-start | bytes 442376 | tf_op jit(solution)/shard_map/ppermute | solution.py:33
  95.7 10.3 %collective-permute-start.15 = (f16[64,1152]{1,0:T(8,128)(2,1)S(1)}, f16[64,1152]{1,0:T(8,128)(2,1)S(1)}, u32[]{:S(2)}, u32[]{:S(2)}) collective-permute-start(f16[64,1152]{1,0:T(8,128)(2,1)S(1)} %get-tuple-element.23), channel_id=1, source_target_pairs={{0,6},{2,4},{4,2},{6,0},{1,7},{3,5},{5,3},{7,1},{8,14},{10,12},{12... | collective-permute-start | bytes 442376 | tf_op jit(solution)/shard_map/ppermute | solution.py:33
  100.4 12.1 %collective-permute-start.14 = (f16[64,1152]{1,0:T(8,128)(2,1)S(1)}, f16[64,1152]{1,0:T(8,128)(2,1)S(1)}, u32[]{:S(2)}, u32[]{:S(2)}) collective-permute-start(f16[64,1152]{1,0:T(8,128)(2,1)S(1)} %get-tuple-element.24), channel_id=1, source_target_pairs={{0,4},{2,6},{4,0},{6,2},{1,5},{3,7},{5,1},{7,3},{8,12},{10,14},{12... | collective-permute-start | bytes 442376 | tf_op jit(solution)/shard_map/ppermute | solution.py:33
  113.6 19.7 %copy-start.1 = (bf16[256,1024]{1,0:T(8,128)(2,1)S(1)}, bf16[256,1024]{1,0:T(8,128)(2,1)}, u32[]{:S(2)}) copy-start(bf16[256,1024]{1,0:T(8,128)(2,1)} %copy-done) | copy-start | bytes 1572868
  114.3 9.3 %collective-permute-start.17 = (bf16[4,64,112]{2,1,0:T(8,128)(2,1)S(1)}, bf16[4,64,112]{2,1,0:T(8,128)(2,1)S(1)}, u32[]{:S(2)}, u32[]{:S(2)}) collective-permute-start(bf16[4,64,112]{2,1,0:T(8,128)(2,1)S(1)} %get-tuple-element.28), channel_id=1, source_target_pairs={{0,4},{2,6},{4,0},{6,2},{1,5},{3,7},{5,1},{7,3},{8,12},{10,14},{12... | collective-permute-start | bytes 172040 | tf_op jit(solution)/shard_map/ppermute | solution.py:33
  116.2 7.4 %collective-permute-start.16 = (bf16[4,64,112]{2,1,0:T(8,128)(2,1)S(1)}, bf16[4,64,112]{2,1,0:T(8,128)(2,1)S(1)}, u32[]{:S(2)}, u32[]{:S(2)}) collective-permute-start(bf16[4,64,112]{2,1,0:T(8,128)(2,1)S(1)} %get-tuple-element.28), channel_id=1, source_target_pairs={{0,2},{2,0},{4,6},{6,4},{1,3},{3,1},{5,7},{7,5},{8,10},{10,8},{12,... | collective-permute-start | bytes 172040 | tf_op jit(solution)/shard_map/ppermute | solution.py:33
  121.3 6.8 %collective-permute-start.18 = (bf16[4,64,112]{2,1,0:T(8,128)(2,1)S(1)}, bf16[4,64,112]{2,1,0:T(8,128)(2,1)S(1)}, u32[]{:S(2)}, u32[]{:S(2)}) collective-permute-start(bf16[4,64,112]{2,1,0:T(8,128)(2,1)S(1)} %get-tuple-element.28), channel_id=1, source_target_pairs={{0,6},{2,4},{4,2},{6,0},{1,7},{3,5},{5,3},{7,1},{8,14},{10,12},{12... | collective-permute-start | bytes 172040 | tf_op jit(solution)/shard_map/ppermute | solution.py:33
  128.1 5.2 %collective-permute-start.19 = (bf16[4,4,64,112]{3,2,1,0:T(8,128)(2,1)S(1)}, bf16[4,4,64,112]{3,2,1,0:T(8,128)(2,1)S(1)}, u32[]{:S(2)}, u32[]{:S(2)}) collective-permute-start(bf16[4,4,64,112]{3,2,1,0:T(8,128)(2,1)S(1)} %pad_maximum_fusion.1.mine), channel_id=1, source_target_pairs={{0,1},{1,0},{2,3},{3,2},{4,5},{5,4},{6,7},{7,6},{8,9},{9,8},{10,11... | collective-permute-start | bytes 688136 | tf_op jit(solution)/shard_map/ppermute | solution.py:24
  133.9 9.4 %collective-permute-start.20 = (bf16[112,1024]{1,0:T(8,128)(2,1)S(1)}, bf16[112,1024]{1,0:T(8,128)(2,1)S(1)}, u32[]{:S(2)}, u32[]{:S(2)}) collective-permute-start(bf16[112,1024]{1,0:T(8,128)(2,1)S(1)} %get-tuple-element.13), channel_id=1, source_target_pairs={{0,192},{64,0},{128,64},{192,128},{1,193},{65,1},{129,65},{193,129... | collective-permute-start | bytes 688136 | tf_op jit(solution)/shard_map/ppermute | solution.py:29
  137.9 9.9 %collective-permute-start.21 = (bf16[112,1024]{1,0:T(8,128)(2,1)S(1)}, bf16[112,1024]{1,0:T(8,128)(2,1)S(1)}, u32[]{:S(2)}, u32[]{:S(2)}) collective-permute-start(bf16[112,1024]{1,0:T(8,128)(2,1)S(1)} %get-tuple-element.14), channel_id=1, source_target_pairs={{0,128},{64,192},{128,0},{192,64},{1,129},{65,193},{129,1},{193,65... | collective-permute-start | bytes 688136 | tf_op jit(solution)/shard_map/ppermute | solution.py:29
  141.1 12.5 %collective-permute-start.22 = (bf16[112,1024]{1,0:T(8,128)(2,1)S(1)}, bf16[112,1024]{1,0:T(8,128)(2,1)S(1)}, u32[]{:S(2)}, u32[]{:S(2)}) collective-permute-start(bf16[112,1024]{1,0:T(8,128)(2,1)S(1)} %get-tuple-element.15), channel_id=1, source_target_pairs={{0,64},{64,128},{128,192},{192,0},{1,65},{65,129},{129,193},{193,1... | collective-permute-start | bytes 688136 | tf_op jit(solution)/shard_map/ppermute | solution.py:29
  143.3 10.4 %copy-start.15 = (bf16[56,1024]{1,0:T(8,128)(2,1)S(1)}, bf16[56,1024]{1,0:T(8,128)(2,1)}, u32[]{:S(2)}) copy-start(bf16[56,1024]{1,0:T(8,128)(2,1)} %param.15) | copy-start | bytes 344068
  143.4 10.4 %copy-start.16 = (bf16[56,1024]{1,0:T(8,128)(2,1)S(1)}, bf16[56,1024]{1,0:T(8,128)(2,1)}, u32[]{:S(2)}) copy-start(bf16[56,1024]{1,0:T(8,128)(2,1)} %param.14) | copy-start | bytes 344068

commit v6 on v3

v6 whole, which is shorter than its diff:
```python
import functools

import jax
import jax.numpy as jnp
from jax import lax
from jax.experimental import pallas as pl
from jax.experimental.pallas import tpu as pltpu
from jax.sharding import Mesh, PartitionSpec as P

NODE = {"zh": 2, "x": 4, "y": 8}
LOCAL = {"zl": 4, "c": 2}

PRE_SCALE = 64.0
TAN_SCALE = 0.5
BACK_SCALE = 32.0

VMEM = pl.BlockSpec(memory_space=pltpu.VMEM)
SMEM = pl.BlockSpec(memory_space=pltpu.SMEM)


def swap(value, axis):
    return lax.ppermute(value, axis, [(0, 1), (1, 0)])


def shift(value, axis, by):
    size = lax.axis_size(axis)
    return lax.ppermute(value, axis, [(i, (i + by) % size) for i in range(size)])


def mix(value, axis, by):
    return lax.ppermute(value, axis, [(i, i ^ by) for i in range(lax.axis_size(axis))])


def local_call(body, out_shape, flops, moved, interpret, *args, **options):
    return pl.pallas_call(
        body,
        out_shape=out_shape,
        cost_estimate=pl.CostEstimate(flops=flops, bytes_accessed=moved, transcendentals=0),
        compiler_params=pltpu.CompilerParams(vmem_limit_bytes=16 * 1024 * 1024),
        interpret=interpret,
        **options,
    )(*args)


def terms_kernel(tok_rows, place, tokens, cotangents, *refs):
    *weights, out, w_all = refs
    cut = len(weights) * tok_rows
    cot_rows = weights[0].shape[0] - tok_rows
    for i, weight in enumerate(weights):
        w_all[i * tok_rows : (i + 1) * tok_rows] = weight[:tok_rows]
        start = cut + i * cot_rows
        w_all[start : start + cot_rows] = weight[tok_rows:]
    count = out.shape[0]
    half = pl.ds(pl.multiple_of(place[0] * count, count), count)
    across = (((1,), (1,)), ((), ()))
    column = lax.rem(lax.broadcasted_iota(jnp.int32, (1, cut), 1), tok_rows)
    out[:, :cut] = lax.dot_general(
        tokens[half], w_all[:cut], across, preferred_element_type=jnp.float32
    ) * jnp.where(column * 2 >= tok_rows, TAN_SCALE, PRE_SCALE)
    out[:, cut:] = BACK_SCALE * lax.dot_general(
        cotangents[half], w_all[cut:], across, preferred_element_type=jnp.float32
    )


def hvp_kernel(nzl, nc, place, fac, tokens, away, own):
    nx, width, _ = away.shape
    lanes = fac.shape[1] // (nzl * nc * nx)
    for i in range(nx):
        step = place[0] ^ i
        step = step ^ (step >> 1)
        parts = []
        for c in range(nc):
            for z in range(nzl):
                start = pl.multiple_of(((z * nc + c) * nx + step) * lanes, lanes)
                parts.append(fac[:, pl.ds(start, lanes)])
        term = lax.dot_general(
            jnp.concatenate(parts, axis=0), tokens[...], (((0,), (0,)), ((), ())),
            preferred_element_type=jnp.float32,
        )[:width]
        away[i] = term.astype(away.dtype)

        @pl.when(place[0] == i)
        def _():
            own[...] = term


def sum_kernel(total, place, away, own, gate_probe, up_probe, gate_diag, up_diag):
    both = own[...]
    for i in range(away.shape[0]):
        both += jnp.where(place[0] == i, 0.0, away[i].astype(jnp.float32))
    both = both / total
    hid = gate_diag.shape[0]
    gate_diag[...] = gate_probe[...].astype(jnp.float32) * both[:hid]
    up_diag[...] = up_probe[...].astype(jnp.float32) * both[hid:]


def factors(pre_gate, pre_up, tan_gate, tan_up, back):
    sig = jax.nn.sigmoid(pre_gate)
    slope = sig * (1.0 + pre_gate * (1.0 - sig))
    bend = sig * (1.0 - sig) * (2.0 + pre_gate * (1.0 - 2.0 * sig))
    fac_gate = (back * (tan_up * slope + pre_up * bend * tan_gate)).astype(jnp.bfloat16)
    fac_up = (back * slope * tan_gate).astype(jnp.bfloat16)
    return (fac_gate, fac_up)


def stacked(parts, rows):
    row, out = 0, None
    for part in parts:
        padded = lax.pad(
            part, jnp.zeros((), part.dtype),
            ((row, rows - row - part.shape[0], 0), (0, 0, 0)),
        )
        out = padded if out is None else out + padded
        row += part.shape[0]
    return out


def on_device(
    tokens, cotangent, gate_weight, up_weight, down_weight, gate_probe, up_probe, interpret
):
    nx, ny, nzl = lax.axis_size("x"), lax.axis_size("y"), lax.axis_size("zl")
    own, feats = tokens.shape
    hid = gate_weight.shape[0]
    total = own * lax.axis_size(("zh", "x", "y"))
    nc = lax.axis_size("c")
    x, core = lax.axis_index("x"), lax.axis_index("c")

    rows = stacked([tokens, cotangent], 2 * own)
    block = jnp.stack([rows, swap(rows, "zh")], axis=0)

    tok_rows, cot_rows = 4 * hid, hid * 8 // 7
    mats = stacked(
        [gate_weight, up_weight, gate_probe, up_probe, down_weight], tok_rows + cot_rows
    )
    beside = mix(mats, "x", 1)
    weights = [mats, beside, mix(mats, "x", 3), mix(beside, "x", 3)]

    ahead = behind = block
    blocks = [block]
    for _ in range(ny // 2 - 1):
        ahead, behind = shift(ahead, "y", 1), shift(behind, "y", -1)
        blocks += [ahead, behind]
    blocks += [shift(ahead[:1], "y", 1), shift(behind[1:], "y", -1)]
    tok_all = jnp.concatenate([b[:, :own] for b in blocks], axis=0).reshape(-1, feats)
    cot_all = jnp.concatenate([b[:, own:] for b in blocks], axis=0).reshape(-1, feats)

    count = tok_all.shape[0] // nc
    cut, columns = nx * tok_rows, nx * (tok_rows + cot_rows)
    def term(which):
        return local_call(
            functools.partial(terms_kernel, tok_rows),
            jax.ShapeDtypeStruct((count, columns), jnp.float32),
            2 * count * columns * feats,
            2 * columns * feats,
            interpret,
            which.reshape(1),
            tok_all,
            cot_all,
            *weights,
            in_specs=[SMEM] + [VMEM] * (2 + nx),
            out_specs=VMEM,
            scratch_shapes=[pltpu.VMEM((columns, feats), jnp.bfloat16)],
        )
    other = swap(term(1 - core), "c")
    terms = term(core) + other

    share = count // nzl
    sent = terms.astype(jnp.float16).reshape(nzl, share, columns)
    got = lax.all_to_all(sent, "zl", 0, 0, tiled=True)
    proj = jnp.sum(got.astype(jnp.float32), axis=0)
    tok_part = proj[:, :cut].reshape(share, nx, 4, hid)
    pre_gate, pre_up = (tok_part[:, :, i] * (1.0 / PRE_SCALE) for i in (0, 1))
    tan_gate, tan_up = (tok_part[:, :, i] * (1.0 / TAN_SCALE) for i in (2, 3))
    back = proj[:, cut:].reshape(share, nx, cot_rows)[:, :, :hid] * (1.0 / BACK_SCALE)
    fac_gate, fac_up = factors(pre_gate, pre_up, tan_gate, tan_up, back)

    lanes = -(-2 * hid // 128) * 128
    fill = fac_up[:, :, : lanes - 2 * hid]
    fac = jnp.concatenate([fac_gate, fac_up, fill], axis=2).reshape(share, nx * lanes)
    fac = lax.all_gather(fac, ("zl", "c"), axis=1, tiled=True)

    away, mine = local_call(
        functools.partial(hvp_kernel, nzl, nc),
        (
            jax.ShapeDtypeStruct((nx, 2 * hid, feats), jnp.bfloat16),
            jax.ShapeDtypeStruct((2 * hid, feats), jnp.float32),
        ),
        4 * nx * hid * nc * count * feats,
        2 * nc * count * feats,
        interpret,
        x.reshape(1),
        fac,
        tok_all,
        in_specs=[SMEM, VMEM, VMEM],
        out_specs=(VMEM, VMEM),
    )
    away = lax.all_to_all(away, "x", 0, 0, tiled=True)
    diag = jax.ShapeDtypeStruct((hid, feats), jnp.float32)
    return local_call(
        functools.partial(sum_kernel, total),
        (diag, diag),
        2 * nx * hid * feats,
        8 * nx * hid * feats,
        interpret,
        x.reshape(1),
        away,
        mine,
        gate_probe,
        up_probe,
        in_specs=[SMEM] + [VMEM] * 4,
        out_specs=(VMEM, VMEM),
    )


def solution(mesh, interpret=False):
    sizes = {**NODE, **LOCAL}
    cut = Mesh(mesh.devices.reshape(tuple(sizes.values())), tuple(sizes))
    placed = P(tuple(NODE), tuple(LOCAL))
    return jax.shard_map(
        functools.partial(on_device, interpret=interpret),
        mesh=cut,
        in_specs=(placed,) * 7,
        out_specs=(placed, placed),
        check_vma=False,
    )
```

time: 165 us -> 135 us (0.82)
  the two profiles are of different devices: /device:TPU:1 before, /device:TPU:24 now
where the time goes in v6:
time: 135 us; the launch traced here: 134 us
  starting transfers between devices  60 us (44%)
  blocking collectives  31.9 us (24%)
  waiting for transfers between devices  30.1 us (22%)
  other arithmetic  4.72 us (3%)
  Pallas kernels  4.1 us (3%)
  local copies, waits for them, and re-layouts  2.16 us (2%)
    ppermute x8, starting transfers between devices, shift(): lax.ppermute(value, axis, [(i, (i + by) % size) for i in range(size)])  28 us
    all_to_all x1, blocking collectives, on_device(): away = lax.all_to_all(away, 'x', 0, 0, tiled=True)  17 us
    all_to_all x1, waiting for transfers between devices, on_device(): got = lax.all_to_all(sent, 'zl', 0, 0, tiled=True)  16.2 us
    all_gather x1, blocking collectives, on_device(): fac = lax.all_gather(fac, ('zl', 'c'), axis=1, tiled=True)  14.8 us
    ppermute x2, starting transfers between devices, swap(): return lax.ppermute(value, axis, [(0, 1), (1, 0)])  12.8 us
    ppermute x3, starting transfers between devices, mix(): lax.ppermute(value, axis, [(i, i ^ by) for i in range(lax.axis_size(axis))])  12.1 us
    ppermute x8, waiting for transfers between devices, shift(): lax.ppermute(value, axis, [(i, (i + by) % size) for i in range(size)])  7.96 us
    all_to_all x1, starting transfers between devices, on_device(): got = lax.all_to_all(sent, 'zl', 0, 0, tiled=True)  7.2 us
  transfers between devices with their start and end apart: 14, of which 7 were waited for; matrix products, arithmetic and copies ran while one was open for 2% of the time, Pallas kernels for 1%

profile of v6, /device:TPU:24, one launch (start us, length us, event | category | flops | bytes accessed | tf_op | source)
XLA Modules:
  0.0 134.0 jit_solution(923884615539797189)
XLA Ops:
  0.6 0.9 pad_add_fusion.1
  1.5 10.9 %collective-permute-start = (bf16[64,1024]{1,0:T(8,128)(2,1)S(1)}, bf16[64,1024]{1,0:T(8,128)(2,1)S(1)}, u32[]{:S(2)}, u32[]{:S(2)}) collective-permute-start(bf16[64,1024]{1,0:T(8,128)(2,1)S(1)} %get-tuple-element.30), channel_id=1, source_target_pairs={{0,256},{256,0},{1,257},{257,1},{2,258},{258,2},{3,259},{259,3},{4... | collective-permute-start | bytes 393224 | tf_op jit(solution)/shard_map/ppermute | solution.py:22
  12.4 3.6 %collective-permute-done = bf16[64,1024]{1,0:T(8,128)(2,1)S(1)} collective-permute-done((bf16[64,1024]{1,0:T(8,128)(2,1)S(1)}, bf16[64,1024]{1,0:T(8,128)(2,1)S(1)}, u32[]{:S(2)}, u32[]{:S(2)}) %collective-permute-start) | collective-permute-done | bytes 131104 | tf_op jit(solution)/shard_map/ppermute | solution.py:22
  16.0 0.7 pad_maximum_fusion
  16.7 4.7 %collective-permute-start.1 = (bf16[2,64,1024]{2,1,0:T(8,128)(2,1)}, bf16[2,64,1024]{2,1,0:T(8,128)(2,1)}, u32[]{:S(2)}, u32[]{:S(2)}) collective-permute-start(bf16[2,64,1024]{2,1,0:T(8,128)(2,1)} %pad_maximum_fusion), channel_id=1, source_target_pairs={{0,8},{8,16},{16,24},{24,32},{32,40},{40,48},{48,56},{56,0},{1,9},... | collective-permute-start | bytes 786440 | tf_op jit(solution)/shard_map/ppermute | solution.py:27
  21.4 1.9 %collective-permute-start.2 = (bf16[2,64,1024]{2,1,0:T(8,128)(2,1)}, bf16[2,64,1024]{2,1,0:T(8,128)(2,1)S(1)}, u32[]{:S(2)}, u32[]{:S(2)}) collective-permute-start(bf16[2,64,1024]{2,1,0:T(8,128)(2,1)} %pad_maximum_fusion), channel_id=1, source_target_pairs={{0,56},{8,0},{16,8},{24,16},{32,24},{40,32},{48,40},{56,48},{1,57}... | collective-permute-start | bytes 786440 | tf_op jit(solution)/shard_map/ppermute | solution.py:27
  23.4 1.2 pad_add_fusion.refs_0_
  24.5 3.4 %collective-permute-start.9 = (bf16[288,1024]{1,0:T(8,128)(2,1)S(1)}, bf16[288,1024]{1,0:T(8,128)(2,1)S(1)}, u32[]{:S(2)}, u32[]{:S(2)}) collective-permute-start(bf16[288,1024]{1,0:T(8,128)(2,1)S(1)} %pad_add_fusion.refs_0_), channel_id=1, source_target_pairs={{0,64},{64,0},{128,192},{192,128},{1,65},{65,1},{129,193},{193,129... | collective-permute-start | bytes 1769480 | tf_op jit(solution)/shard_map/ppermute | solution.py:31
  27.9 4.0 %collective-permute-start.10 = (bf16[288,1024]{1,0:T(8,128)(2,1)S(1)}, bf16[288,1024]{1,0:T(8,128)(2,1)S(1)}, u32[]{:S(2)}, u32[]{:S(2)}) collective-permute-start(bf16[288,1024]{1,0:T(8,128)(2,1)S(1)} %pad_add_fusion.refs_0_), channel_id=1, source_target_pairs={{0,192},{64,128},{128,64},{192,0},{1,193},{65,129},{129,65},{193,1... | collective-permute-start | bytes 1769480 | tf_op jit(solution)/shard_map/ppermute | solution.py:31
  32.0 0.0 collective-permute-done.1
  32.0 5.1 %collective-permute-start.3 = (bf16[2,64,1024]{2,1,0:T(8,128)(2,1)}, bf16[2,64,1024]{2,1,0:T(8,128)(2,1)S(1)}, u32[]{:S(2)}, u32[]{:S(2)}) collective-permute-start(bf16[2,64,1024]{2,1,0:T(8,128)(2,1)} %collective-permute-done.1), channel_id=1, source_target_pairs={{0,8},{8,16},{16,24},{24,32},{32,40},{40,48},{48,56},{56,0},{1,9},... | collective-permute-start | bytes 786440 | tf_op jit(solution)/shard_map/ppermute | solution.py:27
  37.1 0.0 collective-permute-done.2
  37.1 1.9 %collective-permute-start.4 = (bf16[2,64,1024]{2,1,0:T(8,128)(2,1)S(1)}, bf16[2,64,1024]{2,1,0:T(8,128)(2,1)S(1)}, u32[]{:S(2)}, u32[]{:S(2)}) collective-permute-start(bf16[2,64,1024]{2,1,0:T(8,128)(2,1)S(1)} %collective-permute-done.2), channel_id=1, source_target_pairs={{0,56},{8,0},{16,8},{24,16},{32,24},{40,32},{48,40},{56,48},{1,57}... | collective-permute-start | bytes 786440 | tf_op jit(solution)/shard_map/ppermute | solution.py:27
  39.1 1.0 slice_dynamic-update-slice_fusion.5
  40.1 0.5 collective-permute-done.9.refs_1_
  40.6 4.7 %collective-permute-start.11 = (bf16[288,1024]{1,0:T(8,128)(2,1)S(1)}, bf16[288,1024]{1,0:T(8,128)(2,1)S(1)}, u32[]{:S(2)}, u32[]{:S(2)}) collective-permute-start(bf16[288,1024]{1,0:T(8,128)(2,1)S(1)} %collective-permute-done.9.refs_1_), channel_id=1, source_target_pairs={{0,192},{64,128},{128,64},{192,0},{1,193},{65,129},{129,65},{193,1... | collective-permute-start | bytes 1769480 | tf_op jit(solution)/shard_map/ppermute | solution.py:31
  45.2 0.0 collective-permute-done.3
  45.2 4.9 %collective-permute-start.5 = (bf16[2,64,1024]{2,1,0:T(8,128)(2,1)S(1)}, bf16[2,64,1024]{2,1,0:T(8,128)(2,1)S(1)}, u32[]{:S(2)}, u32[]{:S(2)}) collective-permute-start(bf16[2,64,1024]{2,1,0:T(8,128)(2,1)S(1)} %collective-permute-done.3), channel_id=1, source_target_pairs={{0,8},{8,16},{16,24},{24,32},{32,40},{40,48},{48,56},{56,0},{1,9},... | collective-permute-start | bytes 786440 | tf_op jit(solution)/shard_map/ppermute | solution.py:27
  50.1 0.0 collective-permute-done.4
  50.1 1.9 %collective-permute-start.6 = (bf16[2,64,1024]{2,1,0:T(8,128)(2,1)S(1)}, bf16[2,64,1024]{2,1,0:T(8,128)(2,1)S(1)}, u32[]{:S(2)}, u32[]{:S(2)}) collective-permute-start(bf16[2,64,1024]{2,1,0:T(8,128)(2,1)S(1)} %collective-permute-done.4), channel_id=1, source_target_pairs={{0,56},{8,0},{16,8},{24,16},{32,24},{40,32},{48,40},{56,48},{1,57}... | collective-permute-start | bytes 786440 | tf_op jit(solution)/shard_map/ppermute | solution.py:27
  52.1 1.9 %collective-permute-done.5 = bf16[2,64,1024]{2,1,0:T(8,128)(2,1)S(1)} collective-permute-done((bf16[2,64,1024]{2,1,0:T(8,128)(2,1)S(1)}, bf16[2,64,1024]{2,1,0:T(8,128)(2,1)S(1)}, u32[]{:S(2)}, u32[]{:S(2)}) %collective-permute-start.5) | collective-permute-done | bytes 262176 | tf_op jit(solution)/shard_map/ppermute | solution.py:27
  54.0 5.6 %collective-permute-start.7 = (bf16[1,64,1024]{2,1,0:T(8,128)(2,1)S(1)}, bf16[1,64,1024]{2,1,0:T(8,128)(2,1)S(1)}, u32[]{:S(2)}, u32[]{:S(2)}) collective-permute-start(bf16[1,64,1024]{2,1,0:T(8,128)(2,1)S(1)} %slice.120), channel_id=1, source_target_pairs={{0,8},{8,16},{16,24},{24,32},{32,40},{40,48},{48,56},{56,0},{1,9},... | collective-permute-start | bytes 393224 | tf_op jit(solution)/shard_map/ppermute | solution.py:27
  59.6 0.0 collective-permute-done.6
  59.6 1.9 %collective-permute-start.8 = (bf16[1,64,1024]{2,1,0:T(8,128)(2,1)S(1)}, bf16[1,64,1024]{2,1,0:T(8,128)(2,1)S(1)}, u32[]{:S(2)}, u32[]{:S(2)}) collective-permute-start(bf16[1,64,1024]{2,1,0:T(8,128)(2,1)S(1)} %slice.122), channel_id=1, source_target_pairs={{0,56},{8,0},{16,8},{24,16},{32,24},{40,32},{48,40},{56,48},{1,57}... | collective-permute-start | bytes 393224 | tf_op jit(solution)/shard_map/ppermute | solution.py:27
  61.6 0.5 collective-permute-done.7
  62.1 5.6 %collective-permute-done.8 = bf16[1,64,1024]{2,1,0:T(8,128)(2,1)S(1)} collective-permute-done((bf16[1,64,1024]{2,1,0:T(8,128)(2,1)S(1)}, bf16[1,64,1024]{2,1,0:T(8,128)(2,1)S(1)}, u32[]{:S(2)}, u32[]{:S(2)}) %collective-permute-start.8) | collective-permute-done | bytes 131104 | tf_op jit(solution)/shard_map/ppermute | solution.py:27
  67.7 0.0 collective-permute-done.10.refs_2_
  67.7 0.0 collective-permute-done.11.refs_3_
  67.7 0.9 shard_map.87
  68.6 1.9 %collective-permute-start.12 = (f32[256,1152]{1,0:T(8,128)S(1)}, f32[256,1152]{1,0:T(8,128)S(1)}, u32[]{:S(2)}, u32[]{:S(2)}) collective-permute-start(f32[256,1152]{1,0:T(8,128)S(1)} %shard_map.87), channel_id=1, source_target_pairs={{0,1},{1,0},{2,3},{3,2},{4,5},{5,4},{6,7},{7,6},{8,9},{9,8},{10,11... | collective-permute-start | bytes 3538952 | tf_op jit(solution)/shard_map/ppermute | solution.py:22
  70.5 0.9 shard_map.86
  71.4 1.9 %collective-permute-done.12 = f32[256,1152]{1,0:T(8,128)S(1)} collective-permute-done((f32[256,1152]{1,0:T(8,128)S(1)}, f32[256,1152]{1,0:T(8,128)S(1)}, u32[]{:S(2)}, u32[]{:S(2)}) %collective-permute-start.12) | collective-permute-done | bytes 1179680 | tf_op jit(solution)/shard_map/ppermute | solution.py:22
  73.4 1.0 add_convert_fusion
  74.3 7.2 %all-to-all-start = ((f16[4,64,1152]{2,1,0:T(8,128)(2,1)}), f16[4,64,1152]{2,1,0:T(8,128)(2,1)S(1)}, u32[]{:S(2)}, u32[]{:S(2)}) async-start(f16[4,64,1152]{2,1,0:T(8,128)(2,1)} %bitcast.7), calls=%async_computation | async-start | bytes 1179648 | tf_op jit(solution)/shard_map/all_to_all | solution.py:169
  81.5 16.2 %all-to-all-done = f16[4,64,1152]{2,1,0:T(8,128)(2,1)S(1)} async-done(((f16[4,64,1152]{2,1,0:T(8,128)(2,1)}), f16[4,64,1152]{2,1,0:T(8,128)(2,1)S(1)}, u32[]{:S(2)}, u32[]{:S(2)}) %all-to-all-start) | async-done | bytes 589856 | tf_op jit(solution)/shard_map/all_to_all | solution.py:169
  97.7 0.1 convert_reduce_fusion
  97.8 0.9 reshape.47
  98.7 0.1 reshape.46
  98.8 0.5 fusion.17
  99.3 0.3 fusion.15
  99.6 0.2 pad_maximum_fusion.1
  99.8 14.8 %all_gather.3.fac = bf16[64,4096]{1,0:T(8,128)(2,1)S(1)} all-gather(bf16[64,512]{1,0:T(8,128)(2,1)S(1)} %bitcast.66), channel_id=1, replica_groups=mesh['zh'=2,'x'=4,'y'=8,'zl'=4,'c'=2] {'zl','c'}, dimensions={1}, use_global_device_ids=true | all-gather | bytes 589824 | tf_op jit(solution)/shard_map/all_gather | solution.py:180
  114.6 1.4 %shard_map.88 = (bf16[4,112,1024]{2,1,0:T(8,128)(2,1)S(1)}, f32[112,1024]{1,0:T(8,128)S(1)}) custom-call(s32[1]{0:T(128)} %bitcast.place, bf16[64,4096]{1,0:T(8,128)(2,1)S(1)} %all_gather.3.fac, bf16[512,1024]{1,0:T(8,128)(2,1)S(1)} %bitcast.57), custom_call_target="tpu_custom_call" | custom-call | flops 469762048 | bytes 1048576 | tf_op jit(solution)/shard_map/pallas_call | solution.py:35
  116.0 0.0 copy-start
  116.0 0.0 copy-start.1
  116.0 17.0 %all_to_all.10.away = bf16[4,112,1024]{2,1,0:T(8,128)(2,1)S(1)} all-to-all(bf16[4,112,1024]{2,1,0:T(8,128)(2,1)S(1)} %get-tuple-element.4), channel_id=1, replica_groups=mesh['zh'=2,'x'=4,'y'=8,'zl'=4,'c'=2] {'x'}, dimensions={0} | all-to-all | bytes 1835008 | tf_op jit(solution)/shard_map/all_to_all | solution.py:197
  133.1 0.0 copy-done
  133.1 0.0 copy-done.1
  133.1 0.9 shard_map.89
  (14 shorter events, 0.2 us)
Async XLA Ops:
  1.5 14.5 %collective-permute-start = (bf16[64,1024]{1,0:T(8,128)(2,1)S(1)}, bf16[64,1024]{1,0:T(8,128)(2,1)S(1)}, u32[]{:S(2)}, u32[]{:S(2)}) collective-permute-start(bf16[64,1024]{1,0:T(8,128)(2,1)S(1)} %get-tuple-element.30), channel_id=1, source_target_pairs={{0,256},{256,0},{1,257},{257,1},{2,258},{258,2},{3,259},{259,3},{4... | collective-permute-start | bytes 393224 | tf_op jit(solution)/shard_map/ppermute | solution.py:22
  16.7 15.2 %collective-permute-start.1 = (bf16[2,64,1024]{2,1,0:T(8,128)(2,1)}, bf16[2,64,1024]{2,1,0:T(8,128)(2,1)}, u32[]{:S(2)}, u32[]{:S(2)}) collective-permute-start(bf16[2,64,1024]{2,1,0:T(8,128)(2,1)} %pad_maximum_fusion), channel_id=1, source_target_pairs={{0,8},{8,16},{16,24},{24,32},{32,40},{40,48},{48,56},{56,0},{1,9},... | collective-permute-start | bytes 786440 | tf_op jit(solution)/shard_map/ppermute | solution.py:27
  21.4 15.7 %collective-permute-start.2 = (bf16[2,64,1024]{2,1,0:T(8,128)(2,1)}, bf16[2,64,1024]{2,1,0:T(8,128)(2,1)S(1)}, u32[]{:S(2)}, u32[]{:S(2)}) collective-permute-start(bf16[2,64,1024]{2,1,0:T(8,128)(2,1)} %pad_maximum_fusion), channel_id=1, source_target_pairs={{0,56},{8,0},{16,8},{24,16},{32,24},{40,32},{48,40},{56,48},{1,57}... | collective-permute-start | bytes 786440 | tf_op jit(solution)/shard_map/ppermute | solution.py:27
  24.5 16.0 %collective-permute-start.9 = (bf16[288,1024]{1,0:T(8,128)(2,1)S(1)}, bf16[288,1024]{1,0:T(8,128)(2,1)S(1)}, u32[]{:S(2)}, u32[]{:S(2)}) collective-permute-start(bf16[288,1024]{1,0:T(8,128)(2,1)S(1)} %pad_add_fusion.refs_0_), channel_id=1, source_target_pairs={{0,64},{64,0},{128,192},{192,128},{1,65},{65,1},{129,193},{193,129... | collective-permute-start | bytes 1769480 | tf_op jit(solution)/shard_map/ppermute | solution.py:31
  27.9 39.8 %collective-permute-start.10 = (bf16[288,1024]{1,0:T(8,128)(2,1)S(1)}, bf16[288,1024]{1,0:T(8,128)(2,1)S(1)}, u32[]{:S(2)}, u32[]{:S(2)}) collective-permute-start(bf16[288,1024]{1,0:T(8,128)(2,1)S(1)} %pad_add_fusion.refs_0_), channel_id=1, source_target_pairs={{0,192},{64,128},{128,64},{192,0},{1,193},{65,129},{129,65},{193,1... | collective-permute-start | bytes 1769480 | tf_op jit(solution)/shard_map/ppermute | solution.py:31
  32.0 13.2 %collective-permute-start.3 = (bf16[2,64,1024]{2,1,0:T(8,128)(2,1)}, bf16[2,64,1024]{2,1,0:T(8,128)(2,1)S(1)}, u32[]{:S(2)}, u32[]{:S(2)}) collective-permute-start(bf16[2,64,1024]{2,1,0:T(8,128)(2,1)} %collective-permute-done.1), channel_id=1, source_target_pairs={{0,8},{8,16},{16,24},{24,32},{32,40},{40,48},{48,56},{56,0},{1,9},... | collective-permute-start | bytes 786440 | tf_op jit(solution)/shard_map/ppermute | solution.py:27
  37.1 13.0 %collective-permute-start.4 = (bf16[2,64,1024]{2,1,0:T(8,128)(2,1)S(1)}, bf16[2,64,1024]{2,1,0:T(8,128)(2,1)S(1)}, u32[]{:S(2)}, u32[]{:S(2)}) collective-permute-start(bf16[2,64,1024]{2,1,0:T(8,128)(2,1)S(1)} %collective-permute-done.2), channel_id=1, source_target_pairs={{0,56},{8,0},{16,8},{24,16},{32,24},{40,32},{48,40},{56,48},{1,57}... | collective-permute-start | bytes 786440 | tf_op jit(solution)/shard_map/ppermute | solution.py:27
  40.6 27.2 %collective-permute-start.11 = (bf16[288,1024]{1,0:T(8,128)(2,1)S(1)}, bf16[288,1024]{1,0:T(8,128)(2,1)S(1)}, u32[]{:S(2)}, u32[]{:S(2)}) collective-permute-start(bf16[288,1024]{1,0:T(8,128)(2,1)S(1)} %collective-permute-done.9.refs_1_), channel_id=1, source_target_pairs={{0,192},{64,128},{128,64},{192,0},{1,193},{65,129},{129,65},{193,1... | collective-permute-start | bytes 1769480 | tf_op jit(solution)/shard_map/ppermute | solution.py:31
  45.2 8.7 %collective-permute-start.5 = (bf16[2,64,1024]{2,1,0:T(8,128)(2,1)S(1)}, bf16[2,64,1024]{2,1,0:T(8,128)(2,1)S(1)}, u32[]{:S(2)}, u32[]{:S(2)}) collective-permute-start(bf16[2,64,1024]{2,1,0:T(8,128)(2,1)S(1)} %collective-permute-done.3), channel_id=1, source_target_pairs={{0,8},{8,16},{16,24},{24,32},{32,40},{40,48},{48,56},{56,0},{1,9},... | collective-permute-start | bytes 786440 | tf_op jit(solution)/shard_map/ppermute | solution.py:27
  50.1 9.5 %collective-permute-start.6 = (bf16[2,64,1024]{2,1,0:T(8,128)(2,1)S(1)}, bf16[2,64,1024]{2,1,0:T(8,128)(2,1)S(1)}, u32[]{:S(2)}, u32[]{:S(2)}) collective-permute-start(bf16[2,64,1024]{2,1,0:T(8,128)(2,1)S(1)} %collective-permute-done.4), channel_id=1, source_target_pairs={{0,56},{8,0},{16,8},{24,16},{32,24},{40,32},{48,40},{56,48},{1,57}... | collective-permute-start | bytes 786440 | tf_op jit(solution)/shard_map/ppermute | solution.py:27
  54.0 8.1 %collective-permute-start.7 = (bf16[1,64,1024]{2,1,0:T(8,128)(2,1)S(1)}, bf16[1,64,1024]{2,1,0:T(8,128)(2,1)S(1)}, u32[]{:S(2)}, u32[]{:S(2)}) collective-permute-start(bf16[1,64,1024]{2,1,0:T(8,128)(2,1)S(1)} %slice.120), channel_id=1, source_target_pairs={{0,8},{8,16},{16,24},{24,32},{32,40},{40,48},{48,56},{56,0},{1,9},... | collective-permute-start | bytes 393224 | tf_op jit(solution)/shard_map/ppermute | solution.py:27
  59.6 8.1 %collective-permute-start.8 = (bf16[1,64,1024]{2,1,0:T(8,128)(2,1)S(1)}, bf16[1,64,1024]{2,1,0:T(8,128)(2,1)S(1)}, u32[]{:S(2)}, u32[]{:S(2)}) collective-permute-start(bf16[1,64,1024]{2,1,0:T(8,128)(2,1)S(1)} %slice.122), channel_id=1, source_target_pairs={{0,56},{8,0},{16,8},{24,16},{32,24},{40,32},{48,40},{56,48},{1,57}... | collective-permute-start | bytes 393224 | tf_op jit(solution)/shard_map/ppermute | solution.py:27
  68.6 4.7 %collective-permute-start.12 = (f32[256,1152]{1,0:T(8,128)S(1)}, f32[256,1152]{1,0:T(8,128)S(1)}, u32[]{:S(2)}, u32[]{:S(2)}) collective-permute-start(f32[256,1152]{1,0:T(8,128)S(1)} %shard_map.87), channel_id=1, source_target_pairs={{0,1},{1,0},{2,3},{3,2},{4,5},{5,4},{6,7},{7,6},{8,9},{9,8},{10,11... | collective-permute-start | bytes 3538952 | tf_op jit(solution)/shard_map/ppermute | solution.py:22
  74.3 23.4 %all-to-all-start = ((f16[4,64,1152]{2,1,0:T(8,128)(2,1)}), f16[4,64,1152]{2,1,0:T(8,128)(2,1)S(1)}, u32[]{:S(2)}, u32[]{:S(2)}) async-start(f16[4,64,1152]{2,1,0:T(8,128)(2,1)} %bitcast.7), calls=%async_computation | async-start | bytes 1179648 | tf_op jit(solution)/shard_map/all_to_all | solution.py:169
  116.0 17.1 %copy-start = (bf16[56,1024]{1,0:T(8,128)(2,1)S(1)}, bf16[56,1024]{1,0:T(8,128)(2,1)}, u32[]{:S(2)}) copy-start(bf16[56,1024]{1,0:T(8,128)(2,1)} %up_probe.1) | copy-start | bytes 344068
  116.0 17.0 %copy-start.1 = (bf16[56,1024]{1,0:T(8,128)(2,1)S(1)}, bf16[56,1024]{1,0:T(8,128)(2,1)}, u32[]{:S(2)}) copy-start(bf16[56,1024]{1,0:T(8,128)(2,1)} %gate_probe.1) | copy-start | bytes 344068

commit v7 on v6

--- a/solution.py
+++ b/solution.py
@@ -42,7 +42,7 @@
     )(*args)
 
 
-def terms_kernel(tok_rows, place, tokens, cotangents, *refs):
+def terms_kernel(tok_rows, which, place, tokens, cotangents, *refs):
     *weights, out, w_all = refs
     cut = len(weights) * tok_rows
     cot_rows = weights[0].shape[0] - tok_rows
@@ -51,7 +51,7 @@
         start = cut + i * cot_rows
         w_all[start : start + cot_rows] = weight[tok_rows:]
     count = out.shape[0]
-    half = pl.ds(pl.multiple_of(place[0] * count, count), count)
+    half = pl.ds(pl.multiple_of(place[which] * count, count), count)
     across = (((1,), (1,)), ((), ()))
     column = lax.rem(lax.broadcasted_iota(jnp.int32, (1, cut), 1), tok_rows)
     out[:, :cut] = lax.dot_general(
@@ -66,7 +66,7 @@
     nx, width, _ = away.shape
     lanes = fac.shape[1] // (nzl * nc * nx)
     for i in range(nx):
-        step = place[0] ^ i
+        step = place[2] ^ i
         step = step ^ (step >> 1)
         parts = []
         for c in range(nc):
@@ -79,7 +79,7 @@
         )[:width]
         away[i] = term.astype(away.dtype)
 
-        @pl.when(place[0] == i)
+        @pl.when(place[2] == i)
         def _():
             own[...] = term
 
@@ -87,7 +87,7 @@
 def sum_kernel(total, place, away, own, gate_probe, up_probe, gate_diag, up_diag):
     both = own[...]
     for i in range(away.shape[0]):
-        both += jnp.where(place[0] == i, 0.0, away[i].astype(jnp.float32))
+        both += jnp.where(place[2] == i, 0.0, away[i].astype(jnp.float32))
     both = both / total
     hid = gate_diag.shape[0]
     gate_diag[...] = gate_probe[...].astype(jnp.float32) * both[:hid]
@@ -123,7 +123,8 @@
     hid = gate_weight.shape[0]
     total = own * lax.axis_size(("zh", "x", "y"))
     nc = lax.axis_size("c")
-    x, core = lax.axis_index("x"), lax.axis_index("c")
+    core = lax.axis_index("c")
+    place = jnp.stack([core, 1 - core, lax.axis_index("x")])
 
     rows = stacked([tokens, cotangent], 2 * own)
     block = jnp.stack([rows, swap(rows, "zh")], axis=0)
@@ -148,12 +149,12 @@
     cut, columns = nx * tok_rows, nx * (tok_rows + cot_rows)
     def term(which):
         return local_call(
-            functools.partial(terms_kernel, tok_rows),
+            functools.partial(terms_kernel, tok_rows, which),
             jax.ShapeDtypeStruct((count, columns), jnp.float32),
             2 * count * columns * feats,
             2 * columns * feats,
             interpret,
-            which.reshape(1),
+            place,
             tok_all,
             cot_all,
             *weights,
@@ -161,8 +162,8 @@
             out_specs=VMEM,
             scratch_shapes=[pltpu.VMEM((columns, feats), jnp.bfloat16)],
         )
-    other = swap(term(1 - core), "c")
-    terms = term(core) + other
+    other = swap(term(1), "c")
+    terms = term(0) + other
 
     share = count // nzl
     sent = terms.astype(jnp.float16).reshape(nzl, share, columns)
@@ -188,7 +189,7 @@
         4 * nx * hid * nc * count * feats,
         2 * nc * count * feats,
         interpret,
-        x.reshape(1),
+        place,
         fac,
         tok_all,
         in_specs=[SMEM, VMEM, VMEM],
@@ -202,7 +203,7 @@
         2 * nx * hid * feats,
         8 * nx * hid * feats,
         interpret,
-        x.reshape(1),
+        place,
         away,
         mine,
         gate_probe,

time: 135 us -> 135 us (level)
  blocking collectives: 31.9 us -> 55.2 us
  waiting for transfers between devices: 30.1 us -> 13.3 us
  starting transfers between devices: 60 us -> 52.8 us
  Pallas kernels: 4.1 us -> 6.25 us
    all_to_all x0 -> x1, blocking collectives: none -> 23.2 us  [on_device(): got = lax.all_to_all(sent, 'zl', 0, 0, tiled=True)]
    all_to_all x1 -> x0, waiting for transfers between devices: 16.2 us -> none  [on_device(): got = lax.all_to_all(sent, 'zl', 0, 0, tiled=True)]
    all_to_all x1 -> x0, starting transfers between devices: 7.2 us -> none  [on_device(): got = lax.all_to_all(sent, 'zl', 0, 0, tiled=True)]
    pallas_call x4, Pallas kernels: 4.1 us -> 6.25 us  [local_call(): pl.pallas_call(body, out_shape=out_shape, cost_estimate=pl.CostEstimate(f...]
  transfers between devices with their start and end apart: 14 -> 13, of which waited for: 7 -> 6; matrix products, arithmetic and copies ran while one was open for 2% -> 2% of each run, Pallas kernels for 1% -> 1%
where the time goes in v7:
time: 135 us
  blocking collectives  55.2 us (41%)
  starting transfers between devices  52.8 us (39%)
  waiting for transfers between devices  13.3 us (10%)
  Pallas kernels  6.25 us (5%)
  other arithmetic  3.94 us (3%)
  local copies, waits for them, and re-layouts  2.16 us (2%)
    ppermute x8, starting transfers between devices, shift(): lax.ppermute(value, axis, [(i, (i + by) % size) for i in range(size)])  28 us
    all_to_all x1, blocking collectives, on_device(): got = lax.all_to_all(sent, 'zl', 0, 0, tiled=True)  23.2 us
    all_to_all x1, blocking collectives, on_device(): away = lax.all_to_all(away, 'x', 0, 0, tiled=True)  17 us
    all_gather x1, blocking collectives, on_device(): fac = lax.all_gather(fac, ('zl', 'c'), axis=1, tiled=True)  15 us
    ppermute x2, starting transfers between devices, swap(): return lax.ppermute(value, axis, [(0, 1), (1, 0)])  12.8 us
    ppermute x3, starting transfers between devices, mix(): lax.ppermute(value, axis, [(i, i ^ by) for i in range(lax.axis_size(axis))])  12.1 us
    ppermute x8, waiting for transfers between devices, shift(): lax.ppermute(value, axis, [(i, (i + by) % size) for i in range(size)])  7.96 us
    pallas_call x4, Pallas kernels, local_call(): pl.pallas_call(body, out_shape=out_shape, cost_estimate=pl.CostEstimate(f...  6.25 us
  transfers between devices with their start and end apart: 13, of which 6 were waited for; matrix products, arithmetic and copies ran while one was open for 2% of the time, Pallas kernels for 1%

profile of v7, /device:TPU:24, one launch (start us, length us, event | category | flops | bytes accessed | tf_op | source)
XLA Modules:
  0.0 134.7 jit_solution(15990420634068386509)
XLA Ops:
  0.6 0.9 pad_add_fusion.1
  1.5 10.9 %collective-permute-start = (bf16[64,1024]{1,0:T(8,128)(2,1)S(1)}, bf16[64,1024]{1,0:T(8,128)(2,1)S(1)}, u32[]{:S(2)}, u32[]{:S(2)}) collective-permute-start(bf16[64,1024]{1,0:T(8,128)(2,1)S(1)} %get-tuple-element.30), channel_id=1, source_target_pairs={{0,256},{256,0},{1,257},{257,1},{2,258},{258,2},{3,259},{259,3},{4... | collective-permute-start | bytes 393224 | tf_op jit(solution)/shard_map/ppermute | solution.py:22
  12.5 3.6 %collective-permute-done = bf16[64,1024]{1,0:T(8,128)(2,1)S(1)} collective-permute-done((bf16[64,1024]{1,0:T(8,128)(2,1)S(1)}, bf16[64,1024]{1,0:T(8,128)(2,1)S(1)}, u32[]{:S(2)}, u32[]{:S(2)}) %collective-permute-start) | collective-permute-done | bytes 131104 | tf_op jit(solution)/shard_map/ppermute | solution.py:22
  16.0 0.7 pad_maximum_fusion
  16.8 4.7 %collective-permute-start.1 = (bf16[2,64,1024]{2,1,0:T(8,128)(2,1)}, bf16[2,64,1024]{2,1,0:T(8,128)(2,1)}, u32[]{:S(2)}, u32[]{:S(2)}) collective-permute-start(bf16[2,64,1024]{2,1,0:T(8,128)(2,1)} %pad_maximum_fusion), channel_id=1, source_target_pairs={{0,8},{8,16},{16,24},{24,32},{32,40},{40,48},{48,56},{56,0},{1,9},... | collective-permute-start | bytes 786440 | tf_op jit(solution)/shard_map/ppermute | solution.py:27
  21.5 1.9 %collective-permute-start.2 = (bf16[2,64,1024]{2,1,0:T(8,128)(2,1)}, bf16[2,64,1024]{2,1,0:T(8,128)(2,1)S(1)}, u32[]{:S(2)}, u32[]{:S(2)}) collective-permute-start(bf16[2,64,1024]{2,1,0:T(8,128)(2,1)} %pad_maximum_fusion), channel_id=1, source_target_pairs={{0,56},{8,0},{16,8},{24,16},{32,24},{40,32},{48,40},{56,48},{1,57}... | collective-permute-start | bytes 786440 | tf_op jit(solution)/shard_map/ppermute | solution.py:27
  23.4 1.2 pad_add_fusion.refs_0_
  24.5 3.4 %collective-permute-start.9 = (bf16[288,1024]{1,0:T(8,128)(2,1)S(1)}, bf16[288,1024]{1,0:T(8,128)(2,1)S(1)}, u32[]{:S(2)}, u32[]{:S(2)}) collective-permute-start(bf16[288,1024]{1,0:T(8,128)(2,1)S(1)} %pad_add_fusion.refs_0_), channel_id=1, source_target_pairs={{0,64},{64,0},{128,192},{192,128},{1,65},{65,1},{129,193},{193,129... | collective-permute-start | bytes 1769480 | tf_op jit(solution)/shard_map/ppermute | solution.py:31
  28.0 4.0 %collective-permute-start.10 = (bf16[288,1024]{1,0:T(8,128)(2,1)S(1)}, bf16[288,1024]{1,0:T(8,128)(2,1)S(1)}, u32[]{:S(2)}, u32[]{:S(2)}) collective-permute-start(bf16[288,1024]{1,0:T(8,128)(2,1)S(1)} %pad_add_fusion.refs_0_), channel_id=1, source_target_pairs={{0,192},{64,128},{128,64},{192,0},{1,193},{65,129},{129,65},{193,1... | collective-permute-start | bytes 1769480 | tf_op jit(solution)/shard_map/ppermute | solution.py:31
  32.0 0.1 pad_add_fusion.2.place
  32.1 0.0 collective-permute-done.1
  32.1 5.1 %collective-permute-start.3 = (bf16[2,64,1024]{2,1,0:T(8,128)(2,1)}, bf16[2,64,1024]{2,1,0:T(8,128)(2,1)S(1)}, u32[]{:S(2)}, u32[]{:S(2)}) collective-permute-start(bf16[2,64,1024]{2,1,0:T(8,128)(2,1)} %collective-permute-done.1), channel_id=1, source_target_pairs={{0,8},{8,16},{16,24},{24,32},{32,40},{40,48},{48,56},{56,0},{1,9},... | collective-permute-start | bytes 786440 | tf_op jit(solution)/shard_map/ppermute | solution.py:27
  37.2 0.0 collective-permute-done.2
  37.2 1.9 %collective-permute-start.4 = (bf16[2,64,1024]{2,1,0:T(8,128)(2,1)S(1)}, bf16[2,64,1024]{2,1,0:T(8,128)(2,1)S(1)}, u32[]{:S(2)}, u32[]{:S(2)}) collective-permute-start(bf16[2,64,1024]{2,1,0:T(8,128)(2,1)S(1)} %collective-permute-done.2), channel_id=1, source_target_pairs={{0,56},{8,0},{16,8},{24,16},{32,24},{40,32},{48,40},{56,48},{1,57}... | collective-permute-start | bytes 786440 | tf_op jit(solution)/shard_map/ppermute | solution.py:27
  39.2 1.0 slice_dynamic-update-slice_fusion.5
  40.2 0.4 collective-permute-done.9.refs_1_
  40.6 4.7 %collective-permute-start.11 = (bf16[288,1024]{1,0:T(8,128)(2,1)S(1)}, bf16[288,1024]{1,0:T(8,128)(2,1)S(1)}, u32[]{:S(2)}, u32[]{:S(2)}) collective-permute-start(bf16[288,1024]{1,0:T(8,128)(2,1)S(1)} %collective-permute-done.9.refs_1_), channel_id=1, source_target_pairs={{0,192},{64,128},{128,64},{192,0},{1,193},{65,129},{129,65},{193,1... | collective-permute-start | bytes 1769480 | tf_op jit(solution)/shard_map/ppermute | solution.py:31
  45.2 0.0 collective-permute-done.3
  45.2 4.9 %collective-permute-start.5 = (bf16[2,64,1024]{2,1,0:T(8,128)(2,1)S(1)}, bf16[2,64,1024]{2,1,0:T(8,128)(2,1)S(1)}, u32[]{:S(2)}, u32[]{:S(2)}) collective-permute-start(bf16[2,64,1024]{2,1,0:T(8,128)(2,1)S(1)} %collective-permute-done.3), channel_id=1, source_target_pairs={{0,8},{8,16},{16,24},{24,32},{32,40},{40,48},{48,56},{56,0},{1,9},... | collective-permute-start | bytes 786440 | tf_op jit(solution)/shard_map/ppermute | solution.py:27
  50.1 0.0 collective-permute-done.4
  50.1 1.9 %collective-permute-start.6 = (bf16[2,64,1024]{2,1,0:T(8,128)(2,1)S(1)}, bf16[2,64,1024]{2,1,0:T(8,128)(2,1)S(1)}, u32[]{:S(2)}, u32[]{:S(2)}) collective-permute-start(bf16[2,64,1024]{2,1,0:T(8,128)(2,1)S(1)} %collective-permute-done.4), channel_id=1, source_target_pairs={{0,56},{8,0},{16,8},{24,16},{32,24},{40,32},{48,40},{56,48},{1,57}... | collective-permute-start | bytes 786440 | tf_op jit(solution)/shard_map/ppermute | solution.py:27
  52.1 1.9 %collective-permute-done.5 = bf16[2,64,1024]{2,1,0:T(8,128)(2,1)S(1)} collective-permute-done((bf16[2,64,1024]{2,1,0:T(8,128)(2,1)S(1)}, bf16[2,64,1024]{2,1,0:T(8,128)(2,1)S(1)}, u32[]{:S(2)}, u32[]{:S(2)}) %collective-permute-start.5) | collective-permute-done | bytes 262176 | tf_op jit(solution)/shard_map/ppermute | solution.py:27
  54.0 5.6 %collective-permute-start.7 = (bf16[1,64,1024]{2,1,0:T(8,128)(2,1)S(1)}, bf16[1,64,1024]{2,1,0:T(8,128)(2,1)S(1)}, u32[]{:S(2)}, u32[]{:S(2)}) collective-permute-start(bf16[1,64,1024]{2,1,0:T(8,128)(2,1)S(1)} %slice.120), channel_id=1, source_target_pairs={{0,8},{8,16},{16,24},{24,32},{32,40},{40,48},{48,56},{56,0},{1,9},... | collective-permute-start | bytes 393224 | tf_op jit(solution)/shard_map/ppermute | solution.py:27
  59.6 0.0 collective-permute-done.6
  59.6 1.9 %collective-permute-start.8 = (bf16[1,64,1024]{2,1,0:T(8,128)(2,1)S(1)}, bf16[1,64,1024]{2,1,0:T(8,128)(2,1)S(1)}, u32[]{:S(2)}, u32[]{:S(2)}) collective-permute-start(bf16[1,64,1024]{2,1,0:T(8,128)(2,1)S(1)} %slice.122), channel_id=1, source_target_pairs={{0,56},{8,0},{16,8},{24,16},{32,24},{40,32},{48,40},{56,48},{1,57}... | collective-permute-start | bytes 393224 | tf_op jit(solution)/shard_map/ppermute | solution.py:27
  61.6 0.5 collective-permute-done.7
  62.1 5.6 %collective-permute-done.8 = bf16[1,64,1024]{2,1,0:T(8,128)(2,1)S(1)} collective-permute-done((bf16[1,64,1024]{2,1,0:T(8,128)(2,1)S(1)}, bf16[1,64,1024]{2,1,0:T(8,128)(2,1)S(1)}, u32[]{:S(2)}, u32[]{:S(2)}) %collective-permute-start.8) | collective-permute-done | bytes 131104 | tf_op jit(solution)/shard_map/ppermute | solution.py:27
  67.7 0.0 collective-permute-done.10.refs_2_
  67.7 0.0 collective-permute-done.11.refs_3_
  67.7 1.4 %shard_map.87 = f32[256,1152]{1,0:T(8,128)S(1)} custom-call(s32[3]{0:T(128)S(1)} %pad_add_fusion.2.place, bf16[512,1024]{1,0:T(8,128)(2,1)S(1)} %bitcast.55, bf16[512,1024]{1,0:T(8,128)(2,1)S(1)} %bitcast.53, bf16[288,1024]{1,0:T(8,128)(2,1)S(1)} %pad_add_fusion.refs_0_, bf16[288,1024]{1,0:T(8,128)(2,1)S(1)} %collective-permute-done.9.refs_1_, ...), custom_call_target="tpu_custom_call" | custom-call | flops 603979776 | bytes 2359296 | tf_op jit(solution)/shard_map/pallas_call | solution.py:35
  69.2 1.9 %collective-permute-start.12 = (f32[256,1152]{1,0:T(8,128)S(1)}, f32[256,1152]{1,0:T(8,128)S(1)}, u32[]{:S(2)}, u32[]{:S(2)}) collective-permute-start(f32[256,1152]{1,0:T(8,128)S(1)} %shard_map.87), channel_id=1, source_target_pairs={{0,1},{1,0},{2,3},{3,2},{4,5},{5,4},{6,7},{7,6},{8,9},{9,8},{10,11... | collective-permute-start | bytes 3538952 | tf_op jit(solution)/shard_map/ppermute | solution.py:22
  71.1 1.4 %shard_map.86 = f32[256,1152]{1,0:T(8,128)S(1)} custom-call(s32[3]{0:T(128)S(1)} %pad_add_fusion.2.place, bf16[512,1024]{1,0:T(8,128)(2,1)S(1)} %bitcast.56, bf16[512,1024]{1,0:T(8,128)(2,1)S(1)} %bitcast.54, bf16[288,1024]{1,0:T(8,128)(2,1)S(1)} %pad_add_fusion.refs_0_, bf16[288,1024]{1,0:T(8,128)(2,1)S(1)} %collective-permute-done.9.refs_1_, ...), custom_call_target="tpu_custom_call" | custom-call | flops 603979776 | bytes 2359296 | tf_op jit(solution)/shard_map/pallas_call | solution.py:35
  72.5 1.4 %collective-permute-done.12 = f32[256,1152]{1,0:T(8,128)S(1)} collective-permute-done((f32[256,1152]{1,0:T(8,128)S(1)}, f32[256,1152]{1,0:T(8,128)S(1)}, u32[]{:S(2)}, u32[]{:S(2)}) %collective-permute-start.12) | collective-permute-done | bytes 1179680 | tf_op jit(solution)/shard_map/ppermute | solution.py:22
  73.9 0.1 add_convert_fusion
  74.0 23.2 %all_to_all.10 = f16[4,64,1152]{2,1,0:T(8,128)(2,1)S(1)} all-to-all(f16[4,64,1152]{2,1,0:T(8,128)(2,1)S(1)} %bitcast.58), channel_id=1, replica_groups=mesh['zh'=2,'x'=4,'y'=8,'zl'=4,'c'=2] {'zl'}, dimensions={0} | all-to-all | bytes 1179648 | tf_op jit(solution)/shard_map/all_to_all | solution.py:170
  97.2 0.1 convert_reduce_fusion
  97.3 0.9 reshape.34
  98.2 0.1 reshape.33
  98.4 0.5 fusion.17
  98.8 0.3 fusion.15
  99.1 0.2 pad_maximum_fusion.1
  99.3 15.0 %all_gather.3.fac = bf16[64,4096]{1,0:T(8,128)(2,1)S(1)} all-gather(bf16[64,512]{1,0:T(8,128)(2,1)S(1)} %bitcast.67), channel_id=1, replica_groups=mesh['zh'=2,'x'=4,'y'=8,'zl'=4,'c'=2] {'zl','c'}, dimensions={1}, use_global_device_ids=true | all-gather | bytes 589824 | tf_op jit(solution)/shard_map/all_gather | solution.py:181
  114.2 1.9 %shard_map.88 = (bf16[4,112,1024]{2,1,0:T(8,128)(2,1)S(1)}, f32[112,1024]{1,0:T(8,128)S(1)}) custom-call(s32[3]{0:T(128)S(1)} %pad_add_fusion.2.place, bf16[64,4096]{1,0:T(8,128)(2,1)S(1)} %all_gather.3.fac, bf16[512,1024]{1,0:T(8,128)(2,1)S(1)} %bitcast.57), custom_call_target="tpu_custom_call" | custom-call | flops 469762048 | bytes 1048576 | tf_op jit(solution)/shard_map/pallas_call | solution.py:35
  116.2 0.0 copy-start
  116.2 0.0 copy-start.1
  116.2 17.0 %all_to_all.11.away = bf16[4,112,1024]{2,1,0:T(8,128)(2,1)S(1)} all-to-all(bf16[4,112,1024]{2,1,0:T(8,128)(2,1)S(1)} %get-tuple-element.4), channel_id=1, replica_groups=mesh['zh'=2,'x'=4,'y'=8,'zl'=4,'c'=2] {'x'}, dimensions={0} | all-to-all | bytes 1835008 | tf_op jit(solution)/shard_map/all_to_all | solution.py:198
  133.3 0.0 copy-done
  133.3 0.0 copy-done.1
  133.3 1.5 %shard_map.89 = (f32[56,1024]{1,0:T(8,128)}, f32[56,1024]{1,0:T(8,128)}) custom-call(s32[3]{0:T(128)S(1)} %pad_add_fusion.2.place, bf16[4,112,1024]{2,1,0:T(8,128)(2,1)S(1)} %all_to_all.11.away, f32[112,1024]{1,0:T(8,128)S(1)} %get-tuple-element.5.own, bf16[56,1024]{1,0:T(8,128)(2,1)S(1)} %copy-done.1, bf16[56,1024]{1,0:T(8,128)(2,1)S(1)} %copy-done), custom_call_target="tpu_custom_call" | custom-call | flops 458752 | bytes 1835008 | tf_op jit(solution)/shard_map/pallas_call | solution.py:35
  (14 shorter events, 0.2 us)
Async XLA Ops:
  1.5 14.5 %collective-permute-start = (bf16[64,1024]{1,0:T(8,128)(2,1)S(1)}, bf16[64,1024]{1,0:T(8,128)(2,1)S(1)}, u32[]{:S(2)}, u32[]{:S(2)}) collective-permute-start(bf16[64,1024]{1,0:T(8,128)(2,1)S(1)} %get-tuple-element.30), channel_id=1, source_target_pairs={{0,256},{256,0},{1,257},{257,1},{2,258},{258,2},{3,259},{259,3},{4... | collective-permute-start | bytes 393224 | tf_op jit(solution)/shard_map/ppermute | solution.py:22
  16.8 15.3 %collective-permute-start.1 = (bf16[2,64,1024]{2,1,0:T(8,128)(2,1)}, bf16[2,64,1024]{2,1,0:T(8,128)(2,1)}, u32[]{:S(2)}, u32[]{:S(2)}) collective-permute-start(bf16[2,64,1024]{2,1,0:T(8,128)(2,1)} %pad_maximum_fusion), channel_id=1, source_target_pairs={{0,8},{8,16},{16,24},{24,32},{32,40},{40,48},{48,56},{56,0},{1,9},... | collective-permute-start | bytes 786440 | tf_op jit(solution)/shard_map/ppermute | solution.py:27
  21.5 15.8 %collective-permute-start.2 = (bf16[2,64,1024]{2,1,0:T(8,128)(2,1)}, bf16[2,64,1024]{2,1,0:T(8,128)(2,1)S(1)}, u32[]{:S(2)}, u32[]{:S(2)}) collective-permute-start(bf16[2,64,1024]{2,1,0:T(8,128)(2,1)} %pad_maximum_fusion), channel_id=1, source_target_pairs={{0,56},{8,0},{16,8},{24,16},{32,24},{40,32},{48,40},{56,48},{1,57}... | collective-permute-start | bytes 786440 | tf_op jit(solution)/shard_map/ppermute | solution.py:27
  24.5 16.0 %collective-permute-start.9 = (bf16[288,1024]{1,0:T(8,128)(2,1)S(1)}, bf16[288,1024]{1,0:T(8,128)(2,1)S(1)}, u32[]{:S(2)}, u32[]{:S(2)}) collective-permute-start(bf16[288,1024]{1,0:T(8,128)(2,1)S(1)} %pad_add_fusion.refs_0_), channel_id=1, source_target_pairs={{0,64},{64,0},{128,192},{192,128},{1,65},{65,1},{129,193},{193,129... | collective-permute-start | bytes 1769480 | tf_op jit(solution)/shard_map/ppermute | solution.py:31
  28.0 39.8 %collective-permute-start.10 = (bf16[288,1024]{1,0:T(8,128)(2,1)S(1)}, bf16[288,1024]{1,0:T(8,128)(2,1)S(1)}, u32[]{:S(2)}, u32[]{:S(2)}) collective-permute-start(bf16[288,1024]{1,0:T(8,128)(2,1)S(1)} %pad_add_fusion.refs_0_), channel_id=1, source_target_pairs={{0,192},{64,128},{128,64},{192,0},{1,193},{65,129},{129,65},{193,1... | collective-permute-start | bytes 1769480 | tf_op jit(solution)/shard_map/ppermute | solution.py:31
  32.1 13.2 %collective-permute-start.3 = (bf16[2,64,1024]{2,1,0:T(8,128)(2,1)}, bf16[2,64,1024]{2,1,0:T(8,128)(2,1)S(1)}, u32[]{:S(2)}, u32[]{:S(2)}) collective-permute-start(bf16[2,64,1024]{2,1,0:T(8,128)(2,1)} %collective-permute-done.1), channel_id=1, source_target_pairs={{0,8},{8,16},{16,24},{24,32},{32,40},{40,48},{48,56},{56,0},{1,9},... | collective-permute-start | bytes 786440 | tf_op jit(solution)/shard_map/ppermute | solution.py:27
  37.2 12.9 %collective-permute-start.4 = (bf16[2,64,1024]{2,1,0:T(8,128)(2,1)S(1)}, bf16[2,64,1024]{2,1,0:T(8,128)(2,1)S(1)}, u32[]{:S(2)}, u32[]{:S(2)}) collective-permute-start(bf16[2,64,1024]{2,1,0:T(8,128)(2,1)S(1)} %collective-permute-done.2), channel_id=1, source_target_pairs={{0,56},{8,0},{16,8},{24,16},{32,24},{40,32},{48,40},{56,48},{1,57}... | collective-permute-start | bytes 786440 | tf_op jit(solution)/shard_map/ppermute | solution.py:27
  40.6 27.2 %collective-permute-start.11 = (bf16[288,1024]{1,0:T(8,128)(2,1)S(1)}, bf16[288,1024]{1,0:T(8,128)(2,1)S(1)}, u32[]{:S(2)}, u32[]{:S(2)}) collective-permute-start(bf16[288,1024]{1,0:T(8,128)(2,1)S(1)} %collective-permute-done.9.refs_1_), channel_id=1, source_target_pairs={{0,192},{64,128},{128,64},{192,0},{1,193},{65,129},{129,65},{193,1... | collective-permute-start | bytes 1769480 | tf_op jit(solution)/shard_map/ppermute | solution.py:31
  45.2 8.7 %collective-permute-start.5 = (bf16[2,64,1024]{2,1,0:T(8,128)(2,1)S(1)}, bf16[2,64,1024]{2,1,0:T(8,128)(2,1)S(1)}, u32[]{:S(2)}, u32[]{:S(2)}) collective-permute-start(bf16[2,64,1024]{2,1,0:T(8,128)(2,1)S(1)} %collective-permute-done.3), channel_id=1, source_target_pairs={{0,8},{8,16},{16,24},{24,32},{32,40},{40,48},{48,56},{56,0},{1,9},... | collective-permute-start | bytes 786440 | tf_op jit(solution)/shard_map/ppermute | solution.py:27
  50.1 9.5 %collective-permute-start.6 = (bf16[2,64,1024]{2,1,0:T(8,128)(2,1)S(1)}, bf16[2,64,1024]{2,1,0:T(8,128)(2,1)S(1)}, u32[]{:S(2)}, u32[]{:S(2)}) collective-permute-start(bf16[2,64,1024]{2,1,0:T(8,128)(2,1)S(1)} %collective-permute-done.4), channel_id=1, source_target_pairs={{0,56},{8,0},{16,8},{24,16},{32,24},{40,32},{48,40},{56,48},{1,57}... | collective-permute-start | bytes 786440 | tf_op jit(solution)/shard_map/ppermute | solution.py:27
  54.0 8.1 %collective-permute-start.7 = (bf16[1,64,1024]{2,1,0:T(8,128)(2,1)S(1)}, bf16[1,64,1024]{2,1,0:T(8,128)(2,1)S(1)}, u32[]{:S(2)}, u32[]{:S(2)}) collective-permute-start(bf16[1,64,1024]{2,1,0:T(8,128)(2,1)S(1)} %slice.120), channel_id=1, source_target_pairs={{0,8},{8,16},{16,24},{24,32},{32,40},{40,48},{48,56},{56,0},{1,9},... | collective-permute-start | bytes 393224 | tf_op jit(solution)/shard_map/ppermute | solution.py:27
  59.6 8.1 %collective-permute-start.8 = (bf16[1,64,1024]{2,1,0:T(8,128)(2,1)S(1)}, bf16[1,64,1024]{2,1,0:T(8,128)(2,1)S(1)}, u32[]{:S(2)}, u32[]{:S(2)}) collective-permute-start(bf16[1,64,1024]{2,1,0:T(8,128)(2,1)S(1)} %slice.122), channel_id=1, source_target_pairs={{0,56},{8,0},{16,8},{24,16},{32,24},{40,32},{48,40},{56,48},{1,57}... | collective-permute-start | bytes 393224 | tf_op jit(solution)/shard_map/ppermute | solution.py:27
  69.2 4.7 %collective-permute-start.12 = (f32[256,1152]{1,0:T(8,128)S(1)}, f32[256,1152]{1,0:T(8,128)S(1)}, u32[]{:S(2)}, u32[]{:S(2)}) collective-permute-start(f32[256,1152]{1,0:T(8,128)S(1)} %shard_map.87), channel_id=1, source_target_pairs={{0,1},{1,0},{2,3},{3,2},{4,5},{5,4},{6,7},{7,6},{8,9},{9,8},{10,11... | collective-permute-start | bytes 3538952 | tf_op jit(solution)/shard_map/ppermute | solution.py:22
  116.2 17.1 %copy-start = (bf16[56,1024]{1,0:T(8,128)(2,1)S(1)}, bf16[56,1024]{1,0:T(8,128)(2,1)}, u32[]{:S(2)}) copy-start(bf16[56,1024]{1,0:T(8,128)(2,1)} %up_probe.1) | copy-start | bytes 344068
  116.2 17.0 %copy-start.1 = (bf16[56,1024]{1,0:T(8,128)(2,1)S(1)}, bf16[56,1024]{1,0:T(8,128)(2,1)}, u32[]{:S(2)}) copy-start(bf16[56,1024]{1,0:T(8,128)(2,1)} %gate_probe.1) | copy-start | bytes 344068

commit v8 on v6

--- a/solution.py
+++ b/solution.py
@@ -15,6 +15,7 @@
 BACK_SCALE = 32.0
 
 VMEM = pl.BlockSpec(memory_space=pltpu.VMEM)
+ANY = pl.BlockSpec(memory_space=pl.ANY)
 SMEM = pl.BlockSpec(memory_space=pltpu.SMEM)
 
 
@@ -40,6 +41,25 @@
         interpret=interpret,
         **options,
     )(*args)
+
+
+def pass_kernel(value, *rest):
+    pass
+
+
+def after(value, others, interpret):
+    return local_call(
+        pass_kernel,
+        jax.ShapeDtypeStruct(value.shape, value.dtype),
+        0,
+        0,
+        interpret,
+        value,
+        *others,
+        in_specs=[ANY] * (1 + len(others)),
+        out_specs=ANY,
+        input_output_aliases={0: 0},
+    )
 
 
 def terms_kernel(tok_rows, place, tokens, cotangents, *refs):
@@ -137,7 +157,9 @@
 
     ahead = behind = block
     blocks = [block]
-    for _ in range(ny // 2 - 1):
+    for step in range(ny // 2 - 1):
+        if step == 1:
+            ahead = after(ahead, weights[1:3], interpret)
         ahead, behind = shift(ahead, "y", 1), shift(behind, "y", -1)
         blocks += [ahead, behind]
     blocks += [shift(ahead[:1], "y", 1), shift(behind[1:], "y", -1)]

time: 135 us -> 135 us (level)
  the two profiles are of different devices: /device:TPU:24 before, /device:TPU:1 now
where the time goes in v8:
time: 135 us; the launch traced here: 134 us
  starting transfers between devices  60.1 us (45%)
  blocking collectives  32.5 us (24%)
  waiting for transfers between devices  22.2 us (16%)
  local copies, waits for them, and re-layouts  9.49 us (7%)
  other arithmetic  4.65 us (3%)
  Pallas kernels  4.08 us (3%)
    ppermute x8, starting transfers between devices, shift(): lax.ppermute(value, axis, [(i, (i + by) % size) for i in range(size)])  27.3 us
    ppermute x2, starting transfers between devices, swap(): return lax.ppermute(value, axis, [(0, 1), (1, 0)])  18.9 us
    all_to_all x1, blocking collectives, on_device(): away = lax.all_to_all(away, 'x', 0, 0, tiled=True)  16.4 us
    all_gather x1, blocking collectives, on_device(): fac = lax.all_gather(fac, ('zl', 'c'), axis=1, tiled=True)  16.1 us
    all_to_all x1, waiting for transfers between devices, on_device(): got = lax.all_to_all(sent, 'zl', 0, 0, tiled=True)  15.4 us
    ppermute x3, starting transfers between devices, mix(): lax.ppermute(value, axis, [(i, i ^ by) for i in range(lax.axis_size(axis))])  9.6 us
    unnamed x16, local copies, waits for them, and re-layouts  7.84 us
    ppermute x8, waiting for transfers between devices, shift(): lax.ppermute(value, axis, [(i, (i + by) % size) for i in range(size)])  5.14 us
  transfers between devices with their start and end apart: 14, of which 4 were waited for; matrix products, arithmetic and copies ran while one was open for 7% of the time, Pallas kernels for 1%

profile of v8, /device:TPU:1, one launch (start us, length us, event | category | flops | bytes accessed | tf_op | source)
XLA Modules:
  0.0 133.9 jit_solution(1693790950875272216)
XLA Ops:
  0.6 0.9 pad_add_fusion.1
  1.5 11.5 %collective-permute-start = (bf16[64,1024]{1,0:T(8,128)(2,1)S(1)}, bf16[64,1024]{1,0:T(8,128)(2,1)S(1)}, u32[]{:S(2)}, u32[]{:S(2)}) collective-permute-start(bf16[64,1024]{1,0:T(8,128)(2,1)S(1)} %get-tuple-element.30), channel_id=1, source_target_pairs={{0,256},{256,0},{1,257},{257,1},{2,258},{258,2},{3,259},{259,3},{4... | collective-permute-start | bytes 393224 | tf_op jit(solution)/shard_map/ppermute | solution.py:23
  13.0 1.2 pad_add_fusion.refs_0_
  14.2 3.1 %collective-permute-start.3 = (bf16[288,1024]{1,0:T(8,128)(2,1)S(1)}, bf16[288,1024]{1,0:T(8,128)(2,1)S(1)}, u32[]{:S(2)}, u32[]{:S(2)}) collective-permute-start(bf16[288,1024]{1,0:T(8,128)(2,1)S(1)} %pad_add_fusion.refs_0_), channel_id=1, source_target_pairs={{0,64},{64,0},{128,192},{192,128},{1,65},{65,1},{129,193},{193,129... | collective-permute-start | bytes 1769480 | tf_op jit(solution)/shard_map/ppermute | solution.py:32
  17.3 3.7 %collective-permute-start.4 = (bf16[288,1024]{1,0:T(8,128)(2,1)S(1)}, bf16[288,1024]{1,0:T(8,128)(2,1)S(1)}, u32[]{:S(2)}, u32[]{:S(2)}) collective-permute-start(bf16[288,1024]{1,0:T(8,128)(2,1)S(1)} %pad_add_fusion.refs_0_), channel_id=1, source_target_pairs={{0,192},{64,128},{128,64},{192,0},{1,193},{65,129},{129,65},{193,1... | collective-permute-start | bytes 1769480 | tf_op jit(solution)/shard_map/ppermute | solution.py:32
  21.0 0.0 collective-permute-done
  21.1 5.1 %collective-permute-start.2 = (bf16[2,64,1024]{2,1,0:T(8,128)(2,1)S(1)}, bf16[2,64,1024]{2,1,0:T(8,128)(2,1)}, u32[]{:S(2)}, u32[]{:S(2)}) collective-permute-start(bf16[2,64,1024]{2,1,0:T(8,128)(2,1)S(1)} %pad_maximum_fusion), channel_id=1, source_target_pairs={{0,56},{8,0},{16,8},{24,16},{32,24},{40,32},{48,40},{56,48},{1,57}... | collective-permute-start | bytes 786440 | tf_op jit(solution)/shard_map/ppermute | solution.py:28
  26.2 1.9 %collective-permute-start.1 = (bf16[2,64,1024]{2,1,0:T(8,128)(2,1)S(1)}, bf16[2,64,1024]{2,1,0:T(8,128)(2,1)S(1)}, u32[]{:S(2)}, u32[]{:S(2)}) collective-permute-start(bf16[2,64,1024]{2,1,0:T(8,128)(2,1)S(1)} %pad_maximum_fusion), channel_id=1, source_target_pairs={{0,8},{8,16},{16,24},{24,32},{32,40},{40,48},{48,56},{56,0},{1,9},... | collective-permute-start | bytes 786440 | tf_op jit(solution)/shard_map/ppermute | solution.py:28
  28.1 0.7 fusion.10
  28.8 1.5 %collective-permute-done.2 = bf16[2,64,1024]{2,1,0:T(8,128)(2,1)} collective-permute-done((bf16[2,64,1024]{2,1,0:T(8,128)(2,1)S(1)}, bf16[2,64,1024]{2,1,0:T(8,128)(2,1)}, u32[]{:S(2)}, u32[]{:S(2)}) %collective-permute-start.2) | collective-permute-done | bytes 262176 | tf_op jit(solution)/shard_map/ppermute | solution.py:28
  30.2 5.4 %collective-permute-start.6 = (bf16[2,64,1024]{2,1,0:T(8,128)(2,1)}, bf16[2,64,1024]{2,1,0:T(8,128)(2,1)S(1)}, u32[]{:S(2)}, u32[]{:S(2)}) collective-permute-start(bf16[2,64,1024]{2,1,0:T(8,128)(2,1)} %collective-permute-done.2), channel_id=1, source_target_pairs={{0,56},{8,0},{16,8},{24,16},{32,24},{40,32},{48,40},{56,48},{1,57}... | collective-permute-start | bytes 786440 | tf_op jit(solution)/shard_map/ppermute | solution.py:28
  35.7 0.0 collective-permute-done.1.value
  35.7 0.7 slice_dynamic-update-slice_fusion.5
  36.3 0.0 collective-permute-done.3.rest_0_.refs_1_
  36.3 0.0 collective-permute-done.4.rest_1_.refs_2_
  36.3 1.9 %collective-permute-start.5 = (bf16[2,64,1024]{2,1,0:T(8,128)(2,1)S(1)}, bf16[2,64,1024]{2,1,0:T(8,128)(2,1)}, u32[]{:S(2)}, u32[]{:S(2)}) collective-permute-start(bf16[2,64,1024]{2,1,0:T(8,128)(2,1)S(1)} %shard_map.86), channel_id=1, source_target_pairs={{0,8},{8,16},{16,24},{24,32},{32,40},{40,48},{48,56},{56,0},{1,9},... | collective-permute-start | bytes 786440 | tf_op jit(solution)/shard_map/ppermute | solution.py:28
  38.3 1.6 %slice_dynamic-update-slice_fusion.4 = (bf16[16,32,1024]{2,1,0:T(8,128)(2,1)S(1)}, bf16[16,32,1024]{2,1,0:T(8,128)(2,1)}) fusion(bf16[16,32,1024]{2,1,0:T(8,128)(2,1)S(1)} %get-tuple-element.22, bf16[2,64,1024]{2,1,0:T(8,128)(2,1)} %collective-permute-done.2, bf16[16,32,1024]{2,1,0:T(8,128)(2,1)} %get-tuple-element.23), kind=kLoop, calls=%fused_computation.27 | loop fusion | bytes 524288
  39.9 2.8 %collective-permute-start.11 = (bf16[288,1024]{1,0:T(8,128)(2,1)S(1)}, bf16[288,1024]{1,0:T(8,128)(2,1)S(1)}, u32[]{:S(2)}, u32[]{:S(2)}) collective-permute-start(bf16[288,1024]{1,0:T(8,128)(2,1)S(1)} %collective-permute-done.3.rest_0_.refs_1_), channel_id=1, source_target_pairs={{0,192},{64,128},{128,64},{192,0},{1,193},{65,129},{129,65},{193,1... | collective-permute-start | bytes 1769480 | tf_op jit(solution)/shard_map/ppermute | solution.py:32
  42.7 0.0 collective-permute-done.6
  42.7 4.6 %collective-permute-start.8 = (bf16[2,64,1024]{2,1,0:T(8,128)(2,1)S(1)}, bf16[2,64,1024]{2,1,0:T(8,128)(2,1)S(1)}, u32[]{:S(2)}, u32[]{:S(2)}) collective-permute-start(bf16[2,64,1024]{2,1,0:T(8,128)(2,1)S(1)} %collective-permute-done.6), channel_id=1, source_target_pairs={{0,56},{8,0},{16,8},{24,16},{32,24},{40,32},{48,40},{56,48},{1,57}... | collective-permute-start | bytes 786440 | tf_op jit(solution)/shard_map/ppermute | solution.py:28
  47.3 0.0 collective-permute-done.5
  47.3 1.9 %collective-permute-start.7 = (bf16[2,64,1024]{2,1,0:T(8,128)(2,1)}, bf16[2,64,1024]{2,1,0:T(8,128)(2,1)S(1)}, u32[]{:S(2)}, u32[]{:S(2)}) collective-permute-start(bf16[2,64,1024]{2,1,0:T(8,128)(2,1)} %collective-permute-done.5), channel_id=1, source_target_pairs={{0,8},{8,16},{16,24},{24,32},{32,40},{40,48},{48,56},{56,0},{1,9},... | collective-permute-start | bytes 786440 | tf_op jit(solution)/shard_map/ppermute | solution.py:28
  49.2 1.6 %slice_dynamic-update-slice_fusion.3 = (bf16[16,32,1024]{2,1,0:T(8,128)(2,1)S(1)}, bf16[16,32,1024]{2,1,0:T(8,128)(2,1)}) fusion(bf16[16,32,1024]{2,1,0:T(8,128)(2,1)S(1)} %get-tuple-element.20, bf16[2,64,1024]{2,1,0:T(8,128)(2,1)} %collective-permute-done.5, bf16[16,32,1024]{2,1,0:T(8,128)(2,1)} %get-tuple-element.21), kind=kLoop, calls=%fused_computation.26 | loop fusion | bytes 524288
  50.8 0.7 slice_dynamic-update-slice_fusion.2
  51.5 0.0 collective-permute-done.8
  51.5 4.6 %collective-permute-start.10 = (bf16[1,64,1024]{2,1,0:T(8,128)(2,1)S(1)}, bf16[1,64,1024]{2,1,0:T(8,128)(2,1)S(1)}, u32[]{:S(2)}, u32[]{:S(2)}) collective-permute-start(bf16[1,64,1024]{2,1,0:T(8,128)(2,1)S(1)} %slice.122), channel_id=1, source_target_pairs={{0,56},{8,0},{16,8},{24,16},{32,24},{40,32},{48,40},{56,48},{1,57}... | collective-permute-start | bytes 393224 | tf_op jit(solution)/shard_map/ppermute | solution.py:28
  56.1 0.0 collective-permute-done.7
  56.2 1.9 %collective-permute-start.9 = (bf16[1,64,1024]{2,1,0:T(8,128)(2,1)S(1)}, bf16[1,64,1024]{2,1,0:T(8,128)(2,1)S(1)}, u32[]{:S(2)}, u32[]{:S(2)}) collective-permute-start(bf16[1,64,1024]{2,1,0:T(8,128)(2,1)S(1)} %slice.120), channel_id=1, source_target_pairs={{0,8},{8,16},{16,24},{24,32},{32,40},{40,48},{48,56},{56,0},{1,9},... | collective-permute-start | bytes 393224 | tf_op jit(solution)/shard_map/ppermute | solution.py:28
  58.1 0.7 slice_dynamic-update-slice_fusion.1
  58.7 0.7 slice_dynamic-update-slice_fusion
  59.4 3.7 %collective-permute-done.9 = bf16[1,64,1024]{2,1,0:T(8,128)(2,1)S(1)} collective-permute-done((bf16[1,64,1024]{2,1,0:T(8,128)(2,1)S(1)}, bf16[1,64,1024]{2,1,0:T(8,128)(2,1)S(1)}, u32[]{:S(2)}, u32[]{:S(2)}) %collective-permute-start.9) | collective-permute-done | bytes 131104 | tf_op jit(solution)/shard_map/ppermute | solution.py:28
  63.1 0.6 slice_dynamic-update-slice_fusion.13
  63.7 0.0 collective-permute-done.10
  63.7 0.6 slice_dynamic-update-slice_fusion.12
  64.3 0.0 collective-permute-done.11.refs_3_
  64.3 0.0 copy-start
  64.3 1.2 copy-done
  65.6 0.9 shard_map.88
  66.4 7.4 %collective-permute-start.12 = (f32[256,1152]{1,0:T(8,128)S(1)}, f32[256,1152]{1,0:T(8,128)S(1)}, u32[]{:S(2)}, u32[]{:S(2)}) collective-permute-start(f32[256,1152]{1,0:T(8,128)S(1)} %shard_map.88), channel_id=1, source_target_pairs={{0,1},{1,0},{2,3},{3,2},{4,5},{5,4},{6,7},{7,6},{8,9},{9,8},{10,11... | collective-permute-start | bytes 3538952 | tf_op jit(solution)/shard_map/ppermute | solution.py:23
  73.9 0.9 shard_map.87
  74.8 1.6 %collective-permute-done.12 = f32[256,1152]{1,0:T(8,128)S(1)} collective-permute-done((f32[256,1152]{1,0:T(8,128)S(1)}, f32[256,1152]{1,0:T(8,128)S(1)}, u32[]{:S(2)}, u32[]{:S(2)}) %collective-permute-start.12) | collective-permute-done | bytes 1179680 | tf_op jit(solution)/shard_map/ppermute | solution.py:23
  76.3 0.9 add_convert_fusion
  77.3 4.3 %all-to-all-start = ((f16[4,64,1152]{2,1,0:T(8,128)(2,1)}), f16[4,64,1152]{2,1,0:T(8,128)(2,1)S(1)}, u32[]{:S(2)}, u32[]{:S(2)}) async-start(f16[4,64,1152]{2,1,0:T(8,128)(2,1)} %bitcast.7), calls=%async_computation | async-start | bytes 1179648 | tf_op jit(solution)/shard_map/all_to_all | solution.py:191
  81.6 15.4 %all-to-all-done = f16[4,64,1152]{2,1,0:T(8,128)(2,1)S(1)} async-done(((f16[4,64,1152]{2,1,0:T(8,128)(2,1)}), f16[4,64,1152]{2,1,0:T(8,128)(2,1)S(1)}, u32[]{:S(2)}, u32[]{:S(2)}) %all-to-all-start) | async-done | bytes 589856 | tf_op jit(solution)/shard_map/all_to_all | solution.py:191
  97.0 0.1 convert_reduce_fusion
  97.1 0.9 reshape.47
  98.0 0.1 reshape.46
  98.1 0.5 fusion.17
  98.6 0.0 copy-start.1
  98.6 0.3 fusion.15
  98.9 0.2 pad_maximum_fusion.1
  99.1 16.1 %all_gather.3.fac = bf16[64,4096]{1,0:T(8,128)(2,1)S(1)} all-gather(bf16[64,512]{1,0:T(8,128)(2,1)S(1)} %bitcast.66), channel_id=1, replica_groups=mesh['zh'=2,'x'=4,'y'=8,'zl'=4,'c'=2] {'zl','c'}, dimensions={1}, use_global_device_ids=true | all-gather | bytes 589824 | tf_op jit(solution)/shard_map/all_gather | solution.py:202
  115.1 0.0 copy-done.1
  115.1 1.4 %shard_map.89 = (bf16[4,112,1024]{2,1,0:T(8,128)(2,1)S(1)}, f32[112,1024]{1,0:T(8,128)S(1)}) custom-call(s32[1]{0:T(128)} %bitcast.place, bf16[64,4096]{1,0:T(8,128)(2,1)S(1)} %all_gather.3.fac, bf16[512,1024]{1,0:T(8,128)(2,1)S(1)} %bitcast.57), custom_call_target="tpu_custom_call" | custom-call | flops 469762048 | bytes 1048576 | tf_op jit(solution)/shard_map/pallas_call | solution.py:36
  116.6 0.0 copy-start.2
  116.6 0.0 copy-start.3
  116.6 16.4 %all_to_all.10.away = bf16[4,112,1024]{2,1,0:T(8,128)(2,1)S(1)} all-to-all(bf16[4,112,1024]{2,1,0:T(8,128)(2,1)S(1)} %get-tuple-element.4), channel_id=1, replica_groups=mesh['zh'=2,'x'=4,'y'=8,'zl'=4,'c'=2] {'x'}, dimensions={0} | all-to-all | bytes 1835008 | tf_op jit(solution)/shard_map/all_to_all | solution.py:219
  133.0 0.0 copy-done.2
  133.0 0.0 copy-done.3
  133.0 0.9 shard_map.90
  (8 shorter events, 0.1 us)
Async XLA Ops:
  1.5 19.5 %collective-permute-start = (bf16[64,1024]{1,0:T(8,128)(2,1)S(1)}, bf16[64,1024]{1,0:T(8,128)(2,1)S(1)}, u32[]{:S(2)}, u32[]{:S(2)}) collective-permute-start(bf16[64,1024]{1,0:T(8,128)(2,1)S(1)} %get-tuple-element.30), channel_id=1, source_target_pairs={{0,256},{256,0},{1,257},{257,1},{2,258},{258,2},{3,259},{259,3},{4... | collective-permute-start | bytes 393224 | tf_op jit(solution)/shard_map/ppermute | solution.py:23
  14.2 22.2 %collective-permute-start.3 = (bf16[288,1024]{1,0:T(8,128)(2,1)S(1)}, bf16[288,1024]{1,0:T(8,128)(2,1)S(1)}, u32[]{:S(2)}, u32[]{:S(2)}) collective-permute-start(bf16[288,1024]{1,0:T(8,128)(2,1)S(1)} %pad_add_fusion.refs_0_), channel_id=1, source_target_pairs={{0,64},{64,0},{128,192},{192,128},{1,65},{65,1},{129,193},{193,129... | collective-permute-start | bytes 1769480 | tf_op jit(solution)/shard_map/ppermute | solution.py:32
  17.3 19.0 %collective-permute-start.4 = (bf16[288,1024]{1,0:T(8,128)(2,1)S(1)}, bf16[288,1024]{1,0:T(8,128)(2,1)S(1)}, u32[]{:S(2)}, u32[]{:S(2)}) collective-permute-start(bf16[288,1024]{1,0:T(8,128)(2,1)S(1)} %pad_add_fusion.refs_0_), channel_id=1, source_target_pairs={{0,192},{64,128},{128,64},{192,0},{1,193},{65,129},{129,65},{193,1... | collective-permute-start | bytes 1769480 | tf_op jit(solution)/shard_map/ppermute | solution.py:32
  21.1 9.2 %collective-permute-start.2 = (bf16[2,64,1024]{2,1,0:T(8,128)(2,1)S(1)}, bf16[2,64,1024]{2,1,0:T(8,128)(2,1)}, u32[]{:S(2)}, u32[]{:S(2)}) collective-permute-start(bf16[2,64,1024]{2,1,0:T(8,128)(2,1)S(1)} %pad_maximum_fusion), channel_id=1, source_target_pairs={{0,56},{8,0},{16,8},{24,16},{32,24},{40,32},{48,40},{56,48},{1,57}... | collective-permute-start | bytes 786440 | tf_op jit(solution)/shard_map/ppermute | solution.py:28
  26.2 9.5 %collective-permute-start.1 = (bf16[2,64,1024]{2,1,0:T(8,128)(2,1)S(1)}, bf16[2,64,1024]{2,1,0:T(8,128)(2,1)S(1)}, u32[]{:S(2)}, u32[]{:S(2)}) collective-permute-start(bf16[2,64,1024]{2,1,0:T(8,128)(2,1)S(1)} %pad_maximum_fusion), channel_id=1, source_target_pairs={{0,8},{8,16},{16,24},{24,32},{32,40},{40,48},{48,56},{56,0},{1,9},... | collective-permute-start | bytes 786440 | tf_op jit(solution)/shard_map/ppermute | solution.py:28
  30.2 12.4 %collective-permute-start.6 = (bf16[2,64,1024]{2,1,0:T(8,128)(2,1)}, bf16[2,64,1024]{2,1,0:T(8,128)(2,1)S(1)}, u32[]{:S(2)}, u32[]{:S(2)}) collective-permute-start(bf16[2,64,1024]{2,1,0:T(8,128)(2,1)} %collective-permute-done.2), channel_id=1, source_target_pairs={{0,56},{8,0},{16,8},{24,16},{32,24},{40,32},{48,40},{56,48},{1,57}... | collective-permute-start | bytes 786440 | tf_op jit(solution)/shard_map/ppermute | solution.py:28
  36.3 10.9 %collective-permute-start.5 = (bf16[2,64,1024]{2,1,0:T(8,128)(2,1)S(1)}, bf16[2,64,1024]{2,1,0:T(8,128)(2,1)}, u32[]{:S(2)}, u32[]{:S(2)}) collective-permute-start(bf16[2,64,1024]{2,1,0:T(8,128)(2,1)S(1)} %shard_map.86), channel_id=1, source_target_pairs={{0,8},{8,16},{16,24},{24,32},{32,40},{40,48},{48,56},{56,0},{1,9},... | collective-permute-start | bytes 786440 | tf_op jit(solution)/shard_map/ppermute | solution.py:28
  39.9 24.4 %collective-permute-start.11 = (bf16[288,1024]{1,0:T(8,128)(2,1)S(1)}, bf16[288,1024]{1,0:T(8,128)(2,1)S(1)}, u32[]{:S(2)}, u32[]{:S(2)}) collective-permute-start(bf16[288,1024]{1,0:T(8,128)(2,1)S(1)} %collective-permute-done.3.rest_0_.refs_1_), channel_id=1, source_target_pairs={{0,192},{64,128},{128,64},{192,0},{1,193},{65,129},{129,65},{193,1... | collective-permute-start | bytes 1769480 | tf_op jit(solution)/shard_map/ppermute | solution.py:32
  42.7 8.8 %collective-permute-start.8 = (bf16[2,64,1024]{2,1,0:T(8,128)(2,1)S(1)}, bf16[2,64,1024]{2,1,0:T(8,128)(2,1)S(1)}, u32[]{:S(2)}, u32[]{:S(2)}) collective-permute-start(bf16[2,64,1024]{2,1,0:T(8,128)(2,1)S(1)} %collective-permute-done.6), channel_id=1, source_target_pairs={{0,56},{8,0},{16,8},{24,16},{32,24},{40,32},{48,40},{56,48},{1,57}... | collective-permute-start | bytes 786440 | tf_op jit(solution)/shard_map/ppermute | solution.py:28
  47.3 8.9 %collective-permute-start.7 = (bf16[2,64,1024]{2,1,0:T(8,128)(2,1)}, bf16[2,64,1024]{2,1,0:T(8,128)(2,1)S(1)}, u32[]{:S(2)}, u32[]{:S(2)}) collective-permute-start(bf16[2,64,1024]{2,1,0:T(8,128)(2,1)} %collective-permute-done.5), channel_id=1, source_target_pairs={{0,8},{8,16},{16,24},{24,32},{32,40},{40,48},{48,56},{56,0},{1,9},... | collective-permute-start | bytes 786440 | tf_op jit(solution)/shard_map/ppermute | solution.py:28
  51.5 12.2 %collective-permute-start.10 = (bf16[1,64,1024]{2,1,0:T(8,128)(2,1)S(1)}, bf16[1,64,1024]{2,1,0:T(8,128)(2,1)S(1)}, u32[]{:S(2)}, u32[]{:S(2)}) collective-permute-start(bf16[1,64,1024]{2,1,0:T(8,128)(2,1)S(1)} %slice.122), channel_id=1, source_target_pairs={{0,56},{8,0},{16,8},{24,16},{32,24},{40,32},{48,40},{56,48},{1,57}... | collective-permute-start | bytes 393224 | tf_op jit(solution)/shard_map/ppermute | solution.py:28
  56.2 6.9 %collective-permute-start.9 = (bf16[1,64,1024]{2,1,0:T(8,128)(2,1)S(1)}, bf16[1,64,1024]{2,1,0:T(8,128)(2,1)S(1)}, u32[]{:S(2)}, u32[]{:S(2)}) collective-permute-start(bf16[1,64,1024]{2,1,0:T(8,128)(2,1)S(1)} %slice.120), channel_id=1, source_target_pairs={{0,8},{8,16},{16,24},{24,32},{32,40},{40,48},{48,56},{56,0},{1,9},... | collective-permute-start | bytes 393224 | tf_op jit(solution)/shard_map/ppermute | solution.py:28
  64.3 1.2 copy-start
  66.4 9.9 %collective-permute-start.12 = (f32[256,1152]{1,0:T(8,128)S(1)}, f32[256,1152]{1,0:T(8,128)S(1)}, u32[]{:S(2)}, u32[]{:S(2)}) collective-permute-start(f32[256,1152]{1,0:T(8,128)S(1)} %shard_map.88), channel_id=1, source_target_pairs={{0,1},{1,0},{2,3},{3,2},{4,5},{5,4},{6,7},{7,6},{8,9},{9,8},{10,11... | collective-permute-start | bytes 3538952 | tf_op jit(solution)/shard_map/ppermute | solution.py:23
  77.3 19.7 %all-to-all-start = ((f16[4,64,1152]{2,1,0:T(8,128)(2,1)}), f16[4,64,1152]{2,1,0:T(8,128)(2,1)S(1)}, u32[]{:S(2)}, u32[]{:S(2)}) async-start(f16[4,64,1152]{2,1,0:T(8,128)(2,1)} %bitcast.7), calls=%async_computation | async-start | bytes 1179648 | tf_op jit(solution)/shard_map/all_to_all | solution.py:191
  98.6 16.5 %copy-start.1 = (bf16[16,32,1024]{2,1,0:T(8,128)(2,1)S(1)}, bf16[16,32,1024]{2,1,0:T(8,128)(2,1)}, u32[]{:S(2)}) copy-start(bf16[16,32,1024]{2,1,0:T(8,128)(2,1)} %get-tuple-element.27) | copy-start | bytes 3145732
  116.6 16.4 %copy-start.2 = (bf16[56,1024]{1,0:T(8,128)(2,1)S(1)}, bf16[56,1024]{1,0:T(8,128)(2,1)}, u32[]{:S(2)}) copy-start(bf16[56,1024]{1,0:T(8,128)(2,1)} %up_probe.1) | copy-start | bytes 344068
  116.6 16.4 %copy-start.3 = (bf16[56,1024]{1,0:T(8,128)(2,1)S(1)}, bf16[56,1024]{1,0:T(8,128)(2,1)}, u32[]{:S(2)}) copy-start(bf16[56,1024]{1,0:T(8,128)(2,1)} %gate_probe.1) | copy-start | bytes 344068

commit v9 on v8

--- a/solution.py
+++ b/solution.py
@@ -159,7 +159,7 @@
     blocks = [block]
     for step in range(ny // 2 - 1):
         if step == 1:
-            ahead = after(ahead, weights[1:3], interpret)
+            ahead = after(ahead, weights[2:3], interpret)
         ahead, behind = shift(ahead, "y", 1), shift(behind, "y", -1)
         blocks += [ahead, behind]
     blocks += [shift(ahead[:1], "y", 1), shift(behind[1:], "y", -1)]

time: 135 us -> 135 us (level)
  local copies, waits for them, and re-layouts: 9.49 us -> 4.11 us
  waiting for transfers between devices: 22.2 us -> 25.8 us
  Pallas kernels: 4.08 us -> 6.22 us
    unnamed x16 -> x12, local copies, waits for them, and re-layouts: 7.84 us -> 3.07 us
    ppermute x3, waiting for transfers between devices: 0.01 us -> 4.49 us  [mix(): lax.ppermute(value, axis, [(i, i ^ by) for i in range(lax.axis_size(axis))])]
    all_to_all x1, starting transfers between devices: 4.28 us -> 6.83 us  [on_device(): got = lax.all_to_all(sent, 'zl', 0, 0, tiled=True)]
    pallas_call x5, Pallas kernels: 4.08 us -> 6.22 us  [local_call(): pl.pallas_call(body, out_shape=out_shape, cost_estimate=pl.CostEstimate(f...]
  transfers between devices with their start and end apart: 14 -> 14, of which waited for: 4 -> 5; matrix products, arithmetic and copies ran while one was open for 7% -> 3% of each run, Pallas kernels for 1% -> 1%
where the time goes in v9:
time: 135 us
  starting transfers between devices  61.3 us (45%)
  blocking collectives  32 us (24%)
  waiting for transfers between devices  25.8 us (19%)
  Pallas kernels  6.22 us (5%)
  local copies, waits for them, and re-layouts  4.11 us (3%)
  other arithmetic  4.05 us (3%)
    ppermute x8, starting transfers between devices, shift(): lax.ppermute(value, axis, [(i, (i + by) % size) for i in range(size)])  27.4 us
    ppermute x2, starting transfers between devices, swap(): return lax.ppermute(value, axis, [(0, 1), (1, 0)])  18.7 us
    all_gather x1, blocking collectives, on_device(): fac = lax.all_gather(fac, ('zl', 'c'), axis=1, tiled=True)  16.1 us
    all_to_all x1, blocking collectives, on_device(): away = lax.all_to_all(away, 'x', 0, 0, tiled=True)  16 us
    all_to_all x1, waiting for transfers between devices, on_device(): got = lax.all_to_all(sent, 'zl', 0, 0, tiled=True)  15.4 us
    ppermute x3, starting transfers between devices, mix(): lax.ppermute(value, axis, [(i, i ^ by) for i in range(lax.axis_size(axis))])  8.4 us
    all_to_all x1, starting transfers between devices, on_device(): got = lax.all_to_all(sent, 'zl', 0, 0, tiled=True)  6.83 us
    pallas_call x5, Pallas kernels, local_call(): pl.pallas_call(body, out_shape=out_shape, cost_estimate=pl.CostEstimate(f...  6.22 us
  transfers between devices with their start and end apart: 14, of which 5 were waited for; matrix products, arithmetic and copies ran while one was open for 3% of the time, Pallas kernels for 1%

profile of v9, /device:TPU:1, one launch (start us, length us, event | category | flops | bytes accessed | tf_op | source)
XLA Modules:
  0.0 134.5 jit_solution(10276033840300195886)
XLA Ops:
  0.6 0.9 pad_add_fusion.1
  1.5 11.5 %collective-permute-start = (bf16[64,1024]{1,0:T(8,128)(2,1)S(1)}, bf16[64,1024]{1,0:T(8,128)(2,1)S(1)}, u32[]{:S(2)}, u32[]{:S(2)}) collective-permute-start(bf16[64,1024]{1,0:T(8,128)(2,1)S(1)} %get-tuple-element.30), channel_id=1, source_target_pairs={{0,256},{256,0},{1,257},{257,1},{2,258},{258,2},{3,259},{259,3},{4... | collective-permute-start | bytes 393224 | tf_op jit(solution)/shard_map/ppermute | solution.py:23
  13.0 1.2 pad_add_fusion.refs_0_
  14.2 4.4 %collective-permute-start.3 = (bf16[288,1024]{1,0:T(8,128)(2,1)S(1)}, bf16[288,1024]{1,0:T(8,128)(2,1)S(1)}, u32[]{:S(2)}, u32[]{:S(2)}) collective-permute-start(bf16[288,1024]{1,0:T(8,128)(2,1)S(1)} %pad_add_fusion.refs_0_), channel_id=1, source_target_pairs={{0,192},{64,128},{128,64},{192,0},{1,193},{65,129},{129,65},{193,1... | collective-permute-start | bytes 1769480 | tf_op jit(solution)/shard_map/ppermute | solution.py:32
  18.6 0.0 collective-permute-done
  18.6 5.1 %collective-permute-start.2 = (bf16[2,64,1024]{2,1,0:T(8,128)(2,1)S(1)}, bf16[2,64,1024]{2,1,0:T(8,128)(2,1)}, u32[]{:S(2)}, u32[]{:S(2)}) collective-permute-start(bf16[2,64,1024]{2,1,0:T(8,128)(2,1)S(1)} %pad_maximum_fusion), channel_id=1, source_target_pairs={{0,56},{8,0},{16,8},{24,16},{32,24},{40,32},{48,40},{56,48},{1,57}... | collective-permute-start | bytes 786440 | tf_op jit(solution)/shard_map/ppermute | solution.py:28
  23.7 1.9 %collective-permute-start.1 = (bf16[2,64,1024]{2,1,0:T(8,128)(2,1)S(1)}, bf16[2,64,1024]{2,1,0:T(8,128)(2,1)S(1)}, u32[]{:S(2)}, u32[]{:S(2)}) collective-permute-start(bf16[2,64,1024]{2,1,0:T(8,128)(2,1)S(1)} %pad_maximum_fusion), channel_id=1, source_target_pairs={{0,8},{8,16},{16,24},{24,32},{32,40},{40,48},{48,56},{56,0},{1,9},... | collective-permute-start | bytes 786440 | tf_op jit(solution)/shard_map/ppermute | solution.py:28
  25.6 1.9 %collective-permute-start.10 = (bf16[288,1024]{1,0:T(8,128)(2,1)S(1)}, bf16[288,1024]{1,0:T(8,128)(2,1)}, u32[]{:S(2)}, u32[]{:S(2)}) collective-permute-start(bf16[288,1024]{1,0:T(8,128)(2,1)S(1)} %pad_add_fusion.refs_0_), channel_id=1, source_target_pairs={{0,64},{64,0},{128,192},{192,128},{1,65},{65,1},{129,193},{193,129... | collective-permute-start | bytes 1769480 | tf_op jit(solution)/shard_map/ppermute | solution.py:32
  27.6 0.5 collective-permute-done.2
  28.1 5.4 %collective-permute-start.5 = (bf16[2,64,1024]{2,1,0:T(8,128)(2,1)}, bf16[2,64,1024]{2,1,0:T(8,128)(2,1)}, u32[]{:S(2)}, u32[]{:S(2)}) collective-permute-start(bf16[2,64,1024]{2,1,0:T(8,128)(2,1)} %collective-permute-done.2), channel_id=1, source_target_pairs={{0,56},{8,0},{16,8},{24,16},{32,24},{40,32},{48,40},{56,48},{1,57}... | collective-permute-start | bytes 786440 | tf_op jit(solution)/shard_map/ppermute | solution.py:28
  33.5 0.0 collective-permute-done.1.value
  33.5 0.0 collective-permute-done.3.rest_0_.refs_2_
  33.5 1.9 %collective-permute-start.4 = (bf16[2,64,1024]{2,1,0:T(8,128)(2,1)S(1)}, bf16[2,64,1024]{2,1,0:T(8,128)(2,1)}, u32[]{:S(2)}, u32[]{:S(2)}) collective-permute-start(bf16[2,64,1024]{2,1,0:T(8,128)(2,1)S(1)} %shard_map.86), channel_id=1, source_target_pairs={{0,8},{8,16},{16,24},{24,32},{32,40},{40,48},{48,56},{56,0},{1,9},... | collective-permute-start | bytes 786440 | tf_op jit(solution)/shard_map/ppermute | solution.py:28
  35.5 1.0 slice_dynamic-update-slice_fusion.4
  36.5 4.5 %collective-permute-done.10.refs_1_ = bf16[288,1024]{1,0:T(8,128)(2,1)} collective-permute-done((bf16[288,1024]{1,0:T(8,128)(2,1)S(1)}, bf16[288,1024]{1,0:T(8,128)(2,1)}, u32[]{:S(2)}, u32[]{:S(2)}) %collective-permute-start.10) | collective-permute-done | bytes 589856 | tf_op jit(solution)/shard_map/ppermute | solution.py:32
  40.9 2.1 %collective-permute-start.11 = (bf16[288,1024]{1,0:T(8,128)(2,1)}, bf16[288,1024]{1,0:T(8,128)(2,1)S(1)}, u32[]{:S(2)}, u32[]{:S(2)}) collective-permute-start(bf16[288,1024]{1,0:T(8,128)(2,1)} %collective-permute-done.10.refs_1_), channel_id=1, source_target_pairs={{0,192},{64,128},{128,64},{192,0},{1,193},{65,129},{129,65},{193,1... | collective-permute-start | bytes 1769480 | tf_op jit(solution)/shard_map/ppermute | solution.py:32
  43.0 0.0 collective-permute-done.5
  43.1 4.3 %collective-permute-start.7 = (bf16[2,64,1024]{2,1,0:T(8,128)(2,1)}, bf16[2,64,1024]{2,1,0:T(8,128)(2,1)S(1)}, u32[]{:S(2)}, u32[]{:S(2)}) collective-permute-start(bf16[2,64,1024]{2,1,0:T(8,128)(2,1)} %collective-permute-done.5), channel_id=1, source_target_pairs={{0,56},{8,0},{16,8},{24,16},{32,24},{40,32},{48,40},{56,48},{1,57}... | collective-permute-start | bytes 786440 | tf_op jit(solution)/shard_map/ppermute | solution.py:28
  47.4 0.0 collective-permute-done.4
  47.4 1.9 %collective-permute-start.6 = (bf16[2,64,1024]{2,1,0:T(8,128)(2,1)}, bf16[2,64,1024]{2,1,0:T(8,128)(2,1)S(1)}, u32[]{:S(2)}, u32[]{:S(2)}) collective-permute-start(bf16[2,64,1024]{2,1,0:T(8,128)(2,1)} %collective-permute-done.4), channel_id=1, source_target_pairs={{0,8},{8,16},{16,24},{24,32},{32,40},{40,48},{48,56},{56,0},{1,9},... | collective-permute-start | bytes 786440 | tf_op jit(solution)/shard_map/ppermute | solution.py:28
  49.3 1.0 slice_dynamic-update-slice_fusion.3
  50.3 1.0 slice_dynamic-update-slice_fusion.2
  51.3 0.0 collective-permute-done.7
  51.3 4.9 %collective-permute-start.9 = (bf16[1,64,1024]{2,1,0:T(8,128)(2,1)S(1)}, bf16[1,64,1024]{2,1,0:T(8,128)(2,1)S(1)}, u32[]{:S(2)}, u32[]{:S(2)}) collective-permute-start(bf16[1,64,1024]{2,1,0:T(8,128)(2,1)S(1)} %slice.122), channel_id=1, source_target_pairs={{0,56},{8,0},{16,8},{24,16},{32,24},{40,32},{48,40},{56,48},{1,57}... | collective-permute-start | bytes 393224 | tf_op jit(solution)/shard_map/ppermute | solution.py:28
  56.2 0.0 collective-permute-done.6
  56.2 1.9 %collective-permute-start.8 = (bf16[1,64,1024]{2,1,0:T(8,128)(2,1)S(1)}, bf16[1,64,1024]{2,1,0:T(8,128)(2,1)S(1)}, u32[]{:S(2)}, u32[]{:S(2)}) collective-permute-start(bf16[1,64,1024]{2,1,0:T(8,128)(2,1)S(1)} %slice.120), channel_id=1, source_target_pairs={{0,8},{8,16},{16,24},{24,32},{32,40},{40,48},{48,56},{56,0},{1,9},... | collective-permute-start | bytes 393224 | tf_op jit(solution)/shard_map/ppermute | solution.py:28
  58.2 4.9 %collective-permute-done.8 = bf16[1,64,1024]{2,1,0:T(8,128)(2,1)S(1)} collective-permute-done((bf16[1,64,1024]{2,1,0:T(8,128)(2,1)S(1)}, bf16[1,64,1024]{2,1,0:T(8,128)(2,1)S(1)}, u32[]{:S(2)}, u32[]{:S(2)}) %collective-permute-start.8) | collective-permute-done | bytes 131104 | tf_op jit(solution)/shard_map/ppermute | solution.py:28
  63.2 0.0 collective-permute-done.9
  63.2 0.0 collective-permute-done.11.refs_3_
  63.2 1.9 %shard_map.88 = f32[256,1152]{1,0:T(8,128)S(1)} custom-call(s32[1]{0:T(128)} %bitcast.6.place, bf16[512,1024]{1,0:T(8,128)(2,1)S(1)} %bitcast.55, bf16[512,1024]{1,0:T(8,128)(2,1)S(1)} %bitcast.53, bf16[288,1024]{1,0:T(8,128)(2,1)S(1)} %pad_add_fusion.refs_0_, bf16[288,1024]{1,0:T(8,128)(2,1)} %collective-permute-done.10.refs_1_, ...), custom_call_target="tpu_custom_call" | custom-call | flops 603979776 | bytes 2359296 | tf_op jit(solution)/shard_map/pallas_call | solution.py:36
  65.2 7.2 %collective-permute-start.12 = (f32[256,1152]{1,0:T(8,128)S(1)}, f32[256,1152]{1,0:T(8,128)S(1)}, u32[]{:S(2)}, u32[]{:S(2)}) collective-permute-start(f32[256,1152]{1,0:T(8,128)S(1)} %shard_map.88), channel_id=1, source_target_pairs={{0,1},{1,0},{2,3},{3,2},{4,5},{5,4},{6,7},{7,6},{8,9},{9,8},{10,11... | collective-permute-start | bytes 3538952 | tf_op jit(solution)/shard_map/ppermute | solution.py:23
  72.4 1.9 %shard_map.87 = f32[256,1152]{1,0:T(8,128)S(1)} custom-call(s32[1]{0:T(128)} %bitcast.1.place, bf16[512,1024]{1,0:T(8,128)(2,1)S(1)} %bitcast.56, bf16[512,1024]{1,0:T(8,128)(2,1)S(1)} %bitcast.54, bf16[288,1024]{1,0:T(8,128)(2,1)S(1)} %pad_add_fusion.refs_0_, bf16[288,1024]{1,0:T(8,128)(2,1)} %collective-permute-done.10.refs_1_, ...), custom_call_target="tpu_custom_call" | custom-call | flops 603979776 | bytes 2359296 | tf_op jit(solution)/shard_map/pallas_call | solution.py:36
  74.3 0.5 collective-permute-done.12
  74.8 1.0 add_convert_fusion
  75.8 6.8 %all-to-all-start = ((f16[4,64,1152]{2,1,0:T(8,128)(2,1)}), f16[4,64,1152]{2,1,0:T(8,128)(2,1)S(1)}, u32[]{:S(2)}, u32[]{:S(2)}) async-start(f16[4,64,1152]{2,1,0:T(8,128)(2,1)} %bitcast.7), calls=%async_computation | async-start | bytes 1179648 | tf_op jit(solution)/shard_map/all_to_all | solution.py:191
  82.6 15.4 %all-to-all-done = f16[4,64,1152]{2,1,0:T(8,128)(2,1)S(1)} async-done(((f16[4,64,1152]{2,1,0:T(8,128)(2,1)}), f16[4,64,1152]{2,1,0:T(8,128)(2,1)S(1)}, u32[]{:S(2)}, u32[]{:S(2)}) %all-to-all-start) | async-done | bytes 589856 | tf_op jit(solution)/shard_map/all_to_all | solution.py:191
  98.1 0.1 convert_reduce_fusion
  98.2 0.9 reshape.47
  99.1 0.1 reshape.46
  99.2 0.5 fusion.17
  99.7 0.3 fusion.15
  99.9 0.2 pad_maximum_fusion.1
  100.1 16.1 %all_gather.3.fac = bf16[64,4096]{1,0:T(8,128)(2,1)S(1)} all-gather(bf16[64,512]{1,0:T(8,128)(2,1)S(1)} %bitcast.66), channel_id=1, replica_groups=mesh['zh'=2,'x'=4,'y'=8,'zl'=4,'c'=2] {'zl','c'}, dimensions={1}, use_global_device_ids=true | all-gather | bytes 589824 | tf_op jit(solution)/shard_map/all_gather | solution.py:202
  116.2 1.4 %shard_map.89 = (bf16[4,112,1024]{2,1,0:T(8,128)(2,1)S(1)}, f32[112,1024]{1,0:T(8,128)S(1)}) custom-call(s32[1]{0:T(128)} %bitcast.place, bf16[64,4096]{1,0:T(8,128)(2,1)S(1)} %all_gather.3.fac, bf16[512,1024]{1,0:T(8,128)(2,1)S(1)} %bitcast.57), custom_call_target="tpu_custom_call" | custom-call | flops 469762048 | bytes 1048576 | tf_op jit(solution)/shard_map/pallas_call | solution.py:36
  117.6 0.0 copy-start
  117.6 0.0 copy-start.1
  117.7 16.0 %all_to_all.10.away = bf16[4,112,1024]{2,1,0:T(8,128)(2,1)S(1)} all-to-all(bf16[4,112,1024]{2,1,0:T(8,128)(2,1)S(1)} %get-tuple-element.4), channel_id=1, replica_groups=mesh['zh'=2,'x'=4,'y'=8,'zl'=4,'c'=2] {'x'}, dimensions={0} | all-to-all | bytes 1835008 | tf_op jit(solution)/shard_map/all_to_all | solution.py:219
  133.6 0.0 copy-done
  133.6 0.0 copy-done.1
  133.6 0.9 shard_map.90
  (14 shorter events, 0.2 us)
Async XLA Ops:
  1.5 17.0 %collective-permute-start = (bf16[64,1024]{1,0:T(8,128)(2,1)S(1)}, bf16[64,1024]{1,0:T(8,128)(2,1)S(1)}, u32[]{:S(2)}, u32[]{:S(2)}) collective-permute-start(bf16[64,1024]{1,0:T(8,128)(2,1)S(1)} %get-tuple-element.30), channel_id=1, source_target_pairs={{0,256},{256,0},{1,257},{257,1},{2,258},{258,2},{3,259},{259,3},{4... | collective-permute-start | bytes 393224 | tf_op jit(solution)/shard_map/ppermute | solution.py:23
  14.2 19.3 %collective-permute-start.3 = (bf16[288,1024]{1,0:T(8,128)(2,1)S(1)}, bf16[288,1024]{1,0:T(8,128)(2,1)S(1)}, u32[]{:S(2)}, u32[]{:S(2)}) collective-permute-start(bf16[288,1024]{1,0:T(8,128)(2,1)S(1)} %pad_add_fusion.refs_0_), channel_id=1, source_target_pairs={{0,192},{64,128},{128,64},{192,0},{1,193},{65,129},{129,65},{193,1... | collective-permute-start | bytes 1769480 | tf_op jit(solution)/shard_map/ppermute | solution.py:32
  18.6 9.4 %collective-permute-start.2 = (bf16[2,64,1024]{2,1,0:T(8,128)(2,1)S(1)}, bf16[2,64,1024]{2,1,0:T(8,128)(2,1)}, u32[]{:S(2)}, u32[]{:S(2)}) collective-permute-start(bf16[2,64,1024]{2,1,0:T(8,128)(2,1)S(1)} %pad_maximum_fusion), channel_id=1, source_target_pairs={{0,56},{8,0},{16,8},{24,16},{32,24},{40,32},{48,40},{56,48},{1,57}... | collective-permute-start | bytes 786440 | tf_op jit(solution)/shard_map/ppermute | solution.py:28
  23.7 9.8 %collective-permute-start.1 = (bf16[2,64,1024]{2,1,0:T(8,128)(2,1)S(1)}, bf16[2,64,1024]{2,1,0:T(8,128)(2,1)S(1)}, u32[]{:S(2)}, u32[]{:S(2)}) collective-permute-start(bf16[2,64,1024]{2,1,0:T(8,128)(2,1)S(1)} %pad_maximum_fusion), channel_id=1, source_target_pairs={{0,8},{8,16},{16,24},{24,32},{32,40},{40,48},{48,56},{56,0},{1,9},... | collective-permute-start | bytes 786440 | tf_op jit(solution)/shard_map/ppermute | solution.py:28
  25.6 15.3 %collective-permute-start.10 = (bf16[288,1024]{1,0:T(8,128)(2,1)S(1)}, bf16[288,1024]{1,0:T(8,128)(2,1)}, u32[]{:S(2)}, u32[]{:S(2)}) collective-permute-start(bf16[288,1024]{1,0:T(8,128)(2,1)S(1)} %pad_add_fusion.refs_0_), channel_id=1, source_target_pairs={{0,64},{64,0},{128,192},{192,128},{1,65},{65,1},{129,193},{193,129... | collective-permute-start | bytes 1769480 | tf_op jit(solution)/shard_map/ppermute | solution.py:32
  28.1 15.0 %collective-permute-start.5 = (bf16[2,64,1024]{2,1,0:T(8,128)(2,1)}, bf16[2,64,1024]{2,1,0:T(8,128)(2,1)}, u32[]{:S(2)}, u32[]{:S(2)}) collective-permute-start(bf16[2,64,1024]{2,1,0:T(8,128)(2,1)} %collective-permute-done.2), channel_id=1, source_target_pairs={{0,56},{8,0},{16,8},{24,16},{32,24},{40,32},{48,40},{56,48},{1,57}... | collective-permute-start | bytes 786440 | tf_op jit(solution)/shard_map/ppermute | solution.py:28
  33.5 13.8 %collective-permute-start.4 = (bf16[2,64,1024]{2,1,0:T(8,128)(2,1)S(1)}, bf16[2,64,1024]{2,1,0:T(8,128)(2,1)}, u32[]{:S(2)}, u32[]{:S(2)}) collective-permute-start(bf16[2,64,1024]{2,1,0:T(8,128)(2,1)S(1)} %shard_map.86), channel_id=1, source_target_pairs={{0,8},{8,16},{16,24},{24,32},{32,40},{40,48},{48,56},{56,0},{1,9},... | collective-permute-start | bytes 786440 | tf_op jit(solution)/shard_map/ppermute | solution.py:28
  40.9 22.3 %collective-permute-start.11 = (bf16[288,1024]{1,0:T(8,128)(2,1)}, bf16[288,1024]{1,0:T(8,128)(2,1)S(1)}, u32[]{:S(2)}, u32[]{:S(2)}) collective-permute-start(bf16[288,1024]{1,0:T(8,128)(2,1)} %collective-permute-done.10.refs_1_), channel_id=1, source_target_pairs={{0,192},{64,128},{128,64},{192,0},{1,193},{65,129},{129,65},{193,1... | collective-permute-start | bytes 1769480 | tf_op jit(solution)/shard_map/ppermute | solution.py:32
  43.1 8.2 %collective-permute-start.7 = (bf16[2,64,1024]{2,1,0:T(8,128)(2,1)}, bf16[2,64,1024]{2,1,0:T(8,128)(2,1)S(1)}, u32[]{:S(2)}, u32[]{:S(2)}) collective-permute-start(bf16[2,64,1024]{2,1,0:T(8,128)(2,1)} %collective-permute-done.5), channel_id=1, source_target_pairs={{0,56},{8,0},{16,8},{24,16},{32,24},{40,32},{48,40},{56,48},{1,57}... | collective-permute-start | bytes 786440 | tf_op jit(solution)/shard_map/ppermute | solution.py:28
  47.4 8.8 %collective-permute-start.6 = (bf16[2,64,1024]{2,1,0:T(8,128)(2,1)}, bf16[2,64,1024]{2,1,0:T(8,128)(2,1)S(1)}, u32[]{:S(2)}, u32[]{:S(2)}) collective-permute-start(bf16[2,64,1024]{2,1,0:T(8,128)(2,1)} %collective-permute-done.4), channel_id=1, source_target_pairs={{0,8},{8,16},{16,24},{24,32},{32,40},{40,48},{48,56},{56,0},{1,9},... | collective-permute-start | bytes 786440 | tf_op jit(solution)/shard_map/ppermute | solution.py:28
  51.3 11.9 %collective-permute-start.9 = (bf16[1,64,1024]{2,1,0:T(8,128)(2,1)S(1)}, bf16[1,64,1024]{2,1,0:T(8,128)(2,1)S(1)}, u32[]{:S(2)}, u32[]{:S(2)}) collective-permute-start(bf16[1,64,1024]{2,1,0:T(8,128)(2,1)S(1)} %slice.122), channel_id=1, source_target_pairs={{0,56},{8,0},{16,8},{24,16},{32,24},{40,32},{48,40},{56,48},{1,57}... | collective-permute-start | bytes 393224 | tf_op jit(solution)/shard_map/ppermute | solution.py:28
  56.2 6.9 %collective-permute-start.8 = (bf16[1,64,1024]{2,1,0:T(8,128)(2,1)S(1)}, bf16[1,64,1024]{2,1,0:T(8,128)(2,1)S(1)}, u32[]{:S(2)}, u32[]{:S(2)}) collective-permute-start(bf16[1,64,1024]{2,1,0:T(8,128)(2,1)S(1)} %slice.120), channel_id=1, source_target_pairs={{0,8},{8,16},{16,24},{24,32},{32,40},{40,48},{48,56},{56,0},{1,9},... | collective-permute-start | bytes 393224 | tf_op jit(solution)/shard_map/ppermute | solution.py:28
  65.2 9.7 %collective-permute-start.12 = (f32[256,1152]{1,0:T(8,128)S(1)}, f32[256,1152]{1,0:T(8,128)S(1)}, u32[]{:S(2)}, u32[]{:S(2)}) collective-permute-start(f32[256,1152]{1,0:T(8,128)S(1)} %shard_map.88), channel_id=1, source_target_pairs={{0,1},{1,0},{2,3},{3,2},{4,5},{5,4},{6,7},{7,6},{8,9},{9,8},{10,11... | collective-permute-start | bytes 3538952 | tf_op jit(solution)/shard_map/ppermute | solution.py:23
  75.8 22.3 %all-to-all-start = ((f16[4,64,1152]{2,1,0:T(8,128)(2,1)}), f16[4,64,1152]{2,1,0:T(8,128)(2,1)S(1)}, u32[]{:S(2)}, u32[]{:S(2)}) async-start(f16[4,64,1152]{2,1,0:T(8,128)(2,1)} %bitcast.7), calls=%async_computation | async-start | bytes 1179648 | tf_op jit(solution)/shard_map/all_to_all | solution.py:191
  117.6 16.0 %copy-start = (bf16[56,1024]{1,0:T(8,128)(2,1)S(1)}, bf16[56,1024]{1,0:T(8,128)(2,1)}, u32[]{:S(2)}) copy-start(bf16[56,1024]{1,0:T(8,128)(2,1)} %up_probe.1) | copy-start | bytes 344068
  117.6 16.0 %copy-start.1 = (bf16[56,1024]{1,0:T(8,128)(2,1)S(1)}, bf16[56,1024]{1,0:T(8,128)(2,1)}, u32[]{:S(2)}) copy-start(bf16[56,1024]{1,0:T(8,128)(2,1)} %gate_probe.1) | copy-start | bytes 344068

commit v10 on v9

--- a/solution.py
+++ b/solution.py
@@ -63,13 +63,23 @@
 
 
 def terms_kernel(tok_rows, place, tokens, cotangents, *refs):
-    *weights, out, w_all = refs
+    *weights, out, w_all, sems = refs
     cut = len(weights) * tok_rows
     cot_rows = weights[0].shape[0] - tok_rows
+    copies = []
     for i, weight in enumerate(weights):
-        w_all[i * tok_rows : (i + 1) * tok_rows] = weight[:tok_rows]
-        start = cut + i * cot_rows
-        w_all[start : start + cot_rows] = weight[tok_rows:]
+        for j, (start, rows, to) in enumerate(
+            ((0, tok_rows, i * tok_rows), (tok_rows, cot_rows, cut + i * cot_rows))
+        ):
+            copies.append(
+                pltpu.make_async_copy(
+                    weight.at[pl.ds(start, rows)], w_all.at[pl.ds(to, rows)], sems.at[2 * i + j]
+                )
+            )
+    for copy in copies:
+        copy.start()
+    for copy in copies:
+        copy.wait()
     count = out.shape[0]
     half = pl.ds(pl.multiple_of(place[0] * count, count), count)
     across = (((1,), (1,)), ((), ()))
@@ -123,6 +133,26 @@
     return (fac_gate, fac_up)
 
 
+def factors_kernel(nx, hid, cut, proj, out):
+    tok_rows, cot_rows = cut // nx, (proj.shape[1] - cut) // nx
+    lanes = out.shape[1] // nx
+    for i in range(nx):
+        start = i * tok_rows
+        pre_gate, pre_up, tan_gate, tan_up = (
+            proj[:, start + j * hid : start + (j + 1) * hid] for j in range(4)
+        )
+        start = cut + i * cot_rows
+        fac_gate, fac_up = factors(
+            pre_gate * (1.0 / PRE_SCALE),
+            pre_up * (1.0 / PRE_SCALE),
+            tan_gate * (1.0 / TAN_SCALE),
+            tan_up * (1.0 / TAN_SCALE),
+            proj[:, start : start + hid] * (1.0 / BACK_SCALE),
+        )
+        rest = jnp.zeros((out.shape[0], lanes - 2 * hid), jnp.bfloat16)
+        out[:, i * lanes : (i + 1) * lanes] = jnp.concatenate([fac_gate, fac_up, rest], axis=1)
+
+
 def stacked(parts, rows):
     row, out = 0, None
     for part in parts:
@@ -179,9 +209,12 @@
             tok_all,
             cot_all,
             *weights,
-            in_specs=[SMEM] + [VMEM] * (2 + nx),
+            in_specs=[SMEM] + [VMEM] * 2 + [ANY] * nx,
             out_specs=VMEM,
-            scratch_shapes=[pltpu.VMEM((columns, feats), jnp.bfloat16)],
+            scratch_shapes=[
+                pltpu.VMEM((columns, feats), jnp.bfloat16),
+                pltpu.SemaphoreType.DMA((2 * nx,)),
+            ],
         )
     other = swap(term(1 - core), "c")
     terms = term(core) + other
@@ -190,15 +223,18 @@
     sent = terms.astype(jnp.float16).reshape(nzl, share, columns)
     got = lax.all_to_all(sent, "zl", 0, 0, tiled=True)
     proj = jnp.sum(got.astype(jnp.float32), axis=0)
-    tok_part = proj[:, :cut].reshape(share, nx, 4, hid)
-    pre_gate, pre_up = (tok_part[:, :, i] * (1.0 / PRE_SCALE) for i in (0, 1))
-    tan_gate, tan_up = (tok_part[:, :, i] * (1.0 / TAN_SCALE) for i in (2, 3))
-    back = proj[:, cut:].reshape(share, nx, cot_rows)[:, :, :hid] * (1.0 / BACK_SCALE)
-    fac_gate, fac_up = factors(pre_gate, pre_up, tan_gate, tan_up, back)
 
     lanes = -(-2 * hid // 128) * 128
-    fill = fac_up[:, :, : lanes - 2 * hid]
-    fac = jnp.concatenate([fac_gate, fac_up, fill], axis=2).reshape(share, nx * lanes)
+    fac = local_call(
+        functools.partial(factors_kernel, nx, hid, cut),
+        jax.ShapeDtypeStruct((share, nx * lanes), jnp.bfloat16),
+        32 * share * nx * hid,
+        8 * share * columns,
+        interpret,
+        proj,
+        in_specs=[VMEM],
+        out_specs=VMEM,
+    )
     fac = lax.all_gather(fac, ("zl", "c"), axis=1, tiled=True)
 
     away, mine = local_call(

time: 135 us -> 135 us (level)
  Pallas kernels: 6.22 us -> 7.96 us
    pallas_call x5 -> x6, Pallas kernels: 6.22 us -> 7.96 us  [local_call(): pl.pallas_call(body, out_shape=out_shape, cost_estimate=pl.CostEstimate(f...]
    unnamed x12 -> x11, local copies, waits for them, and re-layouts: 3.07 us -> 3.06 us
  transfers between devices with their start and end apart: 14 -> 14, of which waited for: 5 -> 4; matrix products, arithmetic and copies ran while one was open for 3% -> 3% of each run, Pallas kernels for 1% -> 2%
where the time goes in v10:
time: 135 us; the launch traced here: 134 us
  starting transfers between devices  61.3 us (45%)
  blocking collectives  32 us (24%)
  waiting for transfers between devices  25.3 us (19%)
  Pallas kernels  7.96 us (6%)
  other arithmetic  3.18 us (2%)
  local copies, waits for them, and re-layouts  3.09 us (2%)
    ppermute x8, starting transfers between devices, shift(): lax.ppermute(value, axis, [(i, (i + by) % size) for i in range(size)])  27.4 us
    ppermute x2, starting transfers between devices, swap(): return lax.ppermute(value, axis, [(0, 1), (1, 0)])  18.7 us
    all_gather x1, blocking collectives, on_device(): fac = lax.all_gather(fac, ('zl', 'c'), axis=1, tiled=True)  16.1 us
    all_to_all x1, blocking collectives, on_device(): away = lax.all_to_all(away, 'x', 0, 0, tiled=True)  16 us
    all_to_all x1, waiting for transfers between devices, on_device(): got = lax.all_to_all(sent, 'zl', 0, 0, tiled=True)  15.4 us
    ppermute x3, starting transfers between devices, mix(): lax.ppermute(value, axis, [(i, i ^ by) for i in range(lax.axis_size(axis))])  8.4 us
    pallas_call x6, Pallas kernels, local_call(): pl.pallas_call(body, out_shape=out_shape, cost_estimate=pl.CostEstimate(f...  7.96 us
    all_to_all x1, starting transfers between devices, on_device(): got = lax.all_to_all(sent, 'zl', 0, 0, tiled=True)  6.83 us
  transfers between devices with their start and end apart: 14, of which 4 were waited for; matrix products, arithmetic and copies ran while one was open for 3% of the time, Pallas kernels for 2%

profile of v10, /device:TPU:1, one launch (start us, length us, event | category | flops | bytes accessed | tf_op | source)
XLA Modules:
  0.0 133.8 jit_solution(8775165561806881009)
XLA Ops:
  0.6 0.9 pad_add_fusion.1
  1.5 11.5 %collective-permute-start = (bf16[64,1024]{1,0:T(8,128)(2,1)S(1)}, bf16[64,1024]{1,0:T(8,128)(2,1)S(1)}, u32[]{:S(2)}, u32[]{:S(2)}) collective-permute-start(bf16[64,1024]{1,0:T(8,128)(2,1)S(1)} %get-tuple-element.24), channel_id=1, source_target_pairs={{0,256},{256,0},{1,257},{257,1},{2,258},{258,2},{3,259},{259,3},{4... | collective-permute-start | bytes 393224 | tf_op jit(solution)/shard_map/ppermute | solution.py:23
  13.0 1.2 pad_add_fusion.refs_0_
  14.2 4.4 %collective-permute-start.3 = (bf16[288,1024]{1,0:T(8,128)(2,1)S(1)}, bf16[288,1024]{1,0:T(8,128)(2,1)S(1)}, u32[]{:S(2)}, u32[]{:S(2)}) collective-permute-start(bf16[288,1024]{1,0:T(8,128)(2,1)S(1)} %pad_add_fusion.refs_0_), channel_id=1, source_target_pairs={{0,192},{64,128},{128,64},{192,0},{1,193},{65,129},{129,65},{193,1... | collective-permute-start | bytes 1769480 | tf_op jit(solution)/shard_map/ppermute | solution.py:32
  18.6 0.0 collective-permute-done
  18.6 5.1 %collective-permute-start.2 = (bf16[2,64,1024]{2,1,0:T(8,128)(2,1)S(1)}, bf16[2,64,1024]{2,1,0:T(8,128)(2,1)}, u32[]{:S(2)}, u32[]{:S(2)}) collective-permute-start(bf16[2,64,1024]{2,1,0:T(8,128)(2,1)S(1)} %pad_maximum_fusion), channel_id=1, source_target_pairs={{0,56},{8,0},{16,8},{24,16},{32,24},{40,32},{48,40},{56,48},{1,57}... | collective-permute-start | bytes 786440 | tf_op jit(solution)/shard_map/ppermute | solution.py:28
  23.7 1.9 %collective-permute-start.1 = (bf16[2,64,1024]{2,1,0:T(8,128)(2,1)S(1)}, bf16[2,64,1024]{2,1,0:T(8,128)(2,1)S(1)}, u32[]{:S(2)}, u32[]{:S(2)}) collective-permute-start(bf16[2,64,1024]{2,1,0:T(8,128)(2,1)S(1)} %pad_maximum_fusion), channel_id=1, source_target_pairs={{0,8},{8,16},{16,24},{24,32},{32,40},{40,48},{48,56},{56,0},{1,9},... | collective-permute-start | bytes 786440 | tf_op jit(solution)/shard_map/ppermute | solution.py:28
  25.6 1.9 %collective-permute-start.10 = (bf16[288,1024]{1,0:T(8,128)(2,1)S(1)}, bf16[288,1024]{1,0:T(8,128)(2,1)}, u32[]{:S(2)}, u32[]{:S(2)}) collective-permute-start(bf16[288,1024]{1,0:T(8,128)(2,1)S(1)} %pad_add_fusion.refs_0_), channel_id=1, source_target_pairs={{0,64},{64,0},{128,192},{192,128},{1,65},{65,1},{129,193},{193,129... | collective-permute-start | bytes 1769480 | tf_op jit(solution)/shard_map/ppermute | solution.py:32
  27.6 0.5 collective-permute-done.2
  28.1 5.4 %collective-permute-start.5 = (bf16[2,64,1024]{2,1,0:T(8,128)(2,1)}, bf16[2,64,1024]{2,1,0:T(8,128)(2,1)}, u32[]{:S(2)}, u32[]{:S(2)}) collective-permute-start(bf16[2,64,1024]{2,1,0:T(8,128)(2,1)} %collective-permute-done.2), channel_id=1, source_target_pairs={{0,56},{8,0},{16,8},{24,16},{32,24},{40,32},{48,40},{56,48},{1,57}... | collective-permute-start | bytes 786440 | tf_op jit(solution)/shard_map/ppermute | solution.py:28
  33.5 0.0 collective-permute-done.1.value
  33.5 0.0 collective-permute-done.3.rest_0_.refs_2_
  33.5 1.9 %collective-permute-start.4 = (bf16[2,64,1024]{2,1,0:T(8,128)(2,1)S(1)}, bf16[2,64,1024]{2,1,0:T(8,128)(2,1)}, u32[]{:S(2)}, u32[]{:S(2)}) collective-permute-start(bf16[2,64,1024]{2,1,0:T(8,128)(2,1)S(1)} %shard_map.86), channel_id=1, source_target_pairs={{0,8},{8,16},{16,24},{24,32},{32,40},{40,48},{48,56},{56,0},{1,9},... | collective-permute-start | bytes 786440 | tf_op jit(solution)/shard_map/ppermute | solution.py:28
  35.5 1.0 slice_dynamic-update-slice_fusion.4
  36.5 4.5 %collective-permute-done.10.refs_1_ = bf16[288,1024]{1,0:T(8,128)(2,1)} collective-permute-done((bf16[288,1024]{1,0:T(8,128)(2,1)S(1)}, bf16[288,1024]{1,0:T(8,128)(2,1)}, u32[]{:S(2)}, u32[]{:S(2)}) %collective-permute-start.10) | collective-permute-done | bytes 589856 | tf_op jit(solution)/shard_map/ppermute | solution.py:32
  40.9 2.1 %collective-permute-start.11 = (bf16[288,1024]{1,0:T(8,128)(2,1)}, bf16[288,1024]{1,0:T(8,128)(2,1)S(1)}, u32[]{:S(2)}, u32[]{:S(2)}) collective-permute-start(bf16[288,1024]{1,0:T(8,128)(2,1)} %collective-permute-done.10.refs_1_), channel_id=1, source_target_pairs={{0,192},{64,128},{128,64},{192,0},{1,193},{65,129},{129,65},{193,1... | collective-permute-start | bytes 1769480 | tf_op jit(solution)/shard_map/ppermute | solution.py:32
  43.0 0.0 collective-permute-done.5
  43.1 4.3 %collective-permute-start.7 = (bf16[2,64,1024]{2,1,0:T(8,128)(2,1)}, bf16[2,64,1024]{2,1,0:T(8,128)(2,1)S(1)}, u32[]{:S(2)}, u32[]{:S(2)}) collective-permute-start(bf16[2,64,1024]{2,1,0:T(8,128)(2,1)} %collective-permute-done.5), channel_id=1, source_target_pairs={{0,56},{8,0},{16,8},{24,16},{32,24},{40,32},{48,40},{56,48},{1,57}... | collective-permute-start | bytes 786440 | tf_op jit(solution)/shard_map/ppermute | solution.py:28
  47.4 0.0 collective-permute-done.4
  47.4 1.9 %collective-permute-start.6 = (bf16[2,64,1024]{2,1,0:T(8,128)(2,1)}, bf16[2,64,1024]{2,1,0:T(8,128)(2,1)S(1)}, u32[]{:S(2)}, u32[]{:S(2)}) collective-permute-start(bf16[2,64,1024]{2,1,0:T(8,128)(2,1)} %collective-permute-done.4), channel_id=1, source_target_pairs={{0,8},{8,16},{16,24},{24,32},{32,40},{40,48},{48,56},{56,0},{1,9},... | collective-permute-start | bytes 786440 | tf_op jit(solution)/shard_map/ppermute | solution.py:28
  49.3 1.0 slice_dynamic-update-slice_fusion.3
  50.3 1.0 slice_dynamic-update-slice_fusion.2
  51.3 0.0 collective-permute-done.7
  51.3 4.9 %collective-permute-start.9 = (bf16[1,64,1024]{2,1,0:T(8,128)(2,1)S(1)}, bf16[1,64,1024]{2,1,0:T(8,128)(2,1)S(1)}, u32[]{:S(2)}, u32[]{:S(2)}) collective-permute-start(bf16[1,64,1024]{2,1,0:T(8,128)(2,1)S(1)} %slice.90), channel_id=1, source_target_pairs={{0,56},{8,0},{16,8},{24,16},{32,24},{40,32},{48,40},{56,48},{1,57}... | collective-permute-start | bytes 393224 | tf_op jit(solution)/shard_map/ppermute | solution.py:28
  56.2 0.0 collective-permute-done.6
  56.2 1.9 %collective-permute-start.8 = (bf16[1,64,1024]{2,1,0:T(8,128)(2,1)S(1)}, bf16[1,64,1024]{2,1,0:T(8,128)(2,1)S(1)}, u32[]{:S(2)}, u32[]{:S(2)}) collective-permute-start(bf16[1,64,1024]{2,1,0:T(8,128)(2,1)S(1)} %slice.88), channel_id=1, source_target_pairs={{0,8},{8,16},{16,24},{24,32},{32,40},{40,48},{48,56},{56,0},{1,9},... | collective-permute-start | bytes 393224 | tf_op jit(solution)/shard_map/ppermute | solution.py:28
  58.2 4.9 %collective-permute-done.8 = bf16[1,64,1024]{2,1,0:T(8,128)(2,1)S(1)} collective-permute-done((bf16[1,64,1024]{2,1,0:T(8,128)(2,1)S(1)}, bf16[1,64,1024]{2,1,0:T(8,128)(2,1)S(1)}, u32[]{:S(2)}, u32[]{:S(2)}) %collective-permute-start.8) | collective-permute-done | bytes 131104 | tf_op jit(solution)/shard_map/ppermute | solution.py:28
  63.2 0.0 collective-permute-done.9
  63.2 0.0 collective-permute-done.11.refs_3_
  63.2 2.4 %shard_map.88 = f32[256,1152]{1,0:T(8,128)S(1)} custom-call(s32[1]{0:T(128)} %bitcast.6.place, bf16[512,1024]{1,0:T(8,128)(2,1)S(1)} %bitcast.11, bf16[512,1024]{1,0:T(8,128)(2,1)S(1)} %bitcast.9, bf16[288,1024]{1,0:T(8,128)(2,1)S(1)} %pad_add_fusion.refs_0_, bf16[288,1024]{1,0:T(8,128)(2,1)} %collective-permute-done.10.refs_1_, ...), custom_call_target="tpu_custom_call" | custom-call | flops 603979776 | bytes 2359296 | tf_op jit(solution)/shard_map/pallas_call | solution.py:36
  65.7 7.2 %collective-permute-start.12 = (f32[256,1152]{1,0:T(8,128)S(1)}, f32[256,1152]{1,0:T(8,128)S(1)}, u32[]{:S(2)}, u32[]{:S(2)}) collective-permute-start(f32[256,1152]{1,0:T(8,128)S(1)} %shard_map.88), channel_id=1, source_target_pairs={{0,1},{1,0},{2,3},{3,2},{4,5},{5,4},{6,7},{7,6},{8,9},{9,8},{10,11... | collective-permute-start | bytes 3538952 | tf_op jit(solution)/shard_map/ppermute | solution.py:23
  72.9 2.4 %shard_map.87 = f32[256,1152]{1,0:T(8,128)S(1)} custom-call(s32[1]{0:T(128)} %bitcast.1.place, bf16[512,1024]{1,0:T(8,128)(2,1)S(1)} %bitcast.12, bf16[512,1024]{1,0:T(8,128)(2,1)S(1)} %bitcast.10, bf16[288,1024]{1,0:T(8,128)(2,1)S(1)} %pad_add_fusion.refs_0_, bf16[288,1024]{1,0:T(8,128)(2,1)} %collective-permute-done.10.refs_1_, ...), custom_call_target="tpu_custom_call" | custom-call | flops 603979776 | bytes 2359296 | tf_op jit(solution)/shard_map/pallas_call | solution.py:36
  75.3 0.0 collective-permute-done.12
  75.3 1.0 add_convert_fusion
  76.3 6.8 %all-to-all-start = ((f16[4,64,1152]{2,1,0:T(8,128)(2,1)}), f16[4,64,1152]{2,1,0:T(8,128)(2,1)S(1)}, u32[]{:S(2)}, u32[]{:S(2)}) async-start(f16[4,64,1152]{2,1,0:T(8,128)(2,1)} %bitcast.7), calls=%async_computation | async-start | bytes 1179648 | tf_op jit(solution)/shard_map/all_to_all | solution.py:224
  83.2 15.4 %all-to-all-done = f16[4,64,1152]{2,1,0:T(8,128)(2,1)S(1)} async-done(((f16[4,64,1152]{2,1,0:T(8,128)(2,1)}), f16[4,64,1152]{2,1,0:T(8,128)(2,1)S(1)}, u32[]{:S(2)}, u32[]{:S(2)}) %all-to-all-start) | async-done | bytes 589856 | tf_op jit(solution)/shard_map/all_to_all | solution.py:224
  98.6 0.1 convert_reduce_fusion.proj
  98.7 0.7 shard_map.89
  99.4 16.1 %all_gather.3.fac = bf16[64,4096]{1,0:T(8,128)(2,1)S(1)} all-gather(bf16[64,512]{1,0:T(8,128)(2,1)S(1)} %shard_map.89), channel_id=1, replica_groups=mesh['zh'=2,'x'=4,'y'=8,'zl'=4,'c'=2] {'zl','c'}, dimensions={1}, use_global_device_ids=true | all-gather | bytes 589824 | tf_op jit(solution)/shard_map/all_gather | solution.py:238
  115.5 1.4 %shard_map.90 = (bf16[4,112,1024]{2,1,0:T(8,128)(2,1)S(1)}, f32[112,1024]{1,0:T(8,128)S(1)}) custom-call(s32[1]{0:T(128)} %bitcast.place, bf16[64,4096]{1,0:T(8,128)(2,1)S(1)} %all_gather.3.fac, bf16[512,1024]{1,0:T(8,128)(2,1)S(1)} %bitcast.13), custom_call_target="tpu_custom_call" | custom-call | flops 469762048 | bytes 1048576 | tf_op jit(solution)/shard_map/pallas_call | solution.py:36
  116.9 0.0 copy-start
  116.9 0.0 copy-start.1
  117.0 16.0 %all_to_all.10.away = bf16[4,112,1024]{2,1,0:T(8,128)(2,1)S(1)} all-to-all(bf16[4,112,1024]{2,1,0:T(8,128)(2,1)S(1)} %get-tuple-element.4), channel_id=1, replica_groups=mesh['zh'=2,'x'=4,'y'=8,'zl'=4,'c'=2] {'x'}, dimensions={0} | all-to-all | bytes 1835008 | tf_op jit(solution)/shard_map/all_to_all | solution.py:255
  132.9 0.0 copy-done
  132.9 0.0 copy-done.1
  132.9 0.9 shard_map.91
  (10 shorter events, 0.2 us)
Async XLA Ops:
  1.5 17.0 %collective-permute-start = (bf16[64,1024]{1,0:T(8,128)(2,1)S(1)}, bf16[64,1024]{1,0:T(8,128)(2,1)S(1)}, u32[]{:S(2)}, u32[]{:S(2)}) collective-permute-start(bf16[64,1024]{1,0:T(8,128)(2,1)S(1)} %get-tuple-element.24), channel_id=1, source_target_pairs={{0,256},{256,0},{1,257},{257,1},{2,258},{258,2},{3,259},{259,3},{4... | collective-permute-start | bytes 393224 | tf_op jit(solution)/shard_map/ppermute | solution.py:23
  14.2 19.3 %collective-permute-start.3 = (bf16[288,1024]{1,0:T(8,128)(2,1)S(1)}, bf16[288,1024]{1,0:T(8,128)(2,1)S(1)}, u32[]{:S(2)}, u32[]{:S(2)}) collective-permute-start(bf16[288,1024]{1,0:T(8,128)(2,1)S(1)} %pad_add_fusion.refs_0_), channel_id=1, source_target_pairs={{0,192},{64,128},{128,64},{192,0},{1,193},{65,129},{129,65},{193,1... | collective-permute-start | bytes 1769480 | tf_op jit(solution)/shard_map/ppermute | solution.py:32
  18.6 9.4 %collective-permute-start.2 = (bf16[2,64,1024]{2,1,0:T(8,128)(2,1)S(1)}, bf16[2,64,1024]{2,1,0:T(8,128)(2,1)}, u32[]{:S(2)}, u32[]{:S(2)}) collective-permute-start(bf16[2,64,1024]{2,1,0:T(8,128)(2,1)S(1)} %pad_maximum_fusion), channel_id=1, source_target_pairs={{0,56},{8,0},{16,8},{24,16},{32,24},{40,32},{48,40},{56,48},{1,57}... | collective-permute-start | bytes 786440 | tf_op jit(solution)/shard_map/ppermute | solution.py:28
  23.7 9.8 %collective-permute-start.1 = (bf16[2,64,1024]{2,1,0:T(8,128)(2,1)S(1)}, bf16[2,64,1024]{2,1,0:T(8,128)(2,1)S(1)}, u32[]{:S(2)}, u32[]{:S(2)}) collective-permute-start(bf16[2,64,1024]{2,1,0:T(8,128)(2,1)S(1)} %pad_maximum_fusion), channel_id=1, source_target_pairs={{0,8},{8,16},{16,24},{24,32},{32,40},{40,48},{48,56},{56,0},{1,9},... | collective-permute-start | bytes 786440 | tf_op jit(solution)/shard_map/ppermute | solution.py:28
  25.6 15.3 %collective-permute-start.10 = (bf16[288,1024]{1,0:T(8,128)(2,1)S(1)}, bf16[288,1024]{1,0:T(8,128)(2,1)}, u32[]{:S(2)}, u32[]{:S(2)}) collective-permute-start(bf16[288,1024]{1,0:T(8,128)(2,1)S(1)} %pad_add_fusion.refs_0_), channel_id=1, source_target_pairs={{0,64},{64,0},{128,192},{192,128},{1,65},{65,1},{129,193},{193,129... | collective-permute-start | bytes 1769480 | tf_op jit(solution)/shard_map/ppermute | solution.py:32
  28.1 15.0 %collective-permute-start.5 = (bf16[2,64,1024]{2,1,0:T(8,128)(2,1)}, bf16[2,64,1024]{2,1,0:T(8,128)(2,1)}, u32[]{:S(2)}, u32[]{:S(2)}) collective-permute-start(bf16[2,64,1024]{2,1,0:T(8,128)(2,1)} %collective-permute-done.2), channel_id=1, source_target_pairs={{0,56},{8,0},{16,8},{24,16},{32,24},{40,32},{48,40},{56,48},{1,57}... | collective-permute-start | bytes 786440 | tf_op jit(solution)/shard_map/ppermute | solution.py:28
  33.5 13.8 %collective-permute-start.4 = (bf16[2,64,1024]{2,1,0:T(8,128)(2,1)S(1)}, bf16[2,64,1024]{2,1,0:T(8,128)(2,1)}, u32[]{:S(2)}, u32[]{:S(2)}) collective-permute-start(bf16[2,64,1024]{2,1,0:T(8,128)(2,1)S(1)} %shard_map.86), channel_id=1, source_target_pairs={{0,8},{8,16},{16,24},{24,32},{32,40},{40,48},{48,56},{56,0},{1,9},... | collective-permute-start | bytes 786440 | tf_op jit(solution)/shard_map/ppermute | solution.py:28
  40.9 22.3 %collective-permute-start.11 = (bf16[288,1024]{1,0:T(8,128)(2,1)}, bf16[288,1024]{1,0:T(8,128)(2,1)S(1)}, u32[]{:S(2)}, u32[]{:S(2)}) collective-permute-start(bf16[288,1024]{1,0:T(8,128)(2,1)} %collective-permute-done.10.refs_1_), channel_id=1, source_target_pairs={{0,192},{64,128},{128,64},{192,0},{1,193},{65,129},{129,65},{193,1... | collective-permute-start | bytes 1769480 | tf_op jit(solution)/shard_map/ppermute | solution.py:32
  43.1 8.2 %collective-permute-start.7 = (bf16[2,64,1024]{2,1,0:T(8,128)(2,1)}, bf16[2,64,1024]{2,1,0:T(8,128)(2,1)S(1)}, u32[]{:S(2)}, u32[]{:S(2)}) collective-permute-start(bf16[2,64,1024]{2,1,0:T(8,128)(2,1)} %collective-permute-done.5), channel_id=1, source_target_pairs={{0,56},{8,0},{16,8},{24,16},{32,24},{40,32},{48,40},{56,48},{1,57}... | collective-permute-start | bytes 786440 | tf_op jit(solution)/shard_map/ppermute | solution.py:28
  47.4 8.8 %collective-permute-start.6 = (bf16[2,64,1024]{2,1,0:T(8,128)(2,1)}, bf16[2,64,1024]{2,1,0:T(8,128)(2,1)S(1)}, u32[]{:S(2)}, u32[]{:S(2)}) collective-permute-start(bf16[2,64,1024]{2,1,0:T(8,128)(2,1)} %collective-permute-done.4), channel_id=1, source_target_pairs={{0,8},{8,16},{16,24},{24,32},{32,40},{40,48},{48,56},{56,0},{1,9},... | collective-permute-start | bytes 786440 | tf_op jit(solution)/shard_map/ppermute | solution.py:28
  51.3 11.9 %collective-permute-start.9 = (bf16[1,64,1024]{2,1,0:T(8,128)(2,1)S(1)}, bf16[1,64,1024]{2,1,0:T(8,128)(2,1)S(1)}, u32[]{:S(2)}, u32[]{:S(2)}) collective-permute-start(bf16[1,64,1024]{2,1,0:T(8,128)(2,1)S(1)} %slice.90), channel_id=1, source_target_pairs={{0,56},{8,0},{16,8},{24,16},{32,24},{40,32},{48,40},{56,48},{1,57}... | collective-permute-start | bytes 393224 | tf_op jit(solution)/shard_map/ppermute | solution.py:28
  56.2 6.9 %collective-permute-start.8 = (bf16[1,64,1024]{2,1,0:T(8,128)(2,1)S(1)}, bf16[1,64,1024]{2,1,0:T(8,128)(2,1)S(1)}, u32[]{:S(2)}, u32[]{:S(2)}) collective-permute-start(bf16[1,64,1024]{2,1,0:T(8,128)(2,1)S(1)} %slice.88), channel_id=1, source_target_pairs={{0,8},{8,16},{16,24},{24,32},{32,40},{40,48},{48,56},{56,0},{1,9},... | collective-permute-start | bytes 393224 | tf_op jit(solution)/shard_map/ppermute | solution.py:28
  65.7 9.7 %collective-permute-start.12 = (f32[256,1152]{1,0:T(8,128)S(1)}, f32[256,1152]{1,0:T(8,128)S(1)}, u32[]{:S(2)}, u32[]{:S(2)}) collective-permute-start(f32[256,1152]{1,0:T(8,128)S(1)} %shard_map.88), channel_id=1, source_target_pairs={{0,1},{1,0},{2,3},{3,2},{4,5},{5,4},{6,7},{7,6},{8,9},{9,8},{10,11... | collective-permute-start | bytes 3538952 | tf_op jit(solution)/shard_map/ppermute | solution.py:23
  76.3 22.3 %all-to-all-start = ((f16[4,64,1152]{2,1,0:T(8,128)(2,1)}), f16[4,64,1152]{2,1,0:T(8,128)(2,1)S(1)}, u32[]{:S(2)}, u32[]{:S(2)}) async-start(f16[4,64,1152]{2,1,0:T(8,128)(2,1)} %bitcast.7), calls=%async_computation | async-start | bytes 1179648 | tf_op jit(solution)/shard_map/all_to_all | solution.py:224
  116.9 16.0 %copy-start = (bf16[56,1024]{1,0:T(8,128)(2,1)S(1)}, bf16[56,1024]{1,0:T(8,128)(2,1)}, u32[]{:S(2)}) copy-start(bf16[56,1024]{1,0:T(8,128)(2,1)} %up_probe.1) | copy-start | bytes 344068
  116.9 16.0 %copy-start.1 = (bf16[56,1024]{1,0:T(8,128)(2,1)S(1)}, bf16[56,1024]{1,0:T(8,128)(2,1)}, u32[]{:S(2)}) copy-start(bf16[56,1024]{1,0:T(8,128)(2,1)} %gate_probe.1) | copy-start | bytes 344068

commit v11 on v6

--- a/solution.py
+++ b/solution.py
@@ -103,6 +103,26 @@
     return (fac_gate, fac_up)
 
 
+def factors_kernel(nx, hid, cut, proj, out):
+    tok_rows, cot_rows = cut // nx, (proj.shape[1] - cut) // nx
+    lanes = out.shape[1] // nx
+    for i in range(nx):
+        start = i * tok_rows
+        pre_gate, pre_up, tan_gate, tan_up = (
+            proj[:, start + j * hid : start + (j + 1) * hid] for j in range(4)
+        )
+        start = cut + i * cot_rows
+        fac_gate, fac_up = factors(
+            pre_gate * (1.0 / PRE_SCALE),
+            pre_up * (1.0 / PRE_SCALE),
+            tan_gate * (1.0 / TAN_SCALE),
+            tan_up * (1.0 / TAN_SCALE),
+            proj[:, start : start + hid] * (1.0 / BACK_SCALE),
+        )
+        rest = jnp.zeros((out.shape[0], lanes - 2 * hid), jnp.bfloat16)
+        out[:, i * lanes : (i + 1) * lanes] = jnp.concatenate([fac_gate, fac_up, rest], axis=1)
+
+
 def stacked(parts, rows):
     row, out = 0, None
     for part in parts:
@@ -168,15 +188,18 @@
     sent = terms.astype(jnp.float16).reshape(nzl, share, columns)
     got = lax.all_to_all(sent, "zl", 0, 0, tiled=True)
     proj = jnp.sum(got.astype(jnp.float32), axis=0)
-    tok_part = proj[:, :cut].reshape(share, nx, 4, hid)
-    pre_gate, pre_up = (tok_part[:, :, i] * (1.0 / PRE_SCALE) for i in (0, 1))
-    tan_gate, tan_up = (tok_part[:, :, i] * (1.0 / TAN_SCALE) for i in (2, 3))
-    back = proj[:, cut:].reshape(share, nx, cot_rows)[:, :, :hid] * (1.0 / BACK_SCALE)
-    fac_gate, fac_up = factors(pre_gate, pre_up, tan_gate, tan_up, back)
 
     lanes = -(-2 * hid // 128) * 128
-    fill = fac_up[:, :, : lanes - 2 * hid]
-    fac = jnp.concatenate([fac_gate, fac_up, fill], axis=2).reshape(share, nx * lanes)
+    fac = local_call(
+        functools.partial(factors_kernel, nx, hid, cut),
+        jax.ShapeDtypeStruct((share, nx * lanes), jnp.bfloat16),
+        32 * share * nx * hid,
+        8 * share * columns,
+        interpret,
+        proj,
+        in_specs=[VMEM],
+        out_specs=VMEM,
+    )
     fac = lax.all_gather(fac, ("zl", "c"), axis=1, tiled=True)
 
     away, mine = local_call(

time: 135 us -> 133 us (0.985)
    pallas_call x4 -> x5, Pallas kernels: 4.1 us -> 4.83 us  [local_call(): pl.pallas_call(body, out_shape=out_shape, cost_estimate=pl.CostEstimate(f...]
where the time goes in v11:
time: 133 us
  starting transfers between devices  60.1 us (45%)
  blocking collectives  31.9 us (24%)
  waiting for transfers between devices  30.1 us (23%)
  Pallas kernels  4.83 us (4%)
  other arithmetic  3.83 us (3%)
    ppermute x8, starting transfers between devices, shift(): lax.ppermute(value, axis, [(i, (i + by) % size) for i in range(size)])  28 us
    all_to_all x1, blocking collectives, on_device(): away = lax.all_to_all(away, 'x', 0, 0, tiled=True)  17 us
    all_to_all x1, waiting for transfers between devices, on_device(): got = lax.all_to_all(sent, 'zl', 0, 0, tiled=True)  16.2 us
    all_gather x1, blocking collectives, on_device(): fac = lax.all_gather(fac, ('zl', 'c'), axis=1, tiled=True)  14.8 us
    ppermute x2, starting transfers between devices, swap(): return lax.ppermute(value, axis, [(0, 1), (1, 0)])  12.8 us
    ppermute x3, starting transfers between devices, mix(): lax.ppermute(value, axis, [(i, i ^ by) for i in range(lax.axis_size(axis))])  12.1 us
    ppermute x8, waiting for transfers between devices, shift(): lax.ppermute(value, axis, [(i, (i + by) % size) for i in range(size)])  7.96 us
    all_to_all x1, starting transfers between devices, on_device(): got = lax.all_to_all(sent, 'zl', 0, 0, tiled=True)  7.2 us
  transfers between devices with their start and end apart: 14, of which 7 were waited for; matrix products, arithmetic and copies ran while one was open for 2% of the time, Pallas kernels for 1%

profile of v11, /device:TPU:24, one launch (start us, length us, event | category | flops | bytes accessed | tf_op | source)
XLA Modules:
  0.0 132.8 jit_solution(15908511094395359635)
XLA Ops:
  0.6 0.9 pad_add_fusion.1
  1.5 10.9 %collective-permute-start = (bf16[64,1024]{1,0:T(8,128)(2,1)S(1)}, bf16[64,1024]{1,0:T(8,128)(2,1)S(1)}, u32[]{:S(2)}, u32[]{:S(2)}) collective-permute-start(bf16[64,1024]{1,0:T(8,128)(2,1)S(1)} %get-tuple-element.24), channel_id=1, source_target_pairs={{0,256},{256,0},{1,257},{257,1},{2,258},{258,2},{3,259},{259,3},{4... | collective-permute-start | bytes 393224 | tf_op jit(solution)/shard_map/ppermute | solution.py:22
  12.4 3.6 %collective-permute-done = bf16[64,1024]{1,0:T(8,128)(2,1)S(1)} collective-permute-done((bf16[64,1024]{1,0:T(8,128)(2,1)S(1)}, bf16[64,1024]{1,0:T(8,128)(2,1)S(1)}, u32[]{:S(2)}, u32[]{:S(2)}) %collective-permute-start) | collective-permute-done | bytes 131104 | tf_op jit(solution)/shard_map/ppermute | solution.py:22
  16.0 0.7 pad_maximum_fusion
  16.8 4.7 %collective-permute-start.1 = (bf16[2,64,1024]{2,1,0:T(8,128)(2,1)}, bf16[2,64,1024]{2,1,0:T(8,128)(2,1)}, u32[]{:S(2)}, u32[]{:S(2)}) collective-permute-start(bf16[2,64,1024]{2,1,0:T(8,128)(2,1)} %pad_maximum_fusion), channel_id=1, source_target_pairs={{0,8},{8,16},{16,24},{24,32},{32,40},{40,48},{48,56},{56,0},{1,9},... | collective-permute-start | bytes 786440 | tf_op jit(solution)/shard_map/ppermute | solution.py:27
  21.4 1.9 %collective-permute-start.2 = (bf16[2,64,1024]{2,1,0:T(8,128)(2,1)}, bf16[2,64,1024]{2,1,0:T(8,128)(2,1)S(1)}, u32[]{:S(2)}, u32[]{:S(2)}) collective-permute-start(bf16[2,64,1024]{2,1,0:T(8,128)(2,1)} %pad_maximum_fusion), channel_id=1, source_target_pairs={{0,56},{8,0},{16,8},{24,16},{32,24},{40,32},{48,40},{56,48},{1,57}... | collective-permute-start | bytes 786440 | tf_op jit(solution)/shard_map/ppermute | solution.py:27
  23.4 1.2 pad_add_fusion.refs_0_
  24.5 3.4 %collective-permute-start.9 = (bf16[288,1024]{1,0:T(8,128)(2,1)S(1)}, bf16[288,1024]{1,0:T(8,128)(2,1)S(1)}, u32[]{:S(2)}, u32[]{:S(2)}) collective-permute-start(bf16[288,1024]{1,0:T(8,128)(2,1)S(1)} %pad_add_fusion.refs_0_), channel_id=1, source_target_pairs={{0,64},{64,0},{128,192},{192,128},{1,65},{65,1},{129,193},{193,129... | collective-permute-start | bytes 1769480 | tf_op jit(solution)/shard_map/ppermute | solution.py:31
  27.9 4.0 %collective-permute-start.10 = (bf16[288,1024]{1,0:T(8,128)(2,1)S(1)}, bf16[288,1024]{1,0:T(8,128)(2,1)S(1)}, u32[]{:S(2)}, u32[]{:S(2)}) collective-permute-start(bf16[288,1024]{1,0:T(8,128)(2,1)S(1)} %pad_add_fusion.refs_0_), channel_id=1, source_target_pairs={{0,192},{64,128},{128,64},{192,0},{1,193},{65,129},{129,65},{193,1... | collective-permute-start | bytes 1769480 | tf_op jit(solution)/shard_map/ppermute | solution.py:31
  32.0 0.0 collective-permute-done.1
  32.0 5.1 %collective-permute-start.3 = (bf16[2,64,1024]{2,1,0:T(8,128)(2,1)}, bf16[2,64,1024]{2,1,0:T(8,128)(2,1)S(1)}, u32[]{:S(2)}, u32[]{:S(2)}) collective-permute-start(bf16[2,64,1024]{2,1,0:T(8,128)(2,1)} %collective-permute-done.1), channel_id=1, source_target_pairs={{0,8},{8,16},{16,24},{24,32},{32,40},{40,48},{48,56},{56,0},{1,9},... | collective-permute-start | bytes 786440 | tf_op jit(solution)/shard_map/ppermute | solution.py:27
  37.1 0.0 collective-permute-done.2
  37.2 1.9 %collective-permute-start.4 = (bf16[2,64,1024]{2,1,0:T(8,128)(2,1)S(1)}, bf16[2,64,1024]{2,1,0:T(8,128)(2,1)S(1)}, u32[]{:S(2)}, u32[]{:S(2)}) collective-permute-start(bf16[2,64,1024]{2,1,0:T(8,128)(2,1)S(1)} %collective-permute-done.2), channel_id=1, source_target_pairs={{0,56},{8,0},{16,8},{24,16},{32,24},{40,32},{48,40},{56,48},{1,57}... | collective-permute-start | bytes 786440 | tf_op jit(solution)/shard_map/ppermute | solution.py:27
  39.1 1.0 slice_dynamic-update-slice_fusion.5
  40.1 0.5 collective-permute-done.9.refs_1_
  40.6 4.7 %collective-permute-start.11 = (bf16[288,1024]{1,0:T(8,128)(2,1)S(1)}, bf16[288,1024]{1,0:T(8,128)(2,1)S(1)}, u32[]{:S(2)}, u32[]{:S(2)}) collective-permute-start(bf16[288,1024]{1,0:T(8,128)(2,1)S(1)} %collective-permute-done.9.refs_1_), channel_id=1, source_target_pairs={{0,192},{64,128},{128,64},{192,0},{1,193},{65,129},{129,65},{193,1... | collective-permute-start | bytes 1769480 | tf_op jit(solution)/shard_map/ppermute | solution.py:31
  45.2 0.0 collective-permute-done.3
  45.2 4.9 %collective-permute-start.5 = (bf16[2,64,1024]{2,1,0:T(8,128)(2,1)S(1)}, bf16[2,64,1024]{2,1,0:T(8,128)(2,1)S(1)}, u32[]{:S(2)}, u32[]{:S(2)}) collective-permute-start(bf16[2,64,1024]{2,1,0:T(8,128)(2,1)S(1)} %collective-permute-done.3), channel_id=1, source_target_pairs={{0,8},{8,16},{16,24},{24,32},{32,40},{40,48},{48,56},{56,0},{1,9},... | collective-permute-start | bytes 786440 | tf_op jit(solution)/shard_map/ppermute | solution.py:27
  50.1 0.0 collective-permute-done.4
  50.1 1.9 %collective-permute-start.6 = (bf16[2,64,1024]{2,1,0:T(8,128)(2,1)S(1)}, bf16[2,64,1024]{2,1,0:T(8,128)(2,1)S(1)}, u32[]{:S(2)}, u32[]{:S(2)}) collective-permute-start(bf16[2,64,1024]{2,1,0:T(8,128)(2,1)S(1)} %collective-permute-done.4), channel_id=1, source_target_pairs={{0,56},{8,0},{16,8},{24,16},{32,24},{40,32},{48,40},{56,48},{1,57}... | collective-permute-start | bytes 786440 | tf_op jit(solution)/shard_map/ppermute | solution.py:27
  52.1 1.9 %collective-permute-done.5 = bf16[2,64,1024]{2,1,0:T(8,128)(2,1)S(1)} collective-permute-done((bf16[2,64,1024]{2,1,0:T(8,128)(2,1)S(1)}, bf16[2,64,1024]{2,1,0:T(8,128)(2,1)S(1)}, u32[]{:S(2)}, u32[]{:S(2)}) %collective-permute-start.5) | collective-permute-done | bytes 262176 | tf_op jit(solution)/shard_map/ppermute | solution.py:27
  54.0 5.6 %collective-permute-start.7 = (bf16[1,64,1024]{2,1,0:T(8,128)(2,1)S(1)}, bf16[1,64,1024]{2,1,0:T(8,128)(2,1)S(1)}, u32[]{:S(2)}, u32[]{:S(2)}) collective-permute-start(bf16[1,64,1024]{2,1,0:T(8,128)(2,1)S(1)} %slice.88), channel_id=1, source_target_pairs={{0,8},{8,16},{16,24},{24,32},{32,40},{40,48},{48,56},{56,0},{1,9},... | collective-permute-start | bytes 393224 | tf_op jit(solution)/shard_map/ppermute | solution.py:27
  59.6 0.0 collective-permute-done.6
  59.6 1.9 %collective-permute-start.8 = (bf16[1,64,1024]{2,1,0:T(8,128)(2,1)S(1)}, bf16[1,64,1024]{2,1,0:T(8,128)(2,1)S(1)}, u32[]{:S(2)}, u32[]{:S(2)}) collective-permute-start(bf16[1,64,1024]{2,1,0:T(8,128)(2,1)S(1)} %slice.90), channel_id=1, source_target_pairs={{0,56},{8,0},{16,8},{24,16},{32,24},{40,32},{48,40},{56,48},{1,57}... | collective-permute-start | bytes 393224 | tf_op jit(solution)/shard_map/ppermute | solution.py:27
  61.6 0.5 collective-permute-done.7
  62.1 5.6 %collective-permute-done.8 = bf16[1,64,1024]{2,1,0:T(8,128)(2,1)S(1)} collective-permute-done((bf16[1,64,1024]{2,1,0:T(8,128)(2,1)S(1)}, bf16[1,64,1024]{2,1,0:T(8,128)(2,1)S(1)}, u32[]{:S(2)}, u32[]{:S(2)}) %collective-permute-start.8) | collective-permute-done | bytes 131104 | tf_op jit(solution)/shard_map/ppermute | solution.py:27
  67.7 0.0 collective-permute-done.10.refs_2_
  67.7 0.0 collective-permute-done.11.refs_3_
  67.7 0.9 shard_map.87
  68.6 1.9 %collective-permute-start.12 = (f32[256,1152]{1,0:T(8,128)S(1)}, f32[256,1152]{1,0:T(8,128)S(1)}, u32[]{:S(2)}, u32[]{:S(2)}) collective-permute-start(f32[256,1152]{1,0:T(8,128)S(1)} %shard_map.87), channel_id=1, source_target_pairs={{0,1},{1,0},{2,3},{3,2},{4,5},{5,4},{6,7},{7,6},{8,9},{9,8},{10,11... | collective-permute-start | bytes 3538952 | tf_op jit(solution)/shard_map/ppermute | solution.py:22
  70.5 0.9 shard_map.86
  71.4 1.9 %collective-permute-done.12 = f32[256,1152]{1,0:T(8,128)S(1)} collective-permute-done((f32[256,1152]{1,0:T(8,128)S(1)}, f32[256,1152]{1,0:T(8,128)S(1)}, u32[]{:S(2)}, u32[]{:S(2)}) %collective-permute-start.12) | collective-permute-done | bytes 1179680 | tf_op jit(solution)/shard_map/ppermute | solution.py:22
  73.4 1.0 add_convert_fusion
  74.3 7.2 %all-to-all-start = ((f16[4,64,1152]{2,1,0:T(8,128)(2,1)}), f16[4,64,1152]{2,1,0:T(8,128)(2,1)S(1)}, u32[]{:S(2)}, u32[]{:S(2)}) async-start(f16[4,64,1152]{2,1,0:T(8,128)(2,1)} %bitcast.7), calls=%async_computation | async-start | bytes 1179648 | tf_op jit(solution)/shard_map/all_to_all | solution.py:189
  81.5 16.2 %all-to-all-done = f16[4,64,1152]{2,1,0:T(8,128)(2,1)S(1)} async-done(((f16[4,64,1152]{2,1,0:T(8,128)(2,1)}), f16[4,64,1152]{2,1,0:T(8,128)(2,1)S(1)}, u32[]{:S(2)}, u32[]{:S(2)}) %all-to-all-start) | async-done | bytes 589856 | tf_op jit(solution)/shard_map/all_to_all | solution.py:189
  97.7 0.1 convert_reduce_fusion.proj
  97.8 0.7 shard_map.88
  98.5 14.8 %all_gather.3.fac = bf16[64,4096]{1,0:T(8,128)(2,1)S(1)} all-gather(bf16[64,512]{1,0:T(8,128)(2,1)S(1)} %shard_map.88), channel_id=1, replica_groups=mesh['zh'=2,'x'=4,'y'=8,'zl'=4,'c'=2] {'zl','c'}, dimensions={1}, use_global_device_ids=true | all-gather | bytes 589824 | tf_op jit(solution)/shard_map/all_gather | solution.py:203
  113.4 1.4 %shard_map.89 = (bf16[4,112,1024]{2,1,0:T(8,128)(2,1)S(1)}, f32[112,1024]{1,0:T(8,128)S(1)}) custom-call(s32[1]{0:T(128)} %bitcast.place, bf16[64,4096]{1,0:T(8,128)(2,1)S(1)} %all_gather.3.fac, bf16[512,1024]{1,0:T(8,128)(2,1)S(1)} %bitcast.13), custom_call_target="tpu_custom_call" | custom-call | flops 469762048 | bytes 1048576 | tf_op jit(solution)/shard_map/pallas_call | solution.py:35
  114.8 0.0 copy-start
  114.8 0.0 copy-start.1
  114.8 17.0 %all_to_all.10.away = bf16[4,112,1024]{2,1,0:T(8,128)(2,1)S(1)} all-to-all(bf16[4,112,1024]{2,1,0:T(8,128)(2,1)S(1)} %get-tuple-element.4), channel_id=1, replica_groups=mesh['zh'=2,'x'=4,'y'=8,'zl'=4,'c'=2] {'x'}, dimensions={0} | all-to-all | bytes 1835008 | tf_op jit(solution)/shard_map/all_to_all | solution.py:220
  131.9 0.0 copy-done
  131.9 0.0 copy-done.1
  131.9 0.9 shard_map.90
  (10 shorter events, 0.2 us)
Async XLA Ops:
  1.5 14.5 %collective-permute-start = (bf16[64,1024]{1,0:T(8,128)(2,1)S(1)}, bf16[64,1024]{1,0:T(8,128)(2,1)S(1)}, u32[]{:S(2)}, u32[]{:S(2)}) collective-permute-start(bf16[64,1024]{1,0:T(8,128)(2,1)S(1)} %get-tuple-element.24), channel_id=1, source_target_pairs={{0,256},{256,0},{1,257},{257,1},{2,258},{258,2},{3,259},{259,3},{4... | collective-permute-start | bytes 393224 | tf_op jit(solution)/shard_map/ppermute | solution.py:22
  16.8 15.2 %collective-permute-start.1 = (bf16[2,64,1024]{2,1,0:T(8,128)(2,1)}, bf16[2,64,1024]{2,1,0:T(8,128)(2,1)}, u32[]{:S(2)}, u32[]{:S(2)}) collective-permute-start(bf16[2,64,1024]{2,1,0:T(8,128)(2,1)} %pad_maximum_fusion), channel_id=1, source_target_pairs={{0,8},{8,16},{16,24},{24,32},{32,40},{40,48},{48,56},{56,0},{1,9},... | collective-permute-start | bytes 786440 | tf_op jit(solution)/shard_map/ppermute | solution.py:27
  21.4 15.7 %collective-permute-start.2 = (bf16[2,64,1024]{2,1,0:T(8,128)(2,1)}, bf16[2,64,1024]{2,1,0:T(8,128)(2,1)S(1)}, u32[]{:S(2)}, u32[]{:S(2)}) collective-permute-start(bf16[2,64,1024]{2,1,0:T(8,128)(2,1)} %pad_maximum_fusion), channel_id=1, source_target_pairs={{0,56},{8,0},{16,8},{24,16},{32,24},{40,32},{48,40},{56,48},{1,57}... | collective-permute-start | bytes 786440 | tf_op jit(solution)/shard_map/ppermute | solution.py:27
  24.5 16.0 %collective-permute-start.9 = (bf16[288,1024]{1,0:T(8,128)(2,1)S(1)}, bf16[288,1024]{1,0:T(8,128)(2,1)S(1)}, u32[]{:S(2)}, u32[]{:S(2)}) collective-permute-start(bf16[288,1024]{1,0:T(8,128)(2,1)S(1)} %pad_add_fusion.refs_0_), channel_id=1, source_target_pairs={{0,64},{64,0},{128,192},{192,128},{1,65},{65,1},{129,193},{193,129... | collective-permute-start | bytes 1769480 | tf_op jit(solution)/shard_map/ppermute | solution.py:31
  27.9 39.8 %collective-permute-start.10 = (bf16[288,1024]{1,0:T(8,128)(2,1)S(1)}, bf16[288,1024]{1,0:T(8,128)(2,1)S(1)}, u32[]{:S(2)}, u32[]{:S(2)}) collective-permute-start(bf16[288,1024]{1,0:T(8,128)(2,1)S(1)} %pad_add_fusion.refs_0_), channel_id=1, source_target_pairs={{0,192},{64,128},{128,64},{192,0},{1,193},{65,129},{129,65},{193,1... | collective-permute-start | bytes 1769480 | tf_op jit(solution)/shard_map/ppermute | solution.py:31
  32.0 13.2 %collective-permute-start.3 = (bf16[2,64,1024]{2,1,0:T(8,128)(2,1)}, bf16[2,64,1024]{2,1,0:T(8,128)(2,1)S(1)}, u32[]{:S(2)}, u32[]{:S(2)}) collective-permute-start(bf16[2,64,1024]{2,1,0:T(8,128)(2,1)} %collective-permute-done.1), channel_id=1, source_target_pairs={{0,8},{8,16},{16,24},{24,32},{32,40},{40,48},{48,56},{56,0},{1,9},... | collective-permute-start | bytes 786440 | tf_op jit(solution)/shard_map/ppermute | solution.py:27
  37.2 13.0 %collective-permute-start.4 = (bf16[2,64,1024]{2,1,0:T(8,128)(2,1)S(1)}, bf16[2,64,1024]{2,1,0:T(8,128)(2,1)S(1)}, u32[]{:S(2)}, u32[]{:S(2)}) collective-permute-start(bf16[2,64,1024]{2,1,0:T(8,128)(2,1)S(1)} %collective-permute-done.2), channel_id=1, source_target_pairs={{0,56},{8,0},{16,8},{24,16},{32,24},{40,32},{48,40},{56,48},{1,57}... | collective-permute-start | bytes 786440 | tf_op jit(solution)/shard_map/ppermute | solution.py:27
  40.6 27.2 %collective-permute-start.11 = (bf16[288,1024]{1,0:T(8,128)(2,1)S(1)}, bf16[288,1024]{1,0:T(8,128)(2,1)S(1)}, u32[]{:S(2)}, u32[]{:S(2)}) collective-permute-start(bf16[288,1024]{1,0:T(8,128)(2,1)S(1)} %collective-permute-done.9.refs_1_), channel_id=1, source_target_pairs={{0,192},{64,128},{128,64},{192,0},{1,193},{65,129},{129,65},{193,1... | collective-permute-start | bytes 1769480 | tf_op jit(solution)/shard_map/ppermute | solution.py:31
  45.2 8.7 %collective-permute-start.5 = (bf16[2,64,1024]{2,1,0:T(8,128)(2,1)S(1)}, bf16[2,64,1024]{2,1,0:T(8,128)(2,1)S(1)}, u32[]{:S(2)}, u32[]{:S(2)}) collective-permute-start(bf16[2,64,1024]{2,1,0:T(8,128)(2,1)S(1)} %collective-permute-done.3), channel_id=1, source_target_pairs={{0,8},{8,16},{16,24},{24,32},{32,40},{40,48},{48,56},{56,0},{1,9},... | collective-permute-start | bytes 786440 | tf_op jit(solution)/shard_map/ppermute | solution.py:27
  50.1 9.5 %collective-permute-start.6 = (bf16[2,64,1024]{2,1,0:T(8,128)(2,1)S(1)}, bf16[2,64,1024]{2,1,0:T(8,128)(2,1)S(1)}, u32[]{:S(2)}, u32[]{:S(2)}) collective-permute-start(bf16[2,64,1024]{2,1,0:T(8,128)(2,1)S(1)} %collective-permute-done.4), channel_id=1, source_target_pairs={{0,56},{8,0},{16,8},{24,16},{32,24},{40,32},{48,40},{56,48},{1,57}... | collective-permute-start | bytes 786440 | tf_op jit(solution)/shard_map/ppermute | solution.py:27
  54.0 8.1 %collective-permute-start.7 = (bf16[1,64,1024]{2,1,0:T(8,128)(2,1)S(1)}, bf16[1,64,1024]{2,1,0:T(8,128)(2,1)S(1)}, u32[]{:S(2)}, u32[]{:S(2)}) collective-permute-start(bf16[1,64,1024]{2,1,0:T(8,128)(2,1)S(1)} %slice.88), channel_id=1, source_target_pairs={{0,8},{8,16},{16,24},{24,32},{32,40},{40,48},{48,56},{56,0},{1,9},... | collective-permute-start | bytes 393224 | tf_op jit(solution)/shard_map/ppermute | solution.py:27
  59.6 8.1 %collective-permute-start.8 = (bf16[1,64,1024]{2,1,0:T(8,128)(2,1)S(1)}, bf16[1,64,1024]{2,1,0:T(8,128)(2,1)S(1)}, u32[]{:S(2)}, u32[]{:S(2)}) collective-permute-start(bf16[1,64,1024]{2,1,0:T(8,128)(2,1)S(1)} %slice.90), channel_id=1, source_target_pairs={{0,56},{8,0},{16,8},{24,16},{32,24},{40,32},{48,40},{56,48},{1,57}... | collective-permute-start | bytes 393224 | tf_op jit(solution)/shard_map/ppermute | solution.py:27
  68.6 4.7 %collective-permute-start.12 = (f32[256,1152]{1,0:T(8,128)S(1)}, f32[256,1152]{1,0:T(8,128)S(1)}, u32[]{:S(2)}, u32[]{:S(2)}) collective-permute-start(f32[256,1152]{1,0:T(8,128)S(1)} %shard_map.87), channel_id=1, source_target_pairs={{0,1},{1,0},{2,3},{3,2},{4,5},{5,4},{6,7},{7,6},{8,9},{9,8},{10,11... | collective-permute-start | bytes 3538952 | tf_op jit(solution)/shard_map/ppermute | solution.py:22
  74.3 23.4 %all-to-all-start = ((f16[4,64,1152]{2,1,0:T(8,128)(2,1)}), f16[4,64,1152]{2,1,0:T(8,128)(2,1)S(1)}, u32[]{:S(2)}, u32[]{:S(2)}) async-start(f16[4,64,1152]{2,1,0:T(8,128)(2,1)} %bitcast.7), calls=%async_computation | async-start | bytes 1179648 | tf_op jit(solution)/shard_map/all_to_all | solution.py:189
  114.8 17.1 %copy-start = (bf16[56,1024]{1,0:T(8,128)(2,1)S(1)}, bf16[56,1024]{1,0:T(8,128)(2,1)}, u32[]{:S(2)}) copy-start(bf16[56,1024]{1,0:T(8,128)(2,1)} %up_probe.1) | copy-start | bytes 344068
  114.8 17.0 %copy-start.1 = (bf16[56,1024]{1,0:T(8,128)(2,1)S(1)}, bf16[56,1024]{1,0:T(8,128)(2,1)}, u32[]{:S(2)}) copy-start(bf16[56,1024]{1,0:T(8,128)(2,1)} %gate_probe.1) | copy-start | bytes 344068

commit v12 on v11

--- a/solution.py
+++ b/solution.py
@@ -15,6 +15,7 @@
 BACK_SCALE = 32.0
 
 VMEM = pl.BlockSpec(memory_space=pltpu.VMEM)
+ANY = pl.BlockSpec(memory_space=pl.ANY)
 SMEM = pl.BlockSpec(memory_space=pltpu.SMEM)
 
 
@@ -40,6 +41,25 @@
         interpret=interpret,
         **options,
     )(*args)
+
+
+def pass_kernel(value, *rest):
+    pass
+
+
+def after(value, others, interpret):
+    return local_call(
+        pass_kernel,
+        jax.ShapeDtypeStruct(value.shape, value.dtype),
+        0,
+        0,
+        interpret,
+        value,
+        *others,
+        in_specs=[ANY] * (1 + len(others)),
+        out_specs=ANY,
+        input_output_aliases={0: 0},
+    )
 
 
 def terms_kernel(tok_rows, place, tokens, cotangents, *refs):
@@ -152,9 +172,9 @@
     mats = stacked(
         [gate_weight, up_weight, gate_probe, up_probe, down_weight], tok_rows + cot_rows
     )
-    beside = mix(mats, "x", 1)
-    weights = [mats, beside, mix(mats, "x", 3), mix(beside, "x", 3)]
-
+    weights = [mats] + [mix(mats, "x", by) for by in (1, 3, 2)]
+
+    block = after(block, [mats], interpret)
     ahead = behind = block
     blocks = [block]
     for _ in range(ny // 2 - 1):

time: 133 us -> 133 us (level)
  local copies, waits for them, and re-layouts: 1.14 us -> 3.11 us
  starting transfers between devices: 60.1 us -> 58.5 us
    ppermute x3, starting transfers between devices: 12.1 us -> 9.96 us  [mix(): lax.ppermute(value, axis, [(i, i ^ by) for i in range(lax.axis_size(axis))])]
    unnamed x11 -> x12, local copies, waits for them, and re-layouts: 1.12 us -> 3.08 us
    pallas_call x5 -> x6, Pallas kernels: 4.83 us -> 4.85 us  [local_call(): pl.pallas_call(body, out_shape=out_shape, cost_estimate=pl.CostEstimate(f...]
  transfers between devices with their start and end apart: 14 -> 14, of which waited for: 7 -> 7; matrix products, arithmetic and copies ran while one was open for 2% -> 3% of each run, Pallas kernels for 1% -> 1%
where the time goes in v12:
time: 133 us
  starting transfers between devices  58.5 us (44%)
  blocking collectives  32.8 us (25%)
  waiting for transfers between devices  28.8 us (22%)
  Pallas kernels  4.85 us (4%)
  other arithmetic  3.8 us (3%)
  local copies, waits for them, and re-layouts  3.11 us (2%)
    ppermute x8, starting transfers between devices, shift(): lax.ppermute(value, axis, [(i, (i + by) % size) for i in range(size)])  28.6 us
    all_to_all x1, blocking collectives, on_device(): away = lax.all_to_all(away, 'x', 0, 0, tiled=True)  18 us
    all_to_all x1, waiting for transfers between devices, on_device(): got = lax.all_to_all(sent, 'zl', 0, 0, tiled=True)  16.2 us
    all_gather x1, blocking collectives, on_device(): fac = lax.all_gather(fac, ('zl', 'c'), axis=1, tiled=True)  14.8 us
    ppermute x2, starting transfers between devices, swap(): return lax.ppermute(value, axis, [(0, 1), (1, 0)])  12.8 us
    ppermute x3, starting transfers between devices, mix(): lax.ppermute(value, axis, [(i, i ^ by) for i in range(lax.axis_size(axis))])  9.96 us
    ppermute x8, waiting for transfers between devices, shift(): lax.ppermute(value, axis, [(i, (i + by) % size) for i in range(size)])  8.23 us
    all_to_all x1, starting transfers between devices, on_device(): got = lax.all_to_all(sent, 'zl', 0, 0, tiled=True)  7.09 us
  transfers between devices with their start and end apart: 14, of which 7 were waited for; matrix products, arithmetic and copies ran while one was open for 3% of the time, Pallas kernels for 1%

profile of v12, /device:TPU:24, one launch (start us, length us, event | category | flops | bytes accessed | tf_op | source)
XLA Modules:
  0.0 132.7 jit_solution(10734068208661616658)
XLA Ops:
  0.6 0.9 fusion
  1.5 10.9 %collective-permute-start = (bf16[64,1024]{1,0:T(8,128)(2,1)S(1)}, bf16[64,1024]{1,0:T(8,128)(2,1)S(1)}, u32[]{:S(2)}, u32[]{:S(2)}) collective-permute-start(bf16[64,1024]{1,0:T(8,128)(2,1)S(1)} %get-tuple-element.25), channel_id=1, source_target_pairs={{0,256},{256,0},{1,257},{257,1},{2,258},{258,2},{3,259},{259,3},{4... | collective-permute-start | bytes 393224 | tf_op jit(solution)/shard_map/ppermute | solution.py:23
  12.5 1.2 pad_add_fusion.rest_0_.refs_0_
  13.6 2.4 %collective-permute-done = bf16[64,1024]{1,0:T(8,128)(2,1)S(1)} collective-permute-done((bf16[64,1024]{1,0:T(8,128)(2,1)S(1)}, bf16[64,1024]{1,0:T(8,128)(2,1)S(1)}, u32[]{:S(2)}, u32[]{:S(2)}) %collective-permute-start) | collective-permute-done | bytes 131104 | tf_op jit(solution)/shard_map/ppermute | solution.py:23
  16.0 0.7 pad_maximum_fusion.value
  16.7 4.7 %collective-permute-start.1 = (bf16[2,64,1024]{2,1,0:T(8,128)(2,1)}, bf16[2,64,1024]{2,1,0:T(8,128)(2,1)}, u32[]{:S(2)}, u32[]{:S(2)}) collective-permute-start(bf16[2,64,1024]{2,1,0:T(8,128)(2,1)} %shard_map.86), channel_id=1, source_target_pairs={{0,8},{8,16},{16,24},{24,32},{32,40},{40,48},{48,56},{56,0},{1,9},... | collective-permute-start | bytes 786440 | tf_op jit(solution)/shard_map/ppermute | solution.py:28
  21.4 1.9 %collective-permute-start.2 = (bf16[2,64,1024]{2,1,0:T(8,128)(2,1)}, bf16[2,64,1024]{2,1,0:T(8,128)(2,1)}, u32[]{:S(2)}, u32[]{:S(2)}) collective-permute-start(bf16[2,64,1024]{2,1,0:T(8,128)(2,1)} %shard_map.86), channel_id=1, source_target_pairs={{0,56},{8,0},{16,8},{24,16},{32,24},{40,32},{48,40},{56,48},{1,57}... | collective-permute-start | bytes 786440 | tf_op jit(solution)/shard_map/ppermute | solution.py:28
  23.4 3.4 %collective-permute-start.9 = (bf16[288,1024]{1,0:T(8,128)(2,1)S(1)}, bf16[288,1024]{1,0:T(8,128)(2,1)S(1)}, u32[]{:S(2)}, u32[]{:S(2)}) collective-permute-start(bf16[288,1024]{1,0:T(8,128)(2,1)S(1)} %pad_add_fusion.rest_0_.refs_0_), channel_id=1, source_target_pairs={{0,64},{64,0},{128,192},{192,128},{1,65},{65,1},{129,193},{193,129... | collective-permute-start | bytes 1769480 | tf_op jit(solution)/shard_map/ppermute | solution.py:32
  26.8 4.0 %collective-permute-start.10 = (bf16[288,1024]{1,0:T(8,128)(2,1)S(1)}, bf16[288,1024]{1,0:T(8,128)(2,1)S(1)}, u32[]{:S(2)}, u32[]{:S(2)}) collective-permute-start(bf16[288,1024]{1,0:T(8,128)(2,1)S(1)} %pad_add_fusion.rest_0_.refs_0_), channel_id=1, source_target_pairs={{0,192},{64,128},{128,64},{192,0},{1,193},{65,129},{129,65},{193,1... | collective-permute-start | bytes 1769480 | tf_op jit(solution)/shard_map/ppermute | solution.py:32
  30.8 2.6 %collective-permute-start.11 = (bf16[288,1024]{1,0:T(8,128)(2,1)S(1)}, bf16[288,1024]{1,0:T(8,128)(2,1)S(1)}, u32[]{:S(2)}, u32[]{:S(2)}) collective-permute-start(bf16[288,1024]{1,0:T(8,128)(2,1)S(1)} %pad_add_fusion.rest_0_.refs_0_), channel_id=1, source_target_pairs={{0,128},{64,192},{128,0},{192,64},{1,129},{65,193},{129,1},{193,65... | collective-permute-start | bytes 1769480 | tf_op jit(solution)/shard_map/ppermute | solution.py:32
  33.4 1.0 slice_dynamic-update-slice_fusion.6
  34.4 0.0 collective-permute-done.1
  34.4 5.1 %collective-permute-start.3 = (bf16[2,64,1024]{2,1,0:T(8,128)(2,1)}, bf16[2,64,1024]{2,1,0:T(8,128)(2,1)S(1)}, u32[]{:S(2)}, u32[]{:S(2)}) collective-permute-start(bf16[2,64,1024]{2,1,0:T(8,128)(2,1)} %collective-permute-done.1), channel_id=1, source_target_pairs={{0,8},{8,16},{16,24},{24,32},{32,40},{40,48},{48,56},{56,0},{1,9},... | collective-permute-start | bytes 786440 | tf_op jit(solution)/shard_map/ppermute | solution.py:28
  39.5 0.0 collective-permute-done.2
  39.5 1.9 %collective-permute-start.4 = (bf16[2,64,1024]{2,1,0:T(8,128)(2,1)}, bf16[2,64,1024]{2,1,0:T(8,128)(2,1)S(1)}, u32[]{:S(2)}, u32[]{:S(2)}) collective-permute-start(bf16[2,64,1024]{2,1,0:T(8,128)(2,1)} %collective-permute-done.2), channel_id=1, source_target_pairs={{0,56},{8,0},{16,8},{24,16},{32,24},{40,32},{48,40},{56,48},{1,57}... | collective-permute-start | bytes 786440 | tf_op jit(solution)/shard_map/ppermute | solution.py:28
  41.4 1.0 slice_dynamic-update-slice_fusion.5
  42.4 1.0 slice_dynamic-update-slice_fusion.4
  43.4 0.2 collective-permute-done.3
  43.7 5.5 %collective-permute-start.5 = (bf16[2,64,1024]{2,1,0:T(8,128)(2,1)S(1)}, bf16[2,64,1024]{2,1,0:T(8,128)(2,1)S(1)}, u32[]{:S(2)}, u32[]{:S(2)}) collective-permute-start(bf16[2,64,1024]{2,1,0:T(8,128)(2,1)S(1)} %collective-permute-done.3), channel_id=1, source_target_pairs={{0,8},{8,16},{16,24},{24,32},{32,40},{40,48},{48,56},{56,0},{1,9},... | collective-permute-start | bytes 786440 | tf_op jit(solution)/shard_map/ppermute | solution.py:28
  49.2 0.0 collective-permute-done.4
  49.2 1.9 %collective-permute-start.6 = (bf16[2,64,1024]{2,1,0:T(8,128)(2,1)S(1)}, bf16[2,64,1024]{2,1,0:T(8,128)(2,1)S(1)}, u32[]{:S(2)}, u32[]{:S(2)}) collective-permute-start(bf16[2,64,1024]{2,1,0:T(8,128)(2,1)S(1)} %collective-permute-done.4), channel_id=1, source_target_pairs={{0,56},{8,0},{16,8},{24,16},{32,24},{40,32},{48,40},{56,48},{1,57}... | collective-permute-start | bytes 786440 | tf_op jit(solution)/shard_map/ppermute | solution.py:28
  51.2 1.9 %collective-permute-done.5 = bf16[2,64,1024]{2,1,0:T(8,128)(2,1)S(1)} collective-permute-done((bf16[2,64,1024]{2,1,0:T(8,128)(2,1)S(1)}, bf16[2,64,1024]{2,1,0:T(8,128)(2,1)S(1)}, u32[]{:S(2)}, u32[]{:S(2)}) %collective-permute-start.5) | collective-permute-done | bytes 262176 | tf_op jit(solution)/shard_map/ppermute | solution.py:28
  53.1 5.6 %collective-permute-start.7 = (bf16[1,64,1024]{2,1,0:T(8,128)(2,1)S(1)}, bf16[1,64,1024]{2,1,0:T(8,128)(2,1)S(1)}, u32[]{:S(2)}, u32[]{:S(2)}) collective-permute-start(bf16[1,64,1024]{2,1,0:T(8,128)(2,1)S(1)} %slice.87), channel_id=1, source_target_pairs={{0,8},{8,16},{16,24},{24,32},{32,40},{40,48},{48,56},{56,0},{1,9},... | collective-permute-start | bytes 393224 | tf_op jit(solution)/shard_map/ppermute | solution.py:28
  58.7 0.0 collective-permute-done.6
  58.7 1.9 %collective-permute-start.8 = (bf16[1,64,1024]{2,1,0:T(8,128)(2,1)S(1)}, bf16[1,64,1024]{2,1,0:T(8,128)(2,1)S(1)}, u32[]{:S(2)}, u32[]{:S(2)}) collective-permute-start(bf16[1,64,1024]{2,1,0:T(8,128)(2,1)S(1)} %slice.89), channel_id=1, source_target_pairs={{0,56},{8,0},{16,8},{24,16},{32,24},{40,32},{48,40},{56,48},{1,57}... | collective-permute-start | bytes 393224 | tf_op jit(solution)/shard_map/ppermute | solution.py:28
  60.7 0.5 collective-permute-done.7
  61.2 5.6 %collective-permute-done.8 = bf16[1,64,1024]{2,1,0:T(8,128)(2,1)S(1)} collective-permute-done((bf16[1,64,1024]{2,1,0:T(8,128)(2,1)S(1)}, bf16[1,64,1024]{2,1,0:T(8,128)(2,1)S(1)}, u32[]{:S(2)}, u32[]{:S(2)}) %collective-permute-start.8) | collective-permute-done | bytes 131104 | tf_op jit(solution)/shard_map/ppermute | solution.py:28
  66.8 0.0 collective-permute-done.9.refs_1_
  66.8 0.0 collective-permute-done.10.refs_2_
  66.8 0.0 collective-permute-done.11.refs_3_
  66.8 0.9 shard_map.88
  67.7 1.9 %collective-permute-start.12 = (f32[256,1152]{1,0:T(8,128)S(1)}, f32[256,1152]{1,0:T(8,128)S(1)}, u32[]{:S(2)}, u32[]{:S(2)}) collective-permute-start(f32[256,1152]{1,0:T(8,128)S(1)} %shard_map.88), channel_id=1, source_target_pairs={{0,1},{1,0},{2,3},{3,2},{4,5},{5,4},{6,7},{7,6},{8,9},{9,8},{10,11... | collective-permute-start | bytes 3538952 | tf_op jit(solution)/shard_map/ppermute | solution.py:23
  69.6 0.9 shard_map.87
  70.5 1.9 %collective-permute-done.12 = f32[256,1152]{1,0:T(8,128)S(1)} collective-permute-done((f32[256,1152]{1,0:T(8,128)S(1)}, f32[256,1152]{1,0:T(8,128)S(1)}, u32[]{:S(2)}, u32[]{:S(2)}) %collective-permute-start.12) | collective-permute-done | bytes 1179680 | tf_op jit(solution)/shard_map/ppermute | solution.py:23
  72.5 1.0 add_convert_fusion
  73.4 7.1 %all-to-all-start = ((f16[4,64,1152]{2,1,0:T(8,128)(2,1)}), f16[4,64,1152]{2,1,0:T(8,128)(2,1)S(1)}, u32[]{:S(2)}, u32[]{:S(2)}) async-start(f16[4,64,1152]{2,1,0:T(8,128)(2,1)} %bitcast.7), calls=%async_computation | async-start | bytes 1179648 | tf_op jit(solution)/shard_map/all_to_all | solution.py:209
  80.5 16.2 %all-to-all-done = f16[4,64,1152]{2,1,0:T(8,128)(2,1)S(1)} async-done(((f16[4,64,1152]{2,1,0:T(8,128)(2,1)}), f16[4,64,1152]{2,1,0:T(8,128)(2,1)S(1)}, u32[]{:S(2)}, u32[]{:S(2)}) %all-to-all-start) | async-done | bytes 589856 | tf_op jit(solution)/shard_map/all_to_all | solution.py:209
  96.7 0.1 convert_reduce_fusion.proj
  96.8 0.7 shard_map.89
  97.5 14.8 %all_gather.3.fac = bf16[64,4096]{1,0:T(8,128)(2,1)S(1)} all-gather(bf16[64,512]{1,0:T(8,128)(2,1)S(1)} %shard_map.89), channel_id=1, replica_groups=mesh['zh'=2,'x'=4,'y'=8,'zl'=4,'c'=2] {'zl','c'}, dimensions={1}, use_global_device_ids=true | all-gather | bytes 589824 | tf_op jit(solution)/shard_map/all_gather | solution.py:223
  112.4 1.4 %shard_map.90 = (bf16[4,112,1024]{2,1,0:T(8,128)(2,1)S(1)}, f32[112,1024]{1,0:T(8,128)S(1)}) custom-call(s32[1]{0:T(128)} %bitcast.place, bf16[64,4096]{1,0:T(8,128)(2,1)S(1)} %all_gather.3.fac, bf16[512,1024]{1,0:T(8,128)(2,1)S(1)} %bitcast.13), custom_call_target="tpu_custom_call" | custom-call | flops 469762048 | bytes 1048576 | tf_op jit(solution)/shard_map/pallas_call | solution.py:36
  113.8 0.0 copy-start
  113.8 0.0 copy-start.1
  113.8 18.0 %all_to_all.10.away = bf16[4,112,1024]{2,1,0:T(8,128)(2,1)S(1)} all-to-all(bf16[4,112,1024]{2,1,0:T(8,128)(2,1)S(1)} %get-tuple-element.4), channel_id=1, replica_groups=mesh['zh'=2,'x'=4,'y'=8,'zl'=4,'c'=2] {'x'}, dimensions={0} | all-to-all | bytes 1835008 | tf_op jit(solution)/shard_map/all_to_all | solution.py:240
  131.8 0.0 copy-done
  131.8 0.0 copy-done.1
  131.8 0.9 shard_map.91
  (9 shorter events, 0.1 us)
Async XLA Ops:
  1.5 14.5 %collective-permute-start = (bf16[64,1024]{1,0:T(8,128)(2,1)S(1)}, bf16[64,1024]{1,0:T(8,128)(2,1)S(1)}, u32[]{:S(2)}, u32[]{:S(2)}) collective-permute-start(bf16[64,1024]{1,0:T(8,128)(2,1)S(1)} %get-tuple-element.25), channel_id=1, source_target_pairs={{0,256},{256,0},{1,257},{257,1},{2,258},{258,2},{3,259},{259,3},{4... | collective-permute-start | bytes 393224 | tf_op jit(solution)/shard_map/ppermute | solution.py:23
  16.7 17.6 %collective-permute-start.1 = (bf16[2,64,1024]{2,1,0:T(8,128)(2,1)}, bf16[2,64,1024]{2,1,0:T(8,128)(2,1)}, u32[]{:S(2)}, u32[]{:S(2)}) collective-permute-start(bf16[2,64,1024]{2,1,0:T(8,128)(2,1)} %shard_map.86), channel_id=1, source_target_pairs={{0,8},{8,16},{16,24},{24,32},{32,40},{40,48},{48,56},{56,0},{1,9},... | collective-permute-start | bytes 786440 | tf_op jit(solution)/shard_map/ppermute | solution.py:28
  21.4 18.1 %collective-permute-start.2 = (bf16[2,64,1024]{2,1,0:T(8,128)(2,1)}, bf16[2,64,1024]{2,1,0:T(8,128)(2,1)}, u32[]{:S(2)}, u32[]{:S(2)}) collective-permute-start(bf16[2,64,1024]{2,1,0:T(8,128)(2,1)} %shard_map.86), channel_id=1, source_target_pairs={{0,56},{8,0},{16,8},{24,16},{32,24},{40,32},{48,40},{56,48},{1,57}... | collective-permute-start | bytes 786440 | tf_op jit(solution)/shard_map/ppermute | solution.py:28
  23.4 43.4 %collective-permute-start.9 = (bf16[288,1024]{1,0:T(8,128)(2,1)S(1)}, bf16[288,1024]{1,0:T(8,128)(2,1)S(1)}, u32[]{:S(2)}, u32[]{:S(2)}) collective-permute-start(bf16[288,1024]{1,0:T(8,128)(2,1)S(1)} %pad_add_fusion.rest_0_.refs_0_), channel_id=1, source_target_pairs={{0,64},{64,0},{128,192},{192,128},{1,65},{65,1},{129,193},{193,129... | collective-permute-start | bytes 1769480 | tf_op jit(solution)/shard_map/ppermute | solution.py:32
  26.8 40.0 %collective-permute-start.10 = (bf16[288,1024]{1,0:T(8,128)(2,1)S(1)}, bf16[288,1024]{1,0:T(8,128)(2,1)S(1)}, u32[]{:S(2)}, u32[]{:S(2)}) collective-permute-start(bf16[288,1024]{1,0:T(8,128)(2,1)S(1)} %pad_add_fusion.rest_0_.refs_0_), channel_id=1, source_target_pairs={{0,192},{64,128},{128,64},{192,0},{1,193},{65,129},{129,65},{193,1... | collective-permute-start | bytes 1769480 | tf_op jit(solution)/shard_map/ppermute | solution.py:32
  30.8 36.0 %collective-permute-start.11 = (bf16[288,1024]{1,0:T(8,128)(2,1)S(1)}, bf16[288,1024]{1,0:T(8,128)(2,1)S(1)}, u32[]{:S(2)}, u32[]{:S(2)}) collective-permute-start(bf16[288,1024]{1,0:T(8,128)(2,1)S(1)} %pad_add_fusion.rest_0_.refs_0_), channel_id=1, source_target_pairs={{0,128},{64,192},{128,0},{192,64},{1,129},{65,193},{129,1},{193,65... | collective-permute-start | bytes 1769480 | tf_op jit(solution)/shard_map/ppermute | solution.py:32
  34.4 9.3 %collective-permute-start.3 = (bf16[2,64,1024]{2,1,0:T(8,128)(2,1)}, bf16[2,64,1024]{2,1,0:T(8,128)(2,1)S(1)}, u32[]{:S(2)}, u32[]{:S(2)}) collective-permute-start(bf16[2,64,1024]{2,1,0:T(8,128)(2,1)} %collective-permute-done.1), channel_id=1, source_target_pairs={{0,8},{8,16},{16,24},{24,32},{32,40},{40,48},{48,56},{56,0},{1,9},... | collective-permute-start | bytes 786440 | tf_op jit(solution)/shard_map/ppermute | solution.py:28
  39.5 9.7 %collective-permute-start.4 = (bf16[2,64,1024]{2,1,0:T(8,128)(2,1)}, bf16[2,64,1024]{2,1,0:T(8,128)(2,1)S(1)}, u32[]{:S(2)}, u32[]{:S(2)}) collective-permute-start(bf16[2,64,1024]{2,1,0:T(8,128)(2,1)} %collective-permute-done.2), channel_id=1, source_target_pairs={{0,56},{8,0},{16,8},{24,16},{32,24},{40,32},{48,40},{56,48},{1,57}... | collective-permute-start | bytes 786440 | tf_op jit(solution)/shard_map/ppermute | solution.py:28
  43.7 9.4 %collective-permute-start.5 = (bf16[2,64,1024]{2,1,0:T(8,128)(2,1)S(1)}, bf16[2,64,1024]{2,1,0:T(8,128)(2,1)S(1)}, u32[]{:S(2)}, u32[]{:S(2)}) collective-permute-start(bf16[2,64,1024]{2,1,0:T(8,128)(2,1)S(1)} %collective-permute-done.3), channel_id=1, source_target_pairs={{0,8},{8,16},{16,24},{24,32},{32,40},{40,48},{48,56},{56,0},{1,9},... | collective-permute-start | bytes 786440 | tf_op jit(solution)/shard_map/ppermute | solution.py:28
  49.2 9.5 %collective-permute-start.6 = (bf16[2,64,1024]{2,1,0:T(8,128)(2,1)S(1)}, bf16[2,64,1024]{2,1,0:T(8,128)(2,1)S(1)}, u32[]{:S(2)}, u32[]{:S(2)}) collective-permute-start(bf16[2,64,1024]{2,1,0:T(8,128)(2,1)S(1)} %collective-permute-done.4), channel_id=1, source_target_pairs={{0,56},{8,0},{16,8},{24,16},{32,24},{40,32},{48,40},{56,48},{1,57}... | collective-permute-start | bytes 786440 | tf_op jit(solution)/shard_map/ppermute | solution.py:28
  53.1 8.1 %collective-permute-start.7 = (bf16[1,64,1024]{2,1,0:T(8,128)(2,1)S(1)}, bf16[1,64,1024]{2,1,0:T(8,128)(2,1)S(1)}, u32[]{:S(2)}, u32[]{:S(2)}) collective-permute-start(bf16[1,64,1024]{2,1,0:T(8,128)(2,1)S(1)} %slice.87), channel_id=1, source_target_pairs={{0,8},{8,16},{16,24},{24,32},{32,40},{40,48},{48,56},{56,0},{1,9},... | collective-permute-start | bytes 393224 | tf_op jit(solution)/shard_map/ppermute | solution.py:28
  58.7 8.1 %collective-permute-start.8 = (bf16[1,64,1024]{2,1,0:T(8,128)(2,1)S(1)}, bf16[1,64,1024]{2,1,0:T(8,128)(2,1)S(1)}, u32[]{:S(2)}, u32[]{:S(2)}) collective-permute-start(bf16[1,64,1024]{2,1,0:T(8,128)(2,1)S(1)} %slice.89), channel_id=1, source_target_pairs={{0,56},{8,0},{16,8},{24,16},{32,24},{40,32},{48,40},{56,48},{1,57}... | collective-permute-start | bytes 393224 | tf_op jit(solution)/shard_map/ppermute | solution.py:28
  67.7 4.7 %collective-permute-start.12 = (f32[256,1152]{1,0:T(8,128)S(1)}, f32[256,1152]{1,0:T(8,128)S(1)}, u32[]{:S(2)}, u32[]{:S(2)}) collective-permute-start(f32[256,1152]{1,0:T(8,128)S(1)} %shard_map.88), channel_id=1, source_target_pairs={{0,1},{1,0},{2,3},{3,2},{4,5},{5,4},{6,7},{7,6},{8,9},{9,8},{10,11... | collective-permute-start | bytes 3538952 | tf_op jit(solution)/shard_map/ppermute | solution.py:23
  73.4 23.3 %all-to-all-start = ((f16[4,64,1152]{2,1,0:T(8,128)(2,1)}), f16[4,64,1152]{2,1,0:T(8,128)(2,1)S(1)}, u32[]{:S(2)}, u32[]{:S(2)}) async-start(f16[4,64,1152]{2,1,0:T(8,128)(2,1)} %bitcast.7), calls=%async_computation | async-start | bytes 1179648 | tf_op jit(solution)/shard_map/all_to_all | solution.py:209
  113.8 18.0 %copy-start = (bf16[56,1024]{1,0:T(8,128)(2,1)S(1)}, bf16[56,1024]{1,0:T(8,128)(2,1)}, u32[]{:S(2)}) copy-start(bf16[56,1024]{1,0:T(8,128)(2,1)} %up_probe.1) | copy-start | bytes 344068
  113.8 18.0 %copy-start.1 = (bf16[56,1024]{1,0:T(8,128)(2,1)S(1)}, bf16[56,1024]{1,0:T(8,128)(2,1)}, u32[]{:S(2)}) copy-start(bf16[56,1024]{1,0:T(8,128)(2,1)} %gate_probe.1) | copy-start | bytes 344068

commit v13 on v12

--- a/solution.py
+++ b/solution.py
@@ -174,10 +174,11 @@
     )
     weights = [mats] + [mix(mats, "x", by) for by in (1, 3, 2)]
 
-    block = after(block, [mats], interpret)
     ahead = behind = block
     blocks = [block]
-    for _ in range(ny // 2 - 1):
+    for step in range(ny // 2 - 1):
+        if step == 1:
+            ahead = after(ahead, weights[1:2], interpret)
         ahead, behind = shift(ahead, "y", 1), shift(behind, "y", -1)
         blocks += [ahead, behind]
     blocks += [shift(ahead[:1], "y", 1), shift(behind[1:], "y", -1)]

time: 133 us -> 134 us (level)
  the two profiles are of different devices: /device:TPU:24 before, /device:TPU:1 now
where the time goes in v13:
time: 134 us; the launch traced here: 133 us
  starting transfers between devices  61.9 us (46%)
  blocking collectives  33.1 us (25%)
  waiting for transfers between devices  23.5 us (18%)
  Pallas kernels  7.31 us (5%)
  other arithmetic  3.18 us (2%)
  local copies, waits for them, and re-layouts  3.09 us (2%)
    ppermute x8, starting transfers between devices, shift(): lax.ppermute(value, axis, [(i, (i + by) % size) for i in range(size)])  27.8 us
    ppermute x2, starting transfers between devices, swap(): return lax.ppermute(value, axis, [(0, 1), (1, 0)])  18.2 us
    all_to_all x1, blocking collectives, on_device(): away = lax.all_to_all(away, 'x', 0, 0, tiled=True)  17 us
    all_gather x1, blocking collectives, on_device(): fac = lax.all_gather(fac, ('zl', 'c'), axis=1, tiled=True)  16.1 us
    all_to_all x1, waiting for transfers between devices, on_device(): got = lax.all_to_all(sent, 'zl', 0, 0, tiled=True)  15.4 us
    ppermute x3, starting transfers between devices, mix(): lax.ppermute(value, axis, [(i, i ^ by) for i in range(lax.axis_size(axis))])  9.4 us
    ppermute x8, waiting for transfers between devices, shift(): lax.ppermute(value, axis, [(i, (i + by) % size) for i in range(size)])  7.74 us
    pallas_call x6, Pallas kernels, local_call(): pl.pallas_call(body, out_shape=out_shape, cost_estimate=pl.CostEstimate(f...  7.31 us
  transfers between devices with their start and end apart: 14, of which 4 were waited for; matrix products, arithmetic and copies ran while one was open for 3% of the time, Pallas kernels for 2%

profile of v13, /device:TPU:1, one launch (start us, length us, event | category | flops | bytes accessed | tf_op | source)
XLA Modules:
  0.0 133.1 jit_solution(18347314621649567868)
XLA Ops:
  0.6 0.9 pad_add_fusion.1
  1.5 11.5 %collective-permute-start = (bf16[64,1024]{1,0:T(8,128)(2,1)S(1)}, bf16[64,1024]{1,0:T(8,128)(2,1)S(1)}, u32[]{:S(2)}, u32[]{:S(2)}) collective-permute-start(bf16[64,1024]{1,0:T(8,128)(2,1)S(1)} %get-tuple-element.24), channel_id=1, source_target_pairs={{0,256},{256,0},{1,257},{257,1},{2,258},{258,2},{3,259},{259,3},{4... | collective-permute-start | bytes 393224 | tf_op jit(solution)/shard_map/ppermute | solution.py:23
  13.0 1.2 pad_add_fusion.refs_0_
  14.2 3.1 %collective-permute-start.3 = (bf16[288,1024]{1,0:T(8,128)(2,1)S(1)}, bf16[288,1024]{1,0:T(8,128)(2,1)S(1)}, u32[]{:S(2)}, u32[]{:S(2)}) collective-permute-start(bf16[288,1024]{1,0:T(8,128)(2,1)S(1)} %pad_add_fusion.refs_0_), channel_id=1, source_target_pairs={{0,64},{64,0},{128,192},{192,128},{1,65},{65,1},{129,193},{193,129... | collective-permute-start | bytes 1769480 | tf_op jit(solution)/shard_map/ppermute | solution.py:32
  17.3 0.0 collective-permute-done
  17.3 5.1 %collective-permute-start.2 = (bf16[2,64,1024]{2,1,0:T(8,128)(2,1)S(1)}, bf16[2,64,1024]{2,1,0:T(8,128)(2,1)}, u32[]{:S(2)}, u32[]{:S(2)}) collective-permute-start(bf16[2,64,1024]{2,1,0:T(8,128)(2,1)S(1)} %pad_maximum_fusion), channel_id=1, source_target_pairs={{0,56},{8,0},{16,8},{24,16},{32,24},{40,32},{48,40},{56,48},{1,57}... | collective-permute-start | bytes 786440 | tf_op jit(solution)/shard_map/ppermute | solution.py:28
  22.4 1.9 %collective-permute-start.1 = (bf16[2,64,1024]{2,1,0:T(8,128)(2,1)S(1)}, bf16[2,64,1024]{2,1,0:T(8,128)(2,1)S(1)}, u32[]{:S(2)}, u32[]{:S(2)}) collective-permute-start(bf16[2,64,1024]{2,1,0:T(8,128)(2,1)S(1)} %pad_maximum_fusion), channel_id=1, source_target_pairs={{0,8},{8,16},{16,24},{24,32},{32,40},{40,48},{48,56},{56,0},{1,9},... | collective-permute-start | bytes 786440 | tf_op jit(solution)/shard_map/ppermute | solution.py:28
  24.4 2.4 %collective-permute-done.2 = bf16[2,64,1024]{2,1,0:T(8,128)(2,1)} collective-permute-done((bf16[2,64,1024]{2,1,0:T(8,128)(2,1)S(1)}, bf16[2,64,1024]{2,1,0:T(8,128)(2,1)}, u32[]{:S(2)}, u32[]{:S(2)}) %collective-permute-start.2) | collective-permute-done | bytes 262176 | tf_op jit(solution)/shard_map/ppermute | solution.py:28
  26.8 5.4 %collective-permute-start.5 = (bf16[2,64,1024]{2,1,0:T(8,128)(2,1)}, bf16[2,64,1024]{2,1,0:T(8,128)(2,1)}, u32[]{:S(2)}, u32[]{:S(2)}) collective-permute-start(bf16[2,64,1024]{2,1,0:T(8,128)(2,1)} %collective-permute-done.2), channel_id=1, source_target_pairs={{0,56},{8,0},{16,8},{24,16},{32,24},{40,32},{48,40},{56,48},{1,57}... | collective-permute-start | bytes 786440 | tf_op jit(solution)/shard_map/ppermute | solution.py:28
  32.2 0.0 collective-permute-done.1.value
  32.2 0.0 collective-permute-done.3.rest_0_.refs_1_
  32.3 1.9 %collective-permute-start.4 = (bf16[2,64,1024]{2,1,0:T(8,128)(2,1)S(1)}, bf16[2,64,1024]{2,1,0:T(8,128)(2,1)}, u32[]{:S(2)}, u32[]{:S(2)}) collective-permute-start(bf16[2,64,1024]{2,1,0:T(8,128)(2,1)S(1)} %shard_map.86), channel_id=1, source_target_pairs={{0,8},{8,16},{16,24},{24,32},{32,40},{40,48},{48,56},{56,0},{1,9},... | collective-permute-start | bytes 786440 | tf_op jit(solution)/shard_map/ppermute | solution.py:28
  34.2 3.7 %collective-permute-start.10 = (bf16[288,1024]{1,0:T(8,128)(2,1)S(1)}, bf16[288,1024]{1,0:T(8,128)(2,1)}, u32[]{:S(2)}, u32[]{:S(2)}) collective-permute-start(bf16[288,1024]{1,0:T(8,128)(2,1)S(1)} %pad_add_fusion.refs_0_), channel_id=1, source_target_pairs={{0,192},{64,128},{128,64},{192,0},{1,193},{65,129},{129,65},{193,1... | collective-permute-start | bytes 1769480 | tf_op jit(solution)/shard_map/ppermute | solution.py:32
  37.9 2.6 %collective-permute-start.11 = (bf16[288,1024]{1,0:T(8,128)(2,1)S(1)}, bf16[288,1024]{1,0:T(8,128)(2,1)}, u32[]{:S(2)}, u32[]{:S(2)}) collective-permute-start(bf16[288,1024]{1,0:T(8,128)(2,1)S(1)} %pad_add_fusion.refs_0_), channel_id=1, source_target_pairs={{0,128},{64,192},{128,0},{192,64},{1,129},{65,193},{129,1},{193,65... | collective-permute-start | bytes 1769480 | tf_op jit(solution)/shard_map/ppermute | solution.py:32
  40.5 1.0 slice_dynamic-update-slice_fusion.4
  41.5 0.0 collective-permute-done.5
  41.5 4.6 %collective-permute-start.7 = (bf16[2,64,1024]{2,1,0:T(8,128)(2,1)}, bf16[2,64,1024]{2,1,0:T(8,128)(2,1)S(1)}, u32[]{:S(2)}, u32[]{:S(2)}) collective-permute-start(bf16[2,64,1024]{2,1,0:T(8,128)(2,1)} %collective-permute-done.5), channel_id=1, source_target_pairs={{0,56},{8,0},{16,8},{24,16},{32,24},{40,32},{48,40},{56,48},{1,57}... | collective-permute-start | bytes 786440 | tf_op jit(solution)/shard_map/ppermute | solution.py:28
  46.1 0.0 collective-permute-done.4
  46.1 1.9 %collective-permute-start.6 = (bf16[2,64,1024]{2,1,0:T(8,128)(2,1)}, bf16[2,64,1024]{2,1,0:T(8,128)(2,1)S(1)}, u32[]{:S(2)}, u32[]{:S(2)}) collective-permute-start(bf16[2,64,1024]{2,1,0:T(8,128)(2,1)} %collective-permute-done.4), channel_id=1, source_target_pairs={{0,8},{8,16},{16,24},{24,32},{32,40},{40,48},{48,56},{56,0},{1,9},... | collective-permute-start | bytes 786440 | tf_op jit(solution)/shard_map/ppermute | solution.py:28
  48.0 1.0 slice_dynamic-update-slice_fusion.3
  49.0 1.0 slice_dynamic-update-slice_fusion.2
  50.0 0.0 collective-permute-done.7
  50.0 5.0 %collective-permute-start.9 = (bf16[1,64,1024]{2,1,0:T(8,128)(2,1)S(1)}, bf16[1,64,1024]{2,1,0:T(8,128)(2,1)S(1)}, u32[]{:S(2)}, u32[]{:S(2)}) collective-permute-start(bf16[1,64,1024]{2,1,0:T(8,128)(2,1)S(1)} %slice.90), channel_id=1, source_target_pairs={{0,56},{8,0},{16,8},{24,16},{32,24},{40,32},{48,40},{56,48},{1,57}... | collective-permute-start | bytes 393224 | tf_op jit(solution)/shard_map/ppermute | solution.py:28
  55.0 0.0 collective-permute-done.6
  55.1 1.9 %collective-permute-start.8 = (bf16[1,64,1024]{2,1,0:T(8,128)(2,1)S(1)}, bf16[1,64,1024]{2,1,0:T(8,128)(2,1)S(1)}, u32[]{:S(2)}, u32[]{:S(2)}) collective-permute-start(bf16[1,64,1024]{2,1,0:T(8,128)(2,1)S(1)} %slice.88), channel_id=1, source_target_pairs={{0,8},{8,16},{16,24},{24,32},{32,40},{40,48},{48,56},{56,0},{1,9},... | collective-permute-start | bytes 393224 | tf_op jit(solution)/shard_map/ppermute | solution.py:28
  57.0 5.3 %collective-permute-done.8 = bf16[1,64,1024]{2,1,0:T(8,128)(2,1)S(1)} collective-permute-done((bf16[1,64,1024]{2,1,0:T(8,128)(2,1)S(1)}, bf16[1,64,1024]{2,1,0:T(8,128)(2,1)S(1)}, u32[]{:S(2)}, u32[]{:S(2)}) %collective-permute-start.8) | collective-permute-done | bytes 131104 | tf_op jit(solution)/shard_map/ppermute | solution.py:28
  62.4 0.0 collective-permute-done.9
  62.4 0.0 collective-permute-done.10.refs_2_
  62.4 0.0 collective-permute-done.11.refs_3_
  62.5 2.1 %shard_map.88 = f32[256,1152]{1,0:T(8,128)S(1)} custom-call(s32[1]{0:T(128)} %bitcast.6.place, bf16[512,1024]{1,0:T(8,128)(2,1)S(1)} %bitcast.11, bf16[512,1024]{1,0:T(8,128)(2,1)S(1)} %bitcast.9, bf16[288,1024]{1,0:T(8,128)(2,1)S(1)} %pad_add_fusion.refs_0_, bf16[288,1024]{1,0:T(8,128)(2,1)S(1)} %collective-permute-done.3.rest_0_.refs_1_, ...), custom_call_target="tpu_custom_call" | custom-call | flops 603979776 | bytes 2359296 | tf_op jit(solution)/shard_map/pallas_call | solution.py:36
  64.6 6.7 %collective-permute-start.12 = (f32[256,1152]{1,0:T(8,128)S(1)}, f32[256,1152]{1,0:T(8,128)S(1)}, u32[]{:S(2)}, u32[]{:S(2)}) collective-permute-start(f32[256,1152]{1,0:T(8,128)S(1)} %shard_map.88), channel_id=1, source_target_pairs={{0,1},{1,0},{2,3},{3,2},{4,5},{5,4},{6,7},{7,6},{8,9},{9,8},{10,11... | collective-permute-start | bytes 3538952 | tf_op jit(solution)/shard_map/ppermute | solution.py:23
  71.3 2.1 %shard_map.87 = f32[256,1152]{1,0:T(8,128)S(1)} custom-call(s32[1]{0:T(128)} %bitcast.1.place, bf16[512,1024]{1,0:T(8,128)(2,1)S(1)} %bitcast.12, bf16[512,1024]{1,0:T(8,128)(2,1)S(1)} %bitcast.10, bf16[288,1024]{1,0:T(8,128)(2,1)S(1)} %pad_add_fusion.refs_0_, bf16[288,1024]{1,0:T(8,128)(2,1)S(1)} %collective-permute-done.3.rest_0_.refs_1_, ...), custom_call_target="tpu_custom_call" | custom-call | flops 603979776 | bytes 2359296 | tf_op jit(solution)/shard_map/pallas_call | solution.py:36
  73.4 0.3 collective-permute-done.12
  73.7 1.0 add_convert_fusion
  74.7 6.6 %all-to-all-start = ((f16[4,64,1152]{2,1,0:T(8,128)(2,1)}), f16[4,64,1152]{2,1,0:T(8,128)(2,1)S(1)}, u32[]{:S(2)}, u32[]{:S(2)}) async-start(f16[4,64,1152]{2,1,0:T(8,128)(2,1)} %bitcast.7), calls=%async_computation | async-start | bytes 1179648 | tf_op jit(solution)/shard_map/all_to_all | solution.py:210
  81.3 15.4 %all-to-all-done = f16[4,64,1152]{2,1,0:T(8,128)(2,1)S(1)} async-done(((f16[4,64,1152]{2,1,0:T(8,128)(2,1)}), f16[4,64,1152]{2,1,0:T(8,128)(2,1)S(1)}, u32[]{:S(2)}, u32[]{:S(2)}) %all-to-all-start) | async-done | bytes 589856 | tf_op jit(solution)/shard_map/all_to_all | solution.py:210
  96.8 0.1 convert_reduce_fusion.proj
  96.9 0.7 shard_map.89
  97.6 16.1 %all_gather.3.fac = bf16[64,4096]{1,0:T(8,128)(2,1)S(1)} all-gather(bf16[64,512]{1,0:T(8,128)(2,1)S(1)} %shard_map.89), channel_id=1, replica_groups=mesh['zh'=2,'x'=4,'y'=8,'zl'=4,'c'=2] {'zl','c'}, dimensions={1}, use_global_device_ids=true | all-gather | bytes 589824 | tf_op jit(solution)/shard_map/all_gather | solution.py:224
  113.7 1.4 %shard_map.90 = (bf16[4,112,1024]{2,1,0:T(8,128)(2,1)S(1)}, f32[112,1024]{1,0:T(8,128)S(1)}) custom-call(s32[1]{0:T(128)} %bitcast.place, bf16[64,4096]{1,0:T(8,128)(2,1)S(1)} %all_gather.3.fac, bf16[512,1024]{1,0:T(8,128)(2,1)S(1)} %bitcast.13), custom_call_target="tpu_custom_call" | custom-call | flops 469762048 | bytes 1048576 | tf_op jit(solution)/shard_map/pallas_call | solution.py:36
  115.1 0.0 copy-start
  115.1 0.0 copy-start.1
  115.1 17.0 %all_to_all.10.away = bf16[4,112,1024]{2,1,0:T(8,128)(2,1)S(1)} all-to-all(bf16[4,112,1024]{2,1,0:T(8,128)(2,1)S(1)} %get-tuple-element.4), channel_id=1, replica_groups=mesh['zh'=2,'x'=4,'y'=8,'zl'=4,'c'=2] {'x'}, dimensions={0} | all-to-all | bytes 1835008 | tf_op jit(solution)/shard_map/all_to_all | solution.py:241
  132.2 0.0 copy-done
  132.2 0.0 copy-done.1
  132.2 0.9 shard_map.91
  (10 shorter events, 0.2 us)
Async XLA Ops:
  1.5 15.8 %collective-permute-start = (bf16[64,1024]{1,0:T(8,128)(2,1)S(1)}, bf16[64,1024]{1,0:T(8,128)(2,1)S(1)}, u32[]{:S(2)}, u32[]{:S(2)}) collective-permute-start(bf16[64,1024]{1,0:T(8,128)(2,1)S(1)} %get-tuple-element.24), channel_id=1, source_target_pairs={{0,256},{256,0},{1,257},{257,1},{2,258},{258,2},{3,259},{259,3},{4... | collective-permute-start | bytes 393224 | tf_op jit(solution)/shard_map/ppermute | solution.py:23
  14.2 18.1 %collective-permute-start.3 = (bf16[288,1024]{1,0:T(8,128)(2,1)S(1)}, bf16[288,1024]{1,0:T(8,128)(2,1)S(1)}, u32[]{:S(2)}, u32[]{:S(2)}) collective-permute-start(bf16[288,1024]{1,0:T(8,128)(2,1)S(1)} %pad_add_fusion.refs_0_), channel_id=1, source_target_pairs={{0,64},{64,0},{128,192},{192,128},{1,65},{65,1},{129,193},{193,129... | collective-permute-start | bytes 1769480 | tf_op jit(solution)/shard_map/ppermute | solution.py:32
  17.3 9.4 %collective-permute-start.2 = (bf16[2,64,1024]{2,1,0:T(8,128)(2,1)S(1)}, bf16[2,64,1024]{2,1,0:T(8,128)(2,1)}, u32[]{:S(2)}, u32[]{:S(2)}) collective-permute-start(bf16[2,64,1024]{2,1,0:T(8,128)(2,1)S(1)} %pad_maximum_fusion), channel_id=1, source_target_pairs={{0,56},{8,0},{16,8},{24,16},{32,24},{40,32},{48,40},{56,48},{1,57}... | collective-permute-start | bytes 786440 | tf_op jit(solution)/shard_map/ppermute | solution.py:28
  22.4 9.8 %collective-permute-start.1 = (bf16[2,64,1024]{2,1,0:T(8,128)(2,1)S(1)}, bf16[2,64,1024]{2,1,0:T(8,128)(2,1)S(1)}, u32[]{:S(2)}, u32[]{:S(2)}) collective-permute-start(bf16[2,64,1024]{2,1,0:T(8,128)(2,1)S(1)} %pad_maximum_fusion), channel_id=1, source_target_pairs={{0,8},{8,16},{16,24},{24,32},{32,40},{40,48},{48,56},{56,0},{1,9},... | collective-permute-start | bytes 786440 | tf_op jit(solution)/shard_map/ppermute | solution.py:28
  26.8 14.7 %collective-permute-start.5 = (bf16[2,64,1024]{2,1,0:T(8,128)(2,1)}, bf16[2,64,1024]{2,1,0:T(8,128)(2,1)}, u32[]{:S(2)}, u32[]{:S(2)}) collective-permute-start(bf16[2,64,1024]{2,1,0:T(8,128)(2,1)} %collective-permute-done.2), channel_id=1, source_target_pairs={{0,56},{8,0},{16,8},{24,16},{32,24},{40,32},{48,40},{56,48},{1,57}... | collective-permute-start | bytes 786440 | tf_op jit(solution)/shard_map/ppermute | solution.py:28
  32.3 13.8 %collective-permute-start.4 = (bf16[2,64,1024]{2,1,0:T(8,128)(2,1)S(1)}, bf16[2,64,1024]{2,1,0:T(8,128)(2,1)}, u32[]{:S(2)}, u32[]{:S(2)}) collective-permute-start(bf16[2,64,1024]{2,1,0:T(8,128)(2,1)S(1)} %shard_map.86), channel_id=1, source_target_pairs={{0,8},{8,16},{16,24},{24,32},{32,40},{40,48},{48,56},{56,0},{1,9},... | collective-permute-start | bytes 786440 | tf_op jit(solution)/shard_map/ppermute | solution.py:28
  34.2 28.2 %collective-permute-start.10 = (bf16[288,1024]{1,0:T(8,128)(2,1)S(1)}, bf16[288,1024]{1,0:T(8,128)(2,1)}, u32[]{:S(2)}, u32[]{:S(2)}) collective-permute-start(bf16[288,1024]{1,0:T(8,128)(2,1)S(1)} %pad_add_fusion.refs_0_), channel_id=1, source_target_pairs={{0,192},{64,128},{128,64},{192,0},{1,193},{65,129},{129,65},{193,1... | collective-permute-start | bytes 1769480 | tf_op jit(solution)/shard_map/ppermute | solution.py:32
  37.9 24.5 %collective-permute-start.11 = (bf16[288,1024]{1,0:T(8,128)(2,1)S(1)}, bf16[288,1024]{1,0:T(8,128)(2,1)}, u32[]{:S(2)}, u32[]{:S(2)}) collective-permute-start(bf16[288,1024]{1,0:T(8,128)(2,1)S(1)} %pad_add_fusion.refs_0_), channel_id=1, source_target_pairs={{0,128},{64,192},{128,0},{192,64},{1,129},{65,193},{129,1},{193,65... | collective-permute-start | bytes 1769480 | tf_op jit(solution)/shard_map/ppermute | solution.py:32
  41.5 8.5 %collective-permute-start.7 = (bf16[2,64,1024]{2,1,0:T(8,128)(2,1)}, bf16[2,64,1024]{2,1,0:T(8,128)(2,1)S(1)}, u32[]{:S(2)}, u32[]{:S(2)}) collective-permute-start(bf16[2,64,1024]{2,1,0:T(8,128)(2,1)} %collective-permute-done.5), channel_id=1, source_target_pairs={{0,56},{8,0},{16,8},{24,16},{32,24},{40,32},{48,40},{56,48},{1,57}... | collective-permute-start | bytes 786440 | tf_op jit(solution)/shard_map/ppermute | solution.py:28
  46.1 8.9 %collective-permute-start.6 = (bf16[2,64,1024]{2,1,0:T(8,128)(2,1)}, bf16[2,64,1024]{2,1,0:T(8,128)(2,1)S(1)}, u32[]{:S(2)}, u32[]{:S(2)}) collective-permute-start(bf16[2,64,1024]{2,1,0:T(8,128)(2,1)} %collective-permute-done.4), channel_id=1, source_target_pairs={{0,8},{8,16},{16,24},{24,32},{32,40},{40,48},{48,56},{56,0},{1,9},... | collective-permute-start | bytes 786440 | tf_op jit(solution)/shard_map/ppermute | solution.py:28
  50.0 12.4 %collective-permute-start.9 = (bf16[1,64,1024]{2,1,0:T(8,128)(2,1)S(1)}, bf16[1,64,1024]{2,1,0:T(8,128)(2,1)S(1)}, u32[]{:S(2)}, u32[]{:S(2)}) collective-permute-start(bf16[1,64,1024]{2,1,0:T(8,128)(2,1)S(1)} %slice.90), channel_id=1, source_target_pairs={{0,56},{8,0},{16,8},{24,16},{32,24},{40,32},{48,40},{56,48},{1,57}... | collective-permute-start | bytes 393224 | tf_op jit(solution)/shard_map/ppermute | solution.py:28
  55.1 7.3 %collective-permute-start.8 = (bf16[1,64,1024]{2,1,0:T(8,128)(2,1)S(1)}, bf16[1,64,1024]{2,1,0:T(8,128)(2,1)S(1)}, u32[]{:S(2)}, u32[]{:S(2)}) collective-permute-start(bf16[1,64,1024]{2,1,0:T(8,128)(2,1)S(1)} %slice.88), channel_id=1, source_target_pairs={{0,8},{8,16},{16,24},{24,32},{32,40},{40,48},{48,56},{56,0},{1,9},... | collective-permute-start | bytes 393224 | tf_op jit(solution)/shard_map/ppermute | solution.py:28
  64.6 9.1 %collective-permute-start.12 = (f32[256,1152]{1,0:T(8,128)S(1)}, f32[256,1152]{1,0:T(8,128)S(1)}, u32[]{:S(2)}, u32[]{:S(2)}) collective-permute-start(f32[256,1152]{1,0:T(8,128)S(1)} %shard_map.88), channel_id=1, source_target_pairs={{0,1},{1,0},{2,3},{3,2},{4,5},{5,4},{6,7},{7,6},{8,9},{9,8},{10,11... | collective-permute-start | bytes 3538952 | tf_op jit(solution)/shard_map/ppermute | solution.py:23
  74.7 22.1 %all-to-all-start = ((f16[4,64,1152]{2,1,0:T(8,128)(2,1)}), f16[4,64,1152]{2,1,0:T(8,128)(2,1)S(1)}, u32[]{:S(2)}, u32[]{:S(2)}) async-start(f16[4,64,1152]{2,1,0:T(8,128)(2,1)} %bitcast.7), calls=%async_computation | async-start | bytes 1179648 | tf_op jit(solution)/shard_map/all_to_all | solution.py:210
  115.1 17.0 %copy-start = (bf16[56,1024]{1,0:T(8,128)(2,1)S(1)}, bf16[56,1024]{1,0:T(8,128)(2,1)}, u32[]{:S(2)}) copy-start(bf16[56,1024]{1,0:T(8,128)(2,1)} %up_probe.1) | copy-start | bytes 344068
  115.1 17.0 %copy-start.1 = (bf16[56,1024]{1,0:T(8,128)(2,1)S(1)}, bf16[56,1024]{1,0:T(8,128)(2,1)}, u32[]{:S(2)}) copy-start(bf16[56,1024]{1,0:T(8,128)(2,1)} %gate_probe.1) | copy-start | bytes 344068

commit v14 on v12

--- a/solution.py
+++ b/solution.py
@@ -172,15 +172,18 @@
     mats = stacked(
         [gate_weight, up_weight, gate_probe, up_probe, down_weight], tok_rows + cot_rows
     )
-    weights = [mats] + [mix(mats, "x", by) for by in (1, 3, 2)]
+    beside, across = mix(mats, "x", 1), mix(mats, "x", 3)
 
     block = after(block, [mats], interpret)
     ahead = behind = block
     blocks = [block]
-    for _ in range(ny // 2 - 1):
+    for step in range(ny // 2 - 1):
         ahead, behind = shift(ahead, "y", 1), shift(behind, "y", -1)
+        if step == 1:
+            beside = after(beside, [ahead], interpret)
         blocks += [ahead, behind]
     blocks += [shift(ahead[:1], "y", 1), shift(behind[1:], "y", -1)]
+    weights = [mats, beside, across, mix(beside, "x", 3)]
     tok_all = jnp.concatenate([b[:, :own] for b in blocks], axis=0).reshape(-1, feats)
     cot_all = jnp.concatenate([b[:, own:] for b in blocks], axis=0).reshape(-1, feats)
 

time: 133 us -> 132 us (level)
  local copies, waits for them, and re-layouts: 3.11 us -> 1.16 us
    unnamed x12, local copies, waits for them, and re-layouts: 3.08 us -> 1.13 us
    ppermute x3, starting transfers between devices: 9.96 us -> 11.3 us  [mix(): lax.ppermute(value, axis, [(i, i ^ by) for i in range(lax.axis_size(axis))])]
    pallas_call x6 -> x7, Pallas kernels: 4.85 us -> 4.85 us  [local_call(): pl.pallas_call(body, out_shape=out_shape, cost_estimate=pl.CostEstimate(f...]
  transfers between devices with their start and end apart: 14 -> 14, of which waited for: 7 -> 8; matrix products, arithmetic and copies ran while one was open for 3% -> 2% of each run, Pallas kernels for 1% -> 1%
where the time goes in v14:
time: 132 us; the launch traced here: 131 us
  starting transfers between devices  59.3 us (45%)
  blocking collectives  32 us (24%)
  waiting for transfers between devices  29.7 us (22%)
  Pallas kernels  4.85 us (4%)
  other arithmetic  3.11 us (2%)
    ppermute x8, starting transfers between devices, shift(): lax.ppermute(value, axis, [(i, (i + by) % size) for i in range(size)])  28 us
    all_to_all x1, blocking collectives, on_device(): away = lax.all_to_all(away, 'x', 0, 0, tiled=True)  17.2 us
    all_to_all x1, waiting for transfers between devices, on_device(): got = lax.all_to_all(sent, 'zl', 0, 0, tiled=True)  16.2 us
    all_gather x1, blocking collectives, on_device(): fac = lax.all_gather(fac, ('zl', 'c'), axis=1, tiled=True)  14.8 us
    ppermute x2, starting transfers between devices, swap(): return lax.ppermute(value, axis, [(0, 1), (1, 0)])  12.8 us
    ppermute x3, starting transfers between devices, mix(): lax.ppermute(value, axis, [(i, i ^ by) for i in range(lax.axis_size(axis))])  11.3 us
    ppermute x8, waiting for transfers between devices, shift(): lax.ppermute(value, axis, [(i, (i + by) % size) for i in range(size)])  8.72 us
    all_to_all x1, starting transfers between devices, on_device(): got = lax.all_to_all(sent, 'zl', 0, 0, tiled=True)  7.2 us
  transfers between devices with their start and end apart: 14, of which 8 were waited for; matrix products, arithmetic and copies ran while one was open for 2% of the time, Pallas kernels for 1%

profile of v14, /device:TPU:24, one launch (start us, length us, event | category | flops | bytes accessed | tf_op | source)
XLA Modules:
  0.0 131.1 jit_solution(14456415281237747662)
XLA Ops:
  0.6 0.9 fusion
  1.5 10.9 %collective-permute-start = (bf16[64,1024]{1,0:T(8,128)(2,1)S(1)}, bf16[64,1024]{1,0:T(8,128)(2,1)S(1)}, u32[]{:S(2)}, u32[]{:S(2)}) collective-permute-start(bf16[64,1024]{1,0:T(8,128)(2,1)S(1)} %get-tuple-element.25), channel_id=1, source_target_pairs={{0,256},{256,0},{1,257},{257,1},{2,258},{258,2},{3,259},{259,3},{4... | collective-permute-start | bytes 393224 | tf_op jit(solution)/shard_map/ppermute | solution.py:23
  12.5 1.2 pad_add_fusion.rest_0_.refs_0_
  13.6 2.4 %collective-permute-done = bf16[64,1024]{1,0:T(8,128)(2,1)S(1)} collective-permute-done((bf16[64,1024]{1,0:T(8,128)(2,1)S(1)}, bf16[64,1024]{1,0:T(8,128)(2,1)S(1)}, u32[]{:S(2)}, u32[]{:S(2)}) %collective-permute-start) | collective-permute-done | bytes 131104 | tf_op jit(solution)/shard_map/ppermute | solution.py:23
  16.1 4.7 %collective-permute-start.1 = (bf16[2,64,1024]{2,1,0:T(8,128)(2,1)S(1)}, bf16[2,64,1024]{2,1,0:T(8,128)(2,1)}, u32[]{:S(2)}, u32[]{:S(2)}) collective-permute-start(bf16[2,64,1024]{2,1,0:T(8,128)(2,1)S(1)} %shard_map.86), channel_id=1, source_target_pairs={{0,8},{8,16},{16,24},{24,32},{32,40},{40,48},{48,56},{56,0},{1,9},... | collective-permute-start | bytes 786440 | tf_op jit(solution)/shard_map/ppermute | solution.py:28
  20.8 1.9 %collective-permute-start.2 = (bf16[2,64,1024]{2,1,0:T(8,128)(2,1)S(1)}, bf16[2,64,1024]{2,1,0:T(8,128)(2,1)S(1)}, u32[]{:S(2)}, u32[]{:S(2)}) collective-permute-start(bf16[2,64,1024]{2,1,0:T(8,128)(2,1)S(1)} %shard_map.86), channel_id=1, source_target_pairs={{0,56},{8,0},{16,8},{24,16},{32,24},{40,32},{48,40},{56,48},{1,57}... | collective-permute-start | bytes 786440 | tf_op jit(solution)/shard_map/ppermute | solution.py:28
  22.7 3.4 %collective-permute-start.9 = (bf16[288,1024]{1,0:T(8,128)(2,1)S(1)}, bf16[288,1024]{1,0:T(8,128)(2,1)S(1)}, u32[]{:S(2)}, u32[]{:S(2)}) collective-permute-start(bf16[288,1024]{1,0:T(8,128)(2,1)S(1)} %pad_add_fusion.rest_0_.refs_0_), channel_id=1, source_target_pairs={{0,64},{64,0},{128,192},{192,128},{1,65},{65,1},{129,193},{193,129... | collective-permute-start | bytes 1769480 | tf_op jit(solution)/shard_map/ppermute | solution.py:32
  26.1 4.0 %collective-permute-start.10 = (bf16[288,1024]{1,0:T(8,128)(2,1)S(1)}, bf16[288,1024]{1,0:T(8,128)(2,1)S(1)}, u32[]{:S(2)}, u32[]{:S(2)}) collective-permute-start(bf16[288,1024]{1,0:T(8,128)(2,1)S(1)} %pad_add_fusion.rest_0_.refs_0_), channel_id=1, source_target_pairs={{0,192},{64,128},{128,64},{192,0},{1,193},{65,129},{129,65},{193,1... | collective-permute-start | bytes 1769480 | tf_op jit(solution)/shard_map/ppermute | solution.py:32
  30.2 0.0 collective-permute-done.1
  30.2 5.1 %collective-permute-start.3 = (bf16[2,64,1024]{2,1,0:T(8,128)(2,1)}, bf16[2,64,1024]{2,1,0:T(8,128)(2,1)S(1)}, u32[]{:S(2)}, u32[]{:S(2)}) collective-permute-start(bf16[2,64,1024]{2,1,0:T(8,128)(2,1)} %collective-permute-done.1), channel_id=1, source_target_pairs={{0,8},{8,16},{16,24},{24,32},{32,40},{40,48},{48,56},{56,0},{1,9},... | collective-permute-start | bytes 786440 | tf_op jit(solution)/shard_map/ppermute | solution.py:28
  35.3 0.0 collective-permute-done.2
  35.3 1.9 %collective-permute-start.4 = (bf16[2,64,1024]{2,1,0:T(8,128)(2,1)S(1)}, bf16[2,64,1024]{2,1,0:T(8,128)(2,1)S(1)}, u32[]{:S(2)}, u32[]{:S(2)}) collective-permute-start(bf16[2,64,1024]{2,1,0:T(8,128)(2,1)S(1)} %collective-permute-done.2), channel_id=1, source_target_pairs={{0,56},{8,0},{16,8},{24,16},{32,24},{40,32},{48,40},{56,48},{1,57}... | collective-permute-start | bytes 786440 | tf_op jit(solution)/shard_map/ppermute | solution.py:28
  37.2 1.0 slice_dynamic-update-slice_fusion.5
  38.3 0.5 collective-permute-done.9.value
  38.7 0.8 collective-permute-done.3.rest_0_
  39.5 3.9 %collective-permute-start.11 = (bf16[288,1024]{1,0:T(8,128)(2,1)S(1)}, bf16[288,1024]{1,0:T(8,128)(2,1)S(1)}, u32[]{:S(2)}, u32[]{:S(2)}) collective-permute-start(bf16[288,1024]{1,0:T(8,128)(2,1)S(1)} %shard_map.87.refs_1_), channel_id=1, source_target_pairs={{0,192},{64,128},{128,64},{192,0},{1,193},{65,129},{129,65},{193,1... | collective-permute-start | bytes 1769480 | tf_op jit(solution)/shard_map/ppermute | solution.py:32
  43.4 4.9 %collective-permute-start.5 = (bf16[2,64,1024]{2,1,0:T(8,128)(2,1)S(1)}, bf16[2,64,1024]{2,1,0:T(8,128)(2,1)S(1)}, u32[]{:S(2)}, u32[]{:S(2)}) collective-permute-start(bf16[2,64,1024]{2,1,0:T(8,128)(2,1)S(1)} %collective-permute-done.3.rest_0_), channel_id=1, source_target_pairs={{0,8},{8,16},{16,24},{24,32},{32,40},{40,48},{48,56},{56,0},{1,9},... | collective-permute-start | bytes 786440 | tf_op jit(solution)/shard_map/ppermute | solution.py:28
  48.3 0.0 collective-permute-done.4
  48.3 1.9 %collective-permute-start.6 = (bf16[2,64,1024]{2,1,0:T(8,128)(2,1)S(1)}, bf16[2,64,1024]{2,1,0:T(8,128)(2,1)S(1)}, u32[]{:S(2)}, u32[]{:S(2)}) collective-permute-start(bf16[2,64,1024]{2,1,0:T(8,128)(2,1)S(1)} %collective-permute-done.4), channel_id=1, source_target_pairs={{0,56},{8,0},{16,8},{24,16},{32,24},{40,32},{48,40},{56,48},{1,57}... | collective-permute-start | bytes 786440 | tf_op jit(solution)/shard_map/ppermute | solution.py:28
  50.3 1.9 %collective-permute-done.5 = bf16[2,64,1024]{2,1,0:T(8,128)(2,1)S(1)} collective-permute-done((bf16[2,64,1024]{2,1,0:T(8,128)(2,1)S(1)}, bf16[2,64,1024]{2,1,0:T(8,128)(2,1)S(1)}, u32[]{:S(2)}, u32[]{:S(2)}) %collective-permute-start.5) | collective-permute-done | bytes 262176 | tf_op jit(solution)/shard_map/ppermute | solution.py:28
  52.1 5.6 %collective-permute-start.7 = (bf16[1,64,1024]{2,1,0:T(8,128)(2,1)S(1)}, bf16[1,64,1024]{2,1,0:T(8,128)(2,1)S(1)}, u32[]{:S(2)}, u32[]{:S(2)}) collective-permute-start(bf16[1,64,1024]{2,1,0:T(8,128)(2,1)S(1)} %slice.87), channel_id=1, source_target_pairs={{0,8},{8,16},{16,24},{24,32},{32,40},{40,48},{48,56},{56,0},{1,9},... | collective-permute-start | bytes 393224 | tf_op jit(solution)/shard_map/ppermute | solution.py:28
  57.8 0.0 collective-permute-done.6
  57.8 1.9 %collective-permute-start.8 = (bf16[1,64,1024]{2,1,0:T(8,128)(2,1)S(1)}, bf16[1,64,1024]{2,1,0:T(8,128)(2,1)S(1)}, u32[]{:S(2)}, u32[]{:S(2)}) collective-permute-start(bf16[1,64,1024]{2,1,0:T(8,128)(2,1)S(1)} %slice.89), channel_id=1, source_target_pairs={{0,56},{8,0},{16,8},{24,16},{32,24},{40,32},{48,40},{56,48},{1,57}... | collective-permute-start | bytes 393224 | tf_op jit(solution)/shard_map/ppermute | solution.py:28
  59.8 0.5 collective-permute-done.7
  60.3 5.6 %collective-permute-done.8 = bf16[1,64,1024]{2,1,0:T(8,128)(2,1)S(1)} collective-permute-done((bf16[1,64,1024]{2,1,0:T(8,128)(2,1)S(1)}, bf16[1,64,1024]{2,1,0:T(8,128)(2,1)S(1)}, u32[]{:S(2)}, u32[]{:S(2)}) %collective-permute-start.8) | collective-permute-done | bytes 131104 | tf_op jit(solution)/shard_map/ppermute | solution.py:28
  65.9 0.0 collective-permute-done.10.refs_2_
  65.9 0.0 collective-permute-done.11.refs_3_
  65.9 0.9 shard_map.89
  66.8 1.9 %collective-permute-start.12 = (f32[256,1152]{1,0:T(8,128)S(1)}, f32[256,1152]{1,0:T(8,128)S(1)}, u32[]{:S(2)}, u32[]{:S(2)}) collective-permute-start(f32[256,1152]{1,0:T(8,128)S(1)} %shard_map.89), channel_id=1, source_target_pairs={{0,1},{1,0},{2,3},{3,2},{4,5},{5,4},{6,7},{7,6},{8,9},{9,8},{10,11... | collective-permute-start | bytes 3538952 | tf_op jit(solution)/shard_map/ppermute | solution.py:23
  68.7 0.9 shard_map.88
  69.6 1.9 %collective-permute-done.12 = f32[256,1152]{1,0:T(8,128)S(1)} collective-permute-done((f32[256,1152]{1,0:T(8,128)S(1)}, f32[256,1152]{1,0:T(8,128)S(1)}, u32[]{:S(2)}, u32[]{:S(2)}) %collective-permute-start.12) | collective-permute-done | bytes 1179680 | tf_op jit(solution)/shard_map/ppermute | solution.py:23
  71.5 1.0 add_convert_fusion
  72.5 7.2 %all-to-all-start = ((f16[4,64,1152]{2,1,0:T(8,128)(2,1)}), f16[4,64,1152]{2,1,0:T(8,128)(2,1)S(1)}, u32[]{:S(2)}, u32[]{:S(2)}) async-start(f16[4,64,1152]{2,1,0:T(8,128)(2,1)} %bitcast.7), calls=%async_computation | async-start | bytes 1179648 | tf_op jit(solution)/shard_map/all_to_all | solution.py:212
  79.7 16.2 %all-to-all-done = f16[4,64,1152]{2,1,0:T(8,128)(2,1)S(1)} async-done(((f16[4,64,1152]{2,1,0:T(8,128)(2,1)}), f16[4,64,1152]{2,1,0:T(8,128)(2,1)S(1)}, u32[]{:S(2)}, u32[]{:S(2)}) %all-to-all-start) | async-done | bytes 589856 | tf_op jit(solution)/shard_map/all_to_all | solution.py:212
  95.9 0.1 convert_reduce_fusion.proj
  96.0 0.7 shard_map.90
  96.7 14.8 %all_gather.3.fac = bf16[64,4096]{1,0:T(8,128)(2,1)S(1)} all-gather(bf16[64,512]{1,0:T(8,128)(2,1)S(1)} %shard_map.90), channel_id=1, replica_groups=mesh['zh'=2,'x'=4,'y'=8,'zl'=4,'c'=2] {'zl','c'}, dimensions={1}, use_global_device_ids=true | all-gather | bytes 589824 | tf_op jit(solution)/shard_map/all_gather | solution.py:226
  111.5 1.4 %shard_map.91 = (bf16[4,112,1024]{2,1,0:T(8,128)(2,1)S(1)}, f32[112,1024]{1,0:T(8,128)S(1)}) custom-call(s32[1]{0:T(128)} %bitcast.place, bf16[64,4096]{1,0:T(8,128)(2,1)S(1)} %all_gather.3.fac, bf16[512,1024]{1,0:T(8,128)(2,1)S(1)} %bitcast.13), custom_call_target="tpu_custom_call" | custom-call | flops 469762048 | bytes 1048576 | tf_op jit(solution)/shard_map/pallas_call | solution.py:36
  113.0 0.0 copy-start
  113.0 0.0 copy-start.1
  113.0 17.2 %all_to_all.10.away = bf16[4,112,1024]{2,1,0:T(8,128)(2,1)S(1)} all-to-all(bf16[4,112,1024]{2,1,0:T(8,128)(2,1)S(1)} %get-tuple-element.4), channel_id=1, replica_groups=mesh['zh'=2,'x'=4,'y'=8,'zl'=4,'c'=2] {'x'}, dimensions={0} | all-to-all | bytes 1835008 | tf_op jit(solution)/shard_map/all_to_all | solution.py:243
  130.2 0.0 copy-done
  130.2 0.0 copy-done.1
  130.2 0.9 shard_map.92
  (13 shorter events, 0.2 us)
Async XLA Ops:
  1.5 14.5 %collective-permute-start = (bf16[64,1024]{1,0:T(8,128)(2,1)S(1)}, bf16[64,1024]{1,0:T(8,128)(2,1)S(1)}, u32[]{:S(2)}, u32[]{:S(2)}) collective-permute-start(bf16[64,1024]{1,0:T(8,128)(2,1)S(1)} %get-tuple-element.25), channel_id=1, source_target_pairs={{0,256},{256,0},{1,257},{257,1},{2,258},{258,2},{3,259},{259,3},{4... | collective-permute-start | bytes 393224 | tf_op jit(solution)/shard_map/ppermute | solution.py:23
  16.1 14.1 %collective-permute-start.1 = (bf16[2,64,1024]{2,1,0:T(8,128)(2,1)S(1)}, bf16[2,64,1024]{2,1,0:T(8,128)(2,1)}, u32[]{:S(2)}, u32[]{:S(2)}) collective-permute-start(bf16[2,64,1024]{2,1,0:T(8,128)(2,1)S(1)} %shard_map.86), channel_id=1, source_target_pairs={{0,8},{8,16},{16,24},{24,32},{32,40},{40,48},{48,56},{56,0},{1,9},... | collective-permute-start | bytes 786440 | tf_op jit(solution)/shard_map/ppermute | solution.py:28
  20.8 14.5 %collective-permute-start.2 = (bf16[2,64,1024]{2,1,0:T(8,128)(2,1)S(1)}, bf16[2,64,1024]{2,1,0:T(8,128)(2,1)S(1)}, u32[]{:S(2)}, u32[]{:S(2)}) collective-permute-start(bf16[2,64,1024]{2,1,0:T(8,128)(2,1)S(1)} %shard_map.86), channel_id=1, source_target_pairs={{0,56},{8,0},{16,8},{24,16},{32,24},{40,32},{48,40},{56,48},{1,57}... | collective-permute-start | bytes 786440 | tf_op jit(solution)/shard_map/ppermute | solution.py:28
  22.7 16.0 %collective-permute-start.9 = (bf16[288,1024]{1,0:T(8,128)(2,1)S(1)}, bf16[288,1024]{1,0:T(8,128)(2,1)S(1)}, u32[]{:S(2)}, u32[]{:S(2)}) collective-permute-start(bf16[288,1024]{1,0:T(8,128)(2,1)S(1)} %pad_add_fusion.rest_0_.refs_0_), channel_id=1, source_target_pairs={{0,64},{64,0},{128,192},{192,128},{1,65},{65,1},{129,193},{193,129... | collective-permute-start | bytes 1769480 | tf_op jit(solution)/shard_map/ppermute | solution.py:32
  26.1 39.8 %collective-permute-start.10 = (bf16[288,1024]{1,0:T(8,128)(2,1)S(1)}, bf16[288,1024]{1,0:T(8,128)(2,1)S(1)}, u32[]{:S(2)}, u32[]{:S(2)}) collective-permute-start(bf16[288,1024]{1,0:T(8,128)(2,1)S(1)} %pad_add_fusion.rest_0_.refs_0_), channel_id=1, source_target_pairs={{0,192},{64,128},{128,64},{192,0},{1,193},{65,129},{129,65},{193,1... | collective-permute-start | bytes 1769480 | tf_op jit(solution)/shard_map/ppermute | solution.py:32
  30.2 9.3 %collective-permute-start.3 = (bf16[2,64,1024]{2,1,0:T(8,128)(2,1)}, bf16[2,64,1024]{2,1,0:T(8,128)(2,1)S(1)}, u32[]{:S(2)}, u32[]{:S(2)}) collective-permute-start(bf16[2,64,1024]{2,1,0:T(8,128)(2,1)} %collective-permute-done.1), channel_id=1, source_target_pairs={{0,8},{8,16},{16,24},{24,32},{32,40},{40,48},{48,56},{56,0},{1,9},... | collective-permute-start | bytes 786440 | tf_op jit(solution)/shard_map/ppermute | solution.py:28
  35.3 12.9 %collective-permute-start.4 = (bf16[2,64,1024]{2,1,0:T(8,128)(2,1)S(1)}, bf16[2,64,1024]{2,1,0:T(8,128)(2,1)S(1)}, u32[]{:S(2)}, u32[]{:S(2)}) collective-permute-start(bf16[2,64,1024]{2,1,0:T(8,128)(2,1)S(1)} %collective-permute-done.2), channel_id=1, source_target_pairs={{0,56},{8,0},{16,8},{24,16},{32,24},{40,32},{48,40},{56,48},{1,57}... | collective-permute-start | bytes 786440 | tf_op jit(solution)/shard_map/ppermute | solution.py:28
  39.5 26.4 %collective-permute-start.11 = (bf16[288,1024]{1,0:T(8,128)(2,1)S(1)}, bf16[288,1024]{1,0:T(8,128)(2,1)S(1)}, u32[]{:S(2)}, u32[]{:S(2)}) collective-permute-start(bf16[288,1024]{1,0:T(8,128)(2,1)S(1)} %shard_map.87.refs_1_), channel_id=1, source_target_pairs={{0,192},{64,128},{128,64},{192,0},{1,193},{65,129},{129,65},{193,1... | collective-permute-start | bytes 1769480 | tf_op jit(solution)/shard_map/ppermute | solution.py:32
  43.4 8.7 %collective-permute-start.5 = (bf16[2,64,1024]{2,1,0:T(8,128)(2,1)S(1)}, bf16[2,64,1024]{2,1,0:T(8,128)(2,1)S(1)}, u32[]{:S(2)}, u32[]{:S(2)}) collective-permute-start(bf16[2,64,1024]{2,1,0:T(8,128)(2,1)S(1)} %collective-permute-done.3.rest_0_), channel_id=1, source_target_pairs={{0,8},{8,16},{16,24},{24,32},{32,40},{40,48},{48,56},{56,0},{1,9},... | collective-permute-start | bytes 786440 | tf_op jit(solution)/shard_map/ppermute | solution.py:28
  48.3 9.5 %collective-permute-start.6 = (bf16[2,64,1024]{2,1,0:T(8,128)(2,1)S(1)}, bf16[2,64,1024]{2,1,0:T(8,128)(2,1)S(1)}, u32[]{:S(2)}, u32[]{:S(2)}) collective-permute-start(bf16[2,64,1024]{2,1,0:T(8,128)(2,1)S(1)} %collective-permute-done.4), channel_id=1, source_target_pairs={{0,56},{8,0},{16,8},{24,16},{32,24},{40,32},{48,40},{56,48},{1,57}... | collective-permute-start | bytes 786440 | tf_op jit(solution)/shard_map/ppermute | solution.py:28
  52.1 8.1 %collective-permute-start.7 = (bf16[1,64,1024]{2,1,0:T(8,128)(2,1)S(1)}, bf16[1,64,1024]{2,1,0:T(8,128)(2,1)S(1)}, u32[]{:S(2)}, u32[]{:S(2)}) collective-permute-start(bf16[1,64,1024]{2,1,0:T(8,128)(2,1)S(1)} %slice.87), channel_id=1, source_target_pairs={{0,8},{8,16},{16,24},{24,32},{32,40},{40,48},{48,56},{56,0},{1,9},... | collective-permute-start | bytes 393224 | tf_op jit(solution)/shard_map/ppermute | solution.py:28
  57.8 8.1 %collective-permute-start.8 = (bf16[1,64,1024]{2,1,0:T(8,128)(2,1)S(1)}, bf16[1,64,1024]{2,1,0:T(8,128)(2,1)S(1)}, u32[]{:S(2)}, u32[]{:S(2)}) collective-permute-start(bf16[1,64,1024]{2,1,0:T(8,128)(2,1)S(1)} %slice.89), channel_id=1, source_target_pairs={{0,56},{8,0},{16,8},{24,16},{32,24},{40,32},{48,40},{56,48},{1,57}... | collective-permute-start | bytes 393224 | tf_op jit(solution)/shard_map/ppermute | solution.py:28
  66.8 4.7 %collective-permute-start.12 = (f32[256,1152]{1,0:T(8,128)S(1)}, f32[256,1152]{1,0:T(8,128)S(1)}, u32[]{:S(2)}, u32[]{:S(2)}) collective-permute-start(f32[256,1152]{1,0:T(8,128)S(1)} %shard_map.89), channel_id=1, source_target_pairs={{0,1},{1,0},{2,3},{3,2},{4,5},{5,4},{6,7},{7,6},{8,9},{9,8},{10,11... | collective-permute-start | bytes 3538952 | tf_op jit(solution)/shard_map/ppermute | solution.py:23
  72.5 23.4 %all-to-all-start = ((f16[4,64,1152]{2,1,0:T(8,128)(2,1)}), f16[4,64,1152]{2,1,0:T(8,128)(2,1)S(1)}, u32[]{:S(2)}, u32[]{:S(2)}) async-start(f16[4,64,1152]{2,1,0:T(8,128)(2,1)} %bitcast.7), calls=%async_computation | async-start | bytes 1179648 | tf_op jit(solution)/shard_map/all_to_all | solution.py:212
  113.0 17.2 %copy-start = (bf16[56,1024]{1,0:T(8,128)(2,1)S(1)}, bf16[56,1024]{1,0:T(8,128)(2,1)}, u32[]{:S(2)}) copy-start(bf16[56,1024]{1,0:T(8,128)(2,1)} %up_probe.1) | copy-start | bytes 344068
  113.0 17.2 %copy-start.1 = (bf16[56,1024]{1,0:T(8,128)(2,1)S(1)}, bf16[56,1024]{1,0:T(8,128)(2,1)}, u32[]{:S(2)}) copy-start(bf16[56,1024]{1,0:T(8,128)(2,1)} %gate_probe.1) | copy-start | bytes 344068

commit v15 on v14

--- a/solution.py
+++ b/solution.py
@@ -174,11 +174,12 @@
     )
     beside, across = mix(mats, "x", 1), mix(mats, "x", 3)
 
-    block = after(block, [mats], interpret)
     ahead = behind = block
     blocks = [block]
     for step in range(ny // 2 - 1):
         ahead, behind = shift(ahead, "y", 1), shift(behind, "y", -1)
+        if step == 0:
+            behind = after(behind, [beside], interpret)
         if step == 1:
             beside = after(beside, [ahead], interpret)
         blocks += [ahead, behind]

time: 132 us -> 131 us (level)
    ppermute x2, waiting for transfers between devices: 4.32 us -> 1.92 us  [swap(): return lax.ppermute(value, axis, [(0, 1), (1, 0)])]
    ppermute x8, waiting for transfers between devices: 8.72 us -> 11.1 us  [shift(): lax.ppermute(value, axis, [(i, (i + by) % size) for i in range(size)])]
  transfers between devices with their start and end apart: 14 -> 14, of which waited for: 8 -> 6; matrix products, arithmetic and copies ran while one was open for 2% -> 2% of each run, Pallas kernels for 1% -> 1%
where the time goes in v15:
time: 131 us; the launch traced here: 130 us
  starting transfers between devices  59 us (45%)
  blocking collectives  31.9 us (24%)
  waiting for transfers between devices  29.2 us (22%)
  Pallas kernels  4.84 us (4%)
  other arithmetic  3.83 us (3%)
    ppermute x8, starting transfers between devices, shift(): lax.ppermute(value, axis, [(i, (i + by) % size) for i in range(size)])  28.2 us
    all_to_all x1, blocking collectives, on_device(): away = lax.all_to_all(away, 'x', 0, 0, tiled=True)  17 us
    all_to_all x1, waiting for transfers between devices, on_device(): got = lax.all_to_all(sent, 'zl', 0, 0, tiled=True)  16.2 us
    all_gather x1, blocking collectives, on_device(): fac = lax.all_gather(fac, ('zl', 'c'), axis=1, tiled=True)  14.8 us
    ppermute x2, starting transfers between devices, swap(): return lax.ppermute(value, axis, [(0, 1), (1, 0)])  12.8 us
    ppermute x8, waiting for transfers between devices, shift(): lax.ppermute(value, axis, [(i, (i + by) % size) for i in range(size)])  11.1 us
    ppermute x3, starting transfers between devices, mix(): lax.ppermute(value, axis, [(i, i ^ by) for i in range(lax.axis_size(axis))])  10.5 us
    all_to_all x1, starting transfers between devices, on_device(): got = lax.all_to_all(sent, 'zl', 0, 0, tiled=True)  7.47 us
  transfers between devices with their start and end apart: 14, of which 6 were waited for; matrix products, arithmetic and copies ran while one was open for 2% of the time, Pallas kernels for 1%

profile of v15, /device:TPU:24, one launch (start us, length us, event | category | flops | bytes accessed | tf_op | source)
XLA Modules:
  0.0 129.9 jit_solution(2901742114977530532)
XLA Ops:
  0.6 0.9 pad_add_fusion.1
  1.5 10.9 %collective-permute-start = (bf16[64,1024]{1,0:T(8,128)(2,1)S(1)}, bf16[64,1024]{1,0:T(8,128)(2,1)S(1)}, u32[]{:S(2)}, u32[]{:S(2)}) collective-permute-start(bf16[64,1024]{1,0:T(8,128)(2,1)S(1)} %get-tuple-element.24), channel_id=1, source_target_pairs={{0,256},{256,0},{1,257},{257,1},{2,258},{258,2},{3,259},{259,3},{4... | collective-permute-start | bytes 393224 | tf_op jit(solution)/shard_map/ppermute | solution.py:23
  12.5 1.2 pad_add_fusion.refs_0_
  13.6 3.4 %collective-permute-start.3 = (bf16[288,1024]{1,0:T(8,128)(2,1)S(1)}, bf16[288,1024]{1,0:T(8,128)(2,1)S(1)}, u32[]{:S(2)}, u32[]{:S(2)}) collective-permute-start(bf16[288,1024]{1,0:T(8,128)(2,1)S(1)} %pad_add_fusion.refs_0_), channel_id=1, source_target_pairs={{0,64},{64,0},{128,192},{192,128},{1,65},{65,1},{129,193},{193,129... | collective-permute-start | bytes 1769480 | tf_op jit(solution)/shard_map/ppermute | solution.py:32
  17.0 0.0 collective-permute-done
  17.0 0.7 pad_maximum_fusion
  17.8 4.7 %collective-permute-start.1 = (bf16[2,64,1024]{2,1,0:T(8,128)(2,1)}, bf16[2,64,1024]{2,1,0:T(8,128)(2,1)S(1)}, u32[]{:S(2)}, u32[]{:S(2)}) collective-permute-start(bf16[2,64,1024]{2,1,0:T(8,128)(2,1)} %pad_maximum_fusion), channel_id=1, source_target_pairs={{0,8},{8,16},{16,24},{24,32},{32,40},{40,48},{48,56},{56,0},{1,9},... | collective-permute-start | bytes 786440 | tf_op jit(solution)/shard_map/ppermute | solution.py:28
  22.5 4.0 %collective-permute-start.10 = (bf16[288,1024]{1,0:T(8,128)(2,1)S(1)}, bf16[288,1024]{1,0:T(8,128)(2,1)S(1)}, u32[]{:S(2)}, u32[]{:S(2)}) collective-permute-start(bf16[288,1024]{1,0:T(8,128)(2,1)S(1)} %pad_add_fusion.refs_0_), channel_id=1, source_target_pairs={{0,192},{64,128},{128,64},{192,0},{1,193},{65,129},{129,65},{193,1... | collective-permute-start | bytes 1769480 | tf_op jit(solution)/shard_map/ppermute | solution.py:32
  26.5 1.9 %collective-permute-start.2 = (bf16[2,64,1024]{2,1,0:T(8,128)(2,1)}, bf16[2,64,1024]{2,1,0:T(8,128)(2,1)S(1)}, u32[]{:S(2)}, u32[]{:S(2)}) collective-permute-start(bf16[2,64,1024]{2,1,0:T(8,128)(2,1)} %pad_maximum_fusion), channel_id=1, source_target_pairs={{0,56},{8,0},{16,8},{24,16},{32,24},{40,32},{48,40},{56,48},{1,57}... | collective-permute-start | bytes 786440 | tf_op jit(solution)/shard_map/ppermute | solution.py:28
  28.4 0.0 collective-permute-done.1
  28.4 5.1 %collective-permute-start.4 = (bf16[2,64,1024]{2,1,0:T(8,128)(2,1)S(1)}, bf16[2,64,1024]{2,1,0:T(8,128)(2,1)S(1)}, u32[]{:S(2)}, u32[]{:S(2)}) collective-permute-start(bf16[2,64,1024]{2,1,0:T(8,128)(2,1)S(1)} %collective-permute-done.1), channel_id=1, source_target_pairs={{0,8},{8,16},{16,24},{24,32},{32,40},{40,48},{48,56},{56,0},{1,9},... | collective-permute-start | bytes 786440 | tf_op jit(solution)/shard_map/ppermute | solution.py:28
  33.6 3.1 %collective-permute-done.2.value = bf16[2,64,1024]{2,1,0:T(8,128)(2,1)S(1)} collective-permute-done((bf16[2,64,1024]{2,1,0:T(8,128)(2,1)}, bf16[2,64,1024]{2,1,0:T(8,128)(2,1)S(1)}, u32[]{:S(2)}, u32[]{:S(2)}) %collective-permute-start.2) | collective-permute-done | bytes 262176 | tf_op jit(solution)/shard_map/ppermute | solution.py:28
  36.7 0.0 collective-permute-done.3.rest_0_.value
  36.7 1.9 %collective-permute-start.5 = (bf16[2,64,1024]{2,1,0:T(8,128)(2,1)S(1)}, bf16[2,64,1024]{2,1,0:T(8,128)(2,1)S(1)}, u32[]{:S(2)}, u32[]{:S(2)}) collective-permute-start(bf16[2,64,1024]{2,1,0:T(8,128)(2,1)S(1)} %shard_map.86), channel_id=1, source_target_pairs={{0,56},{8,0},{16,8},{24,16},{32,24},{40,32},{48,40},{56,48},{1,57}... | collective-permute-start | bytes 786440 | tf_op jit(solution)/shard_map/ppermute | solution.py:28
  38.7 0.0 collective-permute-done.4.rest_0_
  38.7 3.0 %collective-permute-start.11 = (bf16[288,1024]{1,0:T(8,128)(2,1)S(1)}, bf16[288,1024]{1,0:T(8,128)(2,1)S(1)}, u32[]{:S(2)}, u32[]{:S(2)}) collective-permute-start(bf16[288,1024]{1,0:T(8,128)(2,1)S(1)} %shard_map.87.refs_1_), channel_id=1, source_target_pairs={{0,192},{64,128},{128,64},{192,0},{1,193},{65,129},{129,65},{193,1... | collective-permute-start | bytes 1769480 | tf_op jit(solution)/shard_map/ppermute | solution.py:32
  41.7 5.2 %collective-permute-start.6 = (bf16[2,64,1024]{2,1,0:T(8,128)(2,1)S(1)}, bf16[2,64,1024]{2,1,0:T(8,128)(2,1)S(1)}, u32[]{:S(2)}, u32[]{:S(2)}) collective-permute-start(bf16[2,64,1024]{2,1,0:T(8,128)(2,1)S(1)} %collective-permute-done.4.rest_0_), channel_id=1, source_target_pairs={{0,8},{8,16},{16,24},{24,32},{32,40},{40,48},{48,56},{56,0},{1,9},... | collective-permute-start | bytes 786440 | tf_op jit(solution)/shard_map/ppermute | solution.py:28
  46.9 0.0 collective-permute-done.5
  46.9 1.9 %collective-permute-start.7 = (bf16[2,64,1024]{2,1,0:T(8,128)(2,1)S(1)}, bf16[2,64,1024]{2,1,0:T(8,128)(2,1)S(1)}, u32[]{:S(2)}, u32[]{:S(2)}) collective-permute-start(bf16[2,64,1024]{2,1,0:T(8,128)(2,1)S(1)} %collective-permute-done.5), channel_id=1, source_target_pairs={{0,56},{8,0},{16,8},{24,16},{32,24},{40,32},{48,40},{56,48},{1,57}... | collective-permute-start | bytes 786440 | tf_op jit(solution)/shard_map/ppermute | solution.py:28
  48.9 1.9 %collective-permute-done.6 = bf16[2,64,1024]{2,1,0:T(8,128)(2,1)S(1)} collective-permute-done((bf16[2,64,1024]{2,1,0:T(8,128)(2,1)S(1)}, bf16[2,64,1024]{2,1,0:T(8,128)(2,1)S(1)}, u32[]{:S(2)}, u32[]{:S(2)}) %collective-permute-start.6) | collective-permute-done | bytes 262176 | tf_op jit(solution)/shard_map/ppermute | solution.py:28
  50.8 5.6 %collective-permute-start.8 = (bf16[1,64,1024]{2,1,0:T(8,128)(2,1)S(1)}, bf16[1,64,1024]{2,1,0:T(8,128)(2,1)S(1)}, u32[]{:S(2)}, u32[]{:S(2)}) collective-permute-start(bf16[1,64,1024]{2,1,0:T(8,128)(2,1)S(1)} %slice.88), channel_id=1, source_target_pairs={{0,8},{8,16},{16,24},{24,32},{32,40},{40,48},{48,56},{56,0},{1,9},... | collective-permute-start | bytes 393224 | tf_op jit(solution)/shard_map/ppermute | solution.py:28
  56.4 0.0 collective-permute-done.7
  56.5 1.9 %collective-permute-start.9 = (bf16[1,64,1024]{2,1,0:T(8,128)(2,1)S(1)}, bf16[1,64,1024]{2,1,0:T(8,128)(2,1)S(1)}, u32[]{:S(2)}, u32[]{:S(2)}) collective-permute-start(bf16[1,64,1024]{2,1,0:T(8,128)(2,1)S(1)} %slice.90), channel_id=1, source_target_pairs={{0,56},{8,0},{16,8},{24,16},{32,24},{40,32},{48,40},{56,48},{1,57}... | collective-permute-start | bytes 393224 | tf_op jit(solution)/shard_map/ppermute | solution.py:28
  58.4 0.5 collective-permute-done.8
  58.9 5.6 %collective-permute-done.9 = bf16[1,64,1024]{2,1,0:T(8,128)(2,1)S(1)} collective-permute-done((bf16[1,64,1024]{2,1,0:T(8,128)(2,1)S(1)}, bf16[1,64,1024]{2,1,0:T(8,128)(2,1)S(1)}, u32[]{:S(2)}, u32[]{:S(2)}) %collective-permute-start.9) | collective-permute-done | bytes 131104 | tf_op jit(solution)/shard_map/ppermute | solution.py:28
  64.5 0.0 collective-permute-done.10.refs_2_
  64.6 0.0 collective-permute-done.11.refs_3_
  64.6 0.9 shard_map.89
  65.5 1.9 %collective-permute-start.12 = (f32[256,1152]{1,0:T(8,128)S(1)}, f32[256,1152]{1,0:T(8,128)S(1)}, u32[]{:S(2)}, u32[]{:S(2)}) collective-permute-start(f32[256,1152]{1,0:T(8,128)S(1)} %shard_map.89), channel_id=1, source_target_pairs={{0,1},{1,0},{2,3},{3,2},{4,5},{5,4},{6,7},{7,6},{8,9},{9,8},{10,11... | collective-permute-start | bytes 3538952 | tf_op jit(solution)/shard_map/ppermute | solution.py:23
  67.4 0.9 shard_map.88
  68.3 1.9 %collective-permute-done.12 = f32[256,1152]{1,0:T(8,128)S(1)} collective-permute-done((f32[256,1152]{1,0:T(8,128)S(1)}, f32[256,1152]{1,0:T(8,128)S(1)}, u32[]{:S(2)}, u32[]{:S(2)}) %collective-permute-start.12) | collective-permute-done | bytes 1179680 | tf_op jit(solution)/shard_map/ppermute | solution.py:23
  70.2 1.0 add_convert_fusion
  71.2 7.5 %all-to-all-start = ((f16[4,64,1152]{2,1,0:T(8,128)(2,1)}), f16[4,64,1152]{2,1,0:T(8,128)(2,1)S(1)}, u32[]{:S(2)}, u32[]{:S(2)}) async-start(f16[4,64,1152]{2,1,0:T(8,128)(2,1)} %bitcast.7), calls=%async_computation | async-start | bytes 1179648 | tf_op jit(solution)/shard_map/all_to_all | solution.py:213
  78.6 16.2 %all-to-all-done = f16[4,64,1152]{2,1,0:T(8,128)(2,1)S(1)} async-done(((f16[4,64,1152]{2,1,0:T(8,128)(2,1)}), f16[4,64,1152]{2,1,0:T(8,128)(2,1)S(1)}, u32[]{:S(2)}, u32[]{:S(2)}) %all-to-all-start) | async-done | bytes 589856 | tf_op jit(solution)/shard_map/all_to_all | solution.py:213
  94.8 0.1 convert_reduce_fusion.proj
  94.9 0.7 shard_map.90
  95.7 14.8 %all_gather.3.fac = bf16[64,4096]{1,0:T(8,128)(2,1)S(1)} all-gather(bf16[64,512]{1,0:T(8,128)(2,1)S(1)} %shard_map.90), channel_id=1, replica_groups=mesh['zh'=2,'x'=4,'y'=8,'zl'=4,'c'=2] {'zl','c'}, dimensions={1}, use_global_device_ids=true | all-gather | bytes 589824 | tf_op jit(solution)/shard_map/all_gather | solution.py:227
  110.5 1.4 %shard_map.91 = (bf16[4,112,1024]{2,1,0:T(8,128)(2,1)S(1)}, f32[112,1024]{1,0:T(8,128)S(1)}) custom-call(s32[1]{0:T(128)} %bitcast.place, bf16[64,4096]{1,0:T(8,128)(2,1)S(1)} %all_gather.3.fac, bf16[512,1024]{1,0:T(8,128)(2,1)S(1)} %bitcast.13), custom_call_target="tpu_custom_call" | custom-call | flops 469762048 | bytes 1048576 | tf_op jit(solution)/shard_map/pallas_call | solution.py:36
  111.9 0.0 copy-start
  111.9 0.0 copy-start.1
  111.9 17.0 %all_to_all.10.away = bf16[4,112,1024]{2,1,0:T(8,128)(2,1)S(1)} all-to-all(bf16[4,112,1024]{2,1,0:T(8,128)(2,1)S(1)} %get-tuple-element.4), channel_id=1, replica_groups=mesh['zh'=2,'x'=4,'y'=8,'zl'=4,'c'=2] {'x'}, dimensions={0} | all-to-all | bytes 1835008 | tf_op jit(solution)/shard_map/all_to_all | solution.py:244
  129.0 0.0 copy-done
  129.0 0.0 copy-done.1
  129.0 0.9 shard_map.92
  (13 shorter events, 0.2 us)
Async XLA Ops:
  1.5 15.5 %collective-permute-start = (bf16[64,1024]{1,0:T(8,128)(2,1)S(1)}, bf16[64,1024]{1,0:T(8,128)(2,1)S(1)}, u32[]{:S(2)}, u32[]{:S(2)}) collective-permute-start(bf16[64,1024]{1,0:T(8,128)(2,1)S(1)} %get-tuple-element.24), channel_id=1, source_target_pairs={{0,256},{256,0},{1,257},{257,1},{2,258},{258,2},{3,259},{259,3},{4... | collective-permute-start | bytes 393224 | tf_op jit(solution)/shard_map/ppermute | solution.py:23
  13.6 23.1 %collective-permute-start.3 = (bf16[288,1024]{1,0:T(8,128)(2,1)S(1)}, bf16[288,1024]{1,0:T(8,128)(2,1)S(1)}, u32[]{:S(2)}, u32[]{:S(2)}) collective-permute-start(bf16[288,1024]{1,0:T(8,128)(2,1)S(1)} %pad_add_fusion.refs_0_), channel_id=1, source_target_pairs={{0,64},{64,0},{128,192},{192,128},{1,65},{65,1},{129,193},{193,129... | collective-permute-start | bytes 1769480 | tf_op jit(solution)/shard_map/ppermute | solution.py:32
  17.8 10.7 %collective-permute-start.1 = (bf16[2,64,1024]{2,1,0:T(8,128)(2,1)}, bf16[2,64,1024]{2,1,0:T(8,128)(2,1)S(1)}, u32[]{:S(2)}, u32[]{:S(2)}) collective-permute-start(bf16[2,64,1024]{2,1,0:T(8,128)(2,1)} %pad_maximum_fusion), channel_id=1, source_target_pairs={{0,8},{8,16},{16,24},{24,32},{32,40},{40,48},{48,56},{56,0},{1,9},... | collective-permute-start | bytes 786440 | tf_op jit(solution)/shard_map/ppermute | solution.py:28
  22.5 42.1 %collective-permute-start.10 = (bf16[288,1024]{1,0:T(8,128)(2,1)S(1)}, bf16[288,1024]{1,0:T(8,128)(2,1)S(1)}, u32[]{:S(2)}, u32[]{:S(2)}) collective-permute-start(bf16[288,1024]{1,0:T(8,128)(2,1)S(1)} %pad_add_fusion.refs_0_), channel_id=1, source_target_pairs={{0,192},{64,128},{128,64},{192,0},{1,193},{65,129},{129,65},{193,1... | collective-permute-start | bytes 1769480 | tf_op jit(solution)/shard_map/ppermute | solution.py:32
  26.5 10.2 %collective-permute-start.2 = (bf16[2,64,1024]{2,1,0:T(8,128)(2,1)}, bf16[2,64,1024]{2,1,0:T(8,128)(2,1)S(1)}, u32[]{:S(2)}, u32[]{:S(2)}) collective-permute-start(bf16[2,64,1024]{2,1,0:T(8,128)(2,1)} %pad_maximum_fusion), channel_id=1, source_target_pairs={{0,56},{8,0},{16,8},{24,16},{32,24},{40,32},{48,40},{56,48},{1,57}... | collective-permute-start | bytes 786440 | tf_op jit(solution)/shard_map/ppermute | solution.py:28
  28.4 10.2 %collective-permute-start.4 = (bf16[2,64,1024]{2,1,0:T(8,128)(2,1)S(1)}, bf16[2,64,1024]{2,1,0:T(8,128)(2,1)S(1)}, u32[]{:S(2)}, u32[]{:S(2)}) collective-permute-start(bf16[2,64,1024]{2,1,0:T(8,128)(2,1)S(1)} %collective-permute-done.1), channel_id=1, source_target_pairs={{0,8},{8,16},{16,24},{24,32},{32,40},{40,48},{48,56},{56,0},{1,9},... | collective-permute-start | bytes 786440 | tf_op jit(solution)/shard_map/ppermute | solution.py:28
  36.7 10.2 %collective-permute-start.5 = (bf16[2,64,1024]{2,1,0:T(8,128)(2,1)S(1)}, bf16[2,64,1024]{2,1,0:T(8,128)(2,1)S(1)}, u32[]{:S(2)}, u32[]{:S(2)}) collective-permute-start(bf16[2,64,1024]{2,1,0:T(8,128)(2,1)S(1)} %shard_map.86), channel_id=1, source_target_pairs={{0,56},{8,0},{16,8},{24,16},{32,24},{40,32},{48,40},{56,48},{1,57}... | collective-permute-start | bytes 786440 | tf_op jit(solution)/shard_map/ppermute | solution.py:28
  38.7 25.9 %collective-permute-start.11 = (bf16[288,1024]{1,0:T(8,128)(2,1)S(1)}, bf16[288,1024]{1,0:T(8,128)(2,1)S(1)}, u32[]{:S(2)}, u32[]{:S(2)}) collective-permute-start(bf16[288,1024]{1,0:T(8,128)(2,1)S(1)} %shard_map.87.refs_1_), channel_id=1, source_target_pairs={{0,192},{64,128},{128,64},{192,0},{1,193},{65,129},{129,65},{193,1... | collective-permute-start | bytes 1769480 | tf_op jit(solution)/shard_map/ppermute | solution.py:32
  41.7 9.0 %collective-permute-start.6 = (bf16[2,64,1024]{2,1,0:T(8,128)(2,1)S(1)}, bf16[2,64,1024]{2,1,0:T(8,128)(2,1)S(1)}, u32[]{:S(2)}, u32[]{:S(2)}) collective-permute-start(bf16[2,64,1024]{2,1,0:T(8,128)(2,1)S(1)} %collective-permute-done.4.rest_0_), channel_id=1, source_target_pairs={{0,8},{8,16},{16,24},{24,32},{32,40},{40,48},{48,56},{56,0},{1,9},... | collective-permute-start | bytes 786440 | tf_op jit(solution)/shard_map/ppermute | solution.py:28
  46.9 9.5 %collective-permute-start.7 = (bf16[2,64,1024]{2,1,0:T(8,128)(2,1)S(1)}, bf16[2,64,1024]{2,1,0:T(8,128)(2,1)S(1)}, u32[]{:S(2)}, u32[]{:S(2)}) collective-permute-start(bf16[2,64,1024]{2,1,0:T(8,128)(2,1)S(1)} %collective-permute-done.5), channel_id=1, source_target_pairs={{0,56},{8,0},{16,8},{24,16},{32,24},{40,32},{48,40},{56,48},{1,57}... | collective-permute-start | bytes 786440 | tf_op jit(solution)/shard_map/ppermute | solution.py:28
  50.8 8.1 %collective-permute-start.8 = (bf16[1,64,1024]{2,1,0:T(8,128)(2,1)S(1)}, bf16[1,64,1024]{2,1,0:T(8,128)(2,1)S(1)}, u32[]{:S(2)}, u32[]{:S(2)}) collective-permute-start(bf16[1,64,1024]{2,1,0:T(8,128)(2,1)S(1)} %slice.88), channel_id=1, source_target_pairs={{0,8},{8,16},{16,24},{24,32},{32,40},{40,48},{48,56},{56,0},{1,9},... | collective-permute-start | bytes 393224 | tf_op jit(solution)/shard_map/ppermute | solution.py:28
  56.5 8.1 %collective-permute-start.9 = (bf16[1,64,1024]{2,1,0:T(8,128)(2,1)S(1)}, bf16[1,64,1024]{2,1,0:T(8,128)(2,1)S(1)}, u32[]{:S(2)}, u32[]{:S(2)}) collective-permute-start(bf16[1,64,1024]{2,1,0:T(8,128)(2,1)S(1)} %slice.90), channel_id=1, source_target_pairs={{0,56},{8,0},{16,8},{24,16},{32,24},{40,32},{48,40},{56,48},{1,57}... | collective-permute-start | bytes 393224 | tf_op jit(solution)/shard_map/ppermute | solution.py:28
  65.5 4.7 %collective-permute-start.12 = (f32[256,1152]{1,0:T(8,128)S(1)}, f32[256,1152]{1,0:T(8,128)S(1)}, u32[]{:S(2)}, u32[]{:S(2)}) collective-permute-start(f32[256,1152]{1,0:T(8,128)S(1)} %shard_map.89), channel_id=1, source_target_pairs={{0,1},{1,0},{2,3},{3,2},{4,5},{5,4},{6,7},{7,6},{8,9},{9,8},{10,11... | collective-permute-start | bytes 3538952 | tf_op jit(solution)/shard_map/ppermute | solution.py:23
  71.2 23.7 %all-to-all-start = ((f16[4,64,1152]{2,1,0:T(8,128)(2,1)}), f16[4,64,1152]{2,1,0:T(8,128)(2,1)S(1)}, u32[]{:S(2)}, u32[]{:S(2)}) async-start(f16[4,64,1152]{2,1,0:T(8,128)(2,1)} %bitcast.7), calls=%async_computation | async-start | bytes 1179648 | tf_op jit(solution)/shard_map/all_to_all | solution.py:213
  111.9 17.1 %copy-start = (bf16[56,1024]{1,0:T(8,128)(2,1)S(1)}, bf16[56,1024]{1,0:T(8,128)(2,1)}, u32[]{:S(2)}) copy-start(bf16[56,1024]{1,0:T(8,128)(2,1)} %up_probe.1) | copy-start | bytes 344068
  111.9 17.1 %copy-start.1 = (bf16[56,1024]{1,0:T(8,128)(2,1)S(1)}, bf16[56,1024]{1,0:T(8,128)(2,1)}, u32[]{:S(2)}) copy-start(bf16[56,1024]{1,0:T(8,128)(2,1)} %gate_probe.1) | copy-start | bytes 344068

commit v16 on v15

--- a/solution.py
+++ b/solution.py
@@ -181,7 +181,7 @@
         if step == 0:
             behind = after(behind, [beside], interpret)
         if step == 1:
-            beside = after(beside, [ahead], interpret)
+            beside = after(beside, [behind], interpret)
         blocks += [ahead, behind]
     blocks += [shift(ahead[:1], "y", 1), shift(behind[1:], "y", -1)]
     weights = [mats, beside, across, mix(beside, "x", 3)]

time: 131 us -> 133 us (1.015)
  waiting for transfers between devices: 29.2 us -> 32 us
  starting transfers between devices: 59 us -> 57.4 us
    ppermute x8, waiting for transfers between devices: 11.1 us -> 13.9 us  [shift(): lax.ppermute(value, axis, [(i, (i + by) % size) for i in range(size)])]
where the time goes in v16:
time: 133 us; the launch traced here: 132 us
  starting transfers between devices  57.4 us (43%)
  blocking collectives  33 us (25%)
  waiting for transfers between devices  32 us (24%)
  Pallas kernels  4.85 us (4%)
  other arithmetic  3.83 us (3%)
    ppermute x8, starting transfers between devices, shift(): lax.ppermute(value, axis, [(i, (i + by) % size) for i in range(size)])  27.8 us
    all_to_all x1, blocking collectives, on_device(): away = lax.all_to_all(away, 'x', 0, 0, tiled=True)  18.2 us
    all_to_all x1, waiting for transfers between devices, on_device(): got = lax.all_to_all(sent, 'zl', 0, 0, tiled=True)  16.2 us
    all_gather x1, blocking collectives, on_device(): fac = lax.all_gather(fac, ('zl', 'c'), axis=1, tiled=True)  14.8 us
    ppermute x8, waiting for transfers between devices, shift(): lax.ppermute(value, axis, [(i, (i + by) % size) for i in range(size)])  13.9 us
    ppermute x2, starting transfers between devices, swap(): return lax.ppermute(value, axis, [(0, 1), (1, 0)])  12.8 us
    ppermute x3, starting transfers between devices, mix(): lax.ppermute(value, axis, [(i, i ^ by) for i in range(lax.axis_size(axis))])  10.4 us
    all_to_all x1, starting transfers between devices, on_device(): got = lax.all_to_all(sent, 'zl', 0, 0, tiled=True)  6.38 us
  transfers between devices with their start and end apart: 14, of which 6 were waited for; matrix products, arithmetic and copies ran while one was open for 2% of the time, Pallas kernels for 1%

profile of v16, /device:TPU:24, one launch (start us, length us, event | category | flops | bytes accessed | tf_op | source)
XLA Modules:
  0.0 132.2 jit_solution(6824447533470356468)
XLA Ops:
  0.6 0.9 pad_add_fusion.1
  1.5 10.9 %collective-permute-start = (bf16[64,1024]{1,0:T(8,128)(2,1)S(1)}, bf16[64,1024]{1,0:T(8,128)(2,1)S(1)}, u32[]{:S(2)}, u32[]{:S(2)}) collective-permute-start(bf16[64,1024]{1,0:T(8,128)(2,1)S(1)} %get-tuple-element.24), channel_id=1, source_target_pairs={{0,256},{256,0},{1,257},{257,1},{2,258},{258,2},{3,259},{259,3},{4... | collective-permute-start | bytes 393224 | tf_op jit(solution)/shard_map/ppermute | solution.py:23
  12.5 1.2 pad_add_fusion.refs_0_
  13.6 3.4 %collective-permute-start.3 = (bf16[288,1024]{1,0:T(8,128)(2,1)S(1)}, bf16[288,1024]{1,0:T(8,128)(2,1)S(1)}, u32[]{:S(2)}, u32[]{:S(2)}) collective-permute-start(bf16[288,1024]{1,0:T(8,128)(2,1)S(1)} %pad_add_fusion.refs_0_), channel_id=1, source_target_pairs={{0,64},{64,0},{128,192},{192,128},{1,65},{65,1},{129,193},{193,129... | collective-permute-start | bytes 1769480 | tf_op jit(solution)/shard_map/ppermute | solution.py:32
  17.0 0.0 collective-permute-done
  17.0 0.7 pad_maximum_fusion
  17.8 4.7 %collective-permute-start.1 = (bf16[2,64,1024]{2,1,0:T(8,128)(2,1)}, bf16[2,64,1024]{2,1,0:T(8,128)(2,1)S(1)}, u32[]{:S(2)}, u32[]{:S(2)}) collective-permute-start(bf16[2,64,1024]{2,1,0:T(8,128)(2,1)} %pad_maximum_fusion), channel_id=1, source_target_pairs={{0,8},{8,16},{16,24},{24,32},{32,40},{40,48},{48,56},{56,0},{1,9},... | collective-permute-start | bytes 786440 | tf_op jit(solution)/shard_map/ppermute | solution.py:28
  22.5 4.0 %collective-permute-start.10 = (bf16[288,1024]{1,0:T(8,128)(2,1)S(1)}, bf16[288,1024]{1,0:T(8,128)(2,1)S(1)}, u32[]{:S(2)}, u32[]{:S(2)}) collective-permute-start(bf16[288,1024]{1,0:T(8,128)(2,1)S(1)} %pad_add_fusion.refs_0_), channel_id=1, source_target_pairs={{0,192},{64,128},{128,64},{192,0},{1,193},{65,129},{129,65},{193,1... | collective-permute-start | bytes 1769480 | tf_op jit(solution)/shard_map/ppermute | solution.py:32
  26.5 1.9 %collective-permute-start.2 = (bf16[2,64,1024]{2,1,0:T(8,128)(2,1)}, bf16[2,64,1024]{2,1,0:T(8,128)(2,1)S(1)}, u32[]{:S(2)}, u32[]{:S(2)}) collective-permute-start(bf16[2,64,1024]{2,1,0:T(8,128)(2,1)} %pad_maximum_fusion), channel_id=1, source_target_pairs={{0,56},{8,0},{16,8},{24,16},{32,24},{40,32},{48,40},{56,48},{1,57}... | collective-permute-start | bytes 786440 | tf_op jit(solution)/shard_map/ppermute | solution.py:28
  28.4 0.0 collective-permute-done.1
  28.4 5.1 %collective-permute-start.4 = (bf16[2,64,1024]{2,1,0:T(8,128)(2,1)S(1)}, bf16[2,64,1024]{2,1,0:T(8,128)(2,1)S(1)}, u32[]{:S(2)}, u32[]{:S(2)}) collective-permute-start(bf16[2,64,1024]{2,1,0:T(8,128)(2,1)S(1)} %collective-permute-done.1), channel_id=1, source_target_pairs={{0,8},{8,16},{16,24},{24,32},{32,40},{40,48},{48,56},{56,0},{1,9},... | collective-permute-start | bytes 786440 | tf_op jit(solution)/shard_map/ppermute | solution.py:28
  33.6 3.1 %collective-permute-done.2.value = bf16[2,64,1024]{2,1,0:T(8,128)(2,1)S(1)} collective-permute-done((bf16[2,64,1024]{2,1,0:T(8,128)(2,1)}, bf16[2,64,1024]{2,1,0:T(8,128)(2,1)S(1)}, u32[]{:S(2)}, u32[]{:S(2)}) %collective-permute-start.2) | collective-permute-done | bytes 262176 | tf_op jit(solution)/shard_map/ppermute | solution.py:28
  36.7 0.0 collective-permute-done.3.rest_0_.value
  36.7 1.9 %collective-permute-start.5 = (bf16[2,64,1024]{2,1,0:T(8,128)(2,1)S(1)}, bf16[2,64,1024]{2,1,0:T(8,128)(2,1)S(1)}, u32[]{:S(2)}, u32[]{:S(2)}) collective-permute-start(bf16[2,64,1024]{2,1,0:T(8,128)(2,1)S(1)} %shard_map.86), channel_id=1, source_target_pairs={{0,56},{8,0},{16,8},{24,16},{32,24},{40,32},{48,40},{56,48},{1,57}... | collective-permute-start | bytes 786440 | tf_op jit(solution)/shard_map/ppermute | solution.py:28
  38.7 0.0 collective-permute-done.4
  38.7 5.1 %collective-permute-start.6 = (bf16[2,64,1024]{2,1,0:T(8,128)(2,1)S(1)}, bf16[2,64,1024]{2,1,0:T(8,128)(2,1)S(1)}, u32[]{:S(2)}, u32[]{:S(2)}) collective-permute-start(bf16[2,64,1024]{2,1,0:T(8,128)(2,1)S(1)} %collective-permute-done.4), channel_id=1, source_target_pairs={{0,8},{8,16},{16,24},{24,32},{32,40},{40,48},{48,56},{56,0},{1,9},... | collective-permute-start | bytes 786440 | tf_op jit(solution)/shard_map/ppermute | solution.py:28
  43.8 2.3 %collective-permute-done.5.rest_0_ = bf16[2,64,1024]{2,1,0:T(8,128)(2,1)S(1)} collective-permute-done((bf16[2,64,1024]{2,1,0:T(8,128)(2,1)S(1)}, bf16[2,64,1024]{2,1,0:T(8,128)(2,1)S(1)}, u32[]{:S(2)}, u32[]{:S(2)}) %collective-permute-start.5) | collective-permute-done | bytes 262176 | tf_op jit(solution)/shard_map/ppermute | solution.py:28
  46.2 3.0 %collective-permute-start.11 = (bf16[288,1024]{1,0:T(8,128)(2,1)S(1)}, bf16[288,1024]{1,0:T(8,128)(2,1)S(1)}, u32[]{:S(2)}, u32[]{:S(2)}) collective-permute-start(bf16[288,1024]{1,0:T(8,128)(2,1)S(1)} %shard_map.87.refs_1_), channel_id=1, source_target_pairs={{0,192},{64,128},{128,64},{192,0},{1,193},{65,129},{129,65},{193,1... | collective-permute-start | bytes 1769480 | tf_op jit(solution)/shard_map/ppermute | solution.py:32
  49.2 1.9 %collective-permute-start.7 = (bf16[2,64,1024]{2,1,0:T(8,128)(2,1)S(1)}, bf16[2,64,1024]{2,1,0:T(8,128)(2,1)S(1)}, u32[]{:S(2)}, u32[]{:S(2)}) collective-permute-start(bf16[2,64,1024]{2,1,0:T(8,128)(2,1)S(1)} %collective-permute-done.5.rest_0_), channel_id=1, source_target_pairs={{0,56},{8,0},{16,8},{24,16},{32,24},{40,32},{48,40},{56,48},{1,57}... | collective-permute-start | bytes 786440 | tf_op jit(solution)/shard_map/ppermute | solution.py:28
  51.2 0.0 collective-permute-done.6
  51.2 5.1 %collective-permute-start.8 = (bf16[1,64,1024]{2,1,0:T(8,128)(2,1)S(1)}, bf16[1,64,1024]{2,1,0:T(8,128)(2,1)S(1)}, u32[]{:S(2)}, u32[]{:S(2)}) collective-permute-start(bf16[1,64,1024]{2,1,0:T(8,128)(2,1)S(1)} %slice.88), channel_id=1, source_target_pairs={{0,8},{8,16},{16,24},{24,32},{32,40},{40,48},{48,56},{56,0},{1,9},... | collective-permute-start | bytes 393224 | tf_op jit(solution)/shard_map/ppermute | solution.py:28
  56.4 2.3 %collective-permute-done.7 = bf16[2,64,1024]{2,1,0:T(8,128)(2,1)S(1)} collective-permute-done((bf16[2,64,1024]{2,1,0:T(8,128)(2,1)S(1)}, bf16[2,64,1024]{2,1,0:T(8,128)(2,1)S(1)}, u32[]{:S(2)}, u32[]{:S(2)}) %collective-permute-start.7) | collective-permute-done | bytes 262176 | tf_op jit(solution)/shard_map/ppermute | solution.py:28
  58.7 1.9 %collective-permute-start.9 = (bf16[1,64,1024]{2,1,0:T(8,128)(2,1)S(1)}, bf16[1,64,1024]{2,1,0:T(8,128)(2,1)S(1)}, u32[]{:S(2)}, u32[]{:S(2)}) collective-permute-start(bf16[1,64,1024]{2,1,0:T(8,128)(2,1)S(1)} %slice.90), channel_id=1, source_target_pairs={{0,56},{8,0},{16,8},{24,16},{32,24},{40,32},{48,40},{56,48},{1,57}... | collective-permute-start | bytes 393224 | tf_op jit(solution)/shard_map/ppermute | solution.py:28
  60.7 0.0 collective-permute-done.8
  60.7 6.1 %collective-permute-done.9 = bf16[1,64,1024]{2,1,0:T(8,128)(2,1)S(1)} collective-permute-done((bf16[1,64,1024]{2,1,0:T(8,128)(2,1)S(1)}, bf16[1,64,1024]{2,1,0:T(8,128)(2,1)S(1)}, u32[]{:S(2)}, u32[]{:S(2)}) %collective-permute-start.9) | collective-permute-done | bytes 131104 | tf_op jit(solution)/shard_map/ppermute | solution.py:28
  66.8 0.0 collective-permute-done.10.refs_2_
  66.8 0.0 collective-permute-done.11.refs_3_
  66.8 0.9 shard_map.89
  67.7 1.9 %collective-permute-start.12 = (f32[256,1152]{1,0:T(8,128)S(1)}, f32[256,1152]{1,0:T(8,128)S(1)}, u32[]{:S(2)}, u32[]{:S(2)}) collective-permute-start(f32[256,1152]{1,0:T(8,128)S(1)} %shard_map.89), channel_id=1, source_target_pairs={{0,1},{1,0},{2,3},{3,2},{4,5},{5,4},{6,7},{7,6},{8,9},{9,8},{10,11... | collective-permute-start | bytes 3538952 | tf_op jit(solution)/shard_map/ppermute | solution.py:23
  69.7 0.9 shard_map.88
  70.6 1.9 %collective-permute-done.12 = f32[256,1152]{1,0:T(8,128)S(1)} collective-permute-done((f32[256,1152]{1,0:T(8,128)S(1)}, f32[256,1152]{1,0:T(8,128)S(1)}, u32[]{:S(2)}, u32[]{:S(2)}) %collective-permute-start.12) | collective-permute-done | bytes 1179680 | tf_op jit(solution)/shard_map/ppermute | solution.py:23
  72.5 1.0 add_convert_fusion
  73.4 6.4 %all-to-all-start = ((f16[4,64,1152]{2,1,0:T(8,128)(2,1)}), f16[4,64,1152]{2,1,0:T(8,128)(2,1)S(1)}, u32[]{:S(2)}, u32[]{:S(2)}) async-start(f16[4,64,1152]{2,1,0:T(8,128)(2,1)} %bitcast.7), calls=%async_computation | async-start | bytes 1179648 | tf_op jit(solution)/shard_map/all_to_all | solution.py:213
  79.8 16.2 %all-to-all-done = f16[4,64,1152]{2,1,0:T(8,128)(2,1)S(1)} async-done(((f16[4,64,1152]{2,1,0:T(8,128)(2,1)}), f16[4,64,1152]{2,1,0:T(8,128)(2,1)S(1)}, u32[]{:S(2)}, u32[]{:S(2)}) %all-to-all-start) | async-done | bytes 589856 | tf_op jit(solution)/shard_map/all_to_all | solution.py:213
  96.0 0.1 convert_reduce_fusion.proj
  96.1 0.7 shard_map.90
  96.8 14.8 %all_gather.3.fac = bf16[64,4096]{1,0:T(8,128)(2,1)S(1)} all-gather(bf16[64,512]{1,0:T(8,128)(2,1)S(1)} %shard_map.90), channel_id=1, replica_groups=mesh['zh'=2,'x'=4,'y'=8,'zl'=4,'c'=2] {'zl','c'}, dimensions={1}, use_global_device_ids=true | all-gather | bytes 589824 | tf_op jit(solution)/shard_map/all_gather | solution.py:227
  111.7 1.4 %shard_map.91 = (bf16[4,112,1024]{2,1,0:T(8,128)(2,1)S(1)}, f32[112,1024]{1,0:T(8,128)S(1)}) custom-call(s32[1]{0:T(128)} %bitcast.place, bf16[64,4096]{1,0:T(8,128)(2,1)S(1)} %all_gather.3.fac, bf16[512,1024]{1,0:T(8,128)(2,1)S(1)} %bitcast.13), custom_call_target="tpu_custom_call" | custom-call | flops 469762048 | bytes 1048576 | tf_op jit(solution)/shard_map/pallas_call | solution.py:36
  113.1 0.0 copy-start
  113.1 0.0 copy-start.1
  113.1 18.2 %all_to_all.10.away = bf16[4,112,1024]{2,1,0:T(8,128)(2,1)S(1)} all-to-all(bf16[4,112,1024]{2,1,0:T(8,128)(2,1)S(1)} %get-tuple-element.4), channel_id=1, replica_groups=mesh['zh'=2,'x'=4,'y'=8,'zl'=4,'c'=2] {'x'}, dimensions={0} | all-to-all | bytes 1835008 | tf_op jit(solution)/shard_map/all_to_all | solution.py:244
  131.3 0.0 copy-done
  131.3 0.0 copy-done.1
  131.3 0.9 shard_map.92
  (13 shorter events, 0.2 us)
Async XLA Ops:
  1.5 15.5 %collective-permute-start = (bf16[64,1024]{1,0:T(8,128)(2,1)S(1)}, bf16[64,1024]{1,0:T(8,128)(2,1)S(1)}, u32[]{:S(2)}, u32[]{:S(2)}) collective-permute-start(bf16[64,1024]{1,0:T(8,128)(2,1)S(1)} %get-tuple-element.24), channel_id=1, source_target_pairs={{0,256},{256,0},{1,257},{257,1},{2,258},{258,2},{3,259},{259,3},{4... | collective-permute-start | bytes 393224 | tf_op jit(solution)/shard_map/ppermute | solution.py:23
  13.6 23.1 %collective-permute-start.3 = (bf16[288,1024]{1,0:T(8,128)(2,1)S(1)}, bf16[288,1024]{1,0:T(8,128)(2,1)S(1)}, u32[]{:S(2)}, u32[]{:S(2)}) collective-permute-start(bf16[288,1024]{1,0:T(8,128)(2,1)S(1)} %pad_add_fusion.refs_0_), channel_id=1, source_target_pairs={{0,64},{64,0},{128,192},{192,128},{1,65},{65,1},{129,193},{193,129... | collective-permute-start | bytes 1769480 | tf_op jit(solution)/shard_map/ppermute | solution.py:32
  17.8 10.7 %collective-permute-start.1 = (bf16[2,64,1024]{2,1,0:T(8,128)(2,1)}, bf16[2,64,1024]{2,1,0:T(8,128)(2,1)S(1)}, u32[]{:S(2)}, u32[]{:S(2)}) collective-permute-start(bf16[2,64,1024]{2,1,0:T(8,128)(2,1)} %pad_maximum_fusion), channel_id=1, source_target_pairs={{0,8},{8,16},{16,24},{24,32},{32,40},{40,48},{48,56},{56,0},{1,9},... | collective-permute-start | bytes 786440 | tf_op jit(solution)/shard_map/ppermute | solution.py:28
  22.5 44.4 %collective-permute-start.10 = (bf16[288,1024]{1,0:T(8,128)(2,1)S(1)}, bf16[288,1024]{1,0:T(8,128)(2,1)S(1)}, u32[]{:S(2)}, u32[]{:S(2)}) collective-permute-start(bf16[288,1024]{1,0:T(8,128)(2,1)S(1)} %pad_add_fusion.refs_0_), channel_id=1, source_target_pairs={{0,192},{64,128},{128,64},{192,0},{1,193},{65,129},{129,65},{193,1... | collective-permute-start | bytes 1769480 | tf_op jit(solution)/shard_map/ppermute | solution.py:32
  26.5 10.2 %collective-permute-start.2 = (bf16[2,64,1024]{2,1,0:T(8,128)(2,1)}, bf16[2,64,1024]{2,1,0:T(8,128)(2,1)S(1)}, u32[]{:S(2)}, u32[]{:S(2)}) collective-permute-start(bf16[2,64,1024]{2,1,0:T(8,128)(2,1)} %pad_maximum_fusion), channel_id=1, source_target_pairs={{0,56},{8,0},{16,8},{24,16},{32,24},{40,32},{48,40},{56,48},{1,57}... | collective-permute-start | bytes 786440 | tf_op jit(solution)/shard_map/ppermute | solution.py:28
  28.4 10.2 %collective-permute-start.4 = (bf16[2,64,1024]{2,1,0:T(8,128)(2,1)S(1)}, bf16[2,64,1024]{2,1,0:T(8,128)(2,1)S(1)}, u32[]{:S(2)}, u32[]{:S(2)}) collective-permute-start(bf16[2,64,1024]{2,1,0:T(8,128)(2,1)S(1)} %collective-permute-done.1), channel_id=1, source_target_pairs={{0,8},{8,16},{16,24},{24,32},{32,40},{40,48},{48,56},{56,0},{1,9},... | collective-permute-start | bytes 786440 | tf_op jit(solution)/shard_map/ppermute | solution.py:28
  36.7 9.5 %collective-permute-start.5 = (bf16[2,64,1024]{2,1,0:T(8,128)(2,1)S(1)}, bf16[2,64,1024]{2,1,0:T(8,128)(2,1)S(1)}, u32[]{:S(2)}, u32[]{:S(2)}) collective-permute-start(bf16[2,64,1024]{2,1,0:T(8,128)(2,1)S(1)} %shard_map.86), channel_id=1, source_target_pairs={{0,56},{8,0},{16,8},{24,16},{32,24},{40,32},{48,40},{56,48},{1,57}... | collective-permute-start | bytes 786440 | tf_op jit(solution)/shard_map/ppermute | solution.py:28
  38.7 12.5 %collective-permute-start.6 = (bf16[2,64,1024]{2,1,0:T(8,128)(2,1)S(1)}, bf16[2,64,1024]{2,1,0:T(8,128)(2,1)S(1)}, u32[]{:S(2)}, u32[]{:S(2)}) collective-permute-start(bf16[2,64,1024]{2,1,0:T(8,128)(2,1)S(1)} %collective-permute-done.4), channel_id=1, source_target_pairs={{0,8},{8,16},{16,24},{24,32},{32,40},{40,48},{48,56},{56,0},{1,9},... | collective-permute-start | bytes 786440 | tf_op jit(solution)/shard_map/ppermute | solution.py:28
  46.2 20.6 %collective-permute-start.11 = (bf16[288,1024]{1,0:T(8,128)(2,1)S(1)}, bf16[288,1024]{1,0:T(8,128)(2,1)S(1)}, u32[]{:S(2)}, u32[]{:S(2)}) collective-permute-start(bf16[288,1024]{1,0:T(8,128)(2,1)S(1)} %shard_map.87.refs_1_), channel_id=1, source_target_pairs={{0,192},{64,128},{128,64},{192,0},{1,193},{65,129},{129,65},{193,1... | collective-permute-start | bytes 1769480 | tf_op jit(solution)/shard_map/ppermute | solution.py:32
  49.2 9.5 %collective-permute-start.7 = (bf16[2,64,1024]{2,1,0:T(8,128)(2,1)S(1)}, bf16[2,64,1024]{2,1,0:T(8,128)(2,1)S(1)}, u32[]{:S(2)}, u32[]{:S(2)}) collective-permute-start(bf16[2,64,1024]{2,1,0:T(8,128)(2,1)S(1)} %collective-permute-done.5.rest_0_), channel_id=1, source_target_pairs={{0,56},{8,0},{16,8},{24,16},{32,24},{40,32},{48,40},{56,48},{1,57}... | collective-permute-start | bytes 786440 | tf_op jit(solution)/shard_map/ppermute | solution.py:28
  51.2 9.5 %collective-permute-start.8 = (bf16[1,64,1024]{2,1,0:T(8,128)(2,1)S(1)}, bf16[1,64,1024]{2,1,0:T(8,128)(2,1)S(1)}, u32[]{:S(2)}, u32[]{:S(2)}) collective-permute-start(bf16[1,64,1024]{2,1,0:T(8,128)(2,1)S(1)} %slice.88), channel_id=1, source_target_pairs={{0,8},{8,16},{16,24},{24,32},{32,40},{40,48},{48,56},{56,0},{1,9},... | collective-permute-start | bytes 393224 | tf_op jit(solution)/shard_map/ppermute | solution.py:28
  58.7 8.1 %collective-permute-start.9 = (bf16[1,64,1024]{2,1,0:T(8,128)(2,1)S(1)}, bf16[1,64,1024]{2,1,0:T(8,128)(2,1)S(1)}, u32[]{:S(2)}, u32[]{:S(2)}) collective-permute-start(bf16[1,64,1024]{2,1,0:T(8,128)(2,1)S(1)} %slice.90), channel_id=1, source_target_pairs={{0,56},{8,0},{16,8},{24,16},{32,24},{40,32},{48,40},{56,48},{1,57}... | collective-permute-start | bytes 393224 | tf_op jit(solution)/shard_map/ppermute | solution.py:28
  67.7 4.7 %collective-permute-start.12 = (f32[256,1152]{1,0:T(8,128)S(1)}, f32[256,1152]{1,0:T(8,128)S(1)}, u32[]{:S(2)}, u32[]{:S(2)}) collective-permute-start(f32[256,1152]{1,0:T(8,128)S(1)} %shard_map.89), channel_id=1, source_target_pairs={{0,1},{1,0},{2,3},{3,2},{4,5},{5,4},{6,7},{7,6},{8,9},{9,8},{10,11... | collective-permute-start | bytes 3538952 | tf_op jit(solution)/shard_map/ppermute | solution.py:23
  73.4 22.6 %all-to-all-start = ((f16[4,64,1152]{2,1,0:T(8,128)(2,1)}), f16[4,64,1152]{2,1,0:T(8,128)(2,1)S(1)}, u32[]{:S(2)}, u32[]{:S(2)}) async-start(f16[4,64,1152]{2,1,0:T(8,128)(2,1)} %bitcast.7), calls=%async_computation | async-start | bytes 1179648 | tf_op jit(solution)/shard_map/all_to_all | solution.py:213
  113.1 18.2 %copy-start = (bf16[56,1024]{1,0:T(8,128)(2,1)S(1)}, bf16[56,1024]{1,0:T(8,128)(2,1)}, u32[]{:S(2)}) copy-start(bf16[56,1024]{1,0:T(8,128)(2,1)} %up_probe.1) | copy-start | bytes 344068
  113.1 18.2 %copy-start.1 = (bf16[56,1024]{1,0:T(8,128)(2,1)S(1)}, bf16[56,1024]{1,0:T(8,128)(2,1)}, u32[]{:S(2)}) copy-start(bf16[56,1024]{1,0:T(8,128)(2,1)} %gate_probe.1) | copy-start | bytes 344068

commit v17 on v15

--- a/solution.py
+++ b/solution.py
@@ -179,7 +179,7 @@
     for step in range(ny // 2 - 1):
         ahead, behind = shift(ahead, "y", 1), shift(behind, "y", -1)
         if step == 0:
-            behind = after(behind, [beside], interpret)
+            behind = after(behind, [beside, across], interpret)
         if step == 1:
             beside = after(beside, [ahead], interpret)
         blocks += [ahead, behind]

time: 131 us -> 131 us (level)
  starting transfers between devices: 59 us -> 56.9 us
  waiting for transfers between devices: 29.2 us -> 31 us
    all_to_all x1, starting transfers between devices: 7.47 us -> 4.56 us  [on_device(): got = lax.all_to_all(sent, 'zl', 0, 0, tiled=True)]
    ppermute x8, waiting for transfers between devices: 11.1 us -> 12.9 us  [shift(): lax.ppermute(value, axis, [(i, (i + by) % size) for i in range(size)])]
  transfers between devices with their start and end apart: 14 -> 14, of which waited for: 6 -> 7; matrix products, arithmetic and copies ran while one was open for 2% -> 2% of each run, Pallas kernels for 1% -> 1%
where the time goes in v17:
time: 131 us; the launch traced here: 130 us
  starting transfers between devices  56.9 us (43%)
  blocking collectives  32.3 us (25%)
  waiting for transfers between devices  31 us (24%)
  Pallas kernels  4.84 us (4%)
  other arithmetic  3.83 us (3%)
    ppermute x8, starting transfers between devices, shift(): lax.ppermute(value, axis, [(i, (i + by) % size) for i in range(size)])  29 us
    all_to_all x1, blocking collectives, on_device(): away = lax.all_to_all(away, 'x', 0, 0, tiled=True)  17.5 us
    all_to_all x1, waiting for transfers between devices, on_device(): got = lax.all_to_all(sent, 'zl', 0, 0, tiled=True)  16.2 us
    all_gather x1, blocking collectives, on_device(): fac = lax.all_gather(fac, ('zl', 'c'), axis=1, tiled=True)  14.8 us
    ppermute x8, waiting for transfers between devices, shift(): lax.ppermute(value, axis, [(i, (i + by) % size) for i in range(size)])  12.9 us
    ppermute x2, starting transfers between devices, swap(): return lax.ppermute(value, axis, [(0, 1), (1, 0)])  12.8 us
    ppermute x3, starting transfers between devices, mix(): lax.ppermute(value, axis, [(i, i ^ by) for i in range(lax.axis_size(axis))])  10.4 us
    pallas_call x7, Pallas kernels, local_call(): pl.pallas_call(body, out_shape=out_shape, cost_estimate=pl.CostEstimate(f...  4.84 us
  transfers between devices with their start and end apart: 14, of which 7 were waited for; matrix products, arithmetic and copies ran while one was open for 2% of the time, Pallas kernels for 1%

profile of v17, /device:TPU:24, one launch (start us, length us, event | category | flops | bytes accessed | tf_op | source)
XLA Modules:
  0.0 130.0 jit_solution(17417513944384410709)
XLA Ops:
  0.6 0.9 pad_add_fusion.1
  1.5 10.9 %collective-permute-start = (bf16[64,1024]{1,0:T(8,128)(2,1)S(1)}, bf16[64,1024]{1,0:T(8,128)(2,1)S(1)}, u32[]{:S(2)}, u32[]{:S(2)}) collective-permute-start(bf16[64,1024]{1,0:T(8,128)(2,1)S(1)} %get-tuple-element.24), channel_id=1, source_target_pairs={{0,256},{256,0},{1,257},{257,1},{2,258},{258,2},{3,259},{259,3},{4... | collective-permute-start | bytes 393224 | tf_op jit(solution)/shard_map/ppermute | solution.py:23
  12.5 1.2 pad_add_fusion.refs_0_
  13.6 3.4 %collective-permute-start.3 = (bf16[288,1024]{1,0:T(8,128)(2,1)S(1)}, bf16[288,1024]{1,0:T(8,128)(2,1)S(1)}, u32[]{:S(2)}, u32[]{:S(2)}) collective-permute-start(bf16[288,1024]{1,0:T(8,128)(2,1)S(1)} %pad_add_fusion.refs_0_), channel_id=1, source_target_pairs={{0,64},{64,0},{128,192},{192,128},{1,65},{65,1},{129,193},{193,129... | collective-permute-start | bytes 1769480 | tf_op jit(solution)/shard_map/ppermute | solution.py:32
  17.0 4.0 %collective-permute-start.4 = (bf16[288,1024]{1,0:T(8,128)(2,1)S(1)}, bf16[288,1024]{1,0:T(8,128)(2,1)S(1)}, u32[]{:S(2)}, u32[]{:S(2)}) collective-permute-start(bf16[288,1024]{1,0:T(8,128)(2,1)S(1)} %pad_add_fusion.refs_0_), channel_id=1, source_target_pairs={{0,192},{64,128},{128,64},{192,0},{1,193},{65,129},{129,65},{193,1... | collective-permute-start | bytes 1769480 | tf_op jit(solution)/shard_map/ppermute | solution.py:32
  21.0 0.0 collective-permute-done
  21.0 0.7 pad_maximum_fusion
  21.8 4.7 %collective-permute-start.1 = (bf16[2,64,1024]{2,1,0:T(8,128)(2,1)}, bf16[2,64,1024]{2,1,0:T(8,128)(2,1)S(1)}, u32[]{:S(2)}, u32[]{:S(2)}) collective-permute-start(bf16[2,64,1024]{2,1,0:T(8,128)(2,1)} %pad_maximum_fusion), channel_id=1, source_target_pairs={{0,8},{8,16},{16,24},{24,32},{32,40},{40,48},{48,56},{56,0},{1,9},... | collective-permute-start | bytes 786440 | tf_op jit(solution)/shard_map/ppermute | solution.py:28
  26.5 1.9 %collective-permute-start.2 = (bf16[2,64,1024]{2,1,0:T(8,128)(2,1)}, bf16[2,64,1024]{2,1,0:T(8,128)(2,1)S(1)}, u32[]{:S(2)}, u32[]{:S(2)}) collective-permute-start(bf16[2,64,1024]{2,1,0:T(8,128)(2,1)} %pad_maximum_fusion), channel_id=1, source_target_pairs={{0,56},{8,0},{16,8},{24,16},{32,24},{40,32},{48,40},{56,48},{1,57}... | collective-permute-start | bytes 786440 | tf_op jit(solution)/shard_map/ppermute | solution.py:28
  28.4 3.1 %collective-permute-done.1 = bf16[2,64,1024]{2,1,0:T(8,128)(2,1)S(1)} collective-permute-done((bf16[2,64,1024]{2,1,0:T(8,128)(2,1)}, bf16[2,64,1024]{2,1,0:T(8,128)(2,1)S(1)}, u32[]{:S(2)}, u32[]{:S(2)}) %collective-permute-start.1) | collective-permute-done | bytes 262176 | tf_op jit(solution)/shard_map/ppermute | solution.py:28
  31.5 5.5 %collective-permute-start.5 = (bf16[2,64,1024]{2,1,0:T(8,128)(2,1)S(1)}, bf16[2,64,1024]{2,1,0:T(8,128)(2,1)S(1)}, u32[]{:S(2)}, u32[]{:S(2)}) collective-permute-start(bf16[2,64,1024]{2,1,0:T(8,128)(2,1)S(1)} %collective-permute-done.1), channel_id=1, source_target_pairs={{0,8},{8,16},{16,24},{24,32},{32,40},{40,48},{48,56},{56,0},{1,9},... | collective-permute-start | bytes 786440 | tf_op jit(solution)/shard_map/ppermute | solution.py:28
  37.0 0.0 collective-permute-done.2.value
  37.0 0.0 collective-permute-done.3.rest_0_.value
  37.0 0.0 collective-permute-done.4.rest_1_.refs_2_
  37.0 1.9 %collective-permute-start.6 = (bf16[2,64,1024]{2,1,0:T(8,128)(2,1)S(1)}, bf16[2,64,1024]{2,1,0:T(8,128)(2,1)S(1)}, u32[]{:S(2)}, u32[]{:S(2)}) collective-permute-start(bf16[2,64,1024]{2,1,0:T(8,128)(2,1)S(1)} %shard_map.86), channel_id=1, source_target_pairs={{0,56},{8,0},{16,8},{24,16},{32,24},{40,32},{48,40},{56,48},{1,57}... | collective-permute-start | bytes 786440 | tf_op jit(solution)/shard_map/ppermute | solution.py:28
  39.0 1.8 %collective-permute-done.5.rest_0_ = bf16[2,64,1024]{2,1,0:T(8,128)(2,1)S(1)} collective-permute-done((bf16[2,64,1024]{2,1,0:T(8,128)(2,1)S(1)}, bf16[2,64,1024]{2,1,0:T(8,128)(2,1)S(1)}, u32[]{:S(2)}, u32[]{:S(2)}) %collective-permute-start.5) | collective-permute-done | bytes 262176 | tf_op jit(solution)/shard_map/ppermute | solution.py:28
  40.8 3.0 %collective-permute-start.11 = (bf16[288,1024]{1,0:T(8,128)(2,1)S(1)}, bf16[288,1024]{1,0:T(8,128)(2,1)S(1)}, u32[]{:S(2)}, u32[]{:S(2)}) collective-permute-start(bf16[288,1024]{1,0:T(8,128)(2,1)S(1)} %shard_map.87.refs_1_), channel_id=1, source_target_pairs={{0,192},{64,128},{128,64},{192,0},{1,193},{65,129},{129,65},{193,1... | collective-permute-start | bytes 1769480 | tf_op jit(solution)/shard_map/ppermute | solution.py:32
  43.9 5.6 %collective-permute-start.7 = (bf16[2,64,1024]{2,1,0:T(8,128)(2,1)S(1)}, bf16[2,64,1024]{2,1,0:T(8,128)(2,1)S(1)}, u32[]{:S(2)}, u32[]{:S(2)}) collective-permute-start(bf16[2,64,1024]{2,1,0:T(8,128)(2,1)S(1)} %collective-permute-done.5.rest_0_), channel_id=1, source_target_pairs={{0,8},{8,16},{16,24},{24,32},{32,40},{40,48},{48,56},{56,0},{1,9},... | collective-permute-start | bytes 786440 | tf_op jit(solution)/shard_map/ppermute | solution.py:28
  49.5 0.0 collective-permute-done.6
  49.5 1.9 %collective-permute-start.8 = (bf16[2,64,1024]{2,1,0:T(8,128)(2,1)S(1)}, bf16[2,64,1024]{2,1,0:T(8,128)(2,1)S(1)}, u32[]{:S(2)}, u32[]{:S(2)}) collective-permute-start(bf16[2,64,1024]{2,1,0:T(8,128)(2,1)S(1)} %collective-permute-done.6), channel_id=1, source_target_pairs={{0,56},{8,0},{16,8},{24,16},{32,24},{40,32},{48,40},{56,48},{1,57}... | collective-permute-start | bytes 786440 | tf_op jit(solution)/shard_map/ppermute | solution.py:28
  51.5 1.9 %collective-permute-done.7 = bf16[2,64,1024]{2,1,0:T(8,128)(2,1)S(1)} collective-permute-done((bf16[2,64,1024]{2,1,0:T(8,128)(2,1)S(1)}, bf16[2,64,1024]{2,1,0:T(8,128)(2,1)S(1)}, u32[]{:S(2)}, u32[]{:S(2)}) %collective-permute-start.7) | collective-permute-done | bytes 262176 | tf_op jit(solution)/shard_map/ppermute | solution.py:28
  53.4 5.6 %collective-permute-start.9 = (bf16[1,64,1024]{2,1,0:T(8,128)(2,1)S(1)}, bf16[1,64,1024]{2,1,0:T(8,128)(2,1)S(1)}, u32[]{:S(2)}, u32[]{:S(2)}) collective-permute-start(bf16[1,64,1024]{2,1,0:T(8,128)(2,1)S(1)} %slice.88), channel_id=1, source_target_pairs={{0,8},{8,16},{16,24},{24,32},{32,40},{40,48},{48,56},{56,0},{1,9},... | collective-permute-start | bytes 393224 | tf_op jit(solution)/shard_map/ppermute | solution.py:28
  59.0 0.0 collective-permute-done.8
  59.0 1.9 %collective-permute-start.10 = (bf16[1,64,1024]{2,1,0:T(8,128)(2,1)S(1)}, bf16[1,64,1024]{2,1,0:T(8,128)(2,1)S(1)}, u32[]{:S(2)}, u32[]{:S(2)}) collective-permute-start(bf16[1,64,1024]{2,1,0:T(8,128)(2,1)S(1)} %slice.90), channel_id=1, source_target_pairs={{0,56},{8,0},{16,8},{24,16},{32,24},{40,32},{48,40},{56,48},{1,57}... | collective-permute-start | bytes 393224 | tf_op jit(solution)/shard_map/ppermute | solution.py:28
  61.0 0.5 collective-permute-done.9
  61.5 5.6 %collective-permute-done.10 = bf16[1,64,1024]{2,1,0:T(8,128)(2,1)S(1)} collective-permute-done((bf16[1,64,1024]{2,1,0:T(8,128)(2,1)S(1)}, bf16[1,64,1024]{2,1,0:T(8,128)(2,1)S(1)}, u32[]{:S(2)}, u32[]{:S(2)}) %collective-permute-start.10) | collective-permute-done | bytes 131104 | tf_op jit(solution)/shard_map/ppermute | solution.py:28
  67.1 0.0 collective-permute-done.11.refs_3_
  67.1 0.9 shard_map.89
  68.0 1.9 %collective-permute-start.12 = (f32[256,1152]{1,0:T(8,128)S(1)}, f32[256,1152]{1,0:T(8,128)S(1)}, u32[]{:S(2)}, u32[]{:S(2)}) collective-permute-start(f32[256,1152]{1,0:T(8,128)S(1)} %shard_map.89), channel_id=1, source_target_pairs={{0,1},{1,0},{2,3},{3,2},{4,5},{5,4},{6,7},{7,6},{8,9},{9,8},{10,11... | collective-permute-start | bytes 3538952 | tf_op jit(solution)/shard_map/ppermute | solution.py:23
  70.0 0.9 shard_map.88
  70.9 1.9 %collective-permute-done.12 = f32[256,1152]{1,0:T(8,128)S(1)} collective-permute-done((f32[256,1152]{1,0:T(8,128)S(1)}, f32[256,1152]{1,0:T(8,128)S(1)}, u32[]{:S(2)}, u32[]{:S(2)}) %collective-permute-start.12) | collective-permute-done | bytes 1179680 | tf_op jit(solution)/shard_map/ppermute | solution.py:23
  72.8 1.0 add_convert_fusion
  73.7 4.6 %all-to-all-start = ((f16[4,64,1152]{2,1,0:T(8,128)(2,1)}), f16[4,64,1152]{2,1,0:T(8,128)(2,1)S(1)}, u32[]{:S(2)}, u32[]{:S(2)}) async-start(f16[4,64,1152]{2,1,0:T(8,128)(2,1)} %bitcast.7), calls=%async_computation | async-start | bytes 1179648 | tf_op jit(solution)/shard_map/all_to_all | solution.py:213
  78.3 16.2 %all-to-all-done = f16[4,64,1152]{2,1,0:T(8,128)(2,1)S(1)} async-done(((f16[4,64,1152]{2,1,0:T(8,128)(2,1)}), f16[4,64,1152]{2,1,0:T(8,128)(2,1)S(1)}, u32[]{:S(2)}, u32[]{:S(2)}) %all-to-all-start) | async-done | bytes 589856 | tf_op jit(solution)/shard_map/all_to_all | solution.py:213
  94.5 0.1 convert_reduce_fusion.proj
  94.6 0.7 shard_map.90
  95.3 14.8 %all_gather.3.fac = bf16[64,4096]{1,0:T(8,128)(2,1)S(1)} all-gather(bf16[64,512]{1,0:T(8,128)(2,1)S(1)} %shard_map.90), channel_id=1, replica_groups=mesh['zh'=2,'x'=4,'y'=8,'zl'=4,'c'=2] {'zl','c'}, dimensions={1}, use_global_device_ids=true | all-gather | bytes 589824 | tf_op jit(solution)/shard_map/all_gather | solution.py:227
  110.2 1.4 %shard_map.91 = (bf16[4,112,1024]{2,1,0:T(8,128)(2,1)S(1)}, f32[112,1024]{1,0:T(8,128)S(1)}) custom-call(s32[1]{0:T(128)} %bitcast.place, bf16[64,4096]{1,0:T(8,128)(2,1)S(1)} %all_gather.3.fac, bf16[512,1024]{1,0:T(8,128)(2,1)S(1)} %bitcast.13), custom_call_target="tpu_custom_call" | custom-call | flops 469762048 | bytes 1048576 | tf_op jit(solution)/shard_map/pallas_call | solution.py:36
  111.6 0.0 copy-start
  111.6 0.0 copy-start.1
  111.6 17.5 %all_to_all.10.away = bf16[4,112,1024]{2,1,0:T(8,128)(2,1)S(1)} all-to-all(bf16[4,112,1024]{2,1,0:T(8,128)(2,1)S(1)} %get-tuple-element.4), channel_id=1, replica_groups=mesh['zh'=2,'x'=4,'y'=8,'zl'=4,'c'=2] {'x'}, dimensions={0} | all-to-all | bytes 1835008 | tf_op jit(solution)/shard_map/all_to_all | solution.py:244
  129.1 0.0 copy-done
  129.1 0.0 copy-done.1
  129.1 0.9 shard_map.92
  (13 shorter events, 0.2 us)
Async XLA Ops:
  1.5 19.5 %collective-permute-start = (bf16[64,1024]{1,0:T(8,128)(2,1)S(1)}, bf16[64,1024]{1,0:T(8,128)(2,1)S(1)}, u32[]{:S(2)}, u32[]{:S(2)}) collective-permute-start(bf16[64,1024]{1,0:T(8,128)(2,1)S(1)} %get-tuple-element.24), channel_id=1, source_target_pairs={{0,256},{256,0},{1,257},{257,1},{2,258},{258,2},{3,259},{259,3},{4... | collective-permute-start | bytes 393224 | tf_op jit(solution)/shard_map/ppermute | solution.py:23
  13.6 23.4 %collective-permute-start.3 = (bf16[288,1024]{1,0:T(8,128)(2,1)S(1)}, bf16[288,1024]{1,0:T(8,128)(2,1)S(1)}, u32[]{:S(2)}, u32[]{:S(2)}) collective-permute-start(bf16[288,1024]{1,0:T(8,128)(2,1)S(1)} %pad_add_fusion.refs_0_), channel_id=1, source_target_pairs={{0,64},{64,0},{128,192},{192,128},{1,65},{65,1},{129,193},{193,129... | collective-permute-start | bytes 1769480 | tf_op jit(solution)/shard_map/ppermute | solution.py:32
  17.0 20.0 %collective-permute-start.4 = (bf16[288,1024]{1,0:T(8,128)(2,1)S(1)}, bf16[288,1024]{1,0:T(8,128)(2,1)S(1)}, u32[]{:S(2)}, u32[]{:S(2)}) collective-permute-start(bf16[288,1024]{1,0:T(8,128)(2,1)S(1)} %pad_add_fusion.refs_0_), channel_id=1, source_target_pairs={{0,192},{64,128},{128,64},{192,0},{1,193},{65,129},{129,65},{193,1... | collective-permute-start | bytes 1769480 | tf_op jit(solution)/shard_map/ppermute | solution.py:32
  21.8 9.7 %collective-permute-start.1 = (bf16[2,64,1024]{2,1,0:T(8,128)(2,1)}, bf16[2,64,1024]{2,1,0:T(8,128)(2,1)S(1)}, u32[]{:S(2)}, u32[]{:S(2)}) collective-permute-start(bf16[2,64,1024]{2,1,0:T(8,128)(2,1)} %pad_maximum_fusion), channel_id=1, source_target_pairs={{0,8},{8,16},{16,24},{24,32},{32,40},{40,48},{48,56},{56,0},{1,9},... | collective-permute-start | bytes 786440 | tf_op jit(solution)/shard_map/ppermute | solution.py:28
  26.5 10.5 %collective-permute-start.2 = (bf16[2,64,1024]{2,1,0:T(8,128)(2,1)}, bf16[2,64,1024]{2,1,0:T(8,128)(2,1)S(1)}, u32[]{:S(2)}, u32[]{:S(2)}) collective-permute-start(bf16[2,64,1024]{2,1,0:T(8,128)(2,1)} %pad_maximum_fusion), channel_id=1, source_target_pairs={{0,56},{8,0},{16,8},{24,16},{32,24},{40,32},{48,40},{56,48},{1,57}... | collective-permute-start | bytes 786440 | tf_op jit(solution)/shard_map/ppermute | solution.py:28
  31.5 9.4 %collective-permute-start.5 = (bf16[2,64,1024]{2,1,0:T(8,128)(2,1)S(1)}, bf16[2,64,1024]{2,1,0:T(8,128)(2,1)S(1)}, u32[]{:S(2)}, u32[]{:S(2)}) collective-permute-start(bf16[2,64,1024]{2,1,0:T(8,128)(2,1)S(1)} %collective-permute-done.1), channel_id=1, source_target_pairs={{0,8},{8,16},{16,24},{24,32},{32,40},{40,48},{48,56},{56,0},{1,9},... | collective-permute-start | bytes 786440 | tf_op jit(solution)/shard_map/ppermute | solution.py:28
  37.0 12.5 %collective-permute-start.6 = (bf16[2,64,1024]{2,1,0:T(8,128)(2,1)S(1)}, bf16[2,64,1024]{2,1,0:T(8,128)(2,1)S(1)}, u32[]{:S(2)}, u32[]{:S(2)}) collective-permute-start(bf16[2,64,1024]{2,1,0:T(8,128)(2,1)S(1)} %shard_map.86), channel_id=1, source_target_pairs={{0,56},{8,0},{16,8},{24,16},{32,24},{40,32},{48,40},{56,48},{1,57}... | collective-permute-start | bytes 786440 | tf_op jit(solution)/shard_map/ppermute | solution.py:28
  40.8 26.3 %collective-permute-start.11 = (bf16[288,1024]{1,0:T(8,128)(2,1)S(1)}, bf16[288,1024]{1,0:T(8,128)(2,1)S(1)}, u32[]{:S(2)}, u32[]{:S(2)}) collective-permute-start(bf16[288,1024]{1,0:T(8,128)(2,1)S(1)} %shard_map.87.refs_1_), channel_id=1, source_target_pairs={{0,192},{64,128},{128,64},{192,0},{1,193},{65,129},{129,65},{193,1... | collective-permute-start | bytes 1769480 | tf_op jit(solution)/shard_map/ppermute | solution.py:32
  43.9 9.5 %collective-permute-start.7 = (bf16[2,64,1024]{2,1,0:T(8,128)(2,1)S(1)}, bf16[2,64,1024]{2,1,0:T(8,128)(2,1)S(1)}, u32[]{:S(2)}, u32[]{:S(2)}) collective-permute-start(bf16[2,64,1024]{2,1,0:T(8,128)(2,1)S(1)} %collective-permute-done.5.rest_0_), channel_id=1, source_target_pairs={{0,8},{8,16},{16,24},{24,32},{32,40},{40,48},{48,56},{56,0},{1,9},... | collective-permute-start | bytes 786440 | tf_op jit(solution)/shard_map/ppermute | solution.py:28
  49.5 9.5 %collective-permute-start.8 = (bf16[2,64,1024]{2,1,0:T(8,128)(2,1)S(1)}, bf16[2,64,1024]{2,1,0:T(8,128)(2,1)S(1)}, u32[]{:S(2)}, u32[]{:S(2)}) collective-permute-start(bf16[2,64,1024]{2,1,0:T(8,128)(2,1)S(1)} %collective-permute-done.6), channel_id=1, source_target_pairs={{0,56},{8,0},{16,8},{24,16},{32,24},{40,32},{48,40},{56,48},{1,57}... | collective-permute-start | bytes 786440 | tf_op jit(solution)/shard_map/ppermute | solution.py:28
  53.4 8.1 %collective-permute-start.9 = (bf16[1,64,1024]{2,1,0:T(8,128)(2,1)S(1)}, bf16[1,64,1024]{2,1,0:T(8,128)(2,1)S(1)}, u32[]{:S(2)}, u32[]{:S(2)}) collective-permute-start(bf16[1,64,1024]{2,1,0:T(8,128)(2,1)S(1)} %slice.88), channel_id=1, source_target_pairs={{0,8},{8,16},{16,24},{24,32},{32,40},{40,48},{48,56},{56,0},{1,9},... | collective-permute-start | bytes 393224 | tf_op jit(solution)/shard_map/ppermute | solution.py:28
  59.0 8.1 %collective-permute-start.10 = (bf16[1,64,1024]{2,1,0:T(8,128)(2,1)S(1)}, bf16[1,64,1024]{2,1,0:T(8,128)(2,1)S(1)}, u32[]{:S(2)}, u32[]{:S(2)}) collective-permute-start(bf16[1,64,1024]{2,1,0:T(8,128)(2,1)S(1)} %slice.90), channel_id=1, source_target_pairs={{0,56},{8,0},{16,8},{24,16},{32,24},{40,32},{48,40},{56,48},{1,57}... | collective-permute-start | bytes 393224 | tf_op jit(solution)/shard_map/ppermute | solution.py:28
  68.0 4.7 %collective-permute-start.12 = (f32[256,1152]{1,0:T(8,128)S(1)}, f32[256,1152]{1,0:T(8,128)S(1)}, u32[]{:S(2)}, u32[]{:S(2)}) collective-permute-start(f32[256,1152]{1,0:T(8,128)S(1)} %shard_map.89), channel_id=1, source_target_pairs={{0,1},{1,0},{2,3},{3,2},{4,5},{5,4},{6,7},{7,6},{8,9},{9,8},{10,11... | collective-permute-start | bytes 3538952 | tf_op jit(solution)/shard_map/ppermute | solution.py:23
  73.7 20.8 %all-to-all-start = ((f16[4,64,1152]{2,1,0:T(8,128)(2,1)}), f16[4,64,1152]{2,1,0:T(8,128)(2,1)S(1)}, u32[]{:S(2)}, u32[]{:S(2)}) async-start(f16[4,64,1152]{2,1,0:T(8,128)(2,1)} %bitcast.7), calls=%async_computation | async-start | bytes 1179648 | tf_op jit(solution)/shard_map/all_to_all | solution.py:213
  111.6 17.5 %copy-start = (bf16[56,1024]{1,0:T(8,128)(2,1)S(1)}, bf16[56,1024]{1,0:T(8,128)(2,1)}, u32[]{:S(2)}) copy-start(bf16[56,1024]{1,0:T(8,128)(2,1)} %up_probe.1) | copy-start | bytes 344068
  111.6 17.5 %copy-start.1 = (bf16[56,1024]{1,0:T(8,128)(2,1)S(1)}, bf16[56,1024]{1,0:T(8,128)(2,1)}, u32[]{:S(2)}) copy-start(bf16[56,1024]{1,0:T(8,128)(2,1)} %gate_probe.1) | copy-start | bytes 344068
